TPU v7x, 128 devices: a whole 4x4x4 slice. The times are simulated.
128 devices in a mesh: gx: 8 (over y, core), gy: 16 (over z, x).
Axes of the slice: x: 4, y: 4, z: 4, core: 2. Of those that a mesh axis runs over, the one named last changes fastest.
Arguments:
- features: bfloat16 [32, 256, 1536], P('gx', 'gy'), may hold values from -6 to 6
- block_mask: int32 [8, 64, 4], P('gx', 'gy'), may hold values 0 or 1
- weight_first: bfloat16 [27, 96, 128], replicated, may hold values from -0.125 to 0.125
- weight_second: bfloat16 [27, 128, 128], replicated, may hold values from -0.109375 to 0.109375
- weight_down: bfloat16 [8, 128, 128], replicated, may hold values from -0.1875 to 0.1875
- owners: int32 [8, 16, 16, 1], P('gx', 'gy'), may hold values from 0 to 15; in each aligned block of 16 rows (0 to 15, 16 to 31, ..., all dimensions but the last counted through in order) at most 2 rows name the same one
- moved_grad: bfloat16 [8, 16, 32, 1024], P('gx', 'gy'), may hold values from -0.5 to 0.5
Outputs:
- moved: bfloat16 [8, 16, 32, 1024], P('gx', 'gy')
- grad_first: float32 [27, 96, 128], replicated
- grad_second: float32 [27, 128, 128], replicated
- grad_down: float32 [8, 128, 128], replicated
Inputs may be any that keep to these rules, and one draw needn't show every extreme that they name: `owners`: within one device's 16 rows no value appears more than 2 times; in some device's rows one value appears exactly 2 times.
All inputs are finite; a program needn't handle non-finite values. No bound on the sum of `block_mask` on one device may be relied on, other than what follows from the above.
Results may differ from a plain program's by a relative error of at most 0.012.
Values may be sent and summed in bfloat16 or wider, within the bound.
No kernel may reach another device: no remote copies, remote signals or barrier semaphores. Data moves between devices by JAX's collectives and lax.ppermute only.
A program may use at most 64 MiB of HBM per device.

v0:
```python
import jax
import jax.numpy as jnp
from jax import lax
from jax.sharding import PartitionSpec as P


def padded_2(block, sides, width):
    for axis, dim in sides:
        count = lax.axis_size(axis)
        forward = [(i, i + 1) for i in range(count - 1)]
        backward = [(target, source) for source, target in forward]
        low = lax.ppermute(
            lax.slice_in_dim(block, block.shape[dim] - width, None, axis=dim), axis, forward
        )
        high = lax.ppermute(lax.slice_in_dim(block, 0, width, axis=dim), axis, backward)
        block = jnp.concatenate([low, block, high], axis=dim)
    return block


def silu_grad(v):
    s = jax.nn.sigmoid(v)
    return s * (1.0 + v * (1.0 - s))


def extend(v):
    padded = padded_2(v, (("gx", 0), ("gy", 1)), 1)
    return jnp.pad(padded, ((0, 0), (0, 0), (1, 1), (0, 0)))


def taps_forward(padded, w, sx, sy, sz):
    total = jnp.zeros((sx * sy * sz, w.shape[2]), jnp.float32)
    for t in range(27):
        i, j, k = (t // 9, t // 3 % 3, t % 3)
        window = padded[i : i + sx, j : j + sy, k : k + sz].reshape(sx * sy * sz, w.shape[1])
        total = total + jnp.dot(window, w[t], preferred_element_type=jnp.float32)
    return total.reshape(sx, sy, sz, w.shape[2])


def taps_backward(padded, w, sx, sy, sz):
    total = jnp.zeros((sx * sy * sz, w.shape[1]), jnp.float32)
    for t in range(27):
        i, j, k = (t // 9, t // 3 % 3, t % 3)
        window = padded[2 - i : 2 - i + sx, 2 - j : 2 - j + sy, 2 - k : 2 - k + sz].reshape(
            sx * sy * sz, w.shape[2]
        )
        total = total + lax.dot_general(
            window, w[t], (((1,), (1,)), ((), ())), preferred_element_type=jnp.float32
        )
    return total.reshape(sx, sy, sz, w.shape[1])


def taps_weight(padded, grads, sx, sy, sz):
    flat = grads.reshape(sx * sy * sz, grads.shape[3])
    terms = []
    for t in range(27):
        i, j, k = (t // 9, t // 3 % 3, t % 3)
        window = padded[i : i + sx, j : j + sy, k : k + sz].reshape(sx * sy * sz, padded.shape[3])
        terms.append(
            lax.dot_general(
                window, flat, (((0,), (0,)), ((), ())), preferred_element_type=jnp.float32
            )
        )
    return jnp.stack(terms)


def per_device(features, block_mask, weight_first, weight_second, weight_down, owners, moved_grad):
    chan_in = weight_first.shape[1]
    chan = weight_first.shape[2]
    sx, sy = (features.shape[0], features.shape[1])
    sz = features.shape[2] // chan_in
    peers = lax.axis_size("gy")
    slots = moved_grad.shape[2]
    bricks_dev = sx // 4 * (sy // 4) * (sz // 4)
    blocks = block_mask.astype(jnp.float32)
    active = jnp.broadcast_to(
        blocks[:, None, :, None, :, None], (sx // 4, 4, sy // 4, 4, sz // 4, 4)
    ).reshape(sx, sy, sz)[..., None]
    inputs = (features.reshape(sx, sy, sz, chan_in) * active).astype(jnp.bfloat16)
    padded_in = extend(inputs)
    pre_first = active * taps_forward(padded_in, weight_first, sx, sy, sz)
    first = jax.nn.silu(pre_first).astype(jnp.bfloat16)
    padded_first = extend(first)
    pre_second = active * taps_forward(padded_first, weight_second, sx, sy, sz) + first.astype(
        jnp.float32
    )
    second = jax.nn.silu(pre_second).astype(jnp.bfloat16)
    second_r = second.reshape(sx // 2, 2, sy // 2, 2, sz // 2, 2, chan)
    down_w = weight_down.reshape(2, 2, 2, chan, chan)
    coarse = jnp.einsum(
        "xaybzcd,abcde->xyze", second_r, down_w, preferred_element_type=jnp.float32
    ).astype(jnp.bfloat16)
    bricks = (
        coarse.reshape(sx // 4, 2, sy // 4, 2, sz // 4, 2, chan)
        .transpose(0, 2, 4, 1, 3, 5, 6)
        .reshape(bricks_dev, 8 * chan)
    )
    dest = owners.reshape(bricks_dev)
    onehot = (dest[:, None] == jnp.arange(peers, dtype=jnp.int32)[None, :]).astype(jnp.int32)
    rank = jnp.sum((jnp.cumsum(onehot, axis=0) - onehot) * onehot, axis=1)
    slot_of = dest * (slots // peers) + rank
    select = slot_of[:, None] == jnp.arange(slots, dtype=jnp.int32)[None, :]
    select_b = select.astype(jnp.bfloat16)
    outgoing = lax.dot_general(
        select_b, bricks, (((0,), (0,)), ((), ())), preferred_element_type=jnp.float32
    ).astype(jnp.bfloat16)
    arrived = lax.all_to_all(outgoing, "gy", split_axis=0, concat_axis=0, tiled=True)
    moved = arrived.reshape(1, 1, slots, 8 * chan)
    returned = lax.all_to_all(
        moved_grad.reshape(slots, 8 * chan), "gy", split_axis=0, concat_axis=0, tiled=True
    )
    grad_bricks = jnp.dot(select.astype(jnp.bfloat16), returned, preferred_element_type=jnp.float32)
    grad_coarse = grad_bricks.astype(jnp.bfloat16).reshape(sx // 4, sy // 4, sz // 4, 2, 2, 2, chan)
    grad_coarse = grad_coarse.transpose(0, 3, 1, 4, 2, 5, 6).reshape(
        sx // 2, sy // 2, sz // 2, chan
    )
    grad_down = jnp.einsum(
        "xaybzcd,xyze->abcde", second_r, grad_coarse, preferred_element_type=jnp.float32
    ).reshape(8, chan, chan)
    grad_act = jnp.einsum(
        "xyze,abcde->xaybzcd", grad_coarse, down_w, preferred_element_type=jnp.float32
    ).reshape(sx, sy, sz, chan)
    grad_pre_second = (active * grad_act * silu_grad(pre_second)).astype(jnp.bfloat16)
    grad_second = taps_weight(padded_first, grad_pre_second, sx, sy, sz)
    padded_grad = extend(grad_pre_second)
    grad_first_act = grad_pre_second.astype(jnp.float32) + taps_backward(
        padded_grad, weight_second, sx, sy, sz
    )
    grad_pre_first = (active * grad_first_act * silu_grad(pre_first)).astype(jnp.bfloat16)
    grad_first = taps_weight(padded_in, grad_pre_first, sx, sy, sz)
    grad_first, grad_second, grad_down = lax.psum(
        (grad_first, grad_second, grad_down), ("gx", "gy")
    )
    return (moved, grad_first, grad_second, grad_down)


def solution(mesh):
    in_specs = (
        P("gx", "gy", None),
        P("gx", "gy", None),
        P(),
        P(),
        P(),
        P("gx", "gy", None, None),
        P("gx", "gy", None, None),
    )
    out_specs = (P("gx", "gy", None, None), P(), P(), P())
    return jax.shard_map(
        per_device, mesh=mesh, in_specs=in_specs, out_specs=out_specs, check_vma=False
    )
```

profile of v0, /device:TPU:1, one launch (start us, length us, event | category | flops | bytes accessed | tf_op | source)
XLA Modules:
  0.0 279.4 jit_solution(9005948695011541003)
XLA Ops:
  7.2 0.8 convert_bitcast_fusion
  8.1 1.1 reshape.501
  9.4 4.6 %collective-permute-start = (bf16[1,16,16,96]{3,2,1,0:T(8,128)(2,1)S(1)}, bf16[1,16,16,96]{3,2,1,0:T(8,128)(2,1)S(1)}, u32[]{:S(2)}, u32[]{:S(2)}) collective-permute-start(bf16[1,16,16,96]{3,2,1,0:T(8,128)(2,1)S(1)} %get-tuple-element.105), channel_id=1, source_target_pairs={{0,16},{16,32},{32,48},{48,64},{64,80},{80,96},{96,112},{1,17},{17... | collective-permute-start | bytes 147464 | tf_op jit(solution)/shard_map/ppermute | solution.py:12
  14.0 1.9 collective-permute-start.1
  16.0 0.7 all_to_all.16
  16.6 7.6 %all-to-all-start.1 = ((bf16[16,2,1024]{2,1,0:T(2,128)(2,1)}), bf16[16,2,1024]{2,1,0:T(2,128)(2,1)S(1)}, u32[]{:S(2)}, u32[]{:S(2)}) async-start(bf16[16,2,1024]{2,1,0:T(2,128)(2,1)} %all_to_all.16), calls=%async_computation.1 | async-start | bytes 131072 | tf_op jit(solution)/shard_map/all_to_all | solution.py:108
  25.6 3.3 %collective-permute-start.2 = (bf16[6,1,16,96]{3,2,1,0:T(8,128)(2,1)S(1)}, bf16[6,1,16,96]{3,2,1,0:T(8,128)(2,1)S(1)}, u32[]{:S(2)}, u32[]{:S(2)}) collective-permute-start(bf16[6,1,16,96]{3,2,1,0:T(8,128)(2,1)S(1)} %get-tuple-element.93), channel_id=1, source_target_pairs={{0,1},{1,2},{2,3},{3,4},{4,5},{5,6},{6,7},{7,8},{8,9},{9,10},{10,1... | collective-permute-start | bytes 55304 | tf_op jit(solution)/shard_map/ppermute | solution.py:12
  28.9 1.3 collective-permute-start.3
  30.3 0.5 all-to-all-done.1
  31.0 2.4 collective-permute-done.3
  33.4 0.3 select_maximum_fusion.6
  33.8 0.7 fusion.303
  34.5 0.3 copy-done.6
  35.6 0.3 fusion.308
  40.8 0.3 multiply_convert_fusion.8
  41.3 5.7 %collective-permute-start.4 = (bf16[1,16,16,128]{3,2,1,0:T(8,128)(2,1)S(1)}, bf16[1,16,16,128]{3,2,1,0:T(8,128)(2,1)S(1)}, u32[]{:S(2)}, u32[]{:S(2)}) collective-permute-start(bf16[1,16,16,128]{3,2,1,0:T(8,128)(2,1)S(1)} %get-tuple-element.101), channel_id=1, source_target_pairs={{0,16},{16,32},{32,48},{48,64},{64,80},{80,96},{96,112},{1,17},{17... | collective-permute-start | bytes 196616 | tf_op jit(solution)/shard_map/ppermute | solution.py:12
  47.0 1.9 collective-permute-start.5
  49.2 0.3 copy.20
  49.5 3.1 %collective-permute-done.5 = bf16[1,16,16,128]{3,2,1,0:T(8,128)(2,1)S(1)} collective-permute-done((bf16[1,16,16,128]{3,2,1,0:T(8,128)(2,1)S(1)}, bf16[1,16,16,128]{3,2,1,0:T(8,128)(2,1)S(1)}, u32[]{:S(2)}, u32[]{:S(2)}) %collective-permute-start.5) | collective-permute-done | bytes 65568 | tf_op jit(solution)/shard_map/ppermute | solution.py:15
  52.6 3.1 %collective-permute-start.6 = (bf16[6,1,16,128]{3,2,1,0:T(8,128)(2,1)S(1)}, bf16[6,1,16,128]{3,2,1,0:T(8,128)(2,1)S(1)}, u32[]{:S(2)}, u32[]{:S(2)}) collective-permute-start(bf16[6,1,16,128]{3,2,1,0:T(8,128)(2,1)S(1)} %get-tuple-element.89), channel_id=1, source_target_pairs={{0,1},{1,2},{2,3},{3,4},{4,5},{5,6},{6,7},{7,8},{8,9},{9,10},{10,1... | collective-permute-start | bytes 73736 | tf_op jit(solution)/shard_map/ppermute | solution.py:12
  55.7 1.5 collective-permute-start.7
  57.2 3.0 %collective-permute-done.7 = bf16[6,1,16,128]{3,2,1,0:T(8,128)(2,1)S(1)} collective-permute-done((bf16[6,1,16,128]{3,2,1,0:T(8,128)(2,1)S(1)}, bf16[6,1,16,128]{3,2,1,0:T(8,128)(2,1)S(1)}, u32[]{:S(2)}, u32[]{:S(2)}) %collective-permute-start.7) | collective-permute-done | bytes 24608 | tf_op jit(solution)/shard_map/ppermute | solution.py:15
  60.5 0.4 select_maximum_fusion.4
  60.8 0.8 fusion.302
  61.6 0.4 copy-done.1
  67.8 0.5 multiply_convert_fusion.5
  68.2 0.5 multiply_convert_fusion.6
  68.7 0.3 fusion.34
  69.3 0.3 fusion.33
  69.6 0.3 fusion.32
  70.1 0.3 fusion.31
  70.4 0.3 fusion.30
  71.0 0.3 fusion.29
  71.2 0.3 fusion.28
  71.8 0.3 fusion.27
  72.1 0.3 fusion.26
  72.4 0.5 multiply_convert_fusion
  73.3 0.3 fusion.24
  73.6 0.3 fusion.23
  74.2 0.3 fusion.22
  74.5 0.3 fusion.21
  75.0 0.3 fusion.20
  75.3 0.3 fusion.19
  75.9 0.3 fusion.18
  76.1 0.3 fusion.17
  76.7 0.3 fusion.16
  77.0 3.3 %collective-permute-start.8 = (bf16[1,16,16,128]{3,2,1,0:T(8,128)(2,1)S(1)}, bf16[1,16,16,128]{3,2,1,0:T(8,128)(2,1)S(1)}, u32[]{:S(2)}, u32[]{:S(2)}) collective-permute-start(bf16[1,16,16,128]{3,2,1,0:T(8,128)(2,1)S(1)} %get-tuple-element.97), channel_id=1, source_target_pairs={{0,16},{16,32},{32,48},{48,64},{64,80},{80,96},{96,112},{1,17},{17... | collective-permute-start | bytes 196616 | tf_op jit(solution)/shard_map/ppermute | solution.py:12
  80.3 1.9 collective-permute-start.9
  82.2 1.1 convolution_bitcast_fusion
  83.3 2.6 collective-permute-done.9
  85.8 4.4 %collective-permute-start.10 = (bf16[6,1,16,128]{3,2,1,0:T(8,128)(2,1)S(1)}, bf16[6,1,16,128]{3,2,1,0:T(8,128)(2,1)S(1)}, u32[]{:S(2)}, u32[]{:S(2)}) collective-permute-start(bf16[6,1,16,128]{3,2,1,0:T(8,128)(2,1)S(1)} %get-tuple-element.85), channel_id=1, source_target_pairs={{0,1},{1,2},{2,3},{3,4},{4,5},{5,6},{6,7},{7,8},{8,9},{9,10},{10,1... | collective-permute-start | bytes 73736 | tf_op jit(solution)/shard_map/ppermute | solution.py:12
  90.2 1.5 collective-permute-start.11
  91.8 3.3 %collective-permute-done.11 = bf16[6,1,16,128]{3,2,1,0:T(8,128)(2,1)S(1)} collective-permute-done((bf16[6,1,16,128]{3,2,1,0:T(8,128)(2,1)S(1)}, bf16[6,1,16,128]{3,2,1,0:T(8,128)(2,1)S(1)}, u32[]{:S(2)}, u32[]{:S(2)}) %collective-permute-start.11) | collective-permute-done | bytes 24608 | tf_op jit(solution)/shard_map/ppermute | solution.py:15
  95.4 0.4 select_maximum_fusion
  95.7 0.8 fusion.301
  102.7 0.4 multiply_convert_fusion.3
  103.1 0.3 multiply_convert_fusion.4
  110.5 1.1 copy-done.4
  112.2 14.3 %all_to_all.21 = bf16[16,2,1024]{2,1,0:T(2,128)(2,1)S(1)} all-to-all(bf16[16,2,1024]{2,1,0:T(2,128)(2,1)S(1)} %all_to_all.14), channel_id=1, replica_groups=mesh['gx'=8,'gy'=16] {'gy'}, dimensions={0} | all-to-all | bytes 131072 | tf_op jit(solution)/shard_map/all_to_all | solution.py:106
  126.5 0.7 reshape.466
  127.2 140.6 %all-reduce.6.cloned.1.call-done = (f32[27,96,128]{2,1,0:T(8,128)}, f32[27,128,128]{2,1,0:T(8,128)}, f32[8,128,128]{2,1,0:T(8,128)}) async-done(((f32[27,96,128]{2,1,0:T(8,128)}, f32[27,128,128]{2,1,0:T(8,128)}, f32[8,128,128]{2,1,0:T(8,128)}), (f32[27,96,128]{2,1,0:T(8,128)}, f32[27,128,128]{2,1,0:T(8,128)}, f32[8,128,128]{2,1,0:T(8,128)})) %all-reduce.6.cloned.1.call-update) | async-done | bytes 3620880 | tf_op jit(solution)/shard_map/psum | solution.py:130
  267.8 2.6 copy.159
  270.4 1.2 copy.160
  271.8 0.8 copy.161
  (184 shorter events, 30.3 us)
Async XLA Ops:
  7.2 41.8 %copy-start = (bf16[8,128,128]{2,1,0:T(8,128)(2,1)S(1)}, bf16[8,128,128]{2,1,0:T(8,128)(2,1)}, u32[]{:S(2)}) copy-start(bf16[8,128,128]{2,1,0:T(8,128)(2,1)} %param.11) | copy-start | bytes 786436
  7.2 17.3 %copy-start.5 = (bf16[4,16,1536]{2,1,0:T(8,128)(2,1)S(1)}, bf16[4,16,1536]{2,1,0:T(8,128)(2,1)}, u32[]{:S(2)}) copy-start(bf16[4,16,1536]{2,1,0:T(8,128)(2,1)} %param.7) | copy-start | bytes 589828
  7.2 8.7 %copy-start.8 = (bf16[1,1,32,1024]{3,2,1,0:T(8,128)(2,1)S(1)}, bf16[1,1,32,1024]{3,2,1,0:T(8,128)(2,1)}, u32[]{:S(2)}) copy-start(bf16[1,1,32,1024]{3,2,1,0:T(8,128)(2,1)} %param.13) | copy-start | bytes 196612
  8.1 16.4 %copy-start.9 = (s32[1,1,16,1]{2,3,1,0:T(1,128)S(1)}, s32[1,1,16,1]{2,3,1,0:T(1,128)}, u32[]{:S(2)}) copy-start(s32[1,1,16,1]{2,3,1,0:T(1,128)} %param.12) | copy-start | bytes 196
  9.4 16.2 %collective-permute-start = (bf16[1,16,16,96]{3,2,1,0:T(8,128)(2,1)S(1)}, bf16[1,16,16,96]{3,2,1,0:T(8,128)(2,1)S(1)}, u32[]{:S(2)}, u32[]{:S(2)}) collective-permute-start(bf16[1,16,16,96]{3,2,1,0:T(8,128)(2,1)S(1)} %get-tuple-element.105), channel_id=1, source_target_pairs={{0,16},{16,32},{32,48},{48,64},{64,80},{80,96},{96,112},{1,17},{17... | collective-permute-start | bytes 147464 | tf_op jit(solution)/shard_map/ppermute | solution.py:12
  14.0 11.6 %collective-permute-start.1 = (bf16[1,16,16,96]{3,2,1,0:T(8,128)(2,1)S(1)}, bf16[1,16,16,96]{3,2,1,0:T(8,128)(2,1)S(1)}, u32[]{:S(2)}, u32[]{:S(2)}) collective-permute-start(bf16[1,16,16,96]{3,2,1,0:T(8,128)(2,1)S(1)} %get-tuple-element.106), channel_id=1, source_target_pairs={{16,0},{32,16},{48,32},{64,48},{80,64},{96,80},{112,96},{17,1},{33... | collective-permute-start | bytes 147464 | tf_op jit(solution)/shard_map/ppermute | solution.py:15
  16.6 14.1 %all-to-all-start.1 = ((bf16[16,2,1024]{2,1,0:T(2,128)(2,1)}), bf16[16,2,1024]{2,1,0:T(2,128)(2,1)S(1)}, u32[]{:S(2)}, u32[]{:S(2)}) async-start(bf16[16,2,1024]{2,1,0:T(2,128)(2,1)} %all_to_all.16), calls=%async_computation.1 | async-start | bytes 131072 | tf_op jit(solution)/shard_map/all_to_all | solution.py:108
  24.2 243.6 %all-reduce.6.cloned.1.call-start = ((), (), s32[]{:S(2)}) async-start(), calls=%async_computation.2 | async-start | bytes 7241728 | tf_op jit(solution)/shard_map/psum | solution.py:130
  25.6 5.4 %collective-permute-start.2 = (bf16[6,1,16,96]{3,2,1,0:T(8,128)(2,1)S(1)}, bf16[6,1,16,96]{3,2,1,0:T(8,128)(2,1)S(1)}, u32[]{:S(2)}, u32[]{:S(2)}) collective-permute-start(bf16[6,1,16,96]{3,2,1,0:T(8,128)(2,1)S(1)} %get-tuple-element.93), channel_id=1, source_target_pairs={{0,1},{1,2},{2,3},{3,4},{4,5},{5,6},{6,7},{7,8},{8,9},{9,10},{10,1... | collective-permute-start | bytes 55304 | tf_op jit(solution)/shard_map/ppermute | solution.py:12
  28.9 4.6 %collective-permute-start.3 = (bf16[6,1,16,96]{3,2,1,0:T(8,128)(2,1)S(1)}, bf16[6,1,16,96]{3,2,1,0:T(8,128)(2,1)S(1)}, u32[]{:S(2)}, u32[]{:S(2)}) collective-permute-start(bf16[6,1,16,96]{3,2,1,0:T(8,128)(2,1)S(1)} %get-tuple-element.94), channel_id=1, source_target_pairs={{1,0},{2,1},{3,2},{4,3},{5,4},{6,5},{7,6},{8,7},{9,8},{10,9},{11,1... | collective-permute-start | bytes 55304 | tf_op jit(solution)/shard_map/ppermute | solution.py:15
  33.8 1.1 copy-start.6
  41.3 8.1 %collective-permute-start.4 = (bf16[1,16,16,128]{3,2,1,0:T(8,128)(2,1)S(1)}, bf16[1,16,16,128]{3,2,1,0:T(8,128)(2,1)S(1)}, u32[]{:S(2)}, u32[]{:S(2)}) collective-permute-start(bf16[1,16,16,128]{3,2,1,0:T(8,128)(2,1)S(1)} %get-tuple-element.101), channel_id=1, source_target_pairs={{0,16},{16,32},{32,48},{48,64},{64,80},{80,96},{96,112},{1,17},{17... | collective-permute-start | bytes 196616 | tf_op jit(solution)/shard_map/ppermute | solution.py:12
  47.0 5.6 %collective-permute-start.5 = (bf16[1,16,16,128]{3,2,1,0:T(8,128)(2,1)S(1)}, bf16[1,16,16,128]{3,2,1,0:T(8,128)(2,1)S(1)}, u32[]{:S(2)}, u32[]{:S(2)}) collective-permute-start(bf16[1,16,16,128]{3,2,1,0:T(8,128)(2,1)S(1)} %get-tuple-element.102), channel_id=1, source_target_pairs={{16,0},{32,16},{48,32},{64,48},{80,64},{96,80},{112,96},{17,1},{33... | collective-permute-start | bytes 196616 | tf_op jit(solution)/shard_map/ppermute | solution.py:15
  52.6 4.6 %collective-permute-start.6 = (bf16[6,1,16,128]{3,2,1,0:T(8,128)(2,1)S(1)}, bf16[6,1,16,128]{3,2,1,0:T(8,128)(2,1)S(1)}, u32[]{:S(2)}, u32[]{:S(2)}) collective-permute-start(bf16[6,1,16,128]{3,2,1,0:T(8,128)(2,1)S(1)} %get-tuple-element.89), channel_id=1, source_target_pairs={{0,1},{1,2},{2,3},{3,4},{4,5},{5,6},{6,7},{7,8},{8,9},{9,10},{10,1... | collective-permute-start | bytes 73736 | tf_op jit(solution)/shard_map/ppermute | solution.py:12
  55.7 4.6 %collective-permute-start.7 = (bf16[6,1,16,128]{3,2,1,0:T(8,128)(2,1)S(1)}, bf16[6,1,16,128]{3,2,1,0:T(8,128)(2,1)S(1)}, u32[]{:S(2)}, u32[]{:S(2)}) collective-permute-start(bf16[6,1,16,128]{3,2,1,0:T(8,128)(2,1)S(1)} %get-tuple-element.90), channel_id=1, source_target_pairs={{1,0},{2,1},{3,2},{4,3},{5,4},{6,5},{7,6},{8,7},{9,8},{10,9},{11,1... | collective-permute-start | bytes 73736 | tf_op jit(solution)/shard_map/ppermute | solution.py:15
  60.8 1.2 copy-start.1
  77.0 6.3 %copy-start.3 = (f32[27,128,128]{2,1,0:T(8,128)}, f32[27,128,128]{2,1,0:T(8,128)S(1)}, u32[]{:S(2)}) copy-start(f32[27,128,128]{2,1,0:T(8,128)S(1)} %fusion.16) | copy-start | bytes 5308420
  77.0 6.3 %collective-permute-start.8 = (bf16[1,16,16,128]{3,2,1,0:T(8,128)(2,1)S(1)}, bf16[1,16,16,128]{3,2,1,0:T(8,128)(2,1)S(1)}, u32[]{:S(2)}, u32[]{:S(2)}) collective-permute-start(bf16[1,16,16,128]{3,2,1,0:T(8,128)(2,1)S(1)} %get-tuple-element.97), channel_id=1, source_target_pairs={{0,16},{16,32},{32,48},{48,64},{64,80},{80,96},{96,112},{1,17},{17... | collective-permute-start | bytes 196616 | tf_op jit(solution)/shard_map/ppermute | solution.py:12
  80.3 5.6 %collective-permute-start.9 = (bf16[1,16,16,128]{3,2,1,0:T(8,128)(2,1)S(1)}, bf16[1,16,16,128]{3,2,1,0:T(8,128)(2,1)S(1)}, u32[]{:S(2)}, u32[]{:S(2)}) collective-permute-start(bf16[1,16,16,128]{3,2,1,0:T(8,128)(2,1)S(1)} %get-tuple-element.98), channel_id=1, source_target_pairs={{16,0},{32,16},{48,32},{64,48},{80,64},{96,80},{112,96},{17,1},{33... | collective-permute-start | bytes 196616 | tf_op jit(solution)/shard_map/ppermute | solution.py:15
  85.8 6.0 %collective-permute-start.10 = (bf16[6,1,16,128]{3,2,1,0:T(8,128)(2,1)S(1)}, bf16[6,1,16,128]{3,2,1,0:T(8,128)(2,1)S(1)}, u32[]{:S(2)}, u32[]{:S(2)}) collective-permute-start(bf16[6,1,16,128]{3,2,1,0:T(8,128)(2,1)S(1)} %get-tuple-element.85), channel_id=1, source_target_pairs={{0,1},{1,2},{2,3},{3,4},{4,5},{5,6},{6,7},{7,8},{8,9},{9,10},{10,1... | collective-permute-start | bytes 73736 | tf_op jit(solution)/shard_map/ppermute | solution.py:12
  90.2 4.9 %collective-permute-start.11 = (bf16[6,1,16,128]{3,2,1,0:T(8,128)(2,1)S(1)}, bf16[6,1,16,128]{3,2,1,0:T(8,128)(2,1)S(1)}, u32[]{:S(2)}, u32[]{:S(2)}) collective-permute-start(bf16[6,1,16,128]{3,2,1,0:T(8,128)(2,1)S(1)} %get-tuple-element.86), channel_id=1, source_target_pairs={{1,0},{2,1},{3,2},{4,3},{5,4},{6,5},{7,6},{8,7},{9,8},{10,9},{11,1... | collective-permute-start | bytes 73736 | tf_op jit(solution)/shard_map/ppermute | solution.py:15
  110.5 1.1 copy-start.4
  267.8 2.6 copy-start.2
  270.4 1.4 copy-start.7
Sparse Core Ops, SparseCore 0:
  111.7 156.0 all-reduce.5
where the time goes:
time: 280 us; the launch traced here: 279 us
  waiting for transfers between devices  156 us (56%)
  starting transfers between devices  41.9 us (15%)
  matrix products  34 us (12%)
  between operations  15.5 us (6%)
  blocking collectives  14.3 us (5%)
  local copies, waits for them, and re-layouts  13.9 us (5%)
  other arithmetic  4.23 us (2%)
    psum x1, waiting for transfers between devices, per_device(): lax.psum((grad_first, grad_second, grad_down), ('gx', 'gy'))  141 us
    ppermute x6, starting transfers between devices, padded_2(): lax.ppermute(lax.slice_in_dim(block, block.shape[dim] - width, None, axis...  24.2 us
    ppermute x6, waiting for transfers between devices, padded_2(): lax.ppermute(lax.slice_in_dim(block, 0, width, axis=dim), axis, backward)  14.5 us
    all_to_all x1, blocking collectives, per_device(): lax.all_to_all(outgoing, 'gy', split_axis=0, concat_axis=0, tiled=True)  14.3 us
    dot_general x54, matrix products, taps_weight(): lax.dot_general(window, flat, (((0,), (0,)), ((), ())), preferred_element...  14.2 us
    dot_general x54, matrix products, taps_forward(): total = total + jnp.dot(window, w[t], preferred_element_type=jnp.float32)  11.6 us
    ppermute x6, starting transfers between devices, padded_2(): lax.ppermute(lax.slice_in_dim(block, 0, width, axis=dim), axis, backward)  10 us
    all_to_all x1, starting transfers between devices, per_device(): lax.all_to_all(moved_grad.reshape(slots, 8 * chan), 'gy', split_axis=0, c...  7.6 us
  transfers between devices with their start and end apart: 14, of which 7 were waited for; matrix products, arithmetic and copies ran while one was open for 2% of the time, Pallas kernels for 0%

commit v1 on v0

--- a/solution.py
+++ b/solution.py
@@ -1,7 +1,9 @@
 import jax
 import jax.numpy as jnp
 from jax import lax
-from jax.sharding import PartitionSpec as P
+from jax.sharding import Mesh, PartitionSpec as P
+
+GX, GY, CHIPS = ("y", "c"), ("z", "x"), ("y", "z", "x")
 
 
 def padded_2(block, sides, width):
@@ -23,7 +25,7 @@
 
 
 def extend(v):
-    padded = padded_2(v, (("gx", 0), ("gy", 1)), 1)
+    padded = padded_2(v, ((GX, 0), (GY, 1)), 1)
     return jnp.pad(padded, ((0, 0), (0, 0), (1, 1), (0, 0)))
 
 
@@ -63,12 +65,42 @@
     return jnp.stack(terms)
 
 
+def swap_cores(v):
+    return lax.ppermute(v, "c", [(0, 1), (1, 0)])
+
+
+def sum_over_devices(terms):
+    chips = lax.axis_size(CHIPS)
+    core = lax.axis_index("c")
+    flat = jnp.concatenate([t.reshape(-1, 128).astype(jnp.bfloat16) for t in terms])
+    rows = flat.shape[0]
+    part = -(-rows // (2 * chips * 8)) * 8
+    flat = jnp.pad(flat, ((0, 2 * chips * part - rows), (0, 0))).reshape(2, chips * part, 128)
+    mine = lax.dynamic_index_in_dim(flat, core, 0, keepdims=False)
+    theirs = swap_cores(lax.dynamic_index_in_dim(flat, 1 - core, 0, keepdims=False))
+    half = (mine.astype(jnp.float32) + theirs.astype(jnp.float32)).astype(jnp.bfloat16)
+    pieces = lax.all_to_all(half.reshape(chips, part, 128), CHIPS, 0, 0, tiled=True)
+    own = jnp.sum(pieces.astype(jnp.float32), axis=0).astype(jnp.bfloat16)
+    half = lax.all_to_all(
+        jnp.broadcast_to(own[None], (chips, part, 128)), CHIPS, 0, 0, tiled=True
+    ).reshape(chips * part, 128)
+    other = swap_cores(half)
+    total = jnp.where(core == 0, jnp.concatenate([half, other]), jnp.concatenate([other, half]))
+    total = total.astype(jnp.float32)
+    out, at = [], 0
+    for t in terms:
+        n = t.size // 128
+        out.append(total[at : at + n].reshape(t.shape))
+        at += n
+    return out
+
+
 def per_device(features, block_mask, weight_first, weight_second, weight_down, owners, moved_grad):
     chan_in = weight_first.shape[1]
     chan = weight_first.shape[2]
     sx, sy = (features.shape[0], features.shape[1])
     sz = features.shape[2] // chan_in
-    peers = lax.axis_size("gy")
+    peers = lax.axis_size(GY)
     slots = moved_grad.shape[2]
     bricks_dev = sx // 4 * (sy // 4) * (sz // 4)
     blocks = block_mask.astype(jnp.float32)
@@ -103,10 +135,10 @@
     outgoing = lax.dot_general(
         select_b, bricks, (((0,), (0,)), ((), ())), preferred_element_type=jnp.float32
     ).astype(jnp.bfloat16)
-    arrived = lax.all_to_all(outgoing, "gy", split_axis=0, concat_axis=0, tiled=True)
+    arrived = lax.all_to_all(outgoing, GY, split_axis=0, concat_axis=0, tiled=True)
     moved = arrived.reshape(1, 1, slots, 8 * chan)
     returned = lax.all_to_all(
-        moved_grad.reshape(slots, 8 * chan), "gy", split_axis=0, concat_axis=0, tiled=True
+        moved_grad.reshape(slots, 8 * chan), GY, split_axis=0, concat_axis=0, tiled=True
     )
     grad_bricks = jnp.dot(select.astype(jnp.bfloat16), returned, preferred_element_type=jnp.float32)
     grad_coarse = grad_bricks.astype(jnp.bfloat16).reshape(sx // 4, sy // 4, sz // 4, 2, 2, 2, chan)
@@ -127,23 +159,15 @@
     )
     grad_pre_first = (active * grad_first_act * silu_grad(pre_first)).astype(jnp.bfloat16)
     grad_first = taps_weight(padded_in, grad_pre_first, sx, sy, sz)
-    grad_first, grad_second, grad_down = lax.psum(
-        (grad_first, grad_second, grad_down), ("gx", "gy")
-    )
+    grad_first, grad_second, grad_down = sum_over_devices((grad_first, grad_second, grad_down))
     return (moved, grad_first, grad_second, grad_down)
 
 
 def solution(mesh):
-    in_specs = (
-        P("gx", "gy", None),
-        P("gx", "gy", None),
-        P(),
-        P(),
-        P(),
-        P("gx", "gy", None, None),
-        P("gx", "gy", None, None),
+    shape = dict(mesh.shape)
+    fine = Mesh(mesh.devices.reshape(shape["gx"] // 2, 2, 4, shape["gy"] // 4), ("y", "c", "z", "x"))
+    in_specs = (P(GX, GY, None), P(GX, GY, None), P(), P(), P(), P(GX, GY, None, None), P(GX, GY, None, None))
+    out_specs = (P(GX, GY, None, None), P(), P(), P())
+    return jax.shard_map(
+        per_device, mesh=fine, in_specs=in_specs, out_specs=out_specs, check_vma=False
     )
-    out_specs = (P("gx", "gy", None, None), P(), P(), P())
-    return jax.shard_map(
-        per_device, mesh=mesh, in_specs=in_specs, out_specs=out_specs, check_vma=False
-    )

time: 280 us -> 177 us (0.63)
  waiting for transfers between devices: 156 us -> 13.1 us
  blocking collectives: 14.3 us -> 55 us
  between operations: 15.5 us -> 1.91 us
  starting transfers between devices: 41.9 us -> 52.6 us
    psum x1 -> x0, waiting for transfers between devices: 141 us -> none  [per_device(): lax.psum((grad_first, grad_second, grad_down), ('gx', 'gy'))]
    all_to_all x1 -> x2, blocking collectives: 14.3 us -> 55 us  [the longest x1 35.5 us: sum_over_devices(): lax.all_to_all(half.reshape(chips, part, 128), CHIPS, 0, 0, tiled=True)]
    ppermute x6, waiting for transfers between devices: 14.5 us -> 0.02 us  [padded_2(): lax.ppermute(lax.slice_in_dim(block, 0, width, axis=dim), axis, backward)]
    all_to_all x1 -> x2, waiting for transfers between devices: 0.45 us -> 6.74 us  [the longest x1 6.74 us: per_device(): lax.all_to_all(outgoing, GY, split_axis=0, concat_axis=0, tiled=True)]
    unnamed x23 -> x10, local copies, waits for them, and re-layouts: 6.6 us -> 0.69 us
    all_to_all x1 -> x2, starting transfers between devices: 7.6 us -> 11.9 us  [the longest x1 8.43 us: per_device(): lax.all_to_all(moved_grad.reshape(slots, 8 * chan), GY, split_axis=0, con...]
    ppermute x6, waiting for transfers between devices: 0.02 us -> 3.64 us  [padded_2(): lax.ppermute(lax.slice_in_dim(block, block.shape[dim] - width, None, axis...]
    slice x0 -> x3, local copies, waits for them, and re-layouts: none -> 3.3 us  [sum_over_devices(): out.append(total[at:at + n].reshape(t.shape))]
  transfers between devices with their start and end apart: 14 -> 16, of which waited for: 7 -> 7; matrix products, arithmetic and copies ran while one was open for 2% -> 3% of each run, Pallas kernels for 0% -> 0%
where the time goes in v1:
time: 177 us; the launch traced here: 176 us
  blocking collectives  55 us (31%)
  starting transfers between devices  52.6 us (30%)
  matrix products  34.3 us (19%)
  local copies, waits for them, and re-layouts  13.8 us (8%)
  waiting for transfers between devices  13.1 us (7%)
  other arithmetic  5.04 us (3%)
  between operations  1.91 us (1%)
    all_to_all x1, blocking collectives, sum_over_devices(): lax.all_to_all(half.reshape(chips, part, 128), CHIPS, 0, 0, tiled=True)  35.5 us
    ppermute x6, starting transfers between devices, padded_2(): lax.ppermute(lax.slice_in_dim(block, block.shape[dim] - width, None, axis...  26.9 us
    all_to_all x1, blocking collectives, sum_over_devices(): lax.all_to_all(jnp.broadcast_to(own[None], (chips, part, 128)), CHIPS, 0,...  19.5 us
    dot_general x54, matrix products, taps_weight(): lax.dot_general(window, flat, (((0,), (0,)), ((), ())), preferred_element...  15.1 us
    dot_general x54, matrix products, taps_forward(): total = total + jnp.dot(window, w[t], preferred_element_type=jnp.float32)  11.7 us
    ppermute x6, starting transfers between devices, padded_2(): lax.ppermute(lax.slice_in_dim(block, 0, width, axis=dim), axis, backward)  10.8 us
    all_to_all x1, starting transfers between devices, per_device(): lax.all_to_all(moved_grad.reshape(slots, 8 * chan), GY, split_axis=0, con...  8.43 us
    all_to_all x1, waiting for transfers between devices, per_device(): lax.all_to_all(outgoing, GY, split_axis=0, concat_axis=0, tiled=True)  6.74 us
  transfers between devices with their start and end apart: 16, of which 7 were waited for; matrix products, arithmetic and copies ran while one was open for 3% of the time, Pallas kernels for 0%

profile of v1, /device:TPU:1, one launch (start us, length us, event | category | flops | bytes accessed | tf_op | source)
XLA Modules:
  0.0 175.8 jit_solution(5193845635671327224)
XLA Ops:
  0.7 1.6 all_to_all.22
  2.2 8.4 %all-to-all-start.1 = ((bf16[16,2,1024]{2,1,0:T(2,128)(2,1)}), bf16[16,2,1024]{2,1,0:T(2,128)(2,1)S(1)}, u32[]{:S(2)}, u32[]{:S(2)}) async-start(bf16[16,2,1024]{2,1,0:T(2,128)(2,1)} %all_to_all.22), calls=%async_computation.1 | async-start | bytes 131072 | tf_op jit(solution)/shard_map/all_to_all | solution.py:140
  10.7 0.7 convert_bitcast_fusion
  11.5 1.1 reshape.531
  12.8 2.9 %collective-permute-start.1 = (bf16[1,16,16,96]{3,2,1,0:T(8,128)(2,1)S(1)}, bf16[1,16,16,96]{3,2,1,0:T(8,128)(2,1)S(1)}, u32[]{:S(2)}, u32[]{:S(2)}) collective-permute-start(bf16[1,16,16,96]{3,2,1,0:T(8,128)(2,1)S(1)} %get-tuple-element.103), channel_id=1, source_target_pairs={{16,0},{32,16},{48,32},{64,48},{80,64},{96,80},{112,96},{17,1},{33... | collective-permute-start | bytes 147464 | tf_op jit(solution)/shard_map/ppermute | solution.py:17
  15.6 3.1 %collective-permute-start = (bf16[1,16,16,96]{3,2,1,0:T(8,128)(2,1)S(1)}, bf16[1,16,16,96]{3,2,1,0:T(8,128)(2,1)S(1)}, u32[]{:S(2)}, u32[]{:S(2)}) collective-permute-start(bf16[1,16,16,96]{3,2,1,0:T(8,128)(2,1)S(1)} %get-tuple-element.102), channel_id=1, source_target_pairs={{0,16},{16,32},{32,48},{48,64},{64,80},{80,96},{96,112},{1,17},{17... | collective-permute-start | bytes 147464 | tf_op jit(solution)/shard_map/ppermute | solution.py:14
  20.1 1.3 collective-permute-start.3
  21.4 4.2 %collective-permute-start.2 = (bf16[6,1,16,96]{3,2,1,0:T(8,128)(2,1)S(1)}, bf16[6,1,16,96]{3,2,1,0:T(8,128)(2,1)S(1)}, u32[]{:S(2)}, u32[]{:S(2)}) collective-permute-start(bf16[6,1,16,96]{3,2,1,0:T(8,128)(2,1)S(1)} %get-tuple-element.90), channel_id=1, source_target_pairs={{0,1},{1,2},{2,3},{3,4},{4,5},{5,6},{6,7},{7,8},{8,9},{9,10},{10,1... | collective-permute-start | bytes 55304 | tf_op jit(solution)/shard_map/ppermute | solution.py:14
  26.0 0.5 collective-permute-done.2
  26.5 0.3 select_maximum_fusion.6
  26.9 0.8 fusion.419
  27.7 0.3 copy-done.3
  33.9 0.3 multiply_convert_fusion.8
  34.4 2.1 %collective-permute-start.5 = (bf16[1,16,16,128]{3,2,1,0:T(8,128)(2,1)S(1)}, bf16[1,16,16,128]{3,2,1,0:T(8,128)(2,1)S(1)}, u32[]{:S(2)}, u32[]{:S(2)}) collective-permute-start(bf16[1,16,16,128]{3,2,1,0:T(8,128)(2,1)S(1)} %get-tuple-element.99), channel_id=1, source_target_pairs={{16,0},{32,16},{48,32},{64,48},{80,64},{96,80},{112,96},{17,1},{33... | collective-permute-start | bytes 196616 | tf_op jit(solution)/shard_map/ppermute | solution.py:17
  36.6 5.0 %collective-permute-start.4 = (bf16[1,16,16,128]{3,2,1,0:T(8,128)(2,1)S(1)}, bf16[1,16,16,128]{3,2,1,0:T(8,128)(2,1)S(1)}, u32[]{:S(2)}, u32[]{:S(2)}) collective-permute-start(bf16[1,16,16,128]{3,2,1,0:T(8,128)(2,1)S(1)} %get-tuple-element.98), channel_id=1, source_target_pairs={{0,16},{16,32},{32,48},{48,64},{64,80},{80,96},{96,112},{1,17},{17... | collective-permute-start | bytes 196616 | tf_op jit(solution)/shard_map/ppermute | solution.py:14
  42.1 0.8 collective-permute-done.4
  42.9 1.3 collective-permute-start.7
  44.2 4.7 %collective-permute-start.6 = (bf16[6,1,16,128]{3,2,1,0:T(8,128)(2,1)S(1)}, bf16[6,1,16,128]{3,2,1,0:T(8,128)(2,1)S(1)}, u32[]{:S(2)}, u32[]{:S(2)}) collective-permute-start(bf16[6,1,16,128]{3,2,1,0:T(8,128)(2,1)S(1)} %get-tuple-element.86), channel_id=1, source_target_pairs={{0,1},{1,2},{2,3},{3,4},{4,5},{5,6},{6,7},{7,8},{8,9},{9,10},{10,1... | collective-permute-start | bytes 73736 | tf_op jit(solution)/shard_map/ppermute | solution.py:14
  49.0 0.7 collective-permute-done.6
  49.6 0.4 select_maximum_fusion.4
  50.0 0.8 fusion.418
  50.8 0.4 copy-done.1
  57.2 0.5 multiply_convert_fusion.5
  57.7 0.4 multiply_convert_fusion.6
  58.7 0.3 fusion.122
  59.6 0.3 fusion.118
  59.9 0.3 fusion.116
  60.5 0.3 fusion.114
  60.7 0.3 fusion.112
  61.3 0.3 fusion.110
  61.6 0.3 fusion.108
  61.9 0.5 multiply_convert_fusion.1
  62.9 0.3 fusion.104
  63.2 0.3 fusion.102
  63.8 0.3 fusion.100
  64.1 0.3 fusion.98
  64.7 0.3 fusion.96
  65.0 0.3 fusion.94
  65.6 0.3 fusion.92
  65.9 0.3 fusion.90
  66.4 0.3 fusion.88
  66.7 1.9 %collective-permute-start.9 = (bf16[1,16,16,128]{3,2,1,0:T(8,128)(2,1)S(1)}, bf16[1,16,16,128]{3,2,1,0:T(8,128)(2,1)S(1)}, u32[]{:S(2)}, u32[]{:S(2)}) collective-permute-start(bf16[1,16,16,128]{3,2,1,0:T(8,128)(2,1)S(1)} %get-tuple-element.95), channel_id=1, source_target_pairs={{16,0},{32,16},{48,32},{64,48},{80,64},{96,80},{112,96},{17,1},{33... | collective-permute-start | bytes 196616 | tf_op jit(solution)/shard_map/ppermute | solution.py:17
  68.7 5.1 %collective-permute-start.8 = (bf16[1,16,16,128]{3,2,1,0:T(8,128)(2,1)S(1)}, bf16[1,16,16,128]{3,2,1,0:T(8,128)(2,1)S(1)}, u32[]{:S(2)}, u32[]{:S(2)}) collective-permute-start(bf16[1,16,16,128]{3,2,1,0:T(8,128)(2,1)S(1)} %get-tuple-element.94), channel_id=1, source_target_pairs={{0,16},{16,32},{32,48},{48,64},{64,80},{80,96},{96,112},{1,17},{17... | collective-permute-start | bytes 196616 | tf_op jit(solution)/shard_map/ppermute | solution.py:14
  74.1 1.0 collective-permute-done.8
  75.1 1.3 collective-permute-start.11
  76.4 4.8 %collective-permute-start.10 = (bf16[6,1,16,128]{3,2,1,0:T(8,128)(2,1)S(1)}, bf16[6,1,16,128]{3,2,1,0:T(8,128)(2,1)S(1)}, u32[]{:S(2)}, u32[]{:S(2)}) collective-permute-start(bf16[6,1,16,128]{3,2,1,0:T(8,128)(2,1)S(1)} %get-tuple-element.82), channel_id=1, source_target_pairs={{0,1},{1,2},{2,3},{3,4},{4,5},{5,6},{6,7},{7,8},{8,9},{9,10},{10,1... | collective-permute-start | bytes 73736 | tf_op jit(solution)/shard_map/ppermute | solution.py:14
  81.3 0.6 collective-permute-done.10
  81.9 0.4 select_maximum_fusion
  82.3 0.8 fusion.417
  89.5 0.4 multiply_convert_fusion.3
  89.9 0.3 multiply_convert_fusion.4
  97.8 1.0 dynamic-slice_bitcast_fusion
  98.8 2.7 %collective-permute-done.12 = bf16[3584,128]{1,0:T(8,128)(2,1)S(1)} collective-permute-done((bf16[3584,128]{1,0:T(8,128)(2,1)}, bf16[3584,128]{1,0:T(8,128)(2,1)S(1)}, u32[]{:S(2)}, u32[]{:S(2)}) %collective-permute-start.12) | collective-permute-done | bytes 917536 | tf_op jit(solution)/shard_map/ppermute | solution.py:69
  101.7 35.5 %all_to_all.31 = bf16[64,56,128]{2,1,0:T(8,128)(2,1)S(1)} all-to-all(bf16[64,56,128]{2,1,0:T(8,128)(2,1)S(1)} %bitcast.1270), channel_id=1, replica_groups=mesh['y'=4,'c'=2,'z'=4,'x'=4] {'y','z','x'}, dimensions={0} | all-to-all | bytes 1835008 | tf_op jit(solution)/shard_map/all_to_all | solution.py:82
  137.5 19.5 %all_to_all.32 = bf16[64,56,128]{2,1,0:T(8,128)(2,1)S(1)} all-to-all(bf16[64,56,128]{2,1,0:T(8,128)(2,1)S(1)} %broadcast_in_dim.28), channel_id=1, replica_groups=mesh['y'=4,'c'=2,'z'=4,'x'=4] {'y','z','x'}, dimensions={0} | all-to-all | bytes 1835008 | tf_op jit(solution)/shard_map/all_to_all | solution.py:84
  157.0 3.0 %collective-permute-start.13 = (bf16[3584,128]{1,0:T(8,128)(2,1)S(1)}, bf16[3584,128]{1,0:T(8,128)(2,1)S(1)}, u32[]{:S(2)}, u32[]{:S(2)}) collective-permute-start(bf16[3584,128]{1,0:T(8,128)(2,1)S(1)} %bitcast.1271), channel_id=1, source_target_pairs={{0,16},{16,0},{1,17},{17,1},{2,18},{18,2},{3,19},{19,3},{4,20},{20... | collective-permute-start | bytes 2752520 | tf_op jit(solution)/shard_map/ppermute | solution.py:69
  160.5 0.7 all_to_all.20
  161.2 3.5 %all-to-all-start = ((bf16[16,2,1024]{2,1,0:T(2,128)(2,1)}), bf16[16,2,1024]{2,1,0:T(2,128)(2,1)S(1)}, u32[]{:S(2)}, u32[]{:S(2)}) async-start(bf16[16,2,1024]{2,1,0:T(2,128)(2,1)} %all_to_all.20), calls=%async_computation | async-start | bytes 131072 | tf_op jit(solution)/shard_map/all_to_all | solution.py:138
  164.7 6.7 %all-to-all-done = bf16[16,2,1024]{2,1,0:T(2,128)(2,1)S(1)} async-done(((bf16[16,2,1024]{2,1,0:T(2,128)(2,1)}), bf16[16,2,1024]{2,1,0:T(2,128)(2,1)S(1)}, u32[]{:S(2)}, u32[]{:S(2)}) %all-to-all-start) | async-done | bytes 65568 | tf_op jit(solution)/shard_map/all_to_all | solution.py:138
  171.5 0.7 reshape.490
  172.1 0.4 fusion.5
  172.5 1.1 slice.810
  173.6 1.3 slice.811
  175.0 0.8 slice.812
  (184 shorter events, 32.7 us)
Async XLA Ops:
  0.6 40.9 %copy-start = (bf16[8,128,128]{2,1,0:T(8,128)(2,1)S(1)}, bf16[8,128,128]{2,1,0:T(8,128)(2,1)}, u32[]{:S(2)}) copy-start(bf16[8,128,128]{2,1,0:T(8,128)(2,1)} %param.11) | copy-start | bytes 786436
  0.6 18.6 %copy-start.2 = (bf16[4,16,1536]{2,1,0:T(8,128)(2,1)S(1)}, bf16[4,16,1536]{2,1,0:T(8,128)(2,1)}, u32[]{:S(2)}) copy-start(bf16[4,16,1536]{2,1,0:T(8,128)(2,1)} %param.7) | copy-start | bytes 589828
  0.7 18.1 %copy-start.4 = (s32[1,1,16,1]{2,3,1,0:T(1,128)S(1)}, s32[1,1,16,1]{2,3,1,0:T(1,128)}, u32[]{:S(2)}) copy-start(s32[1,1,16,1]{2,3,1,0:T(1,128)} %param.12) | copy-start | bytes 196
  2.2 23.5 %all-to-all-start.1 = ((bf16[16,2,1024]{2,1,0:T(2,128)(2,1)}), bf16[16,2,1024]{2,1,0:T(2,128)(2,1)S(1)}, u32[]{:S(2)}, u32[]{:S(2)}) async-start(bf16[16,2,1024]{2,1,0:T(2,128)(2,1)} %all_to_all.22), calls=%async_computation.1 | async-start | bytes 131072 | tf_op jit(solution)/shard_map/all_to_all | solution.py:140
  12.8 7.3 %collective-permute-start.1 = (bf16[1,16,16,96]{3,2,1,0:T(8,128)(2,1)S(1)}, bf16[1,16,16,96]{3,2,1,0:T(8,128)(2,1)S(1)}, u32[]{:S(2)}, u32[]{:S(2)}) collective-permute-start(bf16[1,16,16,96]{3,2,1,0:T(8,128)(2,1)S(1)} %get-tuple-element.103), channel_id=1, source_target_pairs={{16,0},{32,16},{48,32},{64,48},{80,64},{96,80},{112,96},{17,1},{33... | collective-permute-start | bytes 147464 | tf_op jit(solution)/shard_map/ppermute | solution.py:17
  15.6 4.4 %collective-permute-start = (bf16[1,16,16,96]{3,2,1,0:T(8,128)(2,1)S(1)}, bf16[1,16,16,96]{3,2,1,0:T(8,128)(2,1)S(1)}, u32[]{:S(2)}, u32[]{:S(2)}) collective-permute-start(bf16[1,16,16,96]{3,2,1,0:T(8,128)(2,1)S(1)} %get-tuple-element.102), channel_id=1, source_target_pairs={{0,16},{16,32},{32,48},{48,64},{64,80},{80,96},{96,112},{1,17},{17... | collective-permute-start | bytes 147464 | tf_op jit(solution)/shard_map/ppermute | solution.py:14
  20.1 5.9 %collective-permute-start.3 = (bf16[6,1,16,96]{3,2,1,0:T(8,128)(2,1)S(1)}, bf16[6,1,16,96]{3,2,1,0:T(8,128)(2,1)S(1)}, u32[]{:S(2)}, u32[]{:S(2)}) collective-permute-start(bf16[6,1,16,96]{3,2,1,0:T(8,128)(2,1)S(1)} %get-tuple-element.91), channel_id=1, source_target_pairs={{1,0},{2,1},{3,2},{4,3},{5,4},{6,5},{7,6},{8,7},{9,8},{10,9},{11,1... | collective-permute-start | bytes 55304 | tf_op jit(solution)/shard_map/ppermute | solution.py:17
  21.4 5.1 %collective-permute-start.2 = (bf16[6,1,16,96]{3,2,1,0:T(8,128)(2,1)S(1)}, bf16[6,1,16,96]{3,2,1,0:T(8,128)(2,1)S(1)}, u32[]{:S(2)}, u32[]{:S(2)}) collective-permute-start(bf16[6,1,16,96]{3,2,1,0:T(8,128)(2,1)S(1)} %get-tuple-element.90), channel_id=1, source_target_pairs={{0,1},{1,2},{2,3},{3,4},{4,5},{5,6},{6,7},{7,8},{8,9},{9,10},{10,1... | collective-permute-start | bytes 55304 | tf_op jit(solution)/shard_map/ppermute | solution.py:14
  26.9 1.1 copy-start.3
  34.4 7.7 %collective-permute-start.5 = (bf16[1,16,16,128]{3,2,1,0:T(8,128)(2,1)S(1)}, bf16[1,16,16,128]{3,2,1,0:T(8,128)(2,1)S(1)}, u32[]{:S(2)}, u32[]{:S(2)}) collective-permute-start(bf16[1,16,16,128]{3,2,1,0:T(8,128)(2,1)S(1)} %get-tuple-element.99), channel_id=1, source_target_pairs={{16,0},{32,16},{48,32},{64,48},{80,64},{96,80},{112,96},{17,1},{33... | collective-permute-start | bytes 196616 | tf_op jit(solution)/shard_map/ppermute | solution.py:17
  36.6 6.3 %collective-permute-start.4 = (bf16[1,16,16,128]{3,2,1,0:T(8,128)(2,1)S(1)}, bf16[1,16,16,128]{3,2,1,0:T(8,128)(2,1)S(1)}, u32[]{:S(2)}, u32[]{:S(2)}) collective-permute-start(bf16[1,16,16,128]{3,2,1,0:T(8,128)(2,1)S(1)} %get-tuple-element.98), channel_id=1, source_target_pairs={{0,16},{16,32},{32,48},{48,64},{64,80},{80,96},{96,112},{1,17},{17... | collective-permute-start | bytes 196616 | tf_op jit(solution)/shard_map/ppermute | solution.py:14
  42.9 6.1 %collective-permute-start.7 = (bf16[6,1,16,128]{3,2,1,0:T(8,128)(2,1)S(1)}, bf16[6,1,16,128]{3,2,1,0:T(8,128)(2,1)S(1)}, u32[]{:S(2)}, u32[]{:S(2)}) collective-permute-start(bf16[6,1,16,128]{3,2,1,0:T(8,128)(2,1)S(1)} %get-tuple-element.87), channel_id=1, source_target_pairs={{1,0},{2,1},{3,2},{4,3},{5,4},{6,5},{7,6},{8,7},{9,8},{10,9},{11,1... | collective-permute-start | bytes 73736 | tf_op jit(solution)/shard_map/ppermute | solution.py:17
  44.2 5.5 %collective-permute-start.6 = (bf16[6,1,16,128]{3,2,1,0:T(8,128)(2,1)S(1)}, bf16[6,1,16,128]{3,2,1,0:T(8,128)(2,1)S(1)}, u32[]{:S(2)}, u32[]{:S(2)}) collective-permute-start(bf16[6,1,16,128]{3,2,1,0:T(8,128)(2,1)S(1)} %get-tuple-element.86), channel_id=1, source_target_pairs={{0,1},{1,2},{2,3},{3,4},{4,5},{5,6},{6,7},{7,8},{8,9},{9,10},{10,1... | collective-permute-start | bytes 73736 | tf_op jit(solution)/shard_map/ppermute | solution.py:14
  50.0 1.2 copy-start.1
  66.7 7.3 %collective-permute-start.9 = (bf16[1,16,16,128]{3,2,1,0:T(8,128)(2,1)S(1)}, bf16[1,16,16,128]{3,2,1,0:T(8,128)(2,1)S(1)}, u32[]{:S(2)}, u32[]{:S(2)}) collective-permute-start(bf16[1,16,16,128]{3,2,1,0:T(8,128)(2,1)S(1)} %get-tuple-element.95), channel_id=1, source_target_pairs={{16,0},{32,16},{48,32},{64,48},{80,64},{96,80},{112,96},{17,1},{33... | collective-permute-start | bytes 196616 | tf_op jit(solution)/shard_map/ppermute | solution.py:17
  68.7 6.4 %collective-permute-start.8 = (bf16[1,16,16,128]{3,2,1,0:T(8,128)(2,1)S(1)}, bf16[1,16,16,128]{3,2,1,0:T(8,128)(2,1)S(1)}, u32[]{:S(2)}, u32[]{:S(2)}) collective-permute-start(bf16[1,16,16,128]{3,2,1,0:T(8,128)(2,1)S(1)} %get-tuple-element.94), channel_id=1, source_target_pairs={{0,16},{16,32},{32,48},{48,64},{64,80},{80,96},{96,112},{1,17},{17... | collective-permute-start | bytes 196616 | tf_op jit(solution)/shard_map/ppermute | solution.py:14
  75.1 6.2 %collective-permute-start.11 = (bf16[6,1,16,128]{3,2,1,0:T(8,128)(2,1)S(1)}, bf16[6,1,16,128]{3,2,1,0:T(8,128)(2,1)S(1)}, u32[]{:S(2)}, u32[]{:S(2)}) collective-permute-start(bf16[6,1,16,128]{3,2,1,0:T(8,128)(2,1)S(1)} %get-tuple-element.83), channel_id=1, source_target_pairs={{1,0},{2,1},{3,2},{4,3},{5,4},{6,5},{7,6},{8,7},{9,8},{10,9},{11,1... | collective-permute-start | bytes 73736 | tf_op jit(solution)/shard_map/ppermute | solution.py:17
  76.4 5.5 %collective-permute-start.10 = (bf16[6,1,16,128]{3,2,1,0:T(8,128)(2,1)S(1)}, bf16[6,1,16,128]{3,2,1,0:T(8,128)(2,1)S(1)}, u32[]{:S(2)}, u32[]{:S(2)}) collective-permute-start(bf16[6,1,16,128]{3,2,1,0:T(8,128)(2,1)S(1)} %get-tuple-element.82), channel_id=1, source_target_pairs={{0,1},{1,2},{2,3},{3,4},{4,5},{5,6},{6,7},{7,8},{8,9},{9,10},{10,1... | collective-permute-start | bytes 73736 | tf_op jit(solution)/shard_map/ppermute | solution.py:14
  98.8 2.7 %collective-permute-start.12 = (bf16[3584,128]{1,0:T(8,128)(2,1)}, bf16[3584,128]{1,0:T(8,128)(2,1)S(1)}, u32[]{:S(2)}, u32[]{:S(2)}) collective-permute-start(bf16[3584,128]{1,0:T(8,128)(2,1)} %dynamic-slice_bitcast_fusion), channel_id=1, source_target_pairs={{0,16},{16,0},{1,17},{17,1},{2,18},{18,2},{3,19},{19,3},{4,20},{20... | collective-permute-start | bytes 2752520 | tf_op jit(solution)/shard_map/ppermute | solution.py:69
  157.0 15.1 %collective-permute-start.13 = (bf16[3584,128]{1,0:T(8,128)(2,1)S(1)}, bf16[3584,128]{1,0:T(8,128)(2,1)S(1)}, u32[]{:S(2)}, u32[]{:S(2)}) collective-permute-start(bf16[3584,128]{1,0:T(8,128)(2,1)S(1)} %bitcast.1271), channel_id=1, source_target_pairs={{0,16},{16,0},{1,17},{17,1},{2,18},{18,2},{3,19},{19,3},{4,20},{20... | collective-permute-start | bytes 2752520 | tf_op jit(solution)/shard_map/ppermute | solution.py:69
  161.2 10.3 %all-to-all-start = ((bf16[16,2,1024]{2,1,0:T(2,128)(2,1)}), bf16[16,2,1024]{2,1,0:T(2,128)(2,1)S(1)}, u32[]{:S(2)}, u32[]{:S(2)}) async-start(bf16[16,2,1024]{2,1,0:T(2,128)(2,1)} %all_to_all.20), calls=%async_computation | async-start | bytes 131072 | tf_op jit(solution)/shard_map/all_to_all | solution.py:138

commit v2 on v0

v2 whole, which is shorter than its diff:
```python
import jax
import jax.numpy as jnp
import numpy as np
from jax import lax
from jax.experimental import pallas as pl
from jax.experimental.pallas import tpu as pltpu
from jax.sharding import Mesh, PartitionSpec as P

GX, GY, CHIPS = ("y", "c"), ("z", "x"), ("y", "z", "x")
F32, BF = jnp.float32, jnp.bfloat16
X, Y, Z, C, CIN = 4, 16, 16, 128, 96
HALF = 3584
NN = (((1,), (0,)), ((), ()))
NT = (((1,), (1,)), ((), ()))
TN = (((0,), (0,)), ((), ()))


def mm(a, b, dims=NN):
    return lax.dot_general(a, b, dims, preferred_element_type=F32)


def z_of(rows):
    return lax.broadcasted_iota(jnp.int32, (rows, C), 0) % Z


def from_above(v):
    return jnp.where(z_of(v.shape[0]) < Z - 1, pltpu.roll(v, v.shape[0] - 1, 0), 0.0)


def from_below(v):
    return jnp.where(z_of(v.shape[0]) > 0, pltpu.roll(v, 1, 0), 0.0)


def lanes(p, k):
    return p[:, k * C : (k + 1) * C]


def section(
    core_ref, in_ref, mask_ref, w1_ref, w2_ref, wd_ref, gc_ref, up_ref, sel_ref,
    grads_ref, out_ref,
    wa, wb, first, sg1, second, ge, g2, gs, vt,
):
    core = core_ref[0]

    def line(x, y0, cells):
        return jnp.concatenate(
            [mask_ref[(x + 4) // 4, (y + 4) // 4] for y in range(y0, y0 + cells)], axis=0
        )

    def taps(ref, width, x, cells, w, dims=NN, flip=False):
        wins = []
        for i in range(3):
            for j in range(3):
                ii, jj = (2 - i, 2 - j) if flip else (i, j)
                at = ((x + ii) * width + jj) * Z
                wins.append(ref[at : at + cells * Z, :])
        return mm(jnp.concatenate(wins, axis=1), w[...], dims)

    def weight_grad(ref, width, x0, y0, rows, put):
        for j in range(3):
            for x in range(6):
                at = ((x0 + x) * width + y0 + j) * Z
                vt[j * C : (j + 1) * C, x * Y * Z : (x + 1) * Y * Z] = ref[at : at + Y * Z, :].T
        for i in range(3):
            p = mm(vt[:, i * Y * Z : (i + X) * Y * Z], gs[...]).astype(BF)
            for j in range(3):
                for k in range(3):
                    put(9 * i + 3 * j + k, p[j * C : j * C + rows, k * C : (k + 1) * C])

    def put_z_taps(x, g):
        at = x * Y * Z
        gs[at : at + Y * Z, 0:C] = from_above(g).astype(BF)
        gs[at : at + Y * Z, C : 2 * C] = g.astype(BF)
        gs[at : at + Y * Z, 2 * C : 3 * C] = from_below(g).astype(BF)

    for m in range(9):
        for k in range(3):
            wa[m * C : m * C + CIN, k * C : (k + 1) * C] = w1_ref[3 * m + k]
        wa[m * C + CIN : (m + 1) * C, :] = jnp.zeros((C - CIN, 3 * C), BF)

    for x in range(8):
        p = taps(in_ref, 22, x, 20, wa)
        act = line(x - 2, -2, 20)
        pre = act * (lanes(p, 1) + from_below(lanes(p, 0)) + from_above(lanes(p, 2)))
        s = jax.nn.sigmoid(pre)
        first[x * 20 * Z : (x + 1) * 20 * Z, :] = (pre * s).astype(BF)
        if 2 <= x < 6:
            d = act * (s * (1.0 + pre * (1.0 - s)))
            sg1[(x - 2) * Y * Z : (x - 1) * Y * Z, :] = d[2 * Z : 18 * Z]

    for m in range(9):
        for k in range(3):
            wa[m * C : (m + 1) * C, k * C : (k + 1) * C] = w2_ref[3 * m + k]
            wb[k * C : (k + 1) * C, m * C : (m + 1) * C] = w2_ref[3 * m + k]

    even = z_of(6 * Z) % 2 == 0
    for u in range(4):
        both = jnp.concatenate(
            [jnp.concatenate([gc_ref[u, 2 * b + c] for b in range(2)], axis=1) for c in range(2)],
            axis=0,
        )
        r = mm(up_ref[...], both)
        for v in range(10):
            by, b = (v + 1) // 2, (v + 1) % 2
            t = r[by * Z : (by + 1) * Z, b * C : (b + 1) * C]
            at = (u * 10 + v) * Z
            ge[at : at + Z, 0:C] = jnp.where(even[:Z], t, 0.0).astype(BF)
            ge[at : at + Z, C : 2 * C] = jnp.where(even[:Z], 0.0, t).astype(BF)

    for x in range(6):
        p = taps(first, 20, x, 18, wa)
        at = ((x + 1) * 20 + 1) * Z
        act = line(x - 1, -1, 18)
        pre = act * (lanes(p, 1) + from_below(lanes(p, 0)) + from_above(lanes(p, 2)))
        pre = pre + first[at : at + 18 * Z, :].astype(F32)
        s = jax.nn.sigmoid(pre)
        if 1 <= x < 5:
            second[(x - 1) * Y * Z : x * Y * Z, :] = (pre * s)[Z : 17 * Z].astype(BF)
        u, a = (x + 1) // 2, (x + 1) % 2
        back = []
        for b in range(2):
            at = (u * 10 + 1 - b) * Z
            w = jnp.concatenate([wd_ref[4 * a + 2 * b], wd_ref[4 * a + 2 * b + 1]], axis=1)
            back.append(mm(ge[at : at + 9 * Z, :], w, NT))
        g = jnp.concatenate(
            [back[1 - y % 2][y // 2 * Z : (y // 2 + 1) * Z] for y in range(18)], axis=0
        )
        g = (act * g * (s * (1.0 + pre * (1.0 - s)))).astype(BF)
        g2[x * 18 * Z : (x + 1) * 18 * Z, :] = g
        if 1 <= x < 5:
            put_z_taps(x - 1, g[Z : 17 * Z].astype(F32))

    def corner(a, b):
        return jnp.concatenate(
            [
                second[((2 * u + a) * Y + 2 * v + b) * Z : ((2 * u + a) * Y + 2 * v + b + 1) * Z, :]
                for u in range(2)
                for v in range(8)
            ],
            axis=0,
        )

    corners = [corner(a, b) for a in range(2) for b in range(2)]
    wd = jnp.concatenate(
        [jnp.concatenate([wd_ref[2 * q], wd_ref[2 * q + 1]], axis=1) for q in range(4)], axis=0
    )
    p = mm(jnp.concatenate(corners, axis=1), wd)
    coarse = (lanes(p, 0) + from_above(lanes(p, 1))).astype(BF)
    bricks = jnp.concatenate(
        [
            jnp.concatenate(
                [
                    coarse[(a * 8 + 2 * by + b) * Z : (a * 8 + 2 * by + b + 1) * Z]
                    for by in range(4)
                ],
                axis=0,
            )
            for a in range(2)
            for b in range(2)
        ],
        axis=1,
    )
    r = mm(sel_ref[...], bricks).astype(BF)
    for q in range(4):
        for c in range(2):
            out_ref[:, (2 * q + c) * C : (2 * q + c + 1) * C] = r[
                c * 32 : (c + 1) * 32, q * C : (q + 1) * C
            ]

    gec = jnp.concatenate([ge[(u * 10 + 1) * Z : (u * 10 + 9) * Z, :] for u in (1, 2)], axis=0)

    def put_a(at, v):
        grads_ref[core, at : at + v.shape[0], :] = v

    def put_b(at, v):
        grads_ref[1 - core, at : at + v.shape[0], :] = v

    for q in range(4):
        r = mm(corners[q], gec, TN).astype(BF)
        for c in range(2):
            t = 2 * q + c
            if t == 0:
                put_a(27 * C, lanes(r, c))
            else:
                put_b(27 * CIN + (t - 1) * C, lanes(r, c))
    put_b(27 * CIN + 7 * C, jnp.zeros((HALF - 27 * CIN - 7 * C, C), BF))
    weight_grad(first, 20, 1, 1, C, lambda t, v: put_a(t * C, v))

    for x in range(X):
        p = taps(g2, 18, x, Y, wb, NT, flip=True)
        at = ((x + 1) * 18 + 1) * Z
        g = lanes(p, 1) + from_above(lanes(p, 0)) + from_below(lanes(p, 2))
        g = g + g2[at : at + Y * Z, :].astype(F32)
        g = (g * sg1[x * Y * Z : (x + 1) * Y * Z, :]).astype(BF)
        put_z_taps(x, g.astype(F32))
    weight_grad(in_ref, 22, 2, 2, CIN, lambda t, v: put_b(t * CIN, v))


def run_section(core, cells, mask, w1, w2, wd, gc, up, sel):
    vm = pl.BlockSpec(memory_space=pltpu.VMEM)
    return pl.pallas_call(
        section,
        out_shape=(
            jax.ShapeDtypeStruct((2, HALF, C), BF),
            jax.ShapeDtypeStruct((32, 8 * C), BF),
        ),
        in_specs=[pl.BlockSpec(memory_space=pltpu.SMEM)] + [vm] * 8,
        out_specs=(vm, vm),
        scratch_shapes=[
            pltpu.VMEM((9 * C, 3 * C), BF),
            pltpu.VMEM((3 * C, 9 * C), BF),
            pltpu.VMEM((8 * 20 * Z, C), BF),
            pltpu.VMEM((X * Y * Z, C), F32),
            pltpu.VMEM((X * Y * Z, C), BF),
            pltpu.VMEM((40 * Z, 2 * C), BF),
            pltpu.VMEM((6 * 18 * Z, C), BF),
            pltpu.VMEM((X * Y * Z, 3 * C), BF),
            pltpu.VMEM((3 * C, 6 * Y * Z), BF),
        ],
        compiler_params=pltpu.CompilerParams(vmem_limit_bytes=48 * 1024 * 1024),
        cost_estimate=pl.CostEstimate(
            flops=8_000_000_000, bytes_accessed=6_000_000, transcendentals=600_000
        ),
    )(core, cells, mask, w1, w2, wd, gc, up, sel)


def shift(v, axes, step):
    n = lax.axis_size(axes)
    return lax.ppermute(v, axes, [(i, i + step) for i in range(n) if 0 <= i + step < n])


def swap_cores(v):
    return lax.ppermute(v, "c", [(0, 1), (1, 0)])


def tile_of(*rows):
    return jnp.pad(
        jnp.stack([jnp.pad(r.reshape(-1).astype(BF), (0, C - r.size)) for r in rows]),
        ((0, 16 - len(rows)), (0, 0)),
    )


def up_matrix():
    m = np.zeros((6 * Z, 64), np.float32)
    for by in range(6):
        for z in range(Z):
            m[by * Z + z, z // 2 % 2 * 32 + by * 4 + z // 4] = 1
    return jnp.asarray(m, BF)


def per_device(features, block_mask, weight_first, weight_second, weight_down, owners, moved_grad):
    core = lax.axis_index("c")
    blocks = block_mask.reshape(4, 4)
    active = jnp.repeat(jnp.repeat(blocks, 4, axis=0), 4, axis=1).astype(F32)
    own = features.reshape(X, Y, Z, CIN) * active[None, :, :, None]
    own = jnp.pad(own.astype(BF), ((0, 0), (0, 0), (0, 0), (0, C - CIN)))

    dest = owners.reshape(16)
    earlier = jnp.asarray(np.tril(np.ones((16, 16), np.int32), -1))
    rank = jnp.sum((dest[:, None] == dest[None, :]).astype(jnp.int32) * earlier, axis=1)
    slot = dest * 2 + rank

    side = 3 * 4 * Z
    low = shift(
        jnp.concatenate([own[:, 13:].reshape(side, C), tile_of(slot, blocks[3])]), GY, 1
    )
    high = shift(
        jnp.concatenate([own[:, :3].reshape(side, C), tile_of(slot, blocks[0])]), GY, -1
    )
    rows = jnp.pad(moved_grad.reshape(16, 2, 8 * C), ((1, 1), (0, 0), (0, 0)))
    rows = jnp.concatenate([rows[0:16], rows[1:17], rows[2:18]], axis=1)
    rows = lax.all_to_all(rows, GY, 0, 0, tiled=True).reshape(96, 8 * C)

    mid = jnp.concatenate(
        [low[:side].reshape(X, 3, Z, C), own, high[:side].reshape(X, 3, Z, C)], axis=1
    )
    slots = jnp.concatenate(
        [low[side, 12:16].astype(jnp.int32), slot, high[side, :4].astype(jnp.int32)]
    )
    place = slots // 2 * 6 + slots % 2 + jnp.asarray([0] * 4 + [2] * 16 + [4] * 4, jnp.int32)
    pick = jnp.pad(place, (0, 8), constant_values=-1)[:, None] == jnp.arange(96)[None, :]
    bricks = mm(pick.astype(BF), rows).astype(BF)
    blocks = jnp.concatenate(
        [low[side + 1, :4], blocks.reshape(16).astype(BF), high[side + 1, :4]]
    )

    def strip(cells, a):
        cots = [bricks[:, (4 * a + q) * C : (4 * a + q + 1) * C] for q in range(4)]
        return jnp.concatenate([cells.reshape(-1, C)] + cots + [tile_of(blocks)])

    low = shift(strip(mid[1:], 1), GX, 1)
    high = shift(strip(mid[:3], 0), GX, -1)
    side = 3 * 22 * Z
    cells = jnp.concatenate([low[:side], mid.reshape(-1, C), high[:side]])
    own_gc = bricks.reshape(32, 8, C).transpose(1, 0, 2)
    gc = jnp.concatenate(
        [low[side : side + 128].reshape(4, 32, C), own_gc, high[side : side + 128].reshape(4, 32, C)]
    ).reshape(4, 4, 32, C)
    blocks = jnp.stack([low[side + 128, :24], blocks, high[side + 128, :24]])
    mask = jnp.repeat(blocks.reshape(3, 6, 4).astype(F32), 4, axis=2)
    mask = jnp.broadcast_to(mask[..., None], (3, 6, Z, C))

    where = jnp.arange(64)
    slot_z = jnp.repeat(slot, 4)
    sel = (slot_z[None, :] == where[:, None] % 32) & (where[None, :] % 4 == where[:, None] // 32 * 2)
    grads, outgoing = run_section(
        core.reshape(1).astype(jnp.int32), cells, mask, weight_first, weight_second, weight_down,
        gc, up_matrix(), sel.astype(BF),
    )

    moved = lax.all_to_all(outgoing.reshape(16, 2, 8 * C), GY, 0, 0, tiled=True)
    moved = moved.reshape(1, 1, 32, 8 * C)

    chips = lax.axis_size(CHIPS)
    part = HALF // chips
    theirs = swap_cores(grads[1])
    half = (grads[0].astype(F32) + theirs.astype(F32)).astype(BF)
    pieces = lax.all_to_all(half.reshape(chips, part, C), CHIPS, 0, 0, tiled=True)
    total = jnp.sum(pieces.astype(F32), axis=0).astype(BF)
    half = lax.all_to_all(
        jnp.broadcast_to(total[None], (chips, part, C)), CHIPS, 0, 0, tiled=True
    ).reshape(HALF, C)
    other = swap_cores(half)
    a = jnp.where(core == 0, half, other).astype(F32)
    b = jnp.where(core == 0, other, half).astype(F32)
    grad_second = a[: 27 * C].reshape(27, C, C)
    grad_first = b[: 27 * CIN].reshape(27, CIN, C)
    grad_down = jnp.concatenate([a[27 * C :], b[27 * CIN : 27 * CIN + 7 * C]]).reshape(8, C, C)
    return moved, grad_first, grad_second, grad_down


def solution(mesh):
    shape = dict(mesh.shape)
    fine = Mesh(
        mesh.devices.reshape(shape["gx"] // 2, 2, 4, shape["gy"] // 4), ("y", "c", "z", "x")
    )
    whole, tiles = P(GX, GY, None), P(GX, GY, None, None)
    return jax.shard_map(
        per_device,
        mesh=fine,
        in_specs=(whole, whole, P(), P(), P(), tiles, tiles),
        out_specs=(tiles, P(), P(), P()),
        check_vma=False,
    )
```

time: 280 us -> 123 us (0.44)
  waiting for transfers between devices: 156 us -> 18.5 us
  matrix products: 34 us -> 0.2 us
  blocking collectives: 14.3 us -> 47.8 us
  starting transfers between devices: 41.9 us -> 27.3 us
  between operations: 15.5 us -> 1.03 us
  Pallas kernels: 0 us -> 10.4 us
    psum x1 -> x0, waiting for transfers between devices: 141 us -> none  [per_device(): lax.psum((grad_first, grad_second, grad_down), ('gx', 'gy'))]
    dot_general x140 -> x1, matrix products: 34 us -> 0.2 us  [mm(): return lax.dot_general(a, b, dims, preferred_element_type=F32)]
    all_to_all x1 -> x2, blocking collectives: 14.3 us -> 47.8 us  [the longest x1 28.2 us: per_device(): lax.all_to_all(half.reshape(chips, part, C), CHIPS, 0, 0, tiled=True)]
    ppermute x12 -> x6, starting transfers between devices: 34.3 us -> 15.4 us  [the longest x4 12.4 us: shift(): lax.ppermute(v, axes, [(i, i + step) for i in range(n) if 0 <= i + step <...]
    pallas_call x0 -> x1, Pallas kernels: none -> 10.4 us  [run_section(): pl.pallas_call(section, out_shape=(jax.ShapeDtypeStruct((2, HALF, C), BF)...]
    all_to_all x1 -> x2, waiting for transfers between devices: 0.45 us -> 6.74 us  [the longest x1 6.74 us: per_device(): moved = lax.all_to_all(outgoing.reshape(16, 2, 8 * C), GY, 0, 0, tiled=True)]
    all_to_all x1 -> x2, starting transfers between devices: 7.6 us -> 11.9 us  [the longest x1 8.43 us: per_device(): rows = lax.all_to_all(rows, GY, 0, 0, tiled=True).reshape(96, 8 * C)]
    unnamed x23 -> x16, local copies, waits for them, and re-layouts: 6.6 us -> 3.19 us
  transfers between devices with their start and end apart: 14 -> 8, of which waited for: 7 -> 5; matrix products, arithmetic and copies ran while one was open for 2% -> 6% of each run, Pallas kernels for 0% -> 0%
where the time goes in v2:
time: 123 us; the launch traced here: 122 us
  blocking collectives  47.8 us (39%)
  starting transfers between devices  27.3 us (22%)
  waiting for transfers between devices  18.5 us (15%)
  local copies, waits for them, and re-layouts  11.3 us (9%)
  Pallas kernels  10.4 us (8%)
  other arithmetic  5.39 us (4%)
    all_to_all x1, blocking collectives, per_device(): lax.all_to_all(half.reshape(chips, part, C), CHIPS, 0, 0, tiled=True)  28.2 us
    all_to_all x1, blocking collectives, per_device(): lax.all_to_all(jnp.broadcast_to(total[None], (chips, part, C)), CHIPS, 0,...  19.5 us
    ppermute x4, starting transfers between devices, shift(): lax.ppermute(v, axes, [(i, i + step) for i in range(n) if 0 <= i + step <...  12.4 us
    pallas_call x1, Pallas kernels, run_section(): pl.pallas_call(section, out_shape=(jax.ShapeDtypeStruct((2, HALF, C), BF)...  10.4 us
    ppermute x4, waiting for transfers between devices, shift(): lax.ppermute(v, axes, [(i, i + step) for i in range(n) if 0 <= i + step <...  9.28 us
    all_to_all x1, starting transfers between devices, per_device(): rows = lax.all_to_all(rows, GY, 0, 0, tiled=True).reshape(96, 8 * C)  8.43 us
    all_to_all x1, waiting for transfers between devices, per_device(): moved = lax.all_to_all(outgoing.reshape(16, 2, 8 * C), GY, 0, 0, tiled=True)  6.74 us
    all_to_all x1, starting transfers between devices, per_device(): moved = lax.all_to_all(outgoing.reshape(16, 2, 8 * C), GY, 0, 0, tiled=True)  3.5 us
  transfers between devices with their start and end apart: 8, of which 5 were waited for; matrix products, arithmetic and copies ran while one was open for 6% of the time, Pallas kernels for 0%

profile of v2, /device:TPU:1, one launch (start us, length us, event | category | flops | bytes accessed | tf_op | source)
XLA Modules:
  0.0 122.0 jit_solution(12133912088101965771)
XLA Ops:
  0.6 0.9 reshape.188
  1.5 0.1 pad_slice_fusion.1
  1.6 0.9 pad_maximum_fusion.3
  2.5 8.4 %all-to-all-start = ((bf16[16,6,1024]{2,1,0:T(8,128)(2,1)}), bf16[16,6,1024]{2,1,0:T(8,128)(2,1)S(1)}, u32[]{:S(2)}, u32[]{:S(2)}) async-start(bf16[16,6,1024]{2,1,0:T(8,128)(2,1)} %pad_maximum_fusion.3), calls=%async_computation | async-start | bytes 524288 | tf_op jit(solution)/shard_map/all_to_all | solution.py:272
  11.0 0.9 select_reduce_fusion
  11.9 0.7 fusion.11
  12.5 0.8 convert_bitcast_fusion
  13.3 0.1 copy.22
  13.4 0.1 broadcast_in_dim.14
  13.5 0.1 convert_element_type.109
  13.6 0.1 copy.23
  13.6 1.1 reshape.203
  14.8 0.1 multiply_convert_fusion
  14.9 0.0 copy-start.4
  15.0 3.3 %collective-permute-start = (bf16[208,128]{1,0:T(8,128)(2,1)S(1)}, bf16[208,128]{1,0:T(8,128)(2,1)S(1)}, u32[]{:S(2)}, u32[]{:S(2)}) collective-permute-start(bf16[208,128]{1,0:T(8,128)(2,1)S(1)} %fusion.3), channel_id=1, source_target_pairs={{0,1},{1,2},{2,3},{3,4},{4,5},{5,6},{6,7},{7,8},{8,9},{9,10},{10,1... | collective-permute-start | bytes 159752 | tf_op jit(solution)/shard_map/ppermute | solution.py:229
  18.3 1.3 %collective-permute-start.1 = (bf16[208,128]{1,0:T(8,128)(2,1)S(1)}, bf16[208,128]{1,0:T(8,128)(2,1)S(1)}, u32[]{:S(2)}, u32[]{:S(2)}) collective-permute-start(bf16[208,128]{1,0:T(8,128)(2,1)S(1)} %fusion.4), channel_id=1, source_target_pairs={{1,0},{2,1},{3,2},{4,3},{5,4},{6,5},{7,6},{8,7},{9,8},{10,9},{11,1... | collective-permute-start | bytes 159752 | tf_op jit(solution)/shard_map/ppermute | solution.py:229
  19.6 0.1 convert_element_type.120
  19.7 0.1 broadcast_in_dim.36
  19.7 0.1 eq.70
  19.8 0.1 pad.41
  19.9 0.1 slice_bitcast_fusion.2
  20.0 3.2 %collective-permute-done.1 = bf16[208,128]{1,0:T(8,128)(2,1)S(1)} collective-permute-done((bf16[208,128]{1,0:T(8,128)(2,1)S(1)}, bf16[208,128]{1,0:T(8,128)(2,1)S(1)}, u32[]{:S(2)}, u32[]{:S(2)}) %collective-permute-start.1) | collective-permute-done | bytes 53280 | tf_op jit(solution)/shard_map/ppermute | solution.py:229
  23.1 0.1 pad_maximum_fusion.7
  23.3 0.1 fusion.12
  23.4 0.1 fusion.10
  23.5 0.7 constant_dynamic-update-slice_fusion.5
  24.2 0.1 reshape.189
  24.3 0.2 convolution_convert_fusion
  24.5 0.6 constant_dynamic-update-slice_fusion.4
  25.1 0.6 constant_dynamic-update-slice_fusion.3
  25.7 0.6 constant_dynamic-update-slice_fusion.2
  26.3 0.6 constant_dynamic-update-slice_fusion.1
  26.9 0.6 constant_dynamic-update-slice_fusion
  27.5 5.7 %collective-permute-start.2 = (bf16[1200,128]{1,0:T(8,128)(2,1)}, bf16[1200,128]{1,0:T(8,128)(2,1)S(1)}, u32[]{:S(2)}, u32[]{:S(2)}) collective-permute-start(bf16[1200,128]{1,0:T(8,128)(2,1)} %get-tuple-element.34), channel_id=1, source_target_pairs={{0,16},{16,32},{32,48},{48,64},{64,80},{80,96},{96,112},{1,17},{17... | collective-permute-start | bytes 921608 | tf_op jit(solution)/shard_map/ppermute | solution.py:229
  33.3 0.1 and_convert_fusion.sel_ref
  33.4 0.1 stack.37
  33.5 0.0 copy-start.3
  33.5 2.1 %collective-permute-start.3 = (bf16[1200,128]{1,0:T(8,128)(2,1)S(1)}, bf16[1200,128]{1,0:T(8,128)(2,1)S(1)}, u32[]{:S(2)}, u32[]{:S(2)}) collective-permute-start(bf16[1200,128]{1,0:T(8,128)(2,1)S(1)} %get-tuple-element.35), channel_id=1, source_target_pairs={{16,0},{32,16},{48,32},{64,48},{80,64},{96,80},{112,96},{17,1},{33... | collective-permute-start | bytes 921608 | tf_op jit(solution)/shard_map/ppermute | solution.py:229
  35.6 1.8 %collective-permute-done.2 = bf16[1200,128]{1,0:T(8,128)(2,1)S(1)} collective-permute-done((bf16[1200,128]{1,0:T(8,128)(2,1)}, bf16[1200,128]{1,0:T(8,128)(2,1)S(1)}, u32[]{:S(2)}, u32[]{:S(2)}) %collective-permute-start.2) | collective-permute-done | bytes 307232 | tf_op jit(solution)/shard_map/ppermute | solution.py:229
  37.4 0.1 stack.36
  37.5 4.3 %collective-permute-done.3 = bf16[1200,128]{1,0:T(8,128)(2,1)S(1)} collective-permute-done((bf16[1200,128]{1,0:T(8,128)(2,1)S(1)}, bf16[1200,128]{1,0:T(8,128)(2,1)S(1)}, u32[]{:S(2)}, u32[]{:S(2)}) %collective-permute-start.3) | collective-permute-done | bytes 307232 | tf_op jit(solution)/shard_map/ppermute | solution.py:229
  41.8 0.1 stack.38
  41.9 0.1 copy.24
  42.0 0.1 copy.25
  42.2 0.1 pad_maximum_fusion.in_ref
  42.3 0.1 broadcast_in_dim.35.mask_ref
  42.4 10.4 %shard_map.129 = (bf16[2,3584,128]{2,1,0:T(8,128)(2,1)S(1)}, bf16[32,1024]{1,0:T(8,128)(2,1)S(1)}) custom-call(s32[1]{0:T(128)} %bitcast.core_ref, bf16[3520,128]{1,0:T(8,128)(2,1)S(1)} %pad_maximum_fusion.in_ref, f32[3,6,16,128]{3,2,1,0:T(8,128)S(1)} %broadcast_in_dim.35.mask_ref, bf16[27,96,128]{2,1,0:T(8,128)(2,1)S(1)} %copy-done.1, ...), custom_call_target="tpu_custom_call" | custom-call | flops 8000000000 | bytes 6000000 | tf_op jit(solution)/shard_map/pallas_call | solution.py:201
  52.9 0.1 slice_bitcast_fusion
  52.9 0.1 collective-permute-start.4
  53.0 2.5 %collective-permute-done.4 = bf16[3584,128]{1,0:T(8,128)(2,1)S(1)} collective-permute-done((bf16[3584,128]{1,0:T(8,128)(2,1)S(1)}, bf16[3584,128]{1,0:T(8,128)(2,1)S(1)}, u32[]{:S(2)}, u32[]{:S(2)}) %collective-permute-start.4) | collective-permute-done | bytes 917536 | tf_op jit(solution)/shard_map/ppermute | solution.py:233
  55.5 0.2 fusion
  55.7 28.2 %all_to_all.20 = bf16[64,56,128]{2,1,0:T(8,128)(2,1)S(1)} all-to-all(bf16[64,56,128]{2,1,0:T(8,128)(2,1)S(1)} %bitcast.71), channel_id=1, replica_groups=mesh['y'=4,'c'=2,'z'=4,'x'=4] {'y','z','x'}, dimensions={0} | all-to-all | bytes 1835008 | tf_op jit(solution)/shard_map/all_to_all | solution.py:318
  84.0 0.2 reduce_sum.22
  84.1 0.1 broadcast_in_dim.37
  84.3 19.5 %all_to_all.21 = bf16[64,56,128]{2,1,0:T(8,128)(2,1)S(1)} all-to-all(bf16[64,56,128]{2,1,0:T(8,128)(2,1)S(1)} %broadcast_in_dim.37), channel_id=1, replica_groups=mesh['y'=4,'c'=2,'z'=4,'x'=4] {'y','z','x'}, dimensions={0} | all-to-all | bytes 1835008 | tf_op jit(solution)/shard_map/all_to_all | solution.py:320
  103.8 2.9 %collective-permute-start.5 = (bf16[3584,128]{1,0:T(8,128)(2,1)S(1)}, bf16[3584,128]{1,0:T(8,128)(2,1)S(1)}, u32[]{:S(2)}, u32[]{:S(2)}) collective-permute-start(bf16[3584,128]{1,0:T(8,128)(2,1)S(1)} %bitcast.70), channel_id=1, source_target_pairs={{0,16},{16,0},{1,17},{17,1},{2,18},{18,2},{3,19},{19,3},{4,20},{20... | collective-permute-start | bytes 2752520 | tf_op jit(solution)/shard_map/ppermute | solution.py:233
  106.7 0.7 reshape.196
  107.4 3.5 %all-to-all-start.1 = ((bf16[16,2,1024]{2,1,0:T(2,128)(2,1)}), bf16[16,2,1024]{2,1,0:T(2,128)(2,1)S(1)}, u32[]{:S(2)}, u32[]{:S(2)}) async-start(bf16[16,2,1024]{2,1,0:T(2,128)(2,1)} %reshape.196), calls=%async_computation.1 | async-start | bytes 131072 | tf_op jit(solution)/shard_map/all_to_all | solution.py:311
  110.9 6.7 %all-to-all-done.1 = bf16[16,2,1024]{2,1,0:T(2,128)(2,1)S(1)} async-done(((bf16[16,2,1024]{2,1,0:T(2,128)(2,1)}), bf16[16,2,1024]{2,1,0:T(2,128)(2,1)S(1)}, u32[]{:S(2)}, u32[]{:S(2)}) %all-to-all-start.1) | async-done | bytes 65568 | tf_op jit(solution)/shard_map/all_to_all | solution.py:311
  117.6 0.7 reshape.197
  118.3 0.3 select_convert_fusion
  118.6 1.3 %slice.164 = f32[3456,128]{1,0:T(8,128)} slice(f32[3584,128]{1,0:T(8,128)S(1)} %get-tuple-element.10), slice={[0:3456], [0:128]} | slice | bytes 3538944 | tf_op jit(solution)/shard_map/slice | solution.py:326
  120.0 1.1 slice.163
  121.1 0.8 pad_maximum_fusion.1
  (40 shorter events, 0.4 us)
Async XLA Ops:
  2.5 21.7 %all-to-all-start = ((bf16[16,6,1024]{2,1,0:T(8,128)(2,1)}), bf16[16,6,1024]{2,1,0:T(8,128)(2,1)S(1)}, u32[]{:S(2)}, u32[]{:S(2)}) async-start(bf16[16,6,1024]{2,1,0:T(8,128)(2,1)} %pad_maximum_fusion.3), calls=%async_computation | async-start | bytes 524288 | tf_op jit(solution)/shard_map/all_to_all | solution.py:272
  14.9 8.5 %copy-start.4 = (s32[24]{0:T(128)S(1)}, s32[24]{0:T(128)}, u32[]{:S(2)}) copy-start(s32[24]{0:T(128)} %constant.93.clone) | copy-start | bytes 292
  15.0 4.9 %collective-permute-start = (bf16[208,128]{1,0:T(8,128)(2,1)S(1)}, bf16[208,128]{1,0:T(8,128)(2,1)S(1)}, u32[]{:S(2)}, u32[]{:S(2)}) collective-permute-start(bf16[208,128]{1,0:T(8,128)(2,1)S(1)} %fusion.3), channel_id=1, source_target_pairs={{0,1},{1,2},{2,3},{3,4},{4,5},{5,6},{6,7},{7,8},{8,9},{9,10},{10,1... | collective-permute-start | bytes 159752 | tf_op jit(solution)/shard_map/ppermute | solution.py:229
  18.3 4.9 %collective-permute-start.1 = (bf16[208,128]{1,0:T(8,128)(2,1)S(1)}, bf16[208,128]{1,0:T(8,128)(2,1)S(1)}, u32[]{:S(2)}, u32[]{:S(2)}) collective-permute-start(bf16[208,128]{1,0:T(8,128)(2,1)S(1)} %fusion.4), channel_id=1, source_target_pairs={{1,0},{2,1},{3,2},{4,3},{5,4},{6,5},{7,6},{8,7},{9,8},{10,9},{11,1... | collective-permute-start | bytes 159752 | tf_op jit(solution)/shard_map/ppermute | solution.py:229
  27.5 9.8 %collective-permute-start.2 = (bf16[1200,128]{1,0:T(8,128)(2,1)}, bf16[1200,128]{1,0:T(8,128)(2,1)S(1)}, u32[]{:S(2)}, u32[]{:S(2)}) collective-permute-start(bf16[1200,128]{1,0:T(8,128)(2,1)} %get-tuple-element.34), channel_id=1, source_target_pairs={{0,16},{16,32},{32,48},{48,64},{64,80},{80,96},{96,112},{1,17},{17... | collective-permute-start | bytes 921608 | tf_op jit(solution)/shard_map/ppermute | solution.py:229
  33.5 8.9 %copy-start = (bf16[27,128,128]{2,1,0:T(8,128)(2,1)S(1)}, bf16[27,128,128]{2,1,0:T(8,128)(2,1)}, u32[]{:S(2)}) copy-start(bf16[27,128,128]{2,1,0:T(8,128)(2,1)} %w2_ref.1) | copy-start | bytes 2654212
  33.5 8.9 %copy-start.1 = (bf16[27,96,128]{2,1,0:T(8,128)(2,1)S(1)}, bf16[27,96,128]{2,1,0:T(8,128)(2,1)}, u32[]{:S(2)}) copy-start(bf16[27,96,128]{2,1,0:T(8,128)(2,1)} %w1_ref.1) | copy-start | bytes 1990660
  33.5 8.9 %copy-start.2 = (bf16[8,128,128]{2,1,0:T(8,128)(2,1)S(1)}, bf16[8,128,128]{2,1,0:T(8,128)(2,1)}, u32[]{:S(2)}) copy-start(bf16[8,128,128]{2,1,0:T(8,128)(2,1)} %wd_ref.1) | copy-start | bytes 786436
  33.5 9.0 %copy-start.3 = (bf16[96,64]{1,0:T(8,128)(2,1)S(1)}, bf16[96,64]{1,0:T(8,128)(2,1)}, u32[]{:S(2)}) copy-start(bf16[96,64]{1,0:T(8,128)(2,1)} %constant.94.clone.up_ref) | copy-start | bytes 36868
  33.5 8.3 %collective-permute-start.3 = (bf16[1200,128]{1,0:T(8,128)(2,1)S(1)}, bf16[1200,128]{1,0:T(8,128)(2,1)S(1)}, u32[]{:S(2)}, u32[]{:S(2)}) collective-permute-start(bf16[1200,128]{1,0:T(8,128)(2,1)S(1)} %get-tuple-element.35), channel_id=1, source_target_pairs={{16,0},{32,16},{48,32},{64,48},{80,64},{96,80},{112,96},{17,1},{33... | collective-permute-start | bytes 921608 | tf_op jit(solution)/shard_map/ppermute | solution.py:229
  52.9 2.6 %collective-permute-start.4 = (bf16[3584,128]{1,0:T(8,128)(2,1)S(1)}, bf16[3584,128]{1,0:T(8,128)(2,1)S(1)}, u32[]{:S(2)}, u32[]{:S(2)}) collective-permute-start(bf16[3584,128]{1,0:T(8,128)(2,1)S(1)} %slice_bitcast_fusion), channel_id=1, source_target_pairs={{0,16},{16,0},{1,17},{17,1},{2,18},{18,2},{3,19},{19,3},{4,20},{20... | collective-permute-start | bytes 2752520 | tf_op jit(solution)/shard_map/ppermute | solution.py:233
  103.8 14.5 %collective-permute-start.5 = (bf16[3584,128]{1,0:T(8,128)(2,1)S(1)}, bf16[3584,128]{1,0:T(8,128)(2,1)S(1)}, u32[]{:S(2)}, u32[]{:S(2)}) collective-permute-start(bf16[3584,128]{1,0:T(8,128)(2,1)S(1)} %bitcast.70), channel_id=1, source_target_pairs={{0,16},{16,0},{1,17},{17,1},{2,18},{18,2},{3,19},{19,3},{4,20},{20... | collective-permute-start | bytes 2752520 | tf_op jit(solution)/shard_map/ppermute | solution.py:233
  107.4 10.3 %all-to-all-start.1 = ((bf16[16,2,1024]{2,1,0:T(2,128)(2,1)}), bf16[16,2,1024]{2,1,0:T(2,128)(2,1)S(1)}, u32[]{:S(2)}, u32[]{:S(2)}) async-start(bf16[16,2,1024]{2,1,0:T(2,128)(2,1)} %reshape.196), calls=%async_computation.1 | async-start | bytes 131072 | tf_op jit(solution)/shard_map/all_to_all | solution.py:311

commit v3 on v2

v3 whole, which is shorter than its diff:
```python
import math
import jax
import jax.numpy as jnp
import numpy as np
from jax import lax
from jax.experimental import pallas as pl
from jax.experimental.pallas import tpu as pltpu
from jax.sharding import Mesh, PartitionSpec as P

GX, GY, ALL = ("y", "c"), ("z", "x"), ("y", "c", "z", "x")
F32, BF = jnp.float32, jnp.bfloat16
X, Y, Z, C, CIN = 4, 16, 16, 128, 96
HALF, PART = 3584, 224
COTS, MASK, STRIP = 1056, 1248, 1344
NN = (((1,), (0,)), ((), ()))
NT = (((1,), (1,)), ((), ()))
TN = (((0,), (0,)), ((), ()))


def mm(a, b, dims=NN):
    return lax.dot_general(a, b, dims, preferred_element_type=F32)


def iota(shape, axis):
    return lax.broadcasted_iota(jnp.int32, shape, axis)


def one(where):
    return jnp.where(where, 1.0, 0.0).astype(BF)


def z_of(rows):
    return iota((rows, C), 0) % Z


def from_above(v):
    return jnp.where(z_of(v.shape[0]) < Z - 1, pltpu.roll(v, v.shape[0] - 1, 0), 0.0)


def from_below(v):
    return jnp.where(z_of(v.shape[0]) > 0, pltpu.roll(v, 1, 0), 0.0)


def lanes(p, k):
    return p[:, k * C : (k + 1) * C]


def section(
    low_ref, mid_ref, high_ref, mask_ref, gc_ref, place_ref, w1_ref, w2_ref, wd_ref, up_ref,
    grads_ref, out_ref,
    wa, wb, first, sg1, second, ge, g2, gs, vt,
):
    core = lax.axis_index("c")

    def cells(x, y, n):
        ref, x = ((low_ref, x), (mid_ref, x - 3), (high_ref, x - 7))[(x > 2) + (x > 6)]
        return ref[(x * 22 + y) * Z : (x * 22 + y + n) * Z, :]

    def firsts(x, y, n):
        return first[(x * 20 + y) * Z : (x * 20 + y + n) * Z, :]

    def cots(x, y, n):
        return g2[(x * 18 + y) * Z : (x * 18 + y + n) * Z, :]

    def mask_tile(bx, by):
        ref, at = ((low_ref, MASK), (mask_ref, 0), (high_ref, MASK))[bx]
        return ref[at + by * Z : at + (by + 1) * Z, :].astype(F32)

    def cotangent(u, q):
        if u in (1, 2):
            return gc_ref[u - 1, q]
        return (low_ref if u == 0 else high_ref)[COTS + q * 48 : COTS + (q + 1) * 48, :]

    def line(x, y0, cells):
        return jnp.concatenate(
            [mask_tile((x + 4) // 4, (y + 4) // 4) for y in range(y0, y0 + cells)], axis=0
        )

    def taps(get, x, n, w, dims=NN, flip=False):
        wins = []
        for i in range(3):
            for j in range(3):
                ii, jj = (2 - i, 2 - j) if flip else (i, j)
                wins.append(get(x + ii, jj, n))
        return mm(jnp.concatenate(wins, axis=1), w[...], dims)

    def weight_grad(get, x0, y0, rows, put):
        for j in range(3):
            for x in range(6):
                vt[j * C : (j + 1) * C, x * Y * Z : (x + 1) * Y * Z] = get(x0 + x, y0 + j, Y).T
        for i in range(3):
            p = mm(vt[:, i * Y * Z : (i + X) * Y * Z], gs[...]).astype(BF)
            for j in range(3):
                for k in range(3):
                    put(9 * i + 3 * j + k, p[j * C : j * C + rows, k * C : (k + 1) * C])

    def put_z_taps(x, g):
        at = x * Y * Z
        gs[at : at + Y * Z, 0:C] = from_above(g).astype(BF)
        gs[at : at + Y * Z, C : 2 * C] = g.astype(BF)
        gs[at : at + Y * Z, 2 * C : 3 * C] = from_below(g).astype(BF)

    for m in range(9):
        for k in range(3):
            wa[m * C : m * C + CIN, k * C : (k + 1) * C] = w1_ref[3 * m + k]
        wa[m * C + CIN : (m + 1) * C, :] = jnp.zeros((C - CIN, 3 * C), BF)

    for x in range(8):
        p = taps(cells, x, 20, wa)
        act = line(x - 2, -2, 20)
        pre = act * (lanes(p, 1) + from_below(lanes(p, 0)) + from_above(lanes(p, 2)))
        s = jax.nn.sigmoid(pre)
        first[x * 20 * Z : (x + 1) * 20 * Z, :] = (pre * s).astype(BF)
        if 2 <= x < 6:
            d = act * (s * (1.0 + pre * (1.0 - s)))
            sg1[(x - 2) * Y * Z : (x - 1) * Y * Z, :] = d[2 * Z : 18 * Z]

    for m in range(9):
        for k in range(3):
            wa[m * C : (m + 1) * C, k * C : (k + 1) * C] = w2_ref[3 * m + k]
            wb[k * C : (k + 1) * C, m * C : (m + 1) * C] = w2_ref[3 * m + k]

    even = z_of(6 * Z) % 2 == 0
    for u in range(4):
        both = jnp.concatenate(
            [jnp.concatenate([cotangent(u, 2 * b + c) for b in range(2)], axis=1) for c in range(2)],
            axis=0,
        )
        r = mm(up_ref[...], both)
        for v in range(10):
            by, b = (v + 1) // 2, (v + 1) % 2
            t = r[by * Z : (by + 1) * Z, b * C : (b + 1) * C]
            at = (u * 10 + v) * Z
            ge[at : at + Z, 0:C] = jnp.where(even[:Z], t, 0.0).astype(BF)
            ge[at : at + Z, C : 2 * C] = jnp.where(even[:Z], 0.0, t).astype(BF)

    for x in range(6):
        p = taps(firsts, x, 18, wa)
        act = line(x - 1, -1, 18)
        pre = act * (lanes(p, 1) + from_below(lanes(p, 0)) + from_above(lanes(p, 2)))
        pre = pre + firsts(x + 1, 1, 18).astype(F32)
        s = jax.nn.sigmoid(pre)
        if 1 <= x < 5:
            second[(x - 1) * Y * Z : x * Y * Z, :] = (pre * s)[Z : 17 * Z].astype(BF)
        u, a = (x + 1) // 2, (x + 1) % 2
        back = []
        for b in range(2):
            at = (u * 10 + 1 - b) * Z
            w = jnp.concatenate([wd_ref[4 * a + 2 * b], wd_ref[4 * a + 2 * b + 1]], axis=1)
            back.append(mm(ge[at : at + 9 * Z, :], w, NT))
        g = jnp.concatenate(
            [back[1 - y % 2][y // 2 * Z : (y // 2 + 1) * Z] for y in range(18)], axis=0
        )
        g = (act * g * (s * (1.0 + pre * (1.0 - s)))).astype(BF)
        g2[x * 18 * Z : (x + 1) * 18 * Z, :] = g
        if 1 <= x < 5:
            put_z_taps(x - 1, g[Z : 17 * Z].astype(F32))

    def corner(a, b):
        return jnp.concatenate(
            [
                second[((2 * u + a) * Y + 2 * v + b) * Z : ((2 * u + a) * Y + 2 * v + b + 1) * Z, :]
                for u in range(2)
                for v in range(8)
            ],
            axis=0,
        )

    corners = [corner(a, b) for a in range(2) for b in range(2)]
    wd = jnp.concatenate(
        [jnp.concatenate([wd_ref[2 * q], wd_ref[2 * q + 1]], axis=1) for q in range(4)], axis=0
    )
    p = mm(jnp.concatenate(corners, axis=1), wd)
    coarse = (lanes(p, 0) + from_above(lanes(p, 1))).astype(BF)
    row, col = iota((128, 256), 0), iota((128, 256), 1)
    a, by, b, z = col // 128, col // 32 % 4, col // 16 % 2, col % Z
    order = (row // 16 == 4 * a + 2 * b + z // 2 % 2) & (row % 16 == by * 4 + z // 4) & (z % 2 == 0)
    bricks = mm(one(order), coarse).astype(BF)
    place = jnp.concatenate([place_ref[...].astype(F32)] * 8, axis=0)
    place = jnp.concatenate([place] * 2, axis=1)
    target = (8 * (col // 16) + col % 2).astype(F32)
    out_ref[...] = mm(one((place == target) & (row // 16 == col // 2 % 8)), bricks, TN).astype(BF)

    gec = jnp.concatenate([ge[(u * 10 + 1) * Z : (u * 10 + 9) * Z, :] for u in (1, 2)], axis=0)

    def put_a(at, v):
        grads_ref[core, at : at + v.shape[0], :] = v

    def put_b(at, v):
        grads_ref[1 - core, at : at + v.shape[0], :] = v

    for q in range(4):
        r = mm(corners[q], gec, TN).astype(BF)
        for c in range(2):
            t = 2 * q + c
            if t == 0:
                put_a(27 * C, lanes(r, c))
            else:
                put_b(27 * CIN + (t - 1) * C, lanes(r, c))
    put_b(27 * CIN + 7 * C, jnp.zeros((HALF - 27 * CIN - 7 * C, C), BF))
    weight_grad(firsts, 1, 1, C, lambda t, v: put_a(t * C, v))

    for x in range(X):
        p = taps(cots, x, Y, wb, NT, flip=True)
        g = lanes(p, 1) + from_above(lanes(p, 0)) + from_below(lanes(p, 2))
        g = g + cots(x + 1, 1, Y).astype(F32)
        g = (g * sg1[x * Y * Z : (x + 1) * Y * Z, :]).astype(BF)
        put_z_taps(x, g.astype(F32))
    weight_grad(cells, 2, 2, CIN, lambda t, v: put_b(t * CIN, v))


VM = pl.BlockSpec(memory_space=pltpu.VMEM)
SM = pl.BlockSpec(memory_space=pltpu.SMEM)


def call(kernel, outs, args, in_specs=None, scratch=(), flops=10_000_000):
    return pl.pallas_call(
        kernel,
        out_shape=tuple(jax.ShapeDtypeStruct(shape, dtype) for shape, dtype in outs),
        in_specs=in_specs or [VM] * len(args),
        out_specs=tuple([VM] * len(outs)),
        scratch_shapes=[pltpu.VMEM(shape, dtype) for shape, dtype in scratch],
        compiler_params=pltpu.CompilerParams(vmem_limit_bytes=40 * 1024 * 1024),
        cost_estimate=pl.CostEstimate(
            flops=flops, bytes_accessed=1_000_000, transcendentals=0
        ),
    )(*args)


def prepare(feat_ref, blocks_ref, owners_ref, own_ref, low_ref, high_ref, misc_ref, wide):
    lane = iota((Y, C), 1)
    for x in range(X):
        f = feat_ref[x].astype(F32)
        f = jnp.concatenate([f, jnp.zeros((Y, C), F32)], axis=1)
        for z in range(Z):
            t = jnp.where(lane < CIN, f[:, z * CIN : z * CIN + C], 0.0)
            wide[pl.ds(x * Y * Z + z, Y, stride=Z), :] = t
    part = iota((Z, C), 0) // 4
    for by in range(4):
        m = jnp.zeros((Z, C), jnp.int32)
        for bz in range(4):
            m = jnp.where(part == bz, blocks_ref[0, by, bz], m)
        m = m.astype(F32)
        misc_ref[by * Z : (by + 1) * Z, :] = m.astype(BF)
        for x in range(X):
            for y in range(4 * by, 4 * by + 4):
                at = (x * Y + y) * Z
                own_ref[at : at + Z, :] = (wide[at : at + Z, :] * m).astype(BF)
    dest = jnp.broadcast_to(owners_ref[0, 0].astype(F32), (16, C))
    row, lane = iota((16, C), 0), iota((16, C), 1)
    across = jnp.sum(jnp.where(row == lane, dest, 0.0), axis=0, keepdims=True)
    rank = jnp.sum(jnp.where((lane < row) & (dest == across), 1.0, 0.0), axis=1, keepdims=True)
    place = (dest * 8.0 + rank).astype(BF)
    misc_ref[4 * Z : 5 * Z, :] = place
    for x in range(X):
        low_ref[x * 3 * Z : (x + 1) * 3 * Z, :] = own_ref[(x * Y + 13) * Z : (x + 1) * Y * Z, :]
        high_ref[x * 3 * Z : (x + 1) * 3 * Z, :] = own_ref[x * Y * Z : (x * Y + 3) * Z, :]
    for ref, by in ((low_ref, 3), (high_ref, 0)):
        ref[192:208, :] = place
        ref[208:224, :] = misc_ref[by * Z : (by + 1) * Z, :]


def windows(grad_ref, misc_ref, rows_ref):
    row, col = iota((128, 32), 0), iota((128, 32), 1)
    take = one((col == 2 * (row // 8) - 2 + row % 8) & (row % 8 < 6))
    rows_ref[...] = mm(take, grad_ref[0, 0]).astype(BF)


def widen(own_ref, misc_ref, low_ref, high_ref, rows_ref, mid_ref, mask_ref, gc_ref, up_ref, down_ref):
    for x in range(X):
        at = x * 22 * Z
        mid_ref[at : at + 3 * Z, :] = low_ref[x * 3 * Z : (x + 1) * 3 * Z, :]
        mid_ref[at + 3 * Z : at + 19 * Z, :] = own_ref[x * Y * Z : (x + 1) * Y * Z, :]
        mid_ref[at + 19 * Z : at + 22 * Z, :] = high_ref[x * 3 * Z : (x + 1) * 3 * Z, :]
    mask_ref[0:Z, :] = low_ref[208:224, :]
    mask_ref[Z : 5 * Z, :] = misc_ref[0 : 4 * Z, :]
    mask_ref[5 * Z : 6 * Z, :] = high_ref[208:224, :]
    place = jnp.concatenate(
        [
            low_ref[192:208, :].astype(F32),
            misc_ref[4 * Z : 5 * Z, :].astype(F32) + 2.0,
            high_ref[192:208, :].astype(F32) + 4.0,
        ],
        axis=0,
    )
    bricks = mm(one(place == iota((48, C), 1).astype(F32)), rows_ref[...]).astype(BF)
    for q in range(4):
        gc_ref[0, q] = lanes(bricks, q)
        gc_ref[1, q] = lanes(bricks, 4 + q)
        up_ref[COTS + q * 48 : COTS + (q + 1) * 48, :] = lanes(bricks, 4 + q)
        down_ref[COTS + q * 48 : COTS + (q + 1) * 48, :] = lanes(bricks, q)
    up_ref[0:COTS, :] = mid_ref[22 * Z :, :]
    down_ref[0:COTS, :] = mid_ref[0:COTS, :]
    up_ref[MASK : MASK + 96, :] = mask_ref[...]
    down_ref[MASK : MASK + 96, :] = mask_ref[...]


def unfold(half_ref, other_ref, first_ref, second_ref, down_ref):
    here = (lax.axis_index("z"), lax.axis_index("x"))

    def emit(ref, core, spans):
        for n in range(16):
            s = [lax.rem(h - t + 4, 4) for h, t in zip(here, (n // 4, n % 4))]
            outer, inner = s if core == 0 else (s[1], s[0])
            at = pl.multiple_of((outer * 4 + inner) * PART, 16)
            for lo, hi, out, to in spans:
                i, j = max(lo, n * PART), min(hi, (n + 1) * PART)
                if i < j:
                    v = ref[pl.ds(at + i - n * PART, j - i), :].astype(F32)
                    out[to + i - lo : to + j - lo, :] = v

    def both(a_ref, b_ref):
        emit(a_ref, 0, ((0, 27 * C, second_ref, 0), (27 * C, 28 * C, down_ref, 0)))
        emit(b_ref, 1, ((0, 27 * CIN, first_ref, 0), (27 * CIN, 27 * CIN + 7 * C, down_ref, C)))

    @pl.when(lax.axis_index("c") == 0)
    def _():
        both(half_ref, other_ref)

    @pl.when(lax.axis_index("c") == 1)
    def _():
        both(other_ref, half_ref)


def shift(v, axes, step):
    n = lax.axis_size(axes)
    return lax.ppermute(v, axes, [(i, i + step) for i in range(n) if 0 <= i + step < n])


def swap_cores(v):
    return lax.ppermute(v, "c", [(0, 1), (1, 0)])


def up_matrix():
    m = np.zeros((6 * Z, 96), np.float32)
    for by in range(6):
        for z in range(Z):
            m[by * Z + z, z // 2 % 2 * 48 + (12, 16, 20, 24, 28, 32)[by] + z // 4] = 1
    return jnp.asarray(m, BF)


def turn(v, axes, step):
    size = [lax.axis_size(n) for n in ALL]
    pairs = []
    for d in range(math.prod(size)):
        at = list(np.unravel_index(d, size))
        n = ALL.index(axes[at[1]])
        at[n] = (at[n] + step) % size[n]
        pairs.append((d, int(np.ravel_multi_index(at, size))))
    return lax.ppermute(v, ALL, pairs)


def per_device(features, block_mask, weight_first, weight_second, weight_down, owners, moved_grad):
    own, low, high, misc = call(
        prepare,
        [((X * Y * Z, C), BF), ((224, C), BF), ((224, C), BF), ((80, C), BF)],
        (features, block_mask, owners),
        [VM, SM, VM],
        [((X * Y * Z, C), F32)],
    )
    low, high = shift(low, GY, 1), shift(high, GY, -1)
    (rows,) = call(windows, [((128, 8 * C), BF)], (moved_grad, misc))
    rows = lax.all_to_all(rows, GY, 0, 0, tiled=True)

    mid, mask, gc, up, down = call(
        widen,
        [((4 * 22 * Z, C), BF), ((96, C), BF), ((2, 4, 48, C), BF), ((STRIP, C), BF), ((STRIP, C), BF)],
        (own, misc, low, high, rows),
    )
    low, high = shift(up, GX, 1), shift(down, GX, -1)

    grads, outgoing = call(
        section,
        [((2, HALF, C), BF), ((256, C), BF)],
        (low, mid, high, mask, gc, misc[64:], weight_first, weight_second, weight_down, up_matrix()),
        scratch=[
            ((9 * C, 3 * C), BF),
            ((3 * C, 9 * C), BF),
            ((8 * 20 * Z, C), BF),
            ((X * Y * Z, C), F32),
            ((X * Y * Z, C), BF),
            ((40 * Z, 2 * C), BF),
            ((6 * 18 * Z, C), BF),
            ((X * Y * Z, 3 * C), BF),
            ((3 * C, 6 * Y * Z), BF),
        ],
        flops=8_000_000_000,
    )

    theirs = swap_cores(grads[1])
    half = (grads[0].astype(F32) + theirs.astype(F32)).astype(BF)
    pieces = lax.all_to_all(
        jnp.concatenate([half.reshape(16, PART, C), outgoing.reshape(16, 16, C)], axis=1),
        GY, 0, 0, tiled=True,
    )
    moved = pieces[:, PART:].reshape(16, 8, 2, C).transpose(0, 2, 1, 3).reshape(1, 1, 32, 8 * C)
    part = jnp.sum(pieces[:, :PART].astype(F32), axis=0).astype(BF)
    turned = [turn(part, ("y", "y"), n).astype(F32) for n in (1, 2, 3)]
    part = ((part.astype(F32) + turned[1]) + (turned[0] + turned[2])).astype(BF)
    for axes in (("x", "z"), ("z", "x")):
        part = jnp.concatenate([part] + [turn(part, axes, n) for n in (1, 2, 3)])
    grad_first, grad_second, grad_down = call(
        unfold,
        [((27 * CIN, C), F32), ((27 * C, C), F32), ((8 * C, C), F32)],
        (part, swap_cores(part)),
    )
    return (
        moved,
        grad_first.reshape(27, CIN, C),
        grad_second.reshape(27, C, C),
        grad_down.reshape(8, C, C),
    )


def solution(mesh):
    shape = dict(mesh.shape)
    fine = Mesh(
        mesh.devices.reshape(shape["gx"] // 2, 2, 4, shape["gy"] // 4), ("y", "c", "z", "x")
    )
    whole, tiles = P(GX, GY, None), P(GX, GY, None, None)
    return jax.shard_map(
        per_device,
        mesh=fine,
        in_specs=(whole, whole, P(), P(), P(), tiles, tiles),
        out_specs=(tiles, P(), P(), P()),
        check_vma=False,
    )
```

time: 123 us -> 111 us (0.902)
  blocking collectives: 47.8 us -> 23.6 us
  waiting for transfers between devices: 18.5 us -> 28.4 us
  starting transfers between devices: 27.3 us -> 34.8 us
  other arithmetic: 5.39 us -> 0.48 us
  Pallas kernels: 10.4 us -> 14.6 us
  local copies, waits for them, and re-layouts: 11.3 us -> 8 us
    all_to_all x2 -> x1, blocking collectives: 47.8 us -> 23.6 us  [per_device(): lax.all_to_all(jnp.concatenate([half.reshape(16, PART, C), outgoing.resha...]
    ppermute x0 -> x9, waiting for transfers between devices: none -> 14 us  [turn(): return lax.ppermute(v, ALL, pairs)]
    ppermute x0 -> x9, starting transfers between devices: none -> 7.91 us  [turn(): return lax.ppermute(v, ALL, pairs)]
    all_to_all x2 -> x1, waiting for transfers between devices: 6.74 us -> 0.01 us  [per_device(): rows = lax.all_to_all(rows, GY, 0, 0, tiled=True)]
    pallas_call x1 -> x5, Pallas kernels: 10.4 us -> 14.6 us  [call(): pl.pallas_call(kernel, out_shape=tuple((jax.ShapeDtypeStruct(shape, dtype...]
    unnamed x16 -> x20, local copies, waits for them, and re-layouts: 3.19 us -> 7.22 us
    ppermute x2, starting transfers between devices: 3.02 us -> 6.57 us  [swap_cores(): return lax.ppermute(v, 'c', [(0, 1), (1, 0)])]
    all_to_all x2 -> x1, starting transfers between devices: 11.9 us -> 8.43 us  [per_device(): rows = lax.all_to_all(rows, GY, 0, 0, tiled=True)]
  transfers between devices with their start and end apart: 8 -> 16, of which waited for: 5 -> 11; matrix products, arithmetic and copies ran while one was open for 6% -> 1% of each run, Pallas kernels for 0% -> 0%
where the time goes in v3:
time: 111 us
  starting transfers between devices  34.8 us (31%)
  waiting for transfers between devices  28.4 us (26%)
  blocking collectives  23.6 us (21%)
  Pallas kernels  14.6 us (13%)
  local copies, waits for them, and re-layouts  8 us (7%)
    all_to_all x1, blocking collectives, per_device(): lax.all_to_all(jnp.concatenate([half.reshape(16, PART, C), outgoing.resha...  23.6 us
    pallas_call x5, Pallas kernels, call(): pl.pallas_call(kernel, out_shape=tuple((jax.ShapeDtypeStruct(shape, dtype...  14.6 us
    ppermute x9, waiting for transfers between devices, turn(): return lax.ppermute(v, ALL, pairs)  14 us
    ppermute x4, starting transfers between devices, shift(): lax.ppermute(v, axes, [(i, i + step) for i in range(n) if 0 <= i + step <...  11.9 us
    ppermute x4, waiting for transfers between devices, shift(): lax.ppermute(v, axes, [(i, i + step) for i in range(n) if 0 <= i + step <...  10.5 us
    all_to_all x1, starting transfers between devices, per_device(): rows = lax.all_to_all(rows, GY, 0, 0, tiled=True)  8.43 us
    ppermute x9, starting transfers between devices, turn(): return lax.ppermute(v, ALL, pairs)  7.91 us
    unnamed x20, local copies, waits for them, and re-layouts  7.22 us
  transfers between devices with their start and end apart: 16, of which 11 were waited for; matrix products, arithmetic and copies ran while one was open for 1% of the time, Pallas kernels for 0%

profile of v3, /device:TPU:1, one launch (start us, length us, event | category | flops | bytes accessed | tf_op | source)
XLA Modules:
  0.0 110.8 jit_solution(12548053429826361611)
XLA Ops:
  0.6 0.7 copy.12.owners_ref
  1.4 0.0 copy-start
  1.4 0.9 copy-done
  2.3 0.0 copy-start.2
  2.3 0.7 copy-done.2
  3.0 0.8 shard_map.111
  3.8 0.0 copy-start.1
  3.8 0.8 copy-done.1
  4.6 0.9 shard_map.112
  5.6 8.4 %all-to-all-start = ((bf16[16,8,1024]{2,1,0:T(8,128)(2,1)}), bf16[16,8,1024]{2,1,0:T(8,128)(2,1)S(1)}, u32[]{:S(2)}, u32[]{:S(2)}) async-start(bf16[16,8,1024]{2,1,0:T(8,128)(2,1)} %bitcast), calls=%async_computation | async-start | bytes 524288 | tf_op jit(solution)/shard_map/all_to_all | solution.py:363
  14.0 3.3 %collective-permute-start = (bf16[224,128]{1,0:T(8,128)(2,1)S(1)}, bf16[224,128]{1,0:T(8,128)(2,1)S(1)}, u32[]{:S(2)}, u32[]{:S(2)}) collective-permute-start(bf16[224,128]{1,0:T(8,128)(2,1)S(1)} %get-tuple-element.20), channel_id=1, source_target_pairs={{0,1},{1,2},{2,3},{3,4},{4,5},{5,6},{6,7},{7,8},{8,9},{9,10},{10,1... | collective-permute-start | bytes 172040 | tf_op jit(solution)/shard_map/ppermute | solution.py:327
  17.3 1.3 %collective-permute-start.1 = (bf16[224,128]{1,0:T(8,128)(2,1)S(1)}, bf16[224,128]{1,0:T(8,128)(2,1)S(1)}, u32[]{:S(2)}, u32[]{:S(2)}) collective-permute-start(bf16[224,128]{1,0:T(8,128)(2,1)S(1)} %get-tuple-element.21), channel_id=1, source_target_pairs={{1,0},{2,1},{3,2},{4,3},{5,4},{6,5},{7,6},{8,7},{9,8},{10,9},{11,1... | collective-permute-start | bytes 172040 | tf_op jit(solution)/shard_map/ppermute | solution.py:327
  18.6 0.0 collective-permute-done.low_ref
  18.6 3.9 %collective-permute-done.1.high_ref = bf16[224,128]{1,0:T(8,128)(2,1)S(1)} collective-permute-done((bf16[224,128]{1,0:T(8,128)(2,1)S(1)}, bf16[224,128]{1,0:T(8,128)(2,1)S(1)}, u32[]{:S(2)}, u32[]{:S(2)}) %collective-permute-start.1) | collective-permute-done | bytes 57376 | tf_op jit(solution)/shard_map/ppermute | solution.py:327
  22.5 0.0 all-to-all-done
  22.5 0.2 shard_map.113
  22.7 5.5 %collective-permute-start.2 = (bf16[1344,128]{1,0:T(8,128)(2,1)S(1)}, bf16[1344,128]{1,0:T(8,128)(2,1)S(1)}, u32[]{:S(2)}, u32[]{:S(2)}) collective-permute-start(bf16[1344,128]{1,0:T(8,128)(2,1)S(1)} %get-tuple-element.22), channel_id=1, source_target_pairs={{0,16},{16,32},{32,48},{48,64},{64,80},{80,96},{96,112},{1,17},{17... | collective-permute-start | bytes 1032200 | tf_op jit(solution)/shard_map/ppermute | solution.py:327
  28.2 1.9 %collective-permute-start.3 = (bf16[1344,128]{1,0:T(8,128)(2,1)S(1)}, bf16[1344,128]{1,0:T(8,128)(2,1)S(1)}, u32[]{:S(2)}, u32[]{:S(2)}) collective-permute-start(bf16[1344,128]{1,0:T(8,128)(2,1)S(1)} %get-tuple-element.24), channel_id=1, source_target_pairs={{16,0},{32,16},{48,32},{64,48},{80,64},{96,80},{112,96},{17,1},{33... | collective-permute-start | bytes 1032200 | tf_op jit(solution)/shard_map/ppermute | solution.py:327
  30.1 2.2 %collective-permute-done.2.low_ref = bf16[1344,128]{1,0:T(8,128)(2,1)S(1)} collective-permute-done((bf16[1344,128]{1,0:T(8,128)(2,1)S(1)}, bf16[1344,128]{1,0:T(8,128)(2,1)S(1)}, u32[]{:S(2)}, u32[]{:S(2)}) %collective-permute-start.2) | collective-permute-done | bytes 344096 | tf_op jit(solution)/shard_map/ppermute | solution.py:327
  32.3 4.4 %collective-permute-done.3.high_ref = bf16[1344,128]{1,0:T(8,128)(2,1)S(1)} collective-permute-done((bf16[1344,128]{1,0:T(8,128)(2,1)S(1)}, bf16[1344,128]{1,0:T(8,128)(2,1)S(1)}, u32[]{:S(2)}, u32[]{:S(2)}) %collective-permute-start.3) | collective-permute-done | bytes 344096 | tf_op jit(solution)/shard_map/ppermute | solution.py:327
  36.7 0.0 copy-start.3
  36.7 1.2 %copy-done.3 = bf16[27,128,128]{2,1,0:T(8,128)(2,1)S(1)} copy-done((bf16[27,128,128]{2,1,0:T(8,128)(2,1)S(1)}, bf16[27,128,128]{2,1,0:T(8,128)(2,1)}, u32[]{:S(2)}) %copy-start.3) | copy-done | bytes 884760
  37.9 0.0 copy-start.4
  37.9 1.1 copy-done.4
  39.0 0.0 copy-start.5
  39.0 0.9 copy-done.5
  39.9 0.0 copy-start.6
  39.9 0.7 copy-done.6
  40.7 10.6 %shard_map.114 = (bf16[2,3584,128]{2,1,0:T(8,128)(2,1)S(1)}, bf16[256,128]{1,0:T(8,128)(2,1)S(1)}) custom-call(bf16[1344,128]{1,0:T(8,128)(2,1)S(1)} %collective-permute-done.2.low_ref, bf16[1408,128]{1,0:T(8,128)(2,1)S(1)} %get-tuple-element.23.mid_ref, bf16[1344,128]{1,0:T(8,128)(2,1)S(1)} %collective-permute-done.3.high_ref, ...), custom_call_target="tpu_custom_call" | custom-call | flops 8000000000 | bytes 1000000 | tf_op jit(solution)/shard_map/pallas_call | solution.py:217
  51.3 0.1 slice_bitcast_fusion
  51.4 0.1 collective-permute-start.4
  51.5 2.5 %collective-permute-done.4 = bf16[3584,128]{1,0:T(8,128)(2,1)S(1)} collective-permute-done((bf16[3584,128]{1,0:T(8,128)(2,1)S(1)}, bf16[3584,128]{1,0:T(8,128)(2,1)S(1)}, u32[]{:S(2)}, u32[]{:S(2)}) %collective-permute-start.4) | collective-permute-done | bytes 917536 | tf_op jit(solution)/shard_map/ppermute | solution.py:331
  53.9 0.2 fusion
  54.2 0.1 pad_maximum_fusion
  54.2 23.6 %all_to_all.16 = bf16[16,240,128]{2,1,0:T(8,128)(2,1)S(1)} all-to-all(bf16[16,240,128]{2,1,0:T(8,128)(2,1)S(1)} %pad_maximum_fusion), channel_id=1, replica_groups=mesh['y'=4,'c'=2,'z'=4,'x'=4] {'z','x'}, dimensions={0} | all-to-all | bytes 1966080 | tf_op jit(solution)/shard_map/all_to_all | solution.py:392
  77.9 0.1 slice_reduce_fusion
  78.0 0.9 collective-permute-start.7
  78.9 0.7 collective-permute-start.6
  79.5 2.6 %collective-permute-start.5 = (bf16[224,128]{1,0:T(8,128)(2,1)S(1)}, bf16[224,128]{1,0:T(8,128)(2,1)S(1)}, u32[]{:S(2)}, u32[]{:S(2)}) collective-permute-start(bf16[224,128]{1,0:T(8,128)(2,1)S(1)} %slice_reduce_fusion), channel_id=1, source_target_pairs={{0,64},{1,65},{2,66},{3,67},{4,68},{5,69},{6,70},{7,71},{8,72},{9,... | collective-permute-start | bytes 172040 | tf_op jit(solution)/shard_map/ppermute | solution.py:350
  82.2 0.0 collective-permute-done.7
  82.2 1.0 collective-permute-done.6
  83.1 1.2 %collective-permute-done.5 = bf16[224,128]{1,0:T(8,128)(2,1)S(1)} collective-permute-done((bf16[224,128]{1,0:T(8,128)(2,1)S(1)}, bf16[224,128]{1,0:T(8,128)(2,1)S(1)}, u32[]{:S(2)}, u32[]{:S(2)}) %collective-permute-start.5) | collective-permute-done | bytes 57376 | tf_op jit(solution)/shard_map/ppermute | solution.py:350
  84.4 0.6 collective-permute-start.10
  85.0 0.6 collective-permute-start.9
  85.6 0.3 collective-permute-start.8
  85.9 1.6 %collective-permute-done.10 = bf16[224,128]{1,0:T(8,128)(2,1)S(1)} collective-permute-done((bf16[224,128]{1,0:T(8,128)(2,1)S(1)}, bf16[224,128]{1,0:T(8,128)(2,1)S(1)}, u32[]{:S(2)}, u32[]{:S(2)}) %collective-permute-start.10) | collective-permute-done | bytes 57376 | tf_op jit(solution)/shard_map/ppermute | solution.py:350
  87.5 2.1 %collective-permute-done.9 = bf16[224,128]{1,0:T(8,128)(2,1)S(1)} collective-permute-done((bf16[224,128]{1,0:T(8,128)(2,1)S(1)}, bf16[224,128]{1,0:T(8,128)(2,1)S(1)}, u32[]{:S(2)}, u32[]{:S(2)}) %collective-permute-start.9) | collective-permute-done | bytes 57376 | tf_op jit(solution)/shard_map/ppermute | solution.py:350
  89.6 0.6 collective-permute-done.8
  90.2 0.9 collective-permute-start.13
  91.1 1.2 %collective-permute-start.12 = (bf16[896,128]{1,0:T(8,128)(2,1)S(1)}, bf16[896,128]{1,0:T(8,128)(2,1)S(1)}, u32[]{:S(2)}, u32[]{:S(2)}) collective-permute-start(bf16[896,128]{1,0:T(8,128)(2,1)S(1)} %pad_maximum_fusion.1), channel_id=1, source_target_pairs={{0,8},{1,9},{2,10},{3,11},{4,12},{5,13},{6,14},{7,15},{8,0},{9,1},... | collective-permute-start | bytes 688136 | tf_op jit(solution)/shard_map/ppermute | solution.py:350
  92.3 0.1 collective-permute-start.11
  92.5 7.5 %collective-permute-done.11 = bf16[896,128]{1,0:T(8,128)(2,1)S(1)} collective-permute-done((bf16[896,128]{1,0:T(8,128)(2,1)S(1)}, bf16[896,128]{1,0:T(8,128)(2,1)S(1)}, u32[]{:S(2)}, u32[]{:S(2)}) %collective-permute-start.11) | collective-permute-done | bytes 229408 | tf_op jit(solution)/shard_map/ppermute | solution.py:350
  100.0 0.0 collective-permute-done.12
  100.1 0.0 collective-permute-done.13
  100.1 6.5 %collective-permute-start.14 = (bf16[3584,128]{1,0:T(8,128)(2,1)S(1)}, bf16[3584,128]{1,0:T(8,128)(2,1)S(1)}, u32[]{:S(2)}, u32[]{:S(2)}) collective-permute-start(bf16[3584,128]{1,0:T(8,128)(2,1)S(1)} %constant_dynamic-update-slice_fusion.half_ref), channel_id=1, source_target_pairs={{0,16},{16,0},{1,17},{17,1},{2,18},{18,2},{3,19},{19,3},{4,20},{20... | collective-permute-start | bytes 2752520 | tf_op jit(solution)/shard_map/ppermute | solution.py:331
  106.6 0.7 reshape.36
  107.3 1.4 %collective-permute-done.14.other_ref = bf16[3584,128]{1,0:T(8,128)(2,1)S(1)} collective-permute-done((bf16[3584,128]{1,0:T(8,128)(2,1)S(1)}, bf16[3584,128]{1,0:T(8,128)(2,1)S(1)}, u32[]{:S(2)}, u32[]{:S(2)}) %collective-permute-start.14) | collective-permute-done | bytes 917536 | tf_op jit(solution)/shard_map/ppermute | solution.py:331
  108.7 2.0 %shard_map.115 = (f32[2592,128]{1,0:T(8,128)}, f32[3456,128]{1,0:T(8,128)}, f32[1024,128]{1,0:T(8,128)}) custom-call(bf16[3584,128]{1,0:T(8,128)(2,1)S(1)} %constant_dynamic-update-slice_fusion.half_ref, bf16[3584,128]{1,0:T(8,128)(2,1)S(1)} %collective-permute-done.14.other_ref), custom_call_target="tpu_custom_call" | custom-call | flops 10000000 | bytes 1000000 | tf_op jit(solution)/shard_map/pallas_call | solution.py:217
  (11 shorter events, 0.2 us)
Async XLA Ops:
  1.4 0.9 copy-start
  2.3 0.7 copy-start.2
  3.8 0.8 copy-start.1
  5.6 16.9 %all-to-all-start = ((bf16[16,8,1024]{2,1,0:T(8,128)(2,1)}), bf16[16,8,1024]{2,1,0:T(8,128)(2,1)S(1)}, u32[]{:S(2)}, u32[]{:S(2)}) async-start(bf16[16,8,1024]{2,1,0:T(8,128)(2,1)} %bitcast), calls=%async_computation | async-start | bytes 524288 | tf_op jit(solution)/shard_map/all_to_all | solution.py:363
  14.0 4.6 %collective-permute-start = (bf16[224,128]{1,0:T(8,128)(2,1)S(1)}, bf16[224,128]{1,0:T(8,128)(2,1)S(1)}, u32[]{:S(2)}, u32[]{:S(2)}) collective-permute-start(bf16[224,128]{1,0:T(8,128)(2,1)S(1)} %get-tuple-element.20), channel_id=1, source_target_pairs={{0,1},{1,2},{2,3},{3,4},{4,5},{5,6},{6,7},{7,8},{8,9},{9,10},{10,1... | collective-permute-start | bytes 172040 | tf_op jit(solution)/shard_map/ppermute | solution.py:327
  17.3 5.2 %collective-permute-start.1 = (bf16[224,128]{1,0:T(8,128)(2,1)S(1)}, bf16[224,128]{1,0:T(8,128)(2,1)S(1)}, u32[]{:S(2)}, u32[]{:S(2)}) collective-permute-start(bf16[224,128]{1,0:T(8,128)(2,1)S(1)} %get-tuple-element.21), channel_id=1, source_target_pairs={{1,0},{2,1},{3,2},{4,3},{5,4},{6,5},{7,6},{8,7},{9,8},{10,9},{11,1... | collective-permute-start | bytes 172040 | tf_op jit(solution)/shard_map/ppermute | solution.py:327
  22.7 9.6 %collective-permute-start.2 = (bf16[1344,128]{1,0:T(8,128)(2,1)S(1)}, bf16[1344,128]{1,0:T(8,128)(2,1)S(1)}, u32[]{:S(2)}, u32[]{:S(2)}) collective-permute-start(bf16[1344,128]{1,0:T(8,128)(2,1)S(1)} %get-tuple-element.22), channel_id=1, source_target_pairs={{0,16},{16,32},{32,48},{48,64},{64,80},{80,96},{96,112},{1,17},{17... | collective-permute-start | bytes 1032200 | tf_op jit(solution)/shard_map/ppermute | solution.py:327
  28.2 8.6 %collective-permute-start.3 = (bf16[1344,128]{1,0:T(8,128)(2,1)S(1)}, bf16[1344,128]{1,0:T(8,128)(2,1)S(1)}, u32[]{:S(2)}, u32[]{:S(2)}) collective-permute-start(bf16[1344,128]{1,0:T(8,128)(2,1)S(1)} %get-tuple-element.24), channel_id=1, source_target_pairs={{16,0},{32,16},{48,32},{64,48},{80,64},{96,80},{112,96},{17,1},{33... | collective-permute-start | bytes 1032200 | tf_op jit(solution)/shard_map/ppermute | solution.py:327
  36.7 1.2 %copy-start.3 = (bf16[27,128,128]{2,1,0:T(8,128)(2,1)S(1)}, bf16[27,128,128]{2,1,0:T(8,128)(2,1)}, u32[]{:S(2)}) copy-start(bf16[27,128,128]{2,1,0:T(8,128)(2,1)} %w2_ref.1) | copy-start | bytes 2654212
  37.9 1.1 copy-start.4
  39.0 0.9 copy-start.5
  39.9 0.7 copy-start.6
  51.4 2.6 %collective-permute-start.4 = (bf16[3584,128]{1,0:T(8,128)(2,1)S(1)}, bf16[3584,128]{1,0:T(8,128)(2,1)S(1)}, u32[]{:S(2)}, u32[]{:S(2)}) collective-permute-start(bf16[3584,128]{1,0:T(8,128)(2,1)S(1)} %slice_bitcast_fusion), channel_id=1, source_target_pairs={{0,16},{16,0},{1,17},{17,1},{2,18},{18,2},{3,19},{19,3},{4,20},{20... | collective-permute-start | bytes 2752520 | tf_op jit(solution)/shard_map/ppermute | solution.py:331
  78.0 4.2 %collective-permute-start.7 = (bf16[224,128]{1,0:T(8,128)(2,1)S(1)}, bf16[224,128]{1,0:T(8,128)(2,1)S(1)}, u32[]{:S(2)}, u32[]{:S(2)}) collective-permute-start(bf16[224,128]{1,0:T(8,128)(2,1)S(1)} %slice_reduce_fusion), channel_id=1, source_target_pairs={{0,96},{1,97},{2,98},{3,99},{4,100},{5,101},{6,102},{7,103},{8,104... | collective-permute-start | bytes 172040 | tf_op jit(solution)/shard_map/ppermute | solution.py:350
  78.9 4.2 %collective-permute-start.6 = (bf16[224,128]{1,0:T(8,128)(2,1)S(1)}, bf16[224,128]{1,0:T(8,128)(2,1)S(1)}, u32[]{:S(2)}, u32[]{:S(2)}) collective-permute-start(bf16[224,128]{1,0:T(8,128)(2,1)S(1)} %slice_reduce_fusion), channel_id=1, source_target_pairs={{0,32},{1,33},{2,34},{3,35},{4,36},{5,37},{6,38},{7,39},{8,40},{9,... | collective-permute-start | bytes 172040 | tf_op jit(solution)/shard_map/ppermute | solution.py:350
  79.5 4.8 %collective-permute-start.5 = (bf16[224,128]{1,0:T(8,128)(2,1)S(1)}, bf16[224,128]{1,0:T(8,128)(2,1)S(1)}, u32[]{:S(2)}, u32[]{:S(2)}) collective-permute-start(bf16[224,128]{1,0:T(8,128)(2,1)S(1)} %slice_reduce_fusion), channel_id=1, source_target_pairs={{0,64},{1,65},{2,66},{3,67},{4,68},{5,69},{6,70},{7,71},{8,72},{9,... | collective-permute-start | bytes 172040 | tf_op jit(solution)/shard_map/ppermute | solution.py:350
  84.4 3.1 %collective-permute-start.10 = (bf16[224,128]{1,0:T(8,128)(2,1)S(1)}, bf16[224,128]{1,0:T(8,128)(2,1)S(1)}, u32[]{:S(2)}, u32[]{:S(2)}) collective-permute-start(bf16[224,128]{1,0:T(8,128)(2,1)S(1)} %get-tuple-element.33), channel_id=1, source_target_pairs={{0,3},{1,0},{2,1},{3,2},{4,7},{5,4},{6,5},{7,6},{8,11},{9,8},{10,9... | collective-permute-start | bytes 172040 | tf_op jit(solution)/shard_map/ppermute | solution.py:350
  85.0 4.6 %collective-permute-start.9 = (bf16[224,128]{1,0:T(8,128)(2,1)S(1)}, bf16[224,128]{1,0:T(8,128)(2,1)S(1)}, u32[]{:S(2)}, u32[]{:S(2)}) collective-permute-start(bf16[224,128]{1,0:T(8,128)(2,1)S(1)} %get-tuple-element.33), channel_id=1, source_target_pairs={{0,2},{1,3},{2,0},{3,1},{4,6},{5,7},{6,4},{7,5},{8,10},{9,11},{10,... | collective-permute-start | bytes 172040 | tf_op jit(solution)/shard_map/ppermute | solution.py:350
  85.6 4.6 %collective-permute-start.8 = (bf16[224,128]{1,0:T(8,128)(2,1)S(1)}, bf16[224,128]{1,0:T(8,128)(2,1)S(1)}, u32[]{:S(2)}, u32[]{:S(2)}) collective-permute-start(bf16[224,128]{1,0:T(8,128)(2,1)S(1)} %get-tuple-element.33), channel_id=1, source_target_pairs={{0,1},{1,2},{2,3},{3,0},{4,5},{5,6},{6,7},{7,4},{8,9},{9,10},{10,1... | collective-permute-start | bytes 172040 | tf_op jit(solution)/shard_map/ppermute | solution.py:350
  90.2 9.9 %collective-permute-start.13 = (bf16[896,128]{1,0:T(8,128)(2,1)S(1)}, bf16[896,128]{1,0:T(8,128)(2,1)S(1)}, u32[]{:S(2)}, u32[]{:S(2)}) collective-permute-start(bf16[896,128]{1,0:T(8,128)(2,1)S(1)} %pad_maximum_fusion.1), channel_id=1, source_target_pairs={{0,12},{1,13},{2,14},{3,15},{4,0},{5,1},{6,2},{7,3},{8,4},{9,5},{1... | collective-permute-start | bytes 688136 | tf_op jit(solution)/shard_map/ppermute | solution.py:350
  91.1 8.9 %collective-permute-start.12 = (bf16[896,128]{1,0:T(8,128)(2,1)S(1)}, bf16[896,128]{1,0:T(8,128)(2,1)S(1)}, u32[]{:S(2)}, u32[]{:S(2)}) collective-permute-start(bf16[896,128]{1,0:T(8,128)(2,1)S(1)} %pad_maximum_fusion.1), channel_id=1, source_target_pairs={{0,8},{1,9},{2,10},{3,11},{4,12},{5,13},{6,14},{7,15},{8,0},{9,1},... | collective-permute-start | bytes 688136 | tf_op jit(solution)/shard_map/ppermute | solution.py:350
  92.3 7.7 %collective-permute-start.11 = (bf16[896,128]{1,0:T(8,128)(2,1)S(1)}, bf16[896,128]{1,0:T(8,128)(2,1)S(1)}, u32[]{:S(2)}, u32[]{:S(2)}) collective-permute-start(bf16[896,128]{1,0:T(8,128)(2,1)S(1)} %pad_maximum_fusion.1), channel_id=1, source_target_pairs={{0,4},{1,5},{2,6},{3,7},{4,8},{5,9},{6,10},{7,11},{8,12},{9,13},{1... | collective-permute-start | bytes 688136 | tf_op jit(solution)/shard_map/ppermute | solution.py:350
  100.1 8.6 %collective-permute-start.14 = (bf16[3584,128]{1,0:T(8,128)(2,1)S(1)}, bf16[3584,128]{1,0:T(8,128)(2,1)S(1)}, u32[]{:S(2)}, u32[]{:S(2)}) collective-permute-start(bf16[3584,128]{1,0:T(8,128)(2,1)S(1)} %constant_dynamic-update-slice_fusion.half_ref), channel_id=1, source_target_pairs={{0,16},{16,0},{1,17},{17,1},{2,18},{18,2},{3,19},{19,3},{4,20},{20... | collective-permute-start | bytes 2752520 | tf_op jit(solution)/shard_map/ppermute | solution.py:331

commit v4 on v3

--- a/solution.py
+++ b/solution.py
@@ -46,9 +46,9 @@
 
 
 def section(
-    low_ref, mid_ref, high_ref, mask_ref, gc_ref, place_ref, w1_ref, w2_ref, wd_ref, up_ref,
+    low_ref, mid_ref, high_ref, mask_ref, gc_ref, misc_ref, w1_ref, w2_ref, back_ref, wd_ref, up_ref,
     grads_ref, out_ref,
-    wa, wb, first, sg1, second, ge, g2, gs, vt,
+    first, sg1, second, ge, g2, gs, vt,
 ):
     core = lax.axis_index("c")
 
@@ -100,13 +100,8 @@
         gs[at : at + Y * Z, C : 2 * C] = g.astype(BF)
         gs[at : at + Y * Z, 2 * C : 3 * C] = from_below(g).astype(BF)
 
-    for m in range(9):
-        for k in range(3):
-            wa[m * C : m * C + CIN, k * C : (k + 1) * C] = w1_ref[3 * m + k]
-        wa[m * C + CIN : (m + 1) * C, :] = jnp.zeros((C - CIN, 3 * C), BF)
-
     for x in range(8):
-        p = taps(cells, x, 20, wa)
+        p = taps(cells, x, 20, w1_ref)
         act = line(x - 2, -2, 20)
         pre = act * (lanes(p, 1) + from_below(lanes(p, 0)) + from_above(lanes(p, 2)))
         s = jax.nn.sigmoid(pre)
@@ -114,11 +109,6 @@
         if 2 <= x < 6:
             d = act * (s * (1.0 + pre * (1.0 - s)))
             sg1[(x - 2) * Y * Z : (x - 1) * Y * Z, :] = d[2 * Z : 18 * Z]
-
-    for m in range(9):
-        for k in range(3):
-            wa[m * C : (m + 1) * C, k * C : (k + 1) * C] = w2_ref[3 * m + k]
-            wb[k * C : (k + 1) * C, m * C : (m + 1) * C] = w2_ref[3 * m + k]
 
     even = z_of(6 * Z) % 2 == 0
     for u in range(4):
@@ -135,7 +125,7 @@
             ge[at : at + Z, C : 2 * C] = jnp.where(even[:Z], 0.0, t).astype(BF)
 
     for x in range(6):
-        p = taps(firsts, x, 18, wa)
+        p = taps(firsts, x, 18, w2_ref)
         act = line(x - 1, -1, 18)
         pre = act * (lanes(p, 1) + from_below(lanes(p, 0)) + from_above(lanes(p, 2)))
         pre = pre + firsts(x + 1, 1, 18).astype(F32)
@@ -176,7 +166,7 @@
     a, by, b, z = col // 128, col // 32 % 4, col // 16 % 2, col % Z
     order = (row // 16 == 4 * a + 2 * b + z // 2 % 2) & (row % 16 == by * 4 + z // 4) & (z % 2 == 0)
     bricks = mm(one(order), coarse).astype(BF)
-    place = jnp.concatenate([place_ref[...].astype(F32)] * 8, axis=0)
+    place = jnp.concatenate([misc_ref[4 * Z : 5 * Z, :].astype(F32)] * 8, axis=0)
     place = jnp.concatenate([place] * 2, axis=1)
     target = (8 * (col // 16) + col % 2).astype(F32)
     out_ref[...] = mm(one((place == target) & (row // 16 == col // 2 % 8)), bricks, TN).astype(BF)
@@ -201,7 +191,7 @@
     weight_grad(firsts, 1, 1, C, lambda t, v: put_a(t * C, v))
 
     for x in range(X):
-        p = taps(cots, x, Y, wb, NT, flip=True)
+        p = taps(cots, x, Y, back_ref, NT, flip=True)
         g = lanes(p, 1) + from_above(lanes(p, 0)) + from_below(lanes(p, 2))
         g = g + cots(x + 1, 1, Y).astype(F32)
         g = (g * sg1[x * Y * Z : (x + 1) * Y * Z, :]).astype(BF)
@@ -210,24 +200,49 @@
 
 
 VM = pl.BlockSpec(memory_space=pltpu.VMEM)
-SM = pl.BlockSpec(memory_space=pltpu.SMEM)
-
-
-def call(kernel, outs, args, in_specs=None, scratch=(), flops=10_000_000):
+
+
+def call(kernel, outs, args, in_specs=None, scratch=(), flops=10_000_000, vmem=40 << 20):
     return pl.pallas_call(
         kernel,
         out_shape=tuple(jax.ShapeDtypeStruct(shape, dtype) for shape, dtype in outs),
         in_specs=in_specs or [VM] * len(args),
         out_specs=tuple([VM] * len(outs)),
-        scratch_shapes=[pltpu.VMEM(shape, dtype) for shape, dtype in scratch],
-        compiler_params=pltpu.CompilerParams(vmem_limit_bytes=40 * 1024 * 1024),
+        scratch_shapes=[pltpu.VMEM(*s) if isinstance(s, tuple) else s for s in scratch],
+        compiler_params=pltpu.CompilerParams(vmem_limit_bytes=vmem),
         cost_estimate=pl.CostEstimate(
             flops=flops, bytes_accessed=1_000_000, transcendentals=0
         ),
     )(*args)
 
 
-def prepare(feat_ref, blocks_ref, owners_ref, own_ref, low_ref, high_ref, misc_ref, wide):
+def arrange(w1_ref, w2_ref, after_ref, first_ref, second_ref, back_ref):
+    for m in range(9):
+        for k in range(3):
+            first_ref[m * C : m * C + CIN, k * C : (k + 1) * C] = w1_ref[3 * m + k]
+            second_ref[m * C : (m + 1) * C, k * C : (k + 1) * C] = w2_ref[3 * m + k]
+            back_ref[k * C : (k + 1) * C, m * C : (m + 1) * C] = w2_ref[3 * m + k]
+        first_ref[m * C + CIN : (m + 1) * C, :] = jnp.zeros((C - CIN, 3 * C), BF)
+
+
+def prepare(
+    grad_hbm, feat_hbm, blocks_hbm, owners_hbm, rows_ref, own_ref, low_ref, high_ref, misc_ref,
+    wide, grad_ref, feat_ref, blocks_ref, owners_ref, sems,
+):
+    copies = [
+        pltpu.make_async_copy(a, b, sems.at[n])
+        for n, (a, b) in enumerate(
+            ((grad_hbm, grad_ref), (feat_hbm, feat_ref), (blocks_hbm, blocks_ref), (owners_hbm, owners_ref))
+        )
+    ]
+    for c in copies:
+        c.start()
+    copies[0].wait()
+    row, col = iota((128, 32), 0), iota((128, 32), 1)
+    take = one((col == 2 * (row // 8) - 2 + row % 8) & (row % 8 < 6))
+    rows_ref[...] = mm(take, grad_ref[0, 0]).astype(BF)
+    for c in copies[1:]:
+        c.wait()
     lane = iota((Y, C), 1)
     for x in range(X):
         f = feat_ref[x].astype(F32)
@@ -235,22 +250,21 @@
         for z in range(Z):
             t = jnp.where(lane < CIN, f[:, z * CIN : z * CIN + C], 0.0)
             wide[pl.ds(x * Y * Z + z, Y, stride=Z), :] = t
-    part = iota((Z, C), 0) // 4
+    blocks = blocks_ref[0].astype(F32)
+    mine = iota((Z, 4), 0) // 4 == iota((Z, 4), 1)
     for by in range(4):
-        m = jnp.zeros((Z, C), jnp.int32)
-        for bz in range(4):
-            m = jnp.where(part == bz, blocks_ref[0, by, bz], m)
-        m = m.astype(F32)
+        m = jnp.sum(jnp.where(mine, blocks[by : by + 1, :], 0.0), axis=1, keepdims=True)
+        m = jnp.broadcast_to(m, (Z, C))
         misc_ref[by * Z : (by + 1) * Z, :] = m.astype(BF)
         for x in range(X):
             for y in range(4 * by, 4 * by + 4):
                 at = (x * Y + y) * Z
                 own_ref[at : at + Z, :] = (wide[at : at + Z, :] * m).astype(BF)
-    dest = jnp.broadcast_to(owners_ref[0, 0].astype(F32), (16, C))
-    row, lane = iota((16, C), 0), iota((16, C), 1)
-    across = jnp.sum(jnp.where(row == lane, dest, 0.0), axis=0, keepdims=True)
-    rank = jnp.sum(jnp.where((lane < row) & (dest == across), 1.0, 0.0), axis=1, keepdims=True)
-    place = (dest * 8.0 + rank).astype(BF)
+    row, col = iota((16, 16), 0), iota((16, 16), 1)
+    across = jnp.broadcast_to(owners_ref[...].astype(F32), (16, 16))
+    dest = jnp.sum(jnp.where(row == col, across, 0.0), axis=1, keepdims=True)
+    rank = jnp.sum(jnp.where((col < row) & (dest == across), 1.0, 0.0), axis=1, keepdims=True)
+    place = jnp.broadcast_to(dest * 8.0 + rank, (16, C)).astype(BF)
     misc_ref[4 * Z : 5 * Z, :] = place
     for x in range(X):
         low_ref[x * 3 * Z : (x + 1) * 3 * Z, :] = own_ref[(x * Y + 13) * Z : (x + 1) * Y * Z, :]
@@ -258,12 +272,6 @@
     for ref, by in ((low_ref, 3), (high_ref, 0)):
         ref[192:208, :] = place
         ref[208:224, :] = misc_ref[by * Z : (by + 1) * Z, :]
-
-
-def windows(grad_ref, misc_ref, rows_ref):
-    row, col = iota((128, 32), 0), iota((128, 32), 1)
-    take = one((col == 2 * (row // 8) - 2 + row % 8) & (row % 8 < 6))
-    rows_ref[...] = mm(take, grad_ref[0, 0]).astype(BF)
 
 
 def widen(own_ref, misc_ref, low_ref, high_ref, rows_ref, mid_ref, mask_ref, gc_ref, up_ref, down_ref):
@@ -296,22 +304,11 @@
 
 
 def unfold(half_ref, other_ref, first_ref, second_ref, down_ref):
-    here = (lax.axis_index("z"), lax.axis_index("x"))
-
-    def emit(ref, core, spans):
-        for n in range(16):
-            s = [lax.rem(h - t + 4, 4) for h, t in zip(here, (n // 4, n % 4))]
-            outer, inner = s if core == 0 else (s[1], s[0])
-            at = pl.multiple_of((outer * 4 + inner) * PART, 16)
-            for lo, hi, out, to in spans:
-                i, j = max(lo, n * PART), min(hi, (n + 1) * PART)
-                if i < j:
-                    v = ref[pl.ds(at + i - n * PART, j - i), :].astype(F32)
-                    out[to + i - lo : to + j - lo, :] = v
-
     def both(a_ref, b_ref):
-        emit(a_ref, 0, ((0, 27 * C, second_ref, 0), (27 * C, 28 * C, down_ref, 0)))
-        emit(b_ref, 1, ((0, 27 * CIN, first_ref, 0), (27 * CIN, 27 * CIN + 7 * C, down_ref, C)))
+        second_ref[...] = a_ref[: 27 * C, :].astype(F32)
+        down_ref[:C, :] = a_ref[27 * C :, :].astype(F32)
+        first_ref[...] = b_ref[: 27 * CIN, :].astype(F32)
+        down_ref[C:, :] = b_ref[27 * CIN : 27 * CIN + 7 * C, :].astype(F32)
 
     @pl.when(lax.axis_index("c") == 0)
     def _():
@@ -351,15 +348,22 @@
 
 
 def per_device(features, block_mask, weight_first, weight_second, weight_down, owners, moved_grad):
-    own, low, high, misc = call(
+    rows, own, low, high, misc = call(
         prepare,
-        [((X * Y * Z, C), BF), ((224, C), BF), ((224, C), BF), ((80, C), BF)],
-        (features, block_mask, owners),
-        [VM, SM, VM],
-        [((X * Y * Z, C), F32)],
+        [((128, 8 * C), BF), ((X * Y * Z, C), BF), ((224, C), BF), ((224, C), BF), ((80, C), BF)],
+        (moved_grad, features, block_mask, owners.reshape(1, 16)),
+        [pl.BlockSpec(memory_space=pltpu.HBM)] * 4,
+        [
+            ((X * Y * Z, C), F32),
+            (moved_grad.shape, BF),
+            (features.shape, BF),
+            (block_mask.shape, jnp.int32),
+            ((1, 16), jnp.int32),
+            pltpu.SemaphoreType.DMA((4,)),
+        ],
+        vmem=60 << 20,
     )
     low, high = shift(low, GY, 1), shift(high, GY, -1)
-    (rows,) = call(windows, [((128, 8 * C), BF)], (moved_grad, misc))
     rows = lax.all_to_all(rows, GY, 0, 0, tiled=True)
 
     mid, mask, gc, up, down = call(
@@ -368,14 +372,18 @@
         (own, misc, low, high, rows),
     )
     low, high = shift(up, GX, 1), shift(down, GX, -1)
+    w1, w2, back = call(
+        arrange,
+        [((9 * C, 3 * C), BF), ((9 * C, 3 * C), BF), ((3 * C, 9 * C), BF)],
+        (weight_first, weight_second, mask),
+        flops=2_000_000_000,
+    )
 
     grads, outgoing = call(
         section,
         [((2, HALF, C), BF), ((256, C), BF)],
-        (low, mid, high, mask, gc, misc[64:], weight_first, weight_second, weight_down, up_matrix()),
+        (low, mid, high, mask, gc, misc, w1, w2, back, weight_down, up_matrix()),
         scratch=[
-            ((9 * C, 3 * C), BF),
-            ((3 * C, 9 * C), BF),
             ((8 * 20 * Z, C), BF),
             ((X * Y * Z, C), F32),
             ((X * Y * Z, C), BF),
@@ -397,8 +405,8 @@
     part = jnp.sum(pieces[:, :PART].astype(F32), axis=0).astype(BF)
     turned = [turn(part, ("y", "y"), n).astype(F32) for n in (1, 2, 3)]
     part = ((part.astype(F32) + turned[1]) + (turned[0] + turned[2])).astype(BF)
-    for axes in (("x", "z"), ("z", "x")):
-        part = jnp.concatenate([part] + [turn(part, axes, n) for n in (1, 2, 3)])
+    part = lax.all_to_all(jnp.broadcast_to(part[None], (16, PART, C)), GY, 0, 0, tiled=True)
+    part = part.reshape(HALF, C)
     grad_first, grad_second, grad_down = call(
         unfold,
         [((27 * CIN, C), F32), ((27 * C, C), F32), ((8 * C, C), F32)],

time: 111 us -> 104 us (0.937)
  blocking collectives: 23.6 us -> 39.6 us
  waiting for transfers between devices: 28.4 us -> 14.2 us
  starting transfers between devices: 34.8 us -> 28.5 us
  local copies, waits for them, and re-layouts: 8 us -> 4.8 us
    all_to_all x0 -> x1, blocking collectives: none -> 15.9 us  [per_device(): lax.all_to_all(jnp.broadcast_to(part[None], (16, PART, C)), GY, 0, 0, til...]
    ppermute x9 -> x3, waiting for transfers between devices: 14 us -> 2.17 us  [turn(): return lax.ppermute(v, ALL, pairs)]
    ppermute x9 -> x3, starting transfers between devices: 7.91 us -> 4.16 us  [turn(): return lax.ppermute(v, ALL, pairs)]
    unnamed x20 -> x14, local copies, waits for them, and re-layouts: 7.22 us -> 3.94 us
    ppermute x2, starting transfers between devices: 6.57 us -> 3.99 us  [swap_cores(): return lax.ppermute(v, 'c', [(0, 1), (1, 0)])]
    ppermute x4, waiting for transfers between devices: 10.5 us -> 8.13 us  [shift(): lax.ppermute(v, axes, [(i, i + step) for i in range(n) if 0 <= i + step <...]
  transfers between devices with their start and end apart: 16 -> 10, of which waited for: 11 -> 7; matrix products, arithmetic and copies ran while one was open for 1% -> 1% of each run, Pallas kernels for 0% -> 0%
where the time goes in v4:
time: 104 us
  blocking collectives  39.6 us (38%)
  starting transfers between devices  28.5 us (27%)
  Pallas kernels  15.3 us (15%)
  waiting for transfers between devices  14.2 us (14%)
  local copies, waits for them, and re-layouts  4.8 us (5%)
    all_to_all x1, blocking collectives, per_device(): lax.all_to_all(jnp.concatenate([half.reshape(16, PART, C), outgoing.resha...  23.6 us
    all_to_all x1, blocking collectives, per_device(): lax.all_to_all(jnp.broadcast_to(part[None], (16, PART, C)), GY, 0, 0, til...  15.9 us
    pallas_call x5, Pallas kernels, call(): pl.pallas_call(kernel, out_shape=tuple((jax.ShapeDtypeStruct(shape, dtype...  15.3 us
    ppermute x4, starting transfers between devices, shift(): lax.ppermute(v, axes, [(i, i + step) for i in range(n) if 0 <= i + step <...  11.9 us
    all_to_all x1, starting transfers between devices, per_device(): rows = lax.all_to_all(rows, GY, 0, 0, tiled=True)  8.44 us
    ppermute x4, waiting for transfers between devices, shift(): lax.ppermute(v, axes, [(i, i + step) for i in range(n) if 0 <= i + step <...  8.13 us
    ppermute x3, starting transfers between devices, turn(): return lax.ppermute(v, ALL, pairs)  4.16 us
    ppermute x2, starting transfers between devices, swap_cores(): return lax.ppermute(v, 'c', [(0, 1), (1, 0)])  3.99 us
  transfers between devices with their start and end apart: 10, of which 7 were waited for; matrix products, arithmetic and copies ran while one was open for 1% of the time, Pallas kernels for 0%

profile of v4, /device:TPU:1, one launch (start us, length us, event | category | flops | bytes accessed | tf_op | source)
XLA Modules:
  0.0 103.6 jit_solution(448540885177871878)
XLA Ops:
  0.6 2.1 %shard_map.111 = (bf16[128,1024]{1,0:T(8,128)(2,1)}, bf16[1024,128]{1,0:T(8,128)(2,1)}, bf16[224,128]{1,0:T(8,128)(2,1)}, bf16[224,128]{1,0:T(8,128)(2,1)}, bf16[80,128]{1,0:T(8,128)(2,1)}) custom-call(bf16[1,1,32,1024]{3,2,1,0:T(8,128)(2,1)} %grad_hbm.1, bf16[4,16,1536]{2,1,0:T(8,128)(2,1)} %feat_hbm.1, s32[1,4,4]{2,1,0:T(4,128)} %blocks_hbm.1, ...), custom_call_target="tpu_custom_call" | custom-call | flops 10000000 | bytes 1000000 | tf_op jit(solution)/shard_map/pallas_call | solution.py:206
  2.7 8.4 %all-to-all-start = ((bf16[16,8,1024]{2,1,0:T(8,128)(2,1)}), bf16[16,8,1024]{2,1,0:T(8,128)(2,1)S(1)}, u32[]{:S(2)}, u32[]{:S(2)}) async-start(bf16[16,8,1024]{2,1,0:T(8,128)(2,1)} %bitcast.25), calls=%async_computation | async-start | bytes 524288 | tf_op jit(solution)/shard_map/all_to_all | solution.py:367
  11.2 3.3 %collective-permute-start = (bf16[224,128]{1,0:T(8,128)(2,1)}, bf16[224,128]{1,0:T(8,128)(2,1)S(1)}, u32[]{:S(2)}, u32[]{:S(2)}) collective-permute-start(bf16[224,128]{1,0:T(8,128)(2,1)} %get-tuple-element.24), channel_id=1, source_target_pairs={{0,1},{1,2},{2,3},{3,4},{4,5},{5,6},{6,7},{7,8},{8,9},{9,10},{10,1... | collective-permute-start | bytes 172040 | tf_op jit(solution)/shard_map/ppermute | solution.py:324
  14.4 1.3 %collective-permute-start.1 = (bf16[224,128]{1,0:T(8,128)(2,1)}, bf16[224,128]{1,0:T(8,128)(2,1)S(1)}, u32[]{:S(2)}, u32[]{:S(2)}) collective-permute-start(bf16[224,128]{1,0:T(8,128)(2,1)} %get-tuple-element.25), channel_id=1, source_target_pairs={{1,0},{2,1},{3,2},{4,3},{5,4},{6,5},{7,6},{8,7},{9,8},{10,9},{11,1... | collective-permute-start | bytes 172040 | tf_op jit(solution)/shard_map/ppermute | solution.py:324
  15.7 0.3 collective-permute-done.low_ref
  16.0 3.9 %collective-permute-done.1.high_ref = bf16[224,128]{1,0:T(8,128)(2,1)S(1)} collective-permute-done((bf16[224,128]{1,0:T(8,128)(2,1)}, bf16[224,128]{1,0:T(8,128)(2,1)S(1)}, u32[]{:S(2)}, u32[]{:S(2)}) %collective-permute-start.1) | collective-permute-done | bytes 57376 | tf_op jit(solution)/shard_map/ppermute | solution.py:324
  19.9 0.0 all-to-all-done
  19.9 0.0 copy-start
  19.9 0.9 copy-done
  20.8 0.0 copy-start.1
  20.8 0.7 copy-done.1
  21.5 0.2 shard_map.112
  21.7 5.5 %collective-permute-start.2 = (bf16[1344,128]{1,0:T(8,128)(2,1)S(1)}, bf16[1344,128]{1,0:T(8,128)(2,1)S(1)}, u32[]{:S(2)}, u32[]{:S(2)}) collective-permute-start(bf16[1344,128]{1,0:T(8,128)(2,1)S(1)} %get-tuple-element.27), channel_id=1, source_target_pairs={{0,16},{16,32},{32,48},{48,64},{64,80},{80,96},{96,112},{1,17},{17... | collective-permute-start | bytes 1032200 | tf_op jit(solution)/shard_map/ppermute | solution.py:324
  27.2 1.9 %collective-permute-start.3 = (bf16[1344,128]{1,0:T(8,128)(2,1)S(1)}, bf16[1344,128]{1,0:T(8,128)(2,1)S(1)}, u32[]{:S(2)}, u32[]{:S(2)}) collective-permute-start(bf16[1344,128]{1,0:T(8,128)(2,1)S(1)} %get-tuple-element.29), channel_id=1, source_target_pairs={{16,0},{32,16},{48,32},{64,48},{80,64},{96,80},{112,96},{17,1},{33... | collective-permute-start | bytes 1032200 | tf_op jit(solution)/shard_map/ppermute | solution.py:324
  29.1 0.0 copy-start.3
  29.2 1.2 %copy-done.3 = bf16[27,128,128]{2,1,0:T(8,128)(2,1)S(1)} copy-done((bf16[27,128,128]{2,1,0:T(8,128)(2,1)S(1)}, bf16[27,128,128]{2,1,0:T(8,128)(2,1)}, u32[]{:S(2)}) %copy-start.3) | copy-done | bytes 884760
  30.3 0.0 copy-start.4
  30.3 1.1 %copy-done.4 = bf16[27,96,128]{2,1,0:T(8,128)(2,1)S(1)} copy-done((bf16[27,96,128]{2,1,0:T(8,128)(2,1)S(1)}, bf16[27,96,128]{2,1,0:T(8,128)(2,1)}, u32[]{:S(2)}) %copy-start.4) | copy-done | bytes 663576
  31.4 0.0 copy-start.2
  31.4 0.0 copy-start.5
  31.4 0.0 copy-start.6
  31.4 0.4 shard_map.113
  31.8 0.0 collective-permute-done.2.low_ref
  31.8 4.0 %collective-permute-done.3.high_ref = bf16[1344,128]{1,0:T(8,128)(2,1)S(1)} collective-permute-done((bf16[1344,128]{1,0:T(8,128)(2,1)S(1)}, bf16[1344,128]{1,0:T(8,128)(2,1)S(1)}, u32[]{:S(2)}, u32[]{:S(2)}) %collective-permute-start.3) | collective-permute-done | bytes 344096 | tf_op jit(solution)/shard_map/ppermute | solution.py:324
  35.8 0.0 copy-done.2
  35.8 0.0 copy-done.5
  35.8 0.0 copy-done.6
  35.8 10.7 %shard_map.114 = (bf16[2,3584,128]{2,1,0:T(8,128)(2,1)S(1)}, bf16[256,128]{1,0:T(8,128)(2,1)S(1)}) custom-call(bf16[1344,128]{1,0:T(8,128)(2,1)S(1)} %collective-permute-done.2.low_ref, bf16[1408,128]{1,0:T(8,128)(2,1)S(1)} %get-tuple-element.28.mid_ref, bf16[1344,128]{1,0:T(8,128)(2,1)S(1)} %collective-permute-done.3.high_ref, ...), custom_call_target="tpu_custom_call" | custom-call | flops 8000000000 | bytes 1000000 | tf_op jit(solution)/shard_map/pallas_call | solution.py:206
  46.5 0.1 slice_bitcast_fusion
  46.5 0.1 collective-permute-start.4
  46.6 2.5 %collective-permute-done.4 = bf16[3584,128]{1,0:T(8,128)(2,1)S(1)} collective-permute-done((bf16[3584,128]{1,0:T(8,128)(2,1)S(1)}, bf16[3584,128]{1,0:T(8,128)(2,1)S(1)}, u32[]{:S(2)}, u32[]{:S(2)}) %collective-permute-start.4) | collective-permute-done | bytes 917536 | tf_op jit(solution)/shard_map/ppermute | solution.py:328
  49.1 0.2 fusion
  49.3 0.1 pad_maximum_fusion
  49.4 23.6 %all_to_all.21 = bf16[16,240,128]{2,1,0:T(8,128)(2,1)S(1)} all-to-all(bf16[16,240,128]{2,1,0:T(8,128)(2,1)S(1)} %pad_maximum_fusion), channel_id=1, replica_groups=mesh['y'=4,'c'=2,'z'=4,'x'=4] {'z','x'}, dimensions={0} | all-to-all | bytes 1966080 | tf_op jit(solution)/shard_map/all_to_all | solution.py:400
  73.0 0.1 slice_reduce_fusion
  73.2 0.9 collective-permute-start.7
  74.0 0.7 collective-permute-start.6
  74.7 2.6 %collective-permute-start.5 = (bf16[224,128]{1,0:T(8,128)(2,1)S(1)}, bf16[224,128]{1,0:T(8,128)(2,1)S(1)}, u32[]{:S(2)}, u32[]{:S(2)}) collective-permute-start(bf16[224,128]{1,0:T(8,128)(2,1)S(1)} %slice_reduce_fusion), channel_id=1, source_target_pairs={{0,64},{1,65},{2,66},{3,67},{4,68},{5,69},{6,70},{7,71},{8,72},{9,... | collective-permute-start | bytes 172040 | tf_op jit(solution)/shard_map/ppermute | solution.py:347
  77.3 0.0 collective-permute-done.7
  77.3 0.9 collective-permute-done.6
  78.3 1.2 %collective-permute-done.5 = bf16[224,128]{1,0:T(8,128)(2,1)S(1)} collective-permute-done((bf16[224,128]{1,0:T(8,128)(2,1)S(1)}, bf16[224,128]{1,0:T(8,128)(2,1)S(1)}, u32[]{:S(2)}, u32[]{:S(2)}) %collective-permute-start.5) | collective-permute-done | bytes 57376 | tf_op jit(solution)/shard_map/ppermute | solution.py:347
  79.5 0.1 broadcast_in_dim.2
  79.7 15.9 %all_to_all.22 = bf16[16,224,128]{2,1,0:T(8,128)(2,1)S(1)} all-to-all(bf16[16,224,128]{2,1,0:T(8,128)(2,1)S(1)} %broadcast_in_dim.2), channel_id=1, replica_groups=mesh['y'=4,'c'=2,'z'=4,'x'=4] {'z','x'}, dimensions={0} | all-to-all | bytes 1835008 | tf_op jit(solution)/shard_map/all_to_all | solution.py:408
  95.6 3.9 %collective-permute-start.8 = (bf16[3584,128]{1,0:T(8,128)(2,1)S(1)}, bf16[3584,128]{1,0:T(8,128)(2,1)S(1)}, u32[]{:S(2)}, u32[]{:S(2)}) collective-permute-start(bf16[3584,128]{1,0:T(8,128)(2,1)S(1)} %bitcast.20), channel_id=1, source_target_pairs={{0,16},{16,0},{1,17},{17,1},{2,18},{18,2},{3,19},{19,3},{4,20},{20... | collective-permute-start | bytes 2752520 | tf_op jit(solution)/shard_map/ppermute | solution.py:328
  99.5 0.7 reshape.44
  100.2 1.4 %collective-permute-done.8.other_ref = bf16[3584,128]{1,0:T(8,128)(2,1)S(1)} collective-permute-done((bf16[3584,128]{1,0:T(8,128)(2,1)S(1)}, bf16[3584,128]{1,0:T(8,128)(2,1)S(1)}, u32[]{:S(2)}, u32[]{:S(2)}) %collective-permute-start.8) | collective-permute-done | bytes 917536 | tf_op jit(solution)/shard_map/ppermute | solution.py:328
  101.6 2.0 %shard_map.115 = (f32[2592,128]{1,0:T(8,128)}, f32[3456,128]{1,0:T(8,128)}, f32[1024,128]{1,0:T(8,128)}) custom-call(bf16[3584,128]{1,0:T(8,128)(2,1)S(1)} %bitcast.21, bf16[3584,128]{1,0:T(8,128)(2,1)S(1)} %collective-permute-done.8.other_ref), custom_call_target="tpu_custom_call" | custom-call | flops 10000000 | bytes 1000000 | tf_op jit(solution)/shard_map/pallas_call | solution.py:206
  (3 shorter events, 0.1 us)
Async XLA Ops:
  2.7 17.1 %all-to-all-start = ((bf16[16,8,1024]{2,1,0:T(8,128)(2,1)}), bf16[16,8,1024]{2,1,0:T(8,128)(2,1)S(1)}, u32[]{:S(2)}, u32[]{:S(2)}) async-start(bf16[16,8,1024]{2,1,0:T(8,128)(2,1)} %bitcast.25), calls=%async_computation | async-start | bytes 524288 | tf_op jit(solution)/shard_map/all_to_all | solution.py:367
  11.2 4.8 %collective-permute-start = (bf16[224,128]{1,0:T(8,128)(2,1)}, bf16[224,128]{1,0:T(8,128)(2,1)S(1)}, u32[]{:S(2)}, u32[]{:S(2)}) collective-permute-start(bf16[224,128]{1,0:T(8,128)(2,1)} %get-tuple-element.24), channel_id=1, source_target_pairs={{0,1},{1,2},{2,3},{3,4},{4,5},{5,6},{6,7},{7,8},{8,9},{9,10},{10,1... | collective-permute-start | bytes 172040 | tf_op jit(solution)/shard_map/ppermute | solution.py:324
  14.4 5.4 %collective-permute-start.1 = (bf16[224,128]{1,0:T(8,128)(2,1)}, bf16[224,128]{1,0:T(8,128)(2,1)S(1)}, u32[]{:S(2)}, u32[]{:S(2)}) collective-permute-start(bf16[224,128]{1,0:T(8,128)(2,1)} %get-tuple-element.25), channel_id=1, source_target_pairs={{1,0},{2,1},{3,2},{4,3},{5,4},{6,5},{7,6},{8,7},{9,8},{10,9},{11,1... | collective-permute-start | bytes 172040 | tf_op jit(solution)/shard_map/ppermute | solution.py:324
  19.9 1.0 copy-start
  20.8 0.7 copy-start.1
  21.7 10.0 %collective-permute-start.2 = (bf16[1344,128]{1,0:T(8,128)(2,1)S(1)}, bf16[1344,128]{1,0:T(8,128)(2,1)S(1)}, u32[]{:S(2)}, u32[]{:S(2)}) collective-permute-start(bf16[1344,128]{1,0:T(8,128)(2,1)S(1)} %get-tuple-element.27), channel_id=1, source_target_pairs={{0,16},{16,32},{32,48},{48,64},{64,80},{80,96},{96,112},{1,17},{17... | collective-permute-start | bytes 1032200 | tf_op jit(solution)/shard_map/ppermute | solution.py:324
  27.2 8.6 %collective-permute-start.3 = (bf16[1344,128]{1,0:T(8,128)(2,1)S(1)}, bf16[1344,128]{1,0:T(8,128)(2,1)S(1)}, u32[]{:S(2)}, u32[]{:S(2)}) collective-permute-start(bf16[1344,128]{1,0:T(8,128)(2,1)S(1)} %get-tuple-element.29), channel_id=1, source_target_pairs={{16,0},{32,16},{48,32},{64,48},{80,64},{96,80},{112,96},{17,1},{33... | collective-permute-start | bytes 1032200 | tf_op jit(solution)/shard_map/ppermute | solution.py:324
  29.1 1.2 %copy-start.3 = (bf16[27,128,128]{2,1,0:T(8,128)(2,1)S(1)}, bf16[27,128,128]{2,1,0:T(8,128)(2,1)}, u32[]{:S(2)}) copy-start(bf16[27,128,128]{2,1,0:T(8,128)(2,1)} %w2_ref.1) | copy-start | bytes 2654212
  30.3 1.1 %copy-start.4 = (bf16[27,96,128]{2,1,0:T(8,128)(2,1)S(1)}, bf16[27,96,128]{2,1,0:T(8,128)(2,1)}, u32[]{:S(2)}) copy-start(bf16[27,96,128]{2,1,0:T(8,128)(2,1)} %w1_ref.1) | copy-start | bytes 1990660
  31.4 4.4 %copy-start.2 = (bf16[80,128]{1,0:T(8,128)(2,1)S(1)}, bf16[80,128]{1,0:T(8,128)(2,1)}, u32[]{:S(2)}) copy-start(bf16[80,128]{1,0:T(8,128)(2,1)} %get-tuple-element.23.misc_ref) | copy-start | bytes 61444
  31.4 4.4 %copy-start.5 = (bf16[8,128,128]{2,1,0:T(8,128)(2,1)S(1)}, bf16[8,128,128]{2,1,0:T(8,128)(2,1)}, u32[]{:S(2)}) copy-start(bf16[8,128,128]{2,1,0:T(8,128)(2,1)} %wd_ref.1) | copy-start | bytes 786436
  31.4 4.4 %copy-start.6 = (bf16[96,96]{1,0:T(8,128)(2,1)S(1)}, bf16[96,96]{1,0:T(8,128)(2,1)}, u32[]{:S(2)}) copy-start(bf16[96,96]{1,0:T(8,128)(2,1)} %constant.5.clone.up_ref) | copy-start | bytes 55300
  46.5 2.6 %collective-permute-start.4 = (bf16[3584,128]{1,0:T(8,128)(2,1)S(1)}, bf16[3584,128]{1,0:T(8,128)(2,1)S(1)}, u32[]{:S(2)}, u32[]{:S(2)}) collective-permute-start(bf16[3584,128]{1,0:T(8,128)(2,1)S(1)} %slice_bitcast_fusion), channel_id=1, source_target_pairs={{0,16},{16,0},{1,17},{17,1},{2,18},{18,2},{3,19},{19,3},{4,20},{20... | collective-permute-start | bytes 2752520 | tf_op jit(solution)/shard_map/ppermute | solution.py:328
  73.2 4.2 %collective-permute-start.7 = (bf16[224,128]{1,0:T(8,128)(2,1)S(1)}, bf16[224,128]{1,0:T(8,128)(2,1)S(1)}, u32[]{:S(2)}, u32[]{:S(2)}) collective-permute-start(bf16[224,128]{1,0:T(8,128)(2,1)S(1)} %slice_reduce_fusion), channel_id=1, source_target_pairs={{0,96},{1,97},{2,98},{3,99},{4,100},{5,101},{6,102},{7,103},{8,104... | collective-permute-start | bytes 172040 | tf_op jit(solution)/shard_map/ppermute | solution.py:347
  74.0 4.2 %collective-permute-start.6 = (bf16[224,128]{1,0:T(8,128)(2,1)S(1)}, bf16[224,128]{1,0:T(8,128)(2,1)S(1)}, u32[]{:S(2)}, u32[]{:S(2)}) collective-permute-start(bf16[224,128]{1,0:T(8,128)(2,1)S(1)} %slice_reduce_fusion), channel_id=1, source_target_pairs={{0,32},{1,33},{2,34},{3,35},{4,36},{5,37},{6,38},{7,39},{8,40},{9,... | collective-permute-start | bytes 172040 | tf_op jit(solution)/shard_map/ppermute | solution.py:347
  74.7 4.8 %collective-permute-start.5 = (bf16[224,128]{1,0:T(8,128)(2,1)S(1)}, bf16[224,128]{1,0:T(8,128)(2,1)S(1)}, u32[]{:S(2)}, u32[]{:S(2)}) collective-permute-start(bf16[224,128]{1,0:T(8,128)(2,1)S(1)} %slice_reduce_fusion), channel_id=1, source_target_pairs={{0,64},{1,65},{2,66},{3,67},{4,68},{5,69},{6,70},{7,71},{8,72},{9,... | collective-permute-start | bytes 172040 | tf_op jit(solution)/shard_map/ppermute | solution.py:347
  95.6 6.0 %collective-permute-start.8 = (bf16[3584,128]{1,0:T(8,128)(2,1)S(1)}, bf16[3584,128]{1,0:T(8,128)(2,1)S(1)}, u32[]{:S(2)}, u32[]{:S(2)}) collective-permute-start(bf16[3584,128]{1,0:T(8,128)(2,1)S(1)} %bitcast.20), channel_id=1, source_target_pairs={{0,16},{16,0},{1,17},{17,1},{2,18},{18,2},{3,19},{19,3},{4,20},{20... | collective-permute-start | bytes 2752520 | tf_op jit(solution)/shard_map/ppermute | solution.py:328

commit v5 on v4

--- a/solution.py
+++ b/solution.py
@@ -1,4 +1,3 @@
-import math
 import jax
 import jax.numpy as jnp
 import numpy as np
@@ -7,7 +6,7 @@
 from jax.experimental.pallas import tpu as pltpu
 from jax.sharding import Mesh, PartitionSpec as P
 
-GX, GY, ALL = ("y", "c"), ("z", "x"), ("y", "c", "z", "x")
+GX, GY = ("y", "c"), ("z", "x")
 F32, BF = jnp.float32, jnp.bfloat16
 X, Y, Z, C, CIN = 4, 16, 16, 128, 96
 HALF, PART = 3584, 224
@@ -46,11 +45,14 @@
 
 
 def section(
-    low_ref, mid_ref, high_ref, mask_ref, gc_ref, misc_ref, w1_ref, w2_ref, back_ref, wd_ref, up_ref,
+    near_ref, mid_ref, far_ref, mask_ref, gc_ref, misc_ref, w1_ref, w2_ref, back_ref, wd_ref, up_ref,
     grads_ref, out_ref,
-    first, sg1, second, ge, g2, gs, vt,
+    sides, first, sg1, second, ge, g2, gs, vt,
 ):
     core = lax.axis_index("c")
+    sides[1 - core] = near_ref[...]
+    sides[core] = far_ref[...]
+    low_ref, high_ref = sides.at[0], sides.at[1]
 
     def cells(x, y, n):
         ref, x = ((low_ref, x), (mid_ref, x - 3), (high_ref, x - 7))[(x > 2) + (x > 6)]
@@ -226,7 +228,7 @@
 
 
 def prepare(
-    grad_hbm, feat_hbm, blocks_hbm, owners_hbm, rows_ref, own_ref, low_ref, high_ref, misc_ref,
+    grad_hbm, feat_hbm, blocks_hbm, owners_hbm, rows_ref, own_ref, near_ref, far_ref, misc_ref,
     wide, grad_ref, feat_ref, blocks_ref, owners_ref, sems,
 ):
     copies = [
@@ -266,15 +268,33 @@
     rank = jnp.sum(jnp.where((col < row) & (dest == across), 1.0, 0.0), axis=1, keepdims=True)
     place = jnp.broadcast_to(dest * 8.0 + rank, (16, C)).astype(BF)
     misc_ref[4 * Z : 5 * Z, :] = place
-    for x in range(X):
-        low_ref[x * 3 * Z : (x + 1) * 3 * Z, :] = own_ref[(x * Y + 13) * Z : (x + 1) * Y * Z, :]
-        high_ref[x * 3 * Z : (x + 1) * 3 * Z, :] = own_ref[x * Y * Z : (x * Y + 3) * Z, :]
-    for ref, by in ((low_ref, 3), (high_ref, 0)):
-        ref[192:208, :] = place
-        ref[208:224, :] = misc_ref[by * Z : (by + 1) * Z, :]
-
-
-def widen(own_ref, misc_ref, low_ref, high_ref, rows_ref, mid_ref, mask_ref, gc_ref, up_ref, down_ref):
+
+    def fill(up, down):
+        for x in range(X):
+            up[x * 3 * Z : (x + 1) * 3 * Z, :] = own_ref[(x * Y + 13) * Z : (x + 1) * Y * Z, :]
+            down[x * 3 * Z : (x + 1) * 3 * Z, :] = own_ref[x * Y * Z : (x * Y + 3) * Z, :]
+        for ref, by in ((up, 3), (down, 0)):
+            ref[192:208, :] = place
+            ref[208:224, :] = misc_ref[by * Z : (by + 1) * Z, :]
+
+    @pl.when(lax.rem(lax.axis_index("x"), 2) == 0)
+    def _():
+        fill(near_ref, far_ref)
+
+    @pl.when(lax.rem(lax.axis_index("x"), 2) == 1)
+    def _():
+        fill(far_ref, near_ref)
+
+
+def widen(
+    own_ref, misc_ref, beside_ref, beyond_ref, rows_ref,
+    mid_ref, mask_ref, gc_ref, near_ref, far_ref,
+    sides,
+):
+    odd = lax.rem(lax.axis_index("x"), 2)
+    sides[1 - odd] = beside_ref[...]
+    sides[odd] = beyond_ref[...]
+    low_ref, high_ref = sides.at[0], sides.at[1]
     for x in range(X):
         at = x * 22 * Z
         mid_ref[at : at + 3 * Z, :] = low_ref[x * 3 * Z : (x + 1) * 3 * Z, :]
@@ -292,15 +312,25 @@
         axis=0,
     )
     bricks = mm(one(place == iota((48, C), 1).astype(F32)), rows_ref[...]).astype(BF)
-    for q in range(4):
-        gc_ref[0, q] = lanes(bricks, q)
-        gc_ref[1, q] = lanes(bricks, 4 + q)
-        up_ref[COTS + q * 48 : COTS + (q + 1) * 48, :] = lanes(bricks, 4 + q)
-        down_ref[COTS + q * 48 : COTS + (q + 1) * 48, :] = lanes(bricks, q)
-    up_ref[0:COTS, :] = mid_ref[22 * Z :, :]
-    down_ref[0:COTS, :] = mid_ref[0:COTS, :]
-    up_ref[MASK : MASK + 96, :] = mask_ref[...]
-    down_ref[MASK : MASK + 96, :] = mask_ref[...]
+    for q in range(8):
+        gc_ref[q // 4, q % 4] = lanes(bricks, q)
+
+    def fill(up, down):
+        for q in range(4):
+            up[COTS + q * 48 : COTS + (q + 1) * 48, :] = lanes(bricks, 4 + q)
+            down[COTS + q * 48 : COTS + (q + 1) * 48, :] = lanes(bricks, q)
+        up[0:COTS, :] = mid_ref[22 * Z :, :]
+        down[0:COTS, :] = mid_ref[0:COTS, :]
+        for ref in (up, down):
+            ref[MASK : MASK + 96, :] = mask_ref[...]
+
+    @pl.when(lax.axis_index("c") == 0)
+    def _():
+        fill(near_ref, far_ref)
+
+    @pl.when(lax.axis_index("c") == 1)
+    def _():
+        fill(far_ref, near_ref)
 
 
 def unfold(half_ref, other_ref, first_ref, second_ref, down_ref):
@@ -319,9 +349,10 @@
         both(other_ref, half_ref)
 
 
-def shift(v, axes, step):
+def swap(v, axes, first):
     n = lax.axis_size(axes)
-    return lax.ppermute(v, axes, [(i, i + step) for i in range(n) if 0 <= i + step < n])
+    pairs = [(i, i + 1) for i in range(first, n - 1, 2)]
+    return lax.ppermute(v, axes, pairs + [(j, i) for i, j in pairs])
 
 
 def swap_cores(v):
@@ -336,19 +367,12 @@
     return jnp.asarray(m, BF)
 
 
-def turn(v, axes, step):
-    size = [lax.axis_size(n) for n in ALL]
-    pairs = []
-    for d in range(math.prod(size)):
-        at = list(np.unravel_index(d, size))
-        n = ALL.index(axes[at[1]])
-        at[n] = (at[n] + step) % size[n]
-        pairs.append((d, int(np.ravel_multi_index(at, size))))
-    return lax.ppermute(v, ALL, pairs)
+def flip(v, axis, bits):
+    return lax.ppermute(v, axis, [(i, i ^ bits) for i in range(lax.axis_size(axis))])
 
 
 def per_device(features, block_mask, weight_first, weight_second, weight_down, owners, moved_grad):
-    rows, own, low, high, misc = call(
+    rows, own, beside, beyond, misc = call(
         prepare,
         [((128, 8 * C), BF), ((X * Y * Z, C), BF), ((224, C), BF), ((224, C), BF), ((80, C), BF)],
         (moved_grad, features, block_mask, owners.reshape(1, 16)),
@@ -363,15 +387,16 @@
         ],
         vmem=60 << 20,
     )
-    low, high = shift(low, GY, 1), shift(high, GY, -1)
+    beyond, beside = swap(beyond, GY, 1), swap(beside, GY, 0)
     rows = lax.all_to_all(rows, GY, 0, 0, tiled=True)
 
-    mid, mask, gc, up, down = call(
+    mid, mask, gc, near, far = call(
         widen,
         [((4 * 22 * Z, C), BF), ((96, C), BF), ((2, 4, 48, C), BF), ((STRIP, C), BF), ((STRIP, C), BF)],
-        (own, misc, low, high, rows),
-    )
-    low, high = shift(up, GX, 1), shift(down, GX, -1)
+        (own, misc, beside, beyond, rows),
+        scratch=[((2, 224, C), BF)],
+    )
+    far, near = swap(far, GX, 1), swap(near, GX, 0)
     w1, w2, back = call(
         arrange,
         [((9 * C, 3 * C), BF), ((9 * C, 3 * C), BF), ((3 * C, 9 * C), BF)],
@@ -382,8 +407,9 @@
     grads, outgoing = call(
         section,
         [((2, HALF, C), BF), ((256, C), BF)],
-        (low, mid, high, mask, gc, misc, w1, w2, back, weight_down, up_matrix()),
+        (near, mid, far, mask, gc, misc, w1, w2, back, weight_down, up_matrix()),
         scratch=[
+            ((2, STRIP, C), BF),
             ((8 * 20 * Z, C), BF),
             ((X * Y * Z, C), F32),
             ((X * Y * Z, C), BF),
@@ -403,8 +429,8 @@
     )
     moved = pieces[:, PART:].reshape(16, 8, 2, C).transpose(0, 2, 1, 3).reshape(1, 1, 32, 8 * C)
     part = jnp.sum(pieces[:, :PART].astype(F32), axis=0).astype(BF)
-    turned = [turn(part, ("y", "y"), n).astype(F32) for n in (1, 2, 3)]
-    part = ((part.astype(F32) + turned[1]) + (turned[0] + turned[2])).astype(BF)
+    others = [flip(part, "y", n).astype(F32) for n in (1, 2, 3)]
+    part = ((part.astype(F32) + others[0]) + (others[1] + others[2])).astype(BF)
     part = lax.all_to_all(jnp.broadcast_to(part[None], (16, PART, C)), GY, 0, 0, tiled=True)
     part = part.reshape(HALF, C)
     grad_first, grad_second, grad_down = call(

time: 104 us -> 99.7 us (0.959)
  starting transfers between devices: 28.5 us -> 23.5 us
  waiting for transfers between devices: 14.2 us -> 15.9 us
  blocking collectives: 39.6 us -> 38.3 us
    ppermute x7, starting transfers between devices: 16.1 us -> 11.1 us  [the longest x4 7.8 us: swap(): return lax.ppermute(v, axes, pairs + [(j, i) for i, j in pairs])]
    all_to_all x1, waiting for transfers between devices: 0.01 us -> 2.26 us  [per_device(): rows = lax.all_to_all(rows, GY, 0, 0, tiled=True)]
    all_to_all x1, blocking collectives: 23.6 us -> 22.2 us  [per_device(): lax.all_to_all(jnp.concatenate([half.reshape(16, PART, C), outgoing.resha...]
where the time goes in v5:
time: 99.7 us; the launch traced here: 99.2 us
  blocking collectives  38.3 us (38%)
  starting transfers between devices  23.5 us (24%)
  waiting for transfers between devices  15.9 us (16%)
  Pallas kernels  15.5 us (16%)
  local copies, waits for them, and re-layouts  4.8 us (5%)
    all_to_all x1, blocking collectives, per_device(): lax.all_to_all(jnp.concatenate([half.reshape(16, PART, C), outgoing.resha...  22.2 us
    all_to_all x1, blocking collectives, per_device(): lax.all_to_all(jnp.broadcast_to(part[None], (16, PART, C)), GY, 0, 0, til...  16.1 us
    pallas_call x5, Pallas kernels, call(): pl.pallas_call(kernel, out_shape=tuple((jax.ShapeDtypeStruct(shape, dtype...  15.5 us
    all_to_all x1, starting transfers between devices, per_device(): rows = lax.all_to_all(rows, GY, 0, 0, tiled=True)  8.44 us
    ppermute x4, starting transfers between devices, swap(): return lax.ppermute(v, axes, pairs + [(j, i) for i, j in pairs])  7.8 us
    ppermute x4, waiting for transfers between devices, swap(): return lax.ppermute(v, axes, pairs + [(j, i) for i, j in pairs])  6.17 us
    ppermute x2, starting transfers between devices, swap_cores(): return lax.ppermute(v, 'c', [(0, 1), (1, 0)])  3.97 us
    unnamed x14, local copies, waits for them, and re-layouts  3.94 us
  transfers between devices with their start and end apart: 10, of which 7 were waited for; matrix products, arithmetic and copies ran while one was open for 1% of the time, Pallas kernels for 0%

profile of v5, /device:TPU:1, one launch (start us, length us, event | category | flops | bytes accessed | tf_op | source)
XLA Modules:
  0.0 99.2 jit_solution(6266641136305042477)
XLA Ops:
  0.6 2.2 %shard_map.111 = (bf16[128,1024]{1,0:T(8,128)(2,1)}, bf16[1024,128]{1,0:T(8,128)(2,1)}, bf16[224,128]{1,0:T(8,128)(2,1)}, bf16[224,128]{1,0:T(8,128)(2,1)}, bf16[80,128]{1,0:T(8,128)(2,1)}) custom-call(bf16[1,1,32,1024]{3,2,1,0:T(8,128)(2,1)} %grad_hbm.1, bf16[4,16,1536]{2,1,0:T(8,128)(2,1)} %feat_hbm.1, s32[1,4,4]{2,1,0:T(4,128)} %blocks_hbm.1, ...), custom_call_target="tpu_custom_call" | custom-call | flops 10000000 | bytes 1000000 | tf_op jit(solution)/shard_map/pallas_call | solution.py:208
  2.8 8.4 %all-to-all-start = ((bf16[16,8,1024]{2,1,0:T(8,128)(2,1)}), bf16[16,8,1024]{2,1,0:T(8,128)(2,1)S(1)}, u32[]{:S(2)}, u32[]{:S(2)}) async-start(bf16[16,8,1024]{2,1,0:T(8,128)(2,1)} %bitcast.25), calls=%async_computation | async-start | bytes 524288 | tf_op jit(solution)/shard_map/all_to_all | solution.py:391
  11.3 1.4 %collective-permute-start = (bf16[224,128]{1,0:T(8,128)(2,1)}, bf16[224,128]{1,0:T(8,128)(2,1)S(1)}, u32[]{:S(2)}, u32[]{:S(2)}) collective-permute-start(bf16[224,128]{1,0:T(8,128)(2,1)} %get-tuple-element.24), channel_id=1, source_target_pairs={{0,1},{2,3},{4,5},{6,7},{8,9},{10,11},{12,13},{14,15},{1,0},{3,2},... | collective-permute-start | bytes 172040 | tf_op jit(solution)/shard_map/ppermute | solution.py:355
  12.6 0.7 collective-permute-start.1
  13.3 3.4 %collective-permute-done.beside_ref = bf16[224,128]{1,0:T(8,128)(2,1)S(1)} collective-permute-done((bf16[224,128]{1,0:T(8,128)(2,1)}, bf16[224,128]{1,0:T(8,128)(2,1)S(1)}, u32[]{:S(2)}, u32[]{:S(2)}) %collective-permute-start) | collective-permute-done | bytes 57376 | tf_op jit(solution)/shard_map/ppermute | solution.py:355
  16.7 0.0 collective-permute-done.1.beyond_ref
  16.7 2.3 %all-to-all-done = bf16[16,8,1024]{2,1,0:T(8,128)(2,1)S(1)} async-done(((bf16[16,8,1024]{2,1,0:T(8,128)(2,1)}), bf16[16,8,1024]{2,1,0:T(8,128)(2,1)S(1)}, u32[]{:S(2)}, u32[]{:S(2)}) %all-to-all-start) | async-done | bytes 262176 | tf_op jit(solution)/shard_map/all_to_all | solution.py:391
  18.9 0.0 copy-start
  18.9 0.9 copy-done
  19.9 0.0 copy-start.1
  19.9 0.7 copy-done.1
  20.6 0.3 shard_map.112
  20.9 2.7 %collective-permute-start.2 = (bf16[1344,128]{1,0:T(8,128)(2,1)S(1)}, bf16[1344,128]{1,0:T(8,128)(2,1)S(1)}, u32[]{:S(2)}, u32[]{:S(2)}) collective-permute-start(bf16[1344,128]{1,0:T(8,128)(2,1)S(1)} %get-tuple-element.27), channel_id=1, source_target_pairs={{0,16},{32,48},{64,80},{96,112},{16,0},{48,32},{80,64},{112,96},{1... | collective-permute-start | bytes 1032200 | tf_op jit(solution)/shard_map/ppermute | solution.py:355
  23.5 3.1 %collective-permute-start.3 = (bf16[1344,128]{1,0:T(8,128)(2,1)S(1)}, bf16[1344,128]{1,0:T(8,128)(2,1)S(1)}, u32[]{:S(2)}, u32[]{:S(2)}) collective-permute-start(bf16[1344,128]{1,0:T(8,128)(2,1)S(1)} %get-tuple-element.29), channel_id=1, source_target_pairs={{16,32},{48,64},{80,96},{32,16},{64,48},{96,80},{17,33},{49,65},{8... | collective-permute-start | bytes 1032200 | tf_op jit(solution)/shard_map/ppermute | solution.py:355
  26.7 0.0 copy-start.3
  26.7 1.2 %copy-done.3 = bf16[27,128,128]{2,1,0:T(8,128)(2,1)S(1)} copy-done((bf16[27,128,128]{2,1,0:T(8,128)(2,1)S(1)}, bf16[27,128,128]{2,1,0:T(8,128)(2,1)}, u32[]{:S(2)}) %copy-start.3) | copy-done | bytes 884760
  27.8 0.0 copy-start.4
  27.8 1.1 %copy-done.4 = bf16[27,96,128]{2,1,0:T(8,128)(2,1)S(1)} copy-done((bf16[27,96,128]{2,1,0:T(8,128)(2,1)S(1)}, bf16[27,96,128]{2,1,0:T(8,128)(2,1)}, u32[]{:S(2)}) %copy-start.4) | copy-done | bytes 663576
  28.9 0.0 copy-start.2
  28.9 0.0 copy-start.5
  28.9 0.0 copy-start.6
  28.9 0.4 shard_map.113
  29.3 0.0 collective-permute-done.2.near_ref
  29.3 2.8 %collective-permute-done.3.far_ref = bf16[1344,128]{1,0:T(8,128)(2,1)S(1)} collective-permute-done((bf16[1344,128]{1,0:T(8,128)(2,1)S(1)}, bf16[1344,128]{1,0:T(8,128)(2,1)S(1)}, u32[]{:S(2)}, u32[]{:S(2)}) %collective-permute-start.3) | collective-permute-done | bytes 344096 | tf_op jit(solution)/shard_map/ppermute | solution.py:355
  32.1 0.0 copy-done.2
  32.1 0.0 copy-done.5
  32.1 0.0 copy-done.6
  32.1 10.7 %shard_map.114 = (bf16[2,3584,128]{2,1,0:T(8,128)(2,1)S(1)}, bf16[256,128]{1,0:T(8,128)(2,1)S(1)}) custom-call(bf16[1344,128]{1,0:T(8,128)(2,1)S(1)} %collective-permute-done.2.near_ref, bf16[1408,128]{1,0:T(8,128)(2,1)S(1)} %get-tuple-element.28.mid_ref, bf16[1344,128]{1,0:T(8,128)(2,1)S(1)} %collective-permute-done.3.far_ref, ...), custom_call_target="tpu_custom_call" | custom-call | flops 8000000000 | bytes 1000000 | tf_op jit(solution)/shard_map/pallas_call | solution.py:208
  42.8 0.1 slice_bitcast_fusion
  42.9 0.1 collective-permute-start.4
  43.0 2.5 %collective-permute-done.4 = bf16[3584,128]{1,0:T(8,128)(2,1)S(1)} collective-permute-done((bf16[3584,128]{1,0:T(8,128)(2,1)S(1)}, bf16[3584,128]{1,0:T(8,128)(2,1)S(1)}, u32[]{:S(2)}, u32[]{:S(2)}) %collective-permute-start.4) | collective-permute-done | bytes 917536 | tf_op jit(solution)/shard_map/ppermute | solution.py:359
  45.4 0.2 fusion
  45.7 0.1 pad_maximum_fusion
  45.7 22.2 %all_to_all.21 = bf16[16,240,128]{2,1,0:T(8,128)(2,1)S(1)} all-to-all(bf16[16,240,128]{2,1,0:T(8,128)(2,1)S(1)} %pad_maximum_fusion), channel_id=1, replica_groups=mesh['y'=4,'c'=2,'z'=4,'x'=4] {'z','x'}, dimensions={0} | all-to-all | bytes 1966080 | tf_op jit(solution)/shard_map/all_to_all | solution.py:426
  68.0 0.1 slice_reduce_fusion
  68.1 2.3 %collective-permute-start.7 = (bf16[224,128]{1,0:T(8,128)(2,1)S(1)}, bf16[224,128]{1,0:T(8,128)(2,1)S(1)}, u32[]{:S(2)}, u32[]{:S(2)}) collective-permute-start(bf16[224,128]{1,0:T(8,128)(2,1)S(1)} %slice_reduce_fusion), channel_id=1, source_target_pairs={{0,96},{32,64},{64,32},{96,0},{1,97},{33,65},{65,33},{97,1},{2,98}... | collective-permute-start | bytes 172040 | tf_op jit(solution)/shard_map/ppermute | solution.py:371
  70.3 0.9 collective-permute-start.6
  71.2 0.2 collective-permute-start.5
  71.4 1.0 collective-permute-done.7
  72.4 2.6 %collective-permute-done.6 = bf16[224,128]{1,0:T(8,128)(2,1)S(1)} collective-permute-done((bf16[224,128]{1,0:T(8,128)(2,1)S(1)}, bf16[224,128]{1,0:T(8,128)(2,1)S(1)}, u32[]{:S(2)}, u32[]{:S(2)}) %collective-permute-start.6) | collective-permute-done | bytes 57376 | tf_op jit(solution)/shard_map/ppermute | solution.py:371
  75.0 0.0 collective-permute-done.5
  75.0 0.1 broadcast_in_dim.2
  75.1 16.1 %all_to_all.22 = bf16[16,224,128]{2,1,0:T(8,128)(2,1)S(1)} all-to-all(bf16[16,224,128]{2,1,0:T(8,128)(2,1)S(1)} %broadcast_in_dim.2), channel_id=1, replica_groups=mesh['y'=4,'c'=2,'z'=4,'x'=4] {'z','x'}, dimensions={0} | all-to-all | bytes 1835008 | tf_op jit(solution)/shard_map/all_to_all | solution.py:434
  91.2 3.9 %collective-permute-start.8 = (bf16[3584,128]{1,0:T(8,128)(2,1)S(1)}, bf16[3584,128]{1,0:T(8,128)(2,1)S(1)}, u32[]{:S(2)}, u32[]{:S(2)}) collective-permute-start(bf16[3584,128]{1,0:T(8,128)(2,1)S(1)} %bitcast.20), channel_id=1, source_target_pairs={{0,16},{16,0},{1,17},{17,1},{2,18},{18,2},{3,19},{19,3},{4,20},{20... | collective-permute-start | bytes 2752520 | tf_op jit(solution)/shard_map/ppermute | solution.py:359
  95.1 0.7 reshape.44
  95.8 1.4 %collective-permute-done.8.other_ref = bf16[3584,128]{1,0:T(8,128)(2,1)S(1)} collective-permute-done((bf16[3584,128]{1,0:T(8,128)(2,1)S(1)}, bf16[3584,128]{1,0:T(8,128)(2,1)S(1)}, u32[]{:S(2)}, u32[]{:S(2)}) %collective-permute-start.8) | collective-permute-done | bytes 917536 | tf_op jit(solution)/shard_map/ppermute | solution.py:359
  97.2 2.0 %shard_map.115 = (f32[2592,128]{1,0:T(8,128)}, f32[3456,128]{1,0:T(8,128)}, f32[1024,128]{1,0:T(8,128)}) custom-call(bf16[3584,128]{1,0:T(8,128)(2,1)S(1)} %bitcast.21, bf16[3584,128]{1,0:T(8,128)(2,1)S(1)} %collective-permute-done.8.other_ref), custom_call_target="tpu_custom_call" | custom-call | flops 10000000 | bytes 1000000 | tf_op jit(solution)/shard_map/pallas_call | solution.py:208
  (3 shorter events, 0.1 us)
Async XLA Ops:
  2.8 16.1 %all-to-all-start = ((bf16[16,8,1024]{2,1,0:T(8,128)(2,1)}), bf16[16,8,1024]{2,1,0:T(8,128)(2,1)S(1)}, u32[]{:S(2)}, u32[]{:S(2)}) async-start(bf16[16,8,1024]{2,1,0:T(8,128)(2,1)} %bitcast.25), calls=%async_computation | async-start | bytes 524288 | tf_op jit(solution)/shard_map/all_to_all | solution.py:391
  11.3 5.4 %collective-permute-start = (bf16[224,128]{1,0:T(8,128)(2,1)}, bf16[224,128]{1,0:T(8,128)(2,1)S(1)}, u32[]{:S(2)}, u32[]{:S(2)}) collective-permute-start(bf16[224,128]{1,0:T(8,128)(2,1)} %get-tuple-element.24), channel_id=1, source_target_pairs={{0,1},{2,3},{4,5},{6,7},{8,9},{10,11},{12,13},{14,15},{1,0},{3,2},... | collective-permute-start | bytes 172040 | tf_op jit(solution)/shard_map/ppermute | solution.py:355
  12.6 4.0 %collective-permute-start.1 = (bf16[224,128]{1,0:T(8,128)(2,1)}, bf16[224,128]{1,0:T(8,128)(2,1)S(1)}, u32[]{:S(2)}, u32[]{:S(2)}) collective-permute-start(bf16[224,128]{1,0:T(8,128)(2,1)} %get-tuple-element.25), channel_id=1, source_target_pairs={{1,2},{3,4},{5,6},{7,8},{9,10},{11,12},{13,14},{2,1},{4,3},{6,5},{... | collective-permute-start | bytes 172040 | tf_op jit(solution)/shard_map/ppermute | solution.py:355
  18.9 1.0 copy-start
  19.9 0.7 copy-start.1
  20.9 8.4 %collective-permute-start.2 = (bf16[1344,128]{1,0:T(8,128)(2,1)S(1)}, bf16[1344,128]{1,0:T(8,128)(2,1)S(1)}, u32[]{:S(2)}, u32[]{:S(2)}) collective-permute-start(bf16[1344,128]{1,0:T(8,128)(2,1)S(1)} %get-tuple-element.27), channel_id=1, source_target_pairs={{0,16},{32,48},{64,80},{96,112},{16,0},{48,32},{80,64},{112,96},{1... | collective-permute-start | bytes 1032200 | tf_op jit(solution)/shard_map/ppermute | solution.py:355
  23.5 8.6 %collective-permute-start.3 = (bf16[1344,128]{1,0:T(8,128)(2,1)S(1)}, bf16[1344,128]{1,0:T(8,128)(2,1)S(1)}, u32[]{:S(2)}, u32[]{:S(2)}) collective-permute-start(bf16[1344,128]{1,0:T(8,128)(2,1)S(1)} %get-tuple-element.29), channel_id=1, source_target_pairs={{16,32},{48,64},{80,96},{32,16},{64,48},{96,80},{17,33},{49,65},{8... | collective-permute-start | bytes 1032200 | tf_op jit(solution)/shard_map/ppermute | solution.py:355
  26.7 1.2 %copy-start.3 = (bf16[27,128,128]{2,1,0:T(8,128)(2,1)S(1)}, bf16[27,128,128]{2,1,0:T(8,128)(2,1)}, u32[]{:S(2)}) copy-start(bf16[27,128,128]{2,1,0:T(8,128)(2,1)} %w2_ref.1) | copy-start | bytes 2654212
  27.8 1.1 %copy-start.4 = (bf16[27,96,128]{2,1,0:T(8,128)(2,1)S(1)}, bf16[27,96,128]{2,1,0:T(8,128)(2,1)}, u32[]{:S(2)}) copy-start(bf16[27,96,128]{2,1,0:T(8,128)(2,1)} %w1_ref.1) | copy-start | bytes 1990660
  28.9 3.2 %copy-start.2 = (bf16[80,128]{1,0:T(8,128)(2,1)S(1)}, bf16[80,128]{1,0:T(8,128)(2,1)}, u32[]{:S(2)}) copy-start(bf16[80,128]{1,0:T(8,128)(2,1)} %get-tuple-element.23.misc_ref) | copy-start | bytes 61444
  28.9 3.2 %copy-start.5 = (bf16[8,128,128]{2,1,0:T(8,128)(2,1)S(1)}, bf16[8,128,128]{2,1,0:T(8,128)(2,1)}, u32[]{:S(2)}) copy-start(bf16[8,128,128]{2,1,0:T(8,128)(2,1)} %wd_ref.1) | copy-start | bytes 786436
  28.9 3.2 %copy-start.6 = (bf16[96,96]{1,0:T(8,128)(2,1)S(1)}, bf16[96,96]{1,0:T(8,128)(2,1)}, u32[]{:S(2)}) copy-start(bf16[96,96]{1,0:T(8,128)(2,1)} %constant.5.clone.up_ref) | copy-start | bytes 55300
  42.9 2.6 %collective-permute-start.4 = (bf16[3584,128]{1,0:T(8,128)(2,1)S(1)}, bf16[3584,128]{1,0:T(8,128)(2,1)S(1)}, u32[]{:S(2)}, u32[]{:S(2)}) collective-permute-start(bf16[3584,128]{1,0:T(8,128)(2,1)S(1)} %slice_bitcast_fusion), channel_id=1, source_target_pairs={{0,16},{16,0},{1,17},{17,1},{2,18},{18,2},{3,19},{19,3},{4,20},{20... | collective-permute-start | bytes 2752520 | tf_op jit(solution)/shard_map/ppermute | solution.py:359
  68.1 4.3 %collective-permute-start.7 = (bf16[224,128]{1,0:T(8,128)(2,1)S(1)}, bf16[224,128]{1,0:T(8,128)(2,1)S(1)}, u32[]{:S(2)}, u32[]{:S(2)}) collective-permute-start(bf16[224,128]{1,0:T(8,128)(2,1)S(1)} %slice_reduce_fusion), channel_id=1, source_target_pairs={{0,96},{32,64},{64,32},{96,0},{1,97},{33,65},{65,33},{97,1},{2,98}... | collective-permute-start | bytes 172040 | tf_op jit(solution)/shard_map/ppermute | solution.py:371
  70.3 4.6 %collective-permute-start.6 = (bf16[224,128]{1,0:T(8,128)(2,1)S(1)}, bf16[224,128]{1,0:T(8,128)(2,1)S(1)}, u32[]{:S(2)}, u32[]{:S(2)}) collective-permute-start(bf16[224,128]{1,0:T(8,128)(2,1)S(1)} %slice_reduce_fusion), channel_id=1, source_target_pairs={{0,64},{32,96},{64,0},{96,32},{1,65},{33,97},{65,1},{97,33},{2,66}... | collective-permute-start | bytes 172040 | tf_op jit(solution)/shard_map/ppermute | solution.py:371
  71.2 3.7 %collective-permute-start.5 = (bf16[224,128]{1,0:T(8,128)(2,1)S(1)}, bf16[224,128]{1,0:T(8,128)(2,1)S(1)}, u32[]{:S(2)}, u32[]{:S(2)}) collective-permute-start(bf16[224,128]{1,0:T(8,128)(2,1)S(1)} %slice_reduce_fusion), channel_id=1, source_target_pairs={{0,32},{32,0},{64,96},{96,64},{1,33},{33,1},{65,97},{97,65},{2,34}... | collective-permute-start | bytes 172040 | tf_op jit(solution)/shard_map/ppermute | solution.py:371
  91.2 6.0 %collective-permute-start.8 = (bf16[3584,128]{1,0:T(8,128)(2,1)S(1)}, bf16[3584,128]{1,0:T(8,128)(2,1)S(1)}, u32[]{:S(2)}, u32[]{:S(2)}) collective-permute-start(bf16[3584,128]{1,0:T(8,128)(2,1)S(1)} %bitcast.20), channel_id=1, source_target_pairs={{0,16},{16,0},{1,17},{17,1},{2,18},{18,2},{3,19},{19,3},{4,20},{20... | collective-permute-start | bytes 2752520 | tf_op jit(solution)/shard_map/ppermute | solution.py:359

commit v6 on v5

--- a/solution.py
+++ b/solution.py
@@ -1,3 +1,5 @@
+import functools
+
 import jax
 import jax.numpy as jnp
 import numpy as np
@@ -10,6 +12,7 @@
 F32, BF = jnp.float32, jnp.bfloat16
 X, Y, Z, C, CIN = 4, 16, 16, 128, 96
 HALF, PART = 3584, 224
+OWN = 1024
 COTS, MASK, STRIP = 1056, 1248, 1344
 NN = (((1,), (0,)), ((), ()))
 NT = (((1,), (1,)), ((), ()))
@@ -44,8 +47,20 @@
     return p[:, k * C : (k + 1) * C]
 
 
+def taps(get, x, n, w, dims=NN, flip=False, lines=(0, 1, 2)):
+    wins = []
+    for i in lines:
+        for j in range(3):
+            wins.append(get(x + 2 - i, 2 - j, n) if flip else get(x + i, j, n))
+    if len(lines) < 3:
+        w = w[3 * lines[0] * C : 3 * (lines[-1] + 1) * C, :]
+    else:
+        w = w[...]
+    return mm(jnp.concatenate(wins, axis=1), w, dims)
+
+
 def section(
-    near_ref, mid_ref, far_ref, mask_ref, gc_ref, misc_ref, w1_ref, w2_ref, back_ref, wd_ref, up_ref,
+    near_ref, mid_ref, far_ref, mask_ref, gc_ref, place_ref, part_ref, w1_ref, w2_ref, back_ref, wd_ref, up_ref,
     grads_ref, out_ref,
     sides, first, sg1, second, ge, g2, gs, vt,
 ):
@@ -77,14 +92,6 @@
         return jnp.concatenate(
             [mask_tile((x + 4) // 4, (y + 4) // 4) for y in range(y0, y0 + cells)], axis=0
         )
-
-    def taps(get, x, n, w, dims=NN, flip=False):
-        wins = []
-        for i in range(3):
-            for j in range(3):
-                ii, jj = (2 - i, 2 - j) if flip else (i, j)
-                wins.append(get(x + ii, jj, n))
-        return mm(jnp.concatenate(wins, axis=1), w[...], dims)
 
     def weight_grad(get, x0, y0, rows, put):
         for j in range(3):
@@ -103,9 +110,12 @@
         gs[at : at + Y * Z, 2 * C : 3 * C] = from_below(g).astype(BF)
 
     for x in range(8):
-        p = taps(cells, x, 20, w1_ref)
+        pre = jnp.zeros((20 * Z, C), F32) if x in (0, 7) else part_ref[x - 1]
+        if x not in (3, 4):
+            p = taps(cells, x, 20, w1_ref, lines=[i for i in range(3) if not 3 <= x + i < 7])
+            pre = pre + (lanes(p, 1) + from_below(lanes(p, 0)) + from_above(lanes(p, 2)))
         act = line(x - 2, -2, 20)
-        pre = act * (lanes(p, 1) + from_below(lanes(p, 0)) + from_above(lanes(p, 2)))
+        pre = act * pre
         s = jax.nn.sigmoid(pre)
         first[x * 20 * Z : (x + 1) * 20 * Z, :] = (pre * s).astype(BF)
         if 2 <= x < 6:
@@ -168,7 +178,7 @@
     a, by, b, z = col // 128, col // 32 % 4, col // 16 % 2, col % Z
     order = (row // 16 == 4 * a + 2 * b + z // 2 % 2) & (row % 16 == by * 4 + z // 4) & (z % 2 == 0)
     bricks = mm(one(order), coarse).astype(BF)
-    place = jnp.concatenate([misc_ref[4 * Z : 5 * Z, :].astype(F32)] * 8, axis=0)
+    place = jnp.concatenate([place_ref[...].astype(F32)] * 8, axis=0)
     place = jnp.concatenate([place] * 2, axis=1)
     target = (8 * (col // 16) + col % 2).astype(F32)
     out_ref[...] = mm(one((place == target) & (row // 16 == col // 2 % 8)), bricks, TN).astype(BF)
@@ -204,12 +214,13 @@
 VM = pl.BlockSpec(memory_space=pltpu.VMEM)
 
 
-def call(kernel, outs, args, in_specs=None, scratch=(), flops=10_000_000, vmem=40 << 20):
+def call(kernel, outs, args, in_specs=None, scratch=(), flops=10_000_000, vmem=40 << 20, out_specs=None, aliases={}):
     return pl.pallas_call(
         kernel,
         out_shape=tuple(jax.ShapeDtypeStruct(shape, dtype) for shape, dtype in outs),
         in_specs=in_specs or [VM] * len(args),
-        out_specs=tuple([VM] * len(outs)),
+        out_specs=tuple(out_specs or [VM] * len(outs)),
+        input_output_aliases=aliases,
         scratch_shapes=[pltpu.VMEM(*s) if isinstance(s, tuple) else s for s in scratch],
         compiler_params=pltpu.CompilerParams(vmem_limit_bytes=vmem),
         cost_estimate=pl.CostEstimate(
@@ -227,8 +238,17 @@
         first_ref[m * C + CIN : (m + 1) * C, :] = jnp.zeros((C - CIN, 3 * C), BF)
 
 
+def begin(mid_ref, first_ref, part_ref):
+    def cells(x, y, n):
+        return mid_ref[((x - 3) * 22 + y) * Z : ((x - 3) * 22 + y + n) * Z, :]
+
+    for x in range(1, 7):
+        p = taps(cells, x, 20, first_ref, lines=[i for i in range(3) if 3 <= x + i < 7])
+        part_ref[x - 1] = lanes(p, 1) + from_below(lanes(p, 0)) + from_above(lanes(p, 2))
+
+
 def prepare(
-    grad_hbm, feat_hbm, blocks_hbm, owners_hbm, rows_ref, own_ref, near_ref, far_ref, misc_ref,
+    grad_hbm, feat_hbm, blocks_hbm, owners_hbm, rows_ref, own_ref, near_ref, far_ref,
     wide, grad_ref, feat_ref, blocks_ref, owners_ref, sems,
 ):
     copies = [
@@ -257,7 +277,7 @@
     for by in range(4):
         m = jnp.sum(jnp.where(mine, blocks[by : by + 1, :], 0.0), axis=1, keepdims=True)
         m = jnp.broadcast_to(m, (Z, C))
-        misc_ref[by * Z : (by + 1) * Z, :] = m.astype(BF)
+        own_ref[OWN + by * Z : OWN + (by + 1) * Z, :] = m.astype(BF)
         for x in range(X):
             for y in range(4 * by, 4 * by + 4):
                 at = (x * Y + y) * Z
@@ -267,7 +287,7 @@
     dest = jnp.sum(jnp.where(row == col, across, 0.0), axis=1, keepdims=True)
     rank = jnp.sum(jnp.where((col < row) & (dest == across), 1.0, 0.0), axis=1, keepdims=True)
     place = jnp.broadcast_to(dest * 8.0 + rank, (16, C)).astype(BF)
-    misc_ref[4 * Z : 5 * Z, :] = place
+    own_ref[OWN + 4 * Z : OWN + 5 * Z, :] = place
 
     def fill(up, down):
         for x in range(X):
@@ -275,7 +295,7 @@
             down[x * 3 * Z : (x + 1) * 3 * Z, :] = own_ref[x * Y * Z : (x * Y + 3) * Z, :]
         for ref, by in ((up, 3), (down, 0)):
             ref[192:208, :] = place
-            ref[208:224, :] = misc_ref[by * Z : (by + 1) * Z, :]
+            ref[208:224, :] = own_ref[OWN + by * Z : OWN + (by + 1) * Z, :]
 
     @pl.when(lax.rem(lax.axis_index("x"), 2) == 0)
     def _():
@@ -287,8 +307,8 @@
 
 
 def widen(
-    own_ref, misc_ref, beside_ref, beyond_ref, rows_ref,
-    mid_ref, mask_ref, gc_ref, near_ref, far_ref,
+    own_ref, beside_ref, beyond_ref, rows_ref, after_ref,
+    mid_ref, mask_ref, gc_ref, place_ref, near_ref, far_ref,
     sides,
 ):
     odd = lax.rem(lax.axis_index("x"), 2)
@@ -301,12 +321,13 @@
         mid_ref[at + 3 * Z : at + 19 * Z, :] = own_ref[x * Y * Z : (x + 1) * Y * Z, :]
         mid_ref[at + 19 * Z : at + 22 * Z, :] = high_ref[x * 3 * Z : (x + 1) * 3 * Z, :]
     mask_ref[0:Z, :] = low_ref[208:224, :]
-    mask_ref[Z : 5 * Z, :] = misc_ref[0 : 4 * Z, :]
+    mask_ref[Z : 5 * Z, :] = own_ref[OWN : OWN + 4 * Z, :]
     mask_ref[5 * Z : 6 * Z, :] = high_ref[208:224, :]
+    place_ref[...] = own_ref[OWN + 4 * Z : OWN + 5 * Z, :]
     place = jnp.concatenate(
         [
             low_ref[192:208, :].astype(F32),
-            misc_ref[4 * Z : 5 * Z, :].astype(F32) + 2.0,
+            own_ref[OWN + 4 * Z : OWN + 5 * Z, :].astype(F32) + 2.0,
             high_ref[192:208, :].astype(F32) + 4.0,
         ],
         axis=0,
@@ -333,20 +354,39 @@
         fill(far_ref, near_ref)
 
 
-def unfold(half_ref, other_ref, first_ref, second_ref, down_ref):
-    def both(a_ref, b_ref):
-        second_ref[...] = a_ref[: 27 * C, :].astype(F32)
-        down_ref[:C, :] = a_ref[27 * C :, :].astype(F32)
-        first_ref[...] = b_ref[: 27 * CIN, :].astype(F32)
-        down_ref[C:, :] = b_ref[27 * CIN : 27 * CIN + 7 * C, :].astype(F32)
-
-    @pl.when(lax.axis_index("c") == 0)
-    def _():
-        both(half_ref, other_ref)
-
-    @pl.when(lax.axis_index("c") == 1)
-    def _():
-        both(other_ref, half_ref)
+def unfold(half_ref, core, first_hbm, second_hbm, down_hbm, wide, sems):
+    spans = {
+        0: ((0, 27 * C, second_hbm, 0), (27 * C, 28 * C, down_hbm, 0)),
+        1: ((0, 27 * CIN, first_hbm, 0), (27 * CIN, 27 * CIN + 7 * C, down_hbm, C)),
+    }
+
+    def emit(which):
+        copies = []
+        for lo, hi, out, to in spans[which]:
+            step = 864 if hi - lo > 1024 else hi - lo
+            for at in range(lo, hi, step):
+                wide[at : at + step, :] = half_ref[at : at + step, :].astype(F32)
+                copies.append(
+                    pltpu.make_async_copy(
+                        wide.at[pl.ds(at, step)],
+                        out.at[pl.ds(to + at - lo, step)],
+                        sems.at[len(copies)],
+                    )
+                )
+                copies[-1].start()
+        for c in copies:
+            c.wait()
+
+    for which in range(2):
+        pl.when(core == which)(functools.partial(emit, which))
+
+
+def unfold_own(half_ref, first_hbm, second_hbm, down_hbm, wide, sems):
+    unfold(half_ref, lax.axis_index("c"), first_hbm, second_hbm, down_hbm, wide, sems)
+
+
+def unfold_other(half_ref, a, b, c, first_hbm, second_hbm, down_hbm, wide, sems):
+    unfold(half_ref, 1 - lax.axis_index("c"), first_hbm, second_hbm, down_hbm, wide, sems)
 
 
 def swap(v, axes, first):
@@ -372,9 +412,9 @@
 
 
 def per_device(features, block_mask, weight_first, weight_second, weight_down, owners, moved_grad):
-    rows, own, beside, beyond, misc = call(
+    rows, own, beside, beyond = call(
         prepare,
-        [((128, 8 * C), BF), ((X * Y * Z, C), BF), ((224, C), BF), ((224, C), BF), ((80, C), BF)],
+        [((128, 8 * C), BF), ((X * Y * Z + 80, C), BF), ((224, C), BF), ((224, C), BF)],
         (moved_grad, features, block_mask, owners.reshape(1, 16)),
         [pl.BlockSpec(memory_space=pltpu.HBM)] * 4,
         [
@@ -388,26 +428,28 @@
         vmem=60 << 20,
     )
     beyond, beside = swap(beyond, GY, 1), swap(beside, GY, 0)
-    rows = lax.all_to_all(rows, GY, 0, 0, tiled=True)
-
-    mid, mask, gc, near, far = call(
-        widen,
-        [((4 * 22 * Z, C), BF), ((96, C), BF), ((2, 4, 48, C), BF), ((STRIP, C), BF), ((STRIP, C), BF)],
-        (own, misc, beside, beyond, rows),
-        scratch=[((2, 224, C), BF)],
-    )
-    far, near = swap(far, GX, 1), swap(near, GX, 0)
     w1, w2, back = call(
         arrange,
         [((9 * C, 3 * C), BF), ((9 * C, 3 * C), BF), ((3 * C, 9 * C), BF)],
-        (weight_first, weight_second, mask),
+        (weight_first, weight_second, own),
         flops=2_000_000_000,
     )
+    rows = lax.all_to_all(rows, GY, 0, 0, tiled=True)
+
+    mid, mask, gc, place, near, far = call(
+        widen,
+        [((4 * 22 * Z, C), BF), ((96, C), BF), ((2, 4, 48, C), BF), ((16, C), BF), ((STRIP, C), BF), ((STRIP, C), BF)],
+        (own, beside, beyond, rows, w1),
+        [VM] * 4 + [pl.BlockSpec(memory_space=pl.ANY)],
+        scratch=[((2, 224, C), BF)],
+    )
+    far, near = swap(far, GX, 1), swap(near, GX, 0)
+    (ahead,) = call(begin, [((6, 20 * Z, C), F32)], (mid, w1), flops=2_000_000_000)
 
     grads, outgoing = call(
         section,
         [((2, HALF, C), BF), ((256, C), BF)],
-        (near, mid, far, mask, gc, misc, w1, w2, back, weight_down, up_matrix()),
+        (near, mid, far, mask, gc, place, ahead, w1, w2, back, weight_down, up_matrix()),
         scratch=[
             ((2, STRIP, C), BF),
             ((8 * 20 * Z, C), BF),
@@ -433,10 +475,14 @@
     part = ((part.astype(F32) + others[0]) + (others[1] + others[2])).astype(BF)
     part = lax.all_to_all(jnp.broadcast_to(part[None], (16, PART, C)), GY, 0, 0, tiled=True)
     part = part.reshape(HALF, C)
+    grads = [((27 * CIN, C), F32), ((27 * C, C), F32), ((8 * C, C), F32)]
+    scratch = [((HALF, C), F32), pltpu.SemaphoreType.DMA((5,))]
+    hbm = pl.BlockSpec(memory_space=pl.ANY)
+    other = swap_cores(part)
+    grads_own = call(unfold_own, grads, (part,), [VM], scratch, out_specs=[hbm] * 3)
     grad_first, grad_second, grad_down = call(
-        unfold,
-        [((27 * CIN, C), F32), ((27 * C, C), F32), ((8 * C, C), F32)],
-        (part, swap_cores(part)),
+        unfold_other, grads, (other, *grads_own), [VM] + [hbm] * 3, scratch, out_specs=[hbm] * 3,
+        aliases={1: 0, 2: 1, 3: 2},
     )
     return (
         moved,

time: 99.7 us -> 95.7 us (0.960)
  waiting for transfers between devices: 15.9 us -> 11.8 us
    ppermute x4, waiting for transfers between devices: 6.17 us -> 3.63 us  [swap(): return lax.ppermute(v, axes, pairs + [(j, i) for i, j in pairs])]
    ppermute x2, waiting for transfers between devices: 3.88 us -> 2.59 us  [swap_cores(): return lax.ppermute(v, 'c', [(0, 1), (1, 0)])]
    unnamed x14 -> x12, local copies, waits for them, and re-layouts: 3.94 us -> 3.23 us
    pallas_call x5 -> x7, Pallas kernels: 15.5 us -> 16.2 us  [call(): pl.pallas_call(kernel, out_shape=tuple((jax.ShapeDtypeStruct(shape, dtype...]
  transfers between devices with their start and end apart: 10 -> 10, of which waited for: 7 -> 6; matrix products, arithmetic and copies ran while one was open for 1% -> 1% of each run, Pallas kernels for 0% -> 4%
where the time goes in v6:
time: 95.7 us; the launch traced here: 95.3 us
  blocking collectives  38.3 us (40%)
  starting transfers between devices  23.5 us (25%)
  Pallas kernels  16.2 us (17%)
  waiting for transfers between devices  11.8 us (12%)
  local copies, waits for them, and re-layouts  4.09 us (4%)
  between operations  0.96 us (1%)
    all_to_all x1, blocking collectives, per_device(): lax.all_to_all(jnp.concatenate([half.reshape(16, PART, C), outgoing.resha...  22.2 us
    pallas_call x7, Pallas kernels, call(): pl.pallas_call(kernel, out_shape=tuple((jax.ShapeDtypeStruct(shape, dtype...  16.2 us
    all_to_all x1, blocking collectives, per_device(): lax.all_to_all(jnp.broadcast_to(part[None], (16, PART, C)), GY, 0, 0, til...  16.1 us
    all_to_all x1, starting transfers between devices, per_device(): rows = lax.all_to_all(rows, GY, 0, 0, tiled=True)  8.44 us
    ppermute x4, starting transfers between devices, swap(): return lax.ppermute(v, axes, pairs + [(j, i) for i, j in pairs])  7.8 us
    ppermute x2, starting transfers between devices, swap_cores(): return lax.ppermute(v, 'c', [(0, 1), (1, 0)])  3.97 us
    ppermute x4, waiting for transfers between devices, swap(): return lax.ppermute(v, axes, pairs + [(j, i) for i, j in pairs])  3.63 us
    ppermute x3, waiting for transfers between devices, flip(): lax.ppermute(v, axis, [(i, i ^ bits) for i in range(lax.axis_size(axis))])  3.57 us
  transfers between devices with their start and end apart: 10, of which 6 were waited for; matrix products, arithmetic and copies ran while one was open for 1% of the time, Pallas kernels for 4%

profile of v6, /device:TPU:1, one launch (start us, length us, event | category | flops | bytes accessed | tf_op | source)
XLA Modules:
  0.0 95.3 jit_solution(1112871775090742130)
XLA Ops:
  0.6 2.2 %shard_map.111 = (bf16[128,1024]{1,0:T(8,128)(2,1)}, bf16[1104,128]{1,0:T(8,128)(2,1)}, bf16[224,128]{1,0:T(8,128)(2,1)}, bf16[224,128]{1,0:T(8,128)(2,1)}) custom-call(bf16[1,1,32,1024]{3,2,1,0:T(8,128)(2,1)} %grad_hbm.1, bf16[4,16,1536]{2,1,0:T(8,128)(2,1)} %feat_hbm.1, s32[1,4,4]{2,1,0:T(4,128)} %blocks_hbm.1, s32[1,16]{1,0:T(1,128)} %bitcast.31), custom_call_target="tpu_custom_call" | custom-call | flops 10000000 | bytes 1000000 | tf_op jit(solution)/shard_map/pallas_call | solution.py:218
  2.8 8.4 %all-to-all-start = ((bf16[16,8,1024]{2,1,0:T(8,128)(2,1)}), bf16[16,8,1024]{2,1,0:T(8,128)(2,1)S(1)}, u32[]{:S(2)}, u32[]{:S(2)}) async-start(bf16[16,8,1024]{2,1,0:T(8,128)(2,1)} %bitcast.28), calls=%async_computation | async-start | bytes 524288 | tf_op jit(solution)/shard_map/all_to_all | solution.py:437
  11.3 1.4 %collective-permute-start = (bf16[224,128]{1,0:T(8,128)(2,1)}, bf16[224,128]{1,0:T(8,128)(2,1)S(1)}, u32[]{:S(2)}, u32[]{:S(2)}) collective-permute-start(bf16[224,128]{1,0:T(8,128)(2,1)} %get-tuple-element.26), channel_id=1, source_target_pairs={{0,1},{2,3},{4,5},{6,7},{8,9},{10,11},{12,13},{14,15},{1,0},{3,2},... | collective-permute-start | bytes 172040 | tf_op jit(solution)/shard_map/ppermute | solution.py:395
  12.6 0.7 collective-permute-start.1
  13.3 0.0 copy-start
  13.3 0.9 copy-done
  14.3 0.0 copy-start.2
  14.3 1.2 %copy-done.2 = bf16[27,128,128]{2,1,0:T(8,128)(2,1)S(1)} copy-done((bf16[27,128,128]{2,1,0:T(8,128)(2,1)S(1)}, bf16[27,128,128]{2,1,0:T(8,128)(2,1)}, u32[]{:S(2)}) %copy-start.2) | copy-done | bytes 884760
  15.4 0.0 copy-start.3
  15.4 1.1 %copy-done.3 = bf16[27,96,128]{2,1,0:T(8,128)(2,1)S(1)} copy-done((bf16[27,96,128]{2,1,0:T(8,128)(2,1)S(1)}, bf16[27,96,128]{2,1,0:T(8,128)(2,1)}, u32[]{:S(2)}) %copy-start.3) | copy-done | bytes 663576
  16.5 0.0 copy-start.1
  16.5 0.4 shard_map.112
  16.9 0.0 collective-permute-done.beside_ref
  16.9 0.0 collective-permute-done.1.beyond_ref
  16.9 2.0 %all-to-all-done = bf16[16,8,1024]{2,1,0:T(8,128)(2,1)S(1)} async-done(((bf16[16,8,1024]{2,1,0:T(8,128)(2,1)}), bf16[16,8,1024]{2,1,0:T(8,128)(2,1)S(1)}, u32[]{:S(2)}, u32[]{:S(2)}) %all-to-all-start) | async-done | bytes 262176 | tf_op jit(solution)/shard_map/all_to_all | solution.py:437
  18.9 0.0 copy-done.1
  18.9 0.3 shard_map.113
  19.2 2.7 %collective-permute-start.2 = (bf16[1344,128]{1,0:T(8,128)(2,1)S(1)}, bf16[1344,128]{1,0:T(8,128)(2,1)S(1)}, u32[]{:S(2)}, u32[]{:S(2)}) collective-permute-start(bf16[1344,128]{1,0:T(8,128)(2,1)S(1)} %get-tuple-element.30), channel_id=1, source_target_pairs={{0,16},{32,48},{64,80},{96,112},{16,0},{48,32},{80,64},{112,96},{1... | collective-permute-start | bytes 1032200 | tf_op jit(solution)/shard_map/ppermute | solution.py:395
  21.9 3.1 %collective-permute-start.3 = (bf16[1344,128]{1,0:T(8,128)(2,1)S(1)}, bf16[1344,128]{1,0:T(8,128)(2,1)S(1)}, u32[]{:S(2)}, u32[]{:S(2)}) collective-permute-start(bf16[1344,128]{1,0:T(8,128)(2,1)S(1)} %get-tuple-element.32), channel_id=1, source_target_pairs={{16,32},{48,64},{80,96},{32,16},{64,48},{96,80},{17,33},{49,65},{8... | collective-permute-start | bytes 1032200 | tf_op jit(solution)/shard_map/ppermute | solution.py:395
  25.0 0.0 copy-start.4
  25.0 0.0 copy-start.5
  25.0 1.8 %shard_map.114.part_ref = f32[6,320,128]{2,1,0:T(8,128)S(1)} custom-call(bf16[1408,128]{1,0:T(8,128)(2,1)S(1)} %get-tuple-element.31.mid_ref, bf16[1152,384]{1,0:T(8,128)(2,1)S(1)} %get-tuple-element.29.after_ref.first_ref.w1_ref), custom_call_target="tpu_custom_call" | custom-call | flops 2000000000 | bytes 1000000 | tf_op jit(solution)/shard_map/pallas_call | solution.py:218
  26.8 0.0 collective-permute-done.2.near_ref
  26.8 3.6 %collective-permute-done.3.far_ref = bf16[1344,128]{1,0:T(8,128)(2,1)S(1)} collective-permute-done((bf16[1344,128]{1,0:T(8,128)(2,1)S(1)}, bf16[1344,128]{1,0:T(8,128)(2,1)S(1)}, u32[]{:S(2)}, u32[]{:S(2)}) %collective-permute-start.3) | collective-permute-done | bytes 344096 | tf_op jit(solution)/shard_map/ppermute | solution.py:395
  30.4 0.0 copy-done.4
  30.4 0.0 copy-done.5
  30.4 9.0 %shard_map.115 = (bf16[2,3584,128]{2,1,0:T(8,128)(2,1)S(1)}, bf16[256,128]{1,0:T(8,128)(2,1)S(1)}) custom-call(bf16[1344,128]{1,0:T(8,128)(2,1)S(1)} %collective-permute-done.2.near_ref, bf16[1408,128]{1,0:T(8,128)(2,1)S(1)} %get-tuple-element.31.mid_ref, bf16[1344,128]{1,0:T(8,128)(2,1)S(1)} %collective-permute-done.3.far_ref, ...), custom_call_target="tpu_custom_call" | custom-call | flops 8000000000 | bytes 1000000 | tf_op jit(solution)/shard_map/pallas_call | solution.py:218
  39.4 0.1 slice_bitcast_fusion
  39.5 0.1 collective-permute-start.4
  39.6 2.5 %collective-permute-done.4 = bf16[3584,128]{1,0:T(8,128)(2,1)S(1)} collective-permute-done((bf16[3584,128]{1,0:T(8,128)(2,1)S(1)}, bf16[3584,128]{1,0:T(8,128)(2,1)S(1)}, u32[]{:S(2)}, u32[]{:S(2)}) %collective-permute-start.4) | collective-permute-done | bytes 917536 | tf_op jit(solution)/shard_map/ppermute | solution.py:399
  42.1 0.2 fusion
  42.3 0.1 pad_maximum_fusion
  42.4 22.2 %all_to_all.21 = bf16[16,240,128]{2,1,0:T(8,128)(2,1)S(1)} all-to-all(bf16[16,240,128]{2,1,0:T(8,128)(2,1)S(1)} %pad_maximum_fusion), channel_id=1, replica_groups=mesh['y'=4,'c'=2,'z'=4,'x'=4] {'z','x'}, dimensions={0} | all-to-all | bytes 1966080 | tf_op jit(solution)/shard_map/all_to_all | solution.py:468
  64.6 0.1 slice_reduce_fusion
  64.7 2.3 %collective-permute-start.7 = (bf16[224,128]{1,0:T(8,128)(2,1)S(1)}, bf16[224,128]{1,0:T(8,128)(2,1)S(1)}, u32[]{:S(2)}, u32[]{:S(2)}) collective-permute-start(bf16[224,128]{1,0:T(8,128)(2,1)S(1)} %slice_reduce_fusion), channel_id=1, source_target_pairs={{0,96},{32,64},{64,32},{96,0},{1,97},{33,65},{65,33},{97,1},{2,98}... | collective-permute-start | bytes 172040 | tf_op jit(solution)/shard_map/ppermute | solution.py:411
  67.0 0.9 collective-permute-start.6
  67.9 0.2 collective-permute-start.5
  68.1 1.0 %collective-permute-done.7 = bf16[224,128]{1,0:T(8,128)(2,1)S(1)} collective-permute-done((bf16[224,128]{1,0:T(8,128)(2,1)S(1)}, bf16[224,128]{1,0:T(8,128)(2,1)S(1)}, u32[]{:S(2)}, u32[]{:S(2)}) %collective-permute-start.7) | collective-permute-done | bytes 57376 | tf_op jit(solution)/shard_map/ppermute | solution.py:411
  69.0 2.6 %collective-permute-done.6 = bf16[224,128]{1,0:T(8,128)(2,1)S(1)} collective-permute-done((bf16[224,128]{1,0:T(8,128)(2,1)S(1)}, bf16[224,128]{1,0:T(8,128)(2,1)S(1)}, u32[]{:S(2)}, u32[]{:S(2)}) %collective-permute-start.6) | collective-permute-done | bytes 57376 | tf_op jit(solution)/shard_map/ppermute | solution.py:411
  71.6 0.0 collective-permute-done.5
  71.7 0.1 broadcast_in_dim.2
  71.8 16.1 %all_to_all.22 = bf16[16,224,128]{2,1,0:T(8,128)(2,1)S(1)} all-to-all(bf16[16,224,128]{2,1,0:T(8,128)(2,1)S(1)} %broadcast_in_dim.2), channel_id=1, replica_groups=mesh['y'=4,'c'=2,'z'=4,'x'=4] {'z','x'}, dimensions={0} | all-to-all | bytes 1835008 | tf_op jit(solution)/shard_map/all_to_all | solution.py:476
  87.8 3.9 %collective-permute-start.8 = (bf16[3584,128]{1,0:T(8,128)(2,1)S(1)}, bf16[3584,128]{1,0:T(8,128)(2,1)S(1)}, u32[]{:S(2)}, u32[]{:S(2)}) collective-permute-start(bf16[3584,128]{1,0:T(8,128)(2,1)S(1)} %bitcast.20), channel_id=1, source_target_pairs={{0,16},{16,0},{1,17},{17,1},{2,18},{18,2},{3,19},{19,3},{4,20},{20... | collective-permute-start | bytes 2752520 | tf_op jit(solution)/shard_map/ppermute | solution.py:399
  91.7 0.7 reshape.44
  92.4 1.3 %shard_map.116 = (f32[2592,128]{1,0:T(8,128)}, f32[3456,128]{1,0:T(8,128)}, f32[1024,128]{1,0:T(8,128)}) custom-call(bf16[3584,128]{1,0:T(8,128)(2,1)S(1)} %bitcast.21), custom_call_target="tpu_custom_call" | custom-call | flops 10000000 | bytes 1000000 | tf_op jit(solution)/shard_map/pallas_call | solution.py:218
  93.7 0.1 collective-permute-done.8.half_ref
  93.8 1.3 %shard_map.117 = (f32[2592,128]{1,0:T(8,128)}, f32[3456,128]{1,0:T(8,128)}, f32[1024,128]{1,0:T(8,128)}) custom-call(bf16[3584,128]{1,0:T(8,128)(2,1)S(1)} %collective-permute-done.8.half_ref, f32[2592,128]{1,0:T(8,128)} %get-tuple-element.40.a, f32[3456,128]{1,0:T(8,128)} %get-tuple-element.41.b, ...), custom_call_target="tpu_custom_call", output_to_operand_aliasing={{0}: (1, {}), {1}: (2, {}), {2}: (3, {})} | custom-call | flops 10000000 | bytes 1000000 | tf_op jit(solution)/shard_map/pallas_call | solution.py:218
  (3 shorter events, 0.1 us)
Async XLA Ops:
  2.8 16.1 %all-to-all-start = ((bf16[16,8,1024]{2,1,0:T(8,128)(2,1)}), bf16[16,8,1024]{2,1,0:T(8,128)(2,1)S(1)}, u32[]{:S(2)}, u32[]{:S(2)}) async-start(bf16[16,8,1024]{2,1,0:T(8,128)(2,1)} %bitcast.28), calls=%async_computation | async-start | bytes 524288 | tf_op jit(solution)/shard_map/all_to_all | solution.py:437
  11.3 5.6 %collective-permute-start = (bf16[224,128]{1,0:T(8,128)(2,1)}, bf16[224,128]{1,0:T(8,128)(2,1)S(1)}, u32[]{:S(2)}, u32[]{:S(2)}) collective-permute-start(bf16[224,128]{1,0:T(8,128)(2,1)} %get-tuple-element.26), channel_id=1, source_target_pairs={{0,1},{2,3},{4,5},{6,7},{8,9},{10,11},{12,13},{14,15},{1,0},{3,2},... | collective-permute-start | bytes 172040 | tf_op jit(solution)/shard_map/ppermute | solution.py:395
  12.6 4.3 %collective-permute-start.1 = (bf16[224,128]{1,0:T(8,128)(2,1)}, bf16[224,128]{1,0:T(8,128)(2,1)S(1)}, u32[]{:S(2)}, u32[]{:S(2)}) collective-permute-start(bf16[224,128]{1,0:T(8,128)(2,1)} %get-tuple-element.27), channel_id=1, source_target_pairs={{1,2},{3,4},{5,6},{7,8},{9,10},{11,12},{13,14},{2,1},{4,3},{6,5},{... | collective-permute-start | bytes 172040 | tf_op jit(solution)/shard_map/ppermute | solution.py:395
  13.3 1.0 %copy-start = (bf16[1104,128]{1,0:T(8,128)(2,1)S(1)}, bf16[1104,128]{1,0:T(8,128)(2,1)}, u32[]{:S(2)}) copy-start(bf16[1104,128]{1,0:T(8,128)(2,1)} %get-tuple-element.25.after_ref.own_ref) | copy-start | bytes 847876
  14.3 1.2 %copy-start.2 = (bf16[27,128,128]{2,1,0:T(8,128)(2,1)S(1)}, bf16[27,128,128]{2,1,0:T(8,128)(2,1)}, u32[]{:S(2)}) copy-start(bf16[27,128,128]{2,1,0:T(8,128)(2,1)} %w2_ref.1) | copy-start | bytes 2654212
  15.4 1.1 %copy-start.3 = (bf16[27,96,128]{2,1,0:T(8,128)(2,1)S(1)}, bf16[27,96,128]{2,1,0:T(8,128)(2,1)}, u32[]{:S(2)}) copy-start(bf16[27,96,128]{2,1,0:T(8,128)(2,1)} %w1_ref.1) | copy-start | bytes 1990660
  16.5 2.4 %copy-start.1 = (bf16[1104,128]{1,0:T(8,128)(2,1)S(1)}, bf16[1104,128]{1,0:T(8,128)(2,1)}, u32[]{:S(2)}) copy-start(bf16[1104,128]{1,0:T(8,128)(2,1)} %get-tuple-element.25.after_ref.own_ref) | copy-start | bytes 847876
  19.2 7.6 %collective-permute-start.2 = (bf16[1344,128]{1,0:T(8,128)(2,1)S(1)}, bf16[1344,128]{1,0:T(8,128)(2,1)S(1)}, u32[]{:S(2)}, u32[]{:S(2)}) collective-permute-start(bf16[1344,128]{1,0:T(8,128)(2,1)S(1)} %get-tuple-element.30), channel_id=1, source_target_pairs={{0,16},{32,48},{64,80},{96,112},{16,0},{48,32},{80,64},{112,96},{1... | collective-permute-start | bytes 1032200 | tf_op jit(solution)/shard_map/ppermute | solution.py:395
  21.9 8.6 %collective-permute-start.3 = (bf16[1344,128]{1,0:T(8,128)(2,1)S(1)}, bf16[1344,128]{1,0:T(8,128)(2,1)S(1)}, u32[]{:S(2)}, u32[]{:S(2)}) collective-permute-start(bf16[1344,128]{1,0:T(8,128)(2,1)S(1)} %get-tuple-element.32), channel_id=1, source_target_pairs={{16,32},{48,64},{80,96},{32,16},{64,48},{96,80},{17,33},{49,65},{8... | collective-permute-start | bytes 1032200 | tf_op jit(solution)/shard_map/ppermute | solution.py:395
  25.0 5.4 %copy-start.4 = (bf16[8,128,128]{2,1,0:T(8,128)(2,1)S(1)}, bf16[8,128,128]{2,1,0:T(8,128)(2,1)}, u32[]{:S(2)}) copy-start(bf16[8,128,128]{2,1,0:T(8,128)(2,1)} %wd_ref.1) | copy-start | bytes 786436
  25.0 5.4 %copy-start.5 = (bf16[96,96]{1,0:T(8,128)(2,1)S(1)}, bf16[96,96]{1,0:T(8,128)(2,1)}, u32[]{:S(2)}) copy-start(bf16[96,96]{1,0:T(8,128)(2,1)} %constant.5.clone.up_ref) | copy-start | bytes 55300
  39.5 2.6 %collective-permute-start.4 = (bf16[3584,128]{1,0:T(8,128)(2,1)S(1)}, bf16[3584,128]{1,0:T(8,128)(2,1)S(1)}, u32[]{:S(2)}, u32[]{:S(2)}) collective-permute-start(bf16[3584,128]{1,0:T(8,128)(2,1)S(1)} %slice_bitcast_fusion), channel_id=1, source_target_pairs={{0,16},{16,0},{1,17},{17,1},{2,18},{18,2},{3,19},{19,3},{4,20},{20... | collective-permute-start | bytes 2752520 | tf_op jit(solution)/shard_map/ppermute | solution.py:399
  64.7 4.3 %collective-permute-start.7 = (bf16[224,128]{1,0:T(8,128)(2,1)S(1)}, bf16[224,128]{1,0:T(8,128)(2,1)S(1)}, u32[]{:S(2)}, u32[]{:S(2)}) collective-permute-start(bf16[224,128]{1,0:T(8,128)(2,1)S(1)} %slice_reduce_fusion), channel_id=1, source_target_pairs={{0,96},{32,64},{64,32},{96,0},{1,97},{33,65},{65,33},{97,1},{2,98}... | collective-permute-start | bytes 172040 | tf_op jit(solution)/shard_map/ppermute | solution.py:411
  67.0 4.6 %collective-permute-start.6 = (bf16[224,128]{1,0:T(8,128)(2,1)S(1)}, bf16[224,128]{1,0:T(8,128)(2,1)S(1)}, u32[]{:S(2)}, u32[]{:S(2)}) collective-permute-start(bf16[224,128]{1,0:T(8,128)(2,1)S(1)} %slice_reduce_fusion), channel_id=1, source_target_pairs={{0,64},{32,96},{64,0},{96,32},{1,65},{33,97},{65,1},{97,33},{2,66}... | collective-permute-start | bytes 172040 | tf_op jit(solution)/shard_map/ppermute | solution.py:411
  67.9 3.7 %collective-permute-start.5 = (bf16[224,128]{1,0:T(8,128)(2,1)S(1)}, bf16[224,128]{1,0:T(8,128)(2,1)S(1)}, u32[]{:S(2)}, u32[]{:S(2)}) collective-permute-start(bf16[224,128]{1,0:T(8,128)(2,1)S(1)} %slice_reduce_fusion), channel_id=1, source_target_pairs={{0,32},{32,0},{64,96},{96,64},{1,33},{33,1},{65,97},{97,65},{2,34}... | collective-permute-start | bytes 172040 | tf_op jit(solution)/shard_map/ppermute | solution.py:411
  87.8 6.0 %collective-permute-start.8 = (bf16[3584,128]{1,0:T(8,128)(2,1)S(1)}, bf16[3584,128]{1,0:T(8,128)(2,1)S(1)}, u32[]{:S(2)}, u32[]{:S(2)}) collective-permute-start(bf16[3584,128]{1,0:T(8,128)(2,1)S(1)} %bitcast.20), channel_id=1, source_target_pairs={{0,16},{16,0},{1,17},{17,1},{2,18},{18,2},{3,19},{19,3},{4,20},{20... | collective-permute-start | bytes 2752520 | tf_op jit(solution)/shard_map/ppermute | solution.py:399

commit v7 on v6

--- a/solution.py
+++ b/solution.py
@@ -13,7 +13,8 @@
 X, Y, Z, C, CIN = 4, 16, 16, 128, 96
 HALF, PART = 3584, 224
 OWN = 1024
-COTS, MASK, STRIP = 1056, 1248, 1344
+COTS, MASK, STRIP = 1056, 1184, 1200
+EARLY = {1: 0, 2: 1, 5: 2, 6: 3}
 NN = (((1,), (0,)), ((), ()))
 NT = (((1,), (1,)), ((), ()))
 TN = (((0,), (0,)), ((), ()))
@@ -45,6 +46,15 @@
 
 def lanes(p, k):
     return p[:, k * C : (k + 1) * C]
+
+
+def silu(v):
+    s = jax.nn.sigmoid(v)
+    return v * s, s * (1.0 + v * (1.0 - s))
+
+
+def spread(packed, by):
+    return jnp.broadcast_to(packed[:, 16 * by : 16 * by + 1].astype(F32), (Z, C))
 
 
 def taps(get, x, n, w, dims=NN, flip=False, lines=(0, 1, 2)):
@@ -60,7 +70,7 @@
 
 
 def section(
-    near_ref, mid_ref, far_ref, mask_ref, gc_ref, place_ref, part_ref, w1_ref, w2_ref, back_ref, wd_ref, up_ref,
+    near_ref, mid_ref, far_ref, mask_ref, gc_ref, place_ref, part1_ref, inner_ref, slope_ref, part2_ref, w1_ref, w2_ref, back_ref, wd_ref, up_ref,
     grads_ref, out_ref,
     sides, first, sg1, second, ge, g2, gs, vt,
 ):
@@ -79,18 +89,17 @@
     def cots(x, y, n):
         return g2[(x * 18 + y) * Z : (x * 18 + y + n) * Z, :]
 
-    def mask_tile(bx, by):
-        ref, at = ((low_ref, MASK), (mask_ref, 0), (high_ref, MASK))[bx]
-        return ref[at + by * Z : at + (by + 1) * Z, :].astype(F32)
+    packed = low_ref[MASK:, :], mask_ref[...], high_ref[MASK:, :]
+    masks = [[spread(t, by) for by in range(6)] for t in packed]
 
     def cotangent(u, q):
         if u in (1, 2):
             return gc_ref[u - 1, q]
-        return (low_ref if u == 0 else high_ref)[COTS + q * 48 : COTS + (q + 1) * 48, :]
+        return (low_ref if u == 0 else high_ref)[COTS + q * 32 : COTS + (q + 1) * 32, :]
 
     def line(x, y0, cells):
         return jnp.concatenate(
-            [mask_tile((x + 4) // 4, (y + 4) // 4) for y in range(y0, y0 + cells)], axis=0
+            [masks[(x + 4) // 4][(y + 4) // 4] for y in range(y0, y0 + cells)], axis=0
         )
 
     def weight_grad(get, x0, y0, rows, put):
@@ -109,18 +118,18 @@
         gs[at : at + Y * Z, C : 2 * C] = g.astype(BF)
         gs[at : at + Y * Z, 2 * C : 3 * C] = from_below(g).astype(BF)
 
-    for x in range(8):
-        pre = jnp.zeros((20 * Z, C), F32) if x in (0, 7) else part_ref[x - 1]
-        if x not in (3, 4):
-            p = taps(cells, x, 20, w1_ref, lines=[i for i in range(3) if not 3 <= x + i < 7])
-            pre = pre + (lanes(p, 1) + from_below(lanes(p, 0)) + from_above(lanes(p, 2)))
+    first[3 * 20 * Z : 5 * 20 * Z, :] = inner_ref[...]
+    sg1[Y * Z : 3 * Y * Z, :] = slope_ref[...]
+    for x in (0, 1, 2, 5, 6, 7):
+        p = taps(cells, x, 20, w1_ref, lines=[i for i in range(3) if not 3 <= x + i < 7])
+        pre = lanes(p, 1) + from_below(lanes(p, 0)) + from_above(lanes(p, 2))
+        if x in EARLY:
+            pre = pre + part1_ref[EARLY[x]]
         act = line(x - 2, -2, 20)
-        pre = act * pre
-        s = jax.nn.sigmoid(pre)
-        first[x * 20 * Z : (x + 1) * 20 * Z, :] = (pre * s).astype(BF)
-        if 2 <= x < 6:
-            d = act * (s * (1.0 + pre * (1.0 - s)))
-            sg1[(x - 2) * Y * Z : (x - 1) * Y * Z, :] = d[2 * Z : 18 * Z]
+        value, slope = silu(act * pre)
+        first[x * 20 * Z : (x + 1) * 20 * Z, :] = value.astype(BF)
+        if x in (2, 5):
+            sg1[(x - 2) * Y * Z : (x - 1) * Y * Z, :] = (act * slope)[2 * Z : 18 * Z]
 
     even = z_of(6 * Z) % 2 == 0
     for u in range(4):
@@ -137,13 +146,14 @@
             ge[at : at + Z, C : 2 * C] = jnp.where(even[:Z], 0.0, t).astype(BF)
 
     for x in range(6):
-        p = taps(firsts, x, 18, w2_ref)
+        p = taps(firsts, x, 18, w2_ref, lines=[i for i in range(3) if not 3 <= x + i < 5])
         act = line(x - 1, -1, 18)
-        pre = act * (lanes(p, 1) + from_below(lanes(p, 0)) + from_above(lanes(p, 2)))
-        pre = pre + firsts(x + 1, 1, 18).astype(F32)
-        s = jax.nn.sigmoid(pre)
+        pre = lanes(p, 1) + from_below(lanes(p, 0)) + from_above(lanes(p, 2))
         if 1 <= x < 5:
-            second[(x - 1) * Y * Z : x * Y * Z, :] = (pre * s)[Z : 17 * Z].astype(BF)
+            pre = pre + part2_ref[x - 1]
+        value, slope = silu(act * pre + firsts(x + 1, 1, 18).astype(F32))
+        if 1 <= x < 5:
+            second[(x - 1) * Y * Z : x * Y * Z, :] = value[Z : 17 * Z].astype(BF)
         u, a = (x + 1) // 2, (x + 1) % 2
         back = []
         for b in range(2):
@@ -153,7 +163,7 @@
         g = jnp.concatenate(
             [back[1 - y % 2][y // 2 * Z : (y // 2 + 1) * Z] for y in range(18)], axis=0
         )
-        g = (act * g * (s * (1.0 + pre * (1.0 - s)))).astype(BF)
+        g = (act * g * slope).astype(BF)
         g2[x * 18 * Z : (x + 1) * 18 * Z, :] = g
         if 1 <= x < 5:
             put_z_taps(x - 1, g[Z : 17 * Z].astype(F32))
@@ -238,13 +248,27 @@
         first_ref[m * C + CIN : (m + 1) * C, :] = jnp.zeros((C - CIN, 3 * C), BF)
 
 
-def begin(mid_ref, first_ref, part_ref):
+def begin(mid_ref, mask_ref, w1_ref, w2_ref, part1_ref, first_ref, sg1_ref, part2_ref):
     def cells(x, y, n):
         return mid_ref[((x - 3) * 22 + y) * Z : ((x - 3) * 22 + y + n) * Z, :]
 
-    for x in range(1, 7):
-        p = taps(cells, x, 20, first_ref, lines=[i for i in range(3) if 3 <= x + i < 7])
-        part_ref[x - 1] = lanes(p, 1) + from_below(lanes(p, 0)) + from_above(lanes(p, 2))
+    def firsts(x, y, n):
+        return first_ref[((x - 3) * 20 + y) * Z : ((x - 3) * 20 + y + n) * Z, :]
+
+    masks = [spread(mask_ref[...], by) for by in range(6)]
+    act = jnp.concatenate([masks[(y + 4) // 4] for y in range(-2, 18)], axis=0)
+    for x in (3, 4, 1, 2, 5, 6):
+        p = taps(cells, x, 20, w1_ref, lines=[i for i in range(3) if 3 <= x + i < 7])
+        pre = lanes(p, 1) + from_below(lanes(p, 0)) + from_above(lanes(p, 2))
+        if x in (3, 4):
+            value, slope = silu(act * pre)
+            first_ref[(x - 3) * 20 * Z : (x - 2) * 20 * Z, :] = value.astype(BF)
+            sg1_ref[(x - 3) * Y * Z : (x - 2) * Y * Z, :] = (act * slope)[2 * Z : 18 * Z]
+        else:
+            part1_ref[EARLY[x]] = pre
+    for x in range(1, 5):
+        p = taps(firsts, x, 18, w2_ref, lines=[i for i in range(3) if 3 <= x + i < 5])
+        part2_ref[x - 1] = lanes(p, 1) + from_below(lanes(p, 0)) + from_above(lanes(p, 2))
 
 
 def prepare(
@@ -320,9 +344,14 @@
         mid_ref[at : at + 3 * Z, :] = low_ref[x * 3 * Z : (x + 1) * 3 * Z, :]
         mid_ref[at + 3 * Z : at + 19 * Z, :] = own_ref[x * Y * Z : (x + 1) * Y * Z, :]
         mid_ref[at + 19 * Z : at + 22 * Z, :] = high_ref[x * 3 * Z : (x + 1) * 3 * Z, :]
-    mask_ref[0:Z, :] = low_ref[208:224, :]
-    mask_ref[Z : 5 * Z, :] = own_ref[OWN : OWN + 4 * Z, :]
-    mask_ref[5 * Z : 6 * Z, :] = high_ref[208:224, :]
+    tiles = [low_ref[208:224, :]]
+    tiles += [own_ref[OWN + by * Z : OWN + (by + 1) * Z, :] for by in range(4)]
+    tiles += [high_ref[208:224, :]]
+    which = iota((Z, C), 1) // 16
+    packed = jnp.zeros((Z, C), F32)
+    for by in range(6):
+        packed = jnp.where(which == by, tiles[by].astype(F32), packed)
+    mask_ref[...] = packed.astype(BF)
     place_ref[...] = own_ref[OWN + 4 * Z : OWN + 5 * Z, :]
     place = jnp.concatenate(
         [
@@ -332,18 +361,18 @@
         ],
         axis=0,
     )
-    bricks = mm(one(place == iota((48, C), 1).astype(F32)), rows_ref[...]).astype(BF)
+    bricks = mm(one(place == iota((48, C), 1).astype(F32)), rows_ref[...])[12:44].astype(BF)
     for q in range(8):
         gc_ref[q // 4, q % 4] = lanes(bricks, q)
 
     def fill(up, down):
         for q in range(4):
-            up[COTS + q * 48 : COTS + (q + 1) * 48, :] = lanes(bricks, 4 + q)
-            down[COTS + q * 48 : COTS + (q + 1) * 48, :] = lanes(bricks, q)
+            up[COTS + q * 32 : COTS + (q + 1) * 32, :] = lanes(bricks, 4 + q)
+            down[COTS + q * 32 : COTS + (q + 1) * 32, :] = lanes(bricks, q)
         up[0:COTS, :] = mid_ref[22 * Z :, :]
         down[0:COTS, :] = mid_ref[0:COTS, :]
         for ref in (up, down):
-            ref[MASK : MASK + 96, :] = mask_ref[...]
+            ref[MASK:, :] = mask_ref[...]
 
     @pl.when(lax.axis_index("c") == 0)
     def _():
@@ -400,10 +429,10 @@
 
 
 def up_matrix():
-    m = np.zeros((6 * Z, 96), np.float32)
+    m = np.zeros((6 * Z, 64), np.float32)
     for by in range(6):
         for z in range(Z):
-            m[by * Z + z, z // 2 % 2 * 48 + (12, 16, 20, 24, 28, 32)[by] + z // 4] = 1
+            m[by * Z + z, z // 2 % 2 * 32 + by * 4 + z // 4] = 1
     return jnp.asarray(m, BF)
 
 
@@ -438,18 +467,23 @@
 
     mid, mask, gc, place, near, far = call(
         widen,
-        [((4 * 22 * Z, C), BF), ((96, C), BF), ((2, 4, 48, C), BF), ((16, C), BF), ((STRIP, C), BF), ((STRIP, C), BF)],
+        [((4 * 22 * Z, C), BF), ((16, C), BF), ((2, 4, 32, C), BF), ((16, C), BF), ((STRIP, C), BF), ((STRIP, C), BF)],
         (own, beside, beyond, rows, w1),
         [VM] * 4 + [pl.BlockSpec(memory_space=pl.ANY)],
         scratch=[((2, 224, C), BF)],
     )
     far, near = swap(far, GX, 1), swap(near, GX, 0)
-    (ahead,) = call(begin, [((6, 20 * Z, C), F32)], (mid, w1), flops=2_000_000_000)
+    ahead = call(
+        begin,
+        [((4, 20 * Z, C), F32), ((40 * Z, C), BF), ((2 * Y * Z, C), F32), ((4, 18 * Z, C), F32)],
+        (mid, mask, w1, w2),
+        flops=3_000_000_000,
+    )
 
     grads, outgoing = call(
         section,
         [((2, HALF, C), BF), ((256, C), BF)],
-        (near, mid, far, mask, gc, place, ahead, w1, w2, back, weight_down, up_matrix()),
+        (near, mid, far, mask, gc, place, *ahead, w1, w2, back, weight_down, up_matrix()),
         scratch=[
             ((2, STRIP, C), BF),
             ((8 * 20 * Z, C), BF),

time: 95.7 us -> 94.7 us (0.990)
  waiting for transfers between devices: 11.8 us -> 10.7 us
    ppermute x4, waiting for transfers between devices: 3.63 us -> 2.48 us  [swap(): return lax.ppermute(v, axes, pairs + [(j, i) for i, j in pairs])]
where the time goes in v7:
time: 94.7 us; the launch traced here: 94.3 us
  blocking collectives  38.3 us (40%)
  starting transfers between devices  23.7 us (25%)
  Pallas kernels  16.1 us (17%)
  waiting for transfers between devices  10.7 us (11%)
  local copies, waits for them, and re-layouts  4.09 us (4%)
  between operations  0.96 us (1%)
    all_to_all x1, blocking collectives, per_device(): lax.all_to_all(jnp.concatenate([half.reshape(16, PART, C), outgoing.resha...  22.2 us
    pallas_call x7, Pallas kernels, call(): pl.pallas_call(kernel, out_shape=tuple((jax.ShapeDtypeStruct(shape, dtype...  16.1 us
    all_to_all x1, blocking collectives, per_device(): lax.all_to_all(jnp.broadcast_to(part[None], (16, PART, C)), GY, 0, 0, til...  16 us
    all_to_all x1, starting transfers between devices, per_device(): rows = lax.all_to_all(rows, GY, 0, 0, tiled=True)  8.44 us
    ppermute x4, starting transfers between devices, swap(): return lax.ppermute(v, axes, pairs + [(j, i) for i, j in pairs])  7.81 us
    ppermute x2, starting transfers between devices, swap_cores(): return lax.ppermute(v, 'c', [(0, 1), (1, 0)])  4.15 us
    ppermute x3, waiting for transfers between devices, flip(): lax.ppermute(v, axis, [(i, i ^ bits) for i in range(lax.axis_size(axis))])  3.57 us
    ppermute x3, starting transfers between devices, flip(): lax.ppermute(v, axis, [(i, i ^ bits) for i in range(lax.axis_size(axis))])  3.33 us
  transfers between devices with their start and end apart: 10, of which 6 were waited for; matrix products, arithmetic and copies ran while one was open for 1% of the time, Pallas kernels for 4%

profile of v7, /device:TPU:1, one launch (start us, length us, event | category | flops | bytes accessed | tf_op | source)
XLA Modules:
  0.0 94.3 jit_solution(17663803964781961866)
XLA Ops:
  0.6 2.2 %shard_map.111 = (bf16[128,1024]{1,0:T(8,128)(2,1)}, bf16[1104,128]{1,0:T(8,128)(2,1)}, bf16[224,128]{1,0:T(8,128)(2,1)}, bf16[224,128]{1,0:T(8,128)(2,1)}) custom-call(bf16[1,1,32,1024]{3,2,1,0:T(8,128)(2,1)} %grad_hbm.1, bf16[4,16,1536]{2,1,0:T(8,128)(2,1)} %feat_hbm.1, s32[1,4,4]{2,1,0:T(4,128)} %blocks_hbm.1, s32[1,16]{1,0:T(1,128)} %bitcast.31), custom_call_target="tpu_custom_call" | custom-call | flops 10000000 | bytes 1000000 | tf_op jit(solution)/shard_map/pallas_call | solution.py:228
  2.8 8.4 %all-to-all-start = ((bf16[16,8,1024]{2,1,0:T(8,128)(2,1)}), bf16[16,8,1024]{2,1,0:T(8,128)(2,1)S(1)}, u32[]{:S(2)}, u32[]{:S(2)}) async-start(bf16[16,8,1024]{2,1,0:T(8,128)(2,1)} %bitcast.28), calls=%async_computation | async-start | bytes 524288 | tf_op jit(solution)/shard_map/all_to_all | solution.py:466
  11.3 1.4 %collective-permute-start = (bf16[224,128]{1,0:T(8,128)(2,1)}, bf16[224,128]{1,0:T(8,128)(2,1)S(1)}, u32[]{:S(2)}, u32[]{:S(2)}) collective-permute-start(bf16[224,128]{1,0:T(8,128)(2,1)} %get-tuple-element.30), channel_id=1, source_target_pairs={{0,1},{2,3},{4,5},{6,7},{8,9},{10,11},{12,13},{14,15},{1,0},{3,2},... | collective-permute-start | bytes 172040 | tf_op jit(solution)/shard_map/ppermute | solution.py:424
  12.6 0.7 collective-permute-start.1
  13.3 0.0 copy-start
  13.3 0.9 %copy-done = bf16[1104,128]{1,0:T(8,128)(2,1)S(1)} copy-done((bf16[1104,128]{1,0:T(8,128)(2,1)S(1)}, bf16[1104,128]{1,0:T(8,128)(2,1)}, u32[]{:S(2)}) %copy-start) | copy-done | bytes 282648
  14.3 0.0 copy-start.2
  14.3 1.2 %copy-done.2 = bf16[27,128,128]{2,1,0:T(8,128)(2,1)S(1)} copy-done((bf16[27,128,128]{2,1,0:T(8,128)(2,1)S(1)}, bf16[27,128,128]{2,1,0:T(8,128)(2,1)}, u32[]{:S(2)}) %copy-start.2) | copy-done | bytes 884760
  15.4 0.0 copy-start.3
  15.4 1.1 %copy-done.3 = bf16[27,96,128]{2,1,0:T(8,128)(2,1)S(1)} copy-done((bf16[27,96,128]{2,1,0:T(8,128)(2,1)S(1)}, bf16[27,96,128]{2,1,0:T(8,128)(2,1)}, u32[]{:S(2)}) %copy-start.3) | copy-done | bytes 663576
  16.5 0.0 copy-start.1
  16.5 0.4 shard_map.112
  16.9 0.0 collective-permute-done.beside_ref
  16.9 0.0 collective-permute-done.1.beyond_ref
  16.9 2.0 %all-to-all-done = bf16[16,8,1024]{2,1,0:T(8,128)(2,1)S(1)} async-done(((bf16[16,8,1024]{2,1,0:T(8,128)(2,1)}), bf16[16,8,1024]{2,1,0:T(8,128)(2,1)S(1)}, u32[]{:S(2)}, u32[]{:S(2)}) %all-to-all-start) | async-done | bytes 262176 | tf_op jit(solution)/shard_map/all_to_all | solution.py:466
  18.9 0.0 copy-done.1
  18.9 0.3 shard_map.113
  19.2 2.7 %collective-permute-start.2 = (bf16[1200,128]{1,0:T(8,128)(2,1)S(1)}, bf16[1200,128]{1,0:T(8,128)(2,1)S(1)}, u32[]{:S(2)}, u32[]{:S(2)}) collective-permute-start(bf16[1200,128]{1,0:T(8,128)(2,1)S(1)} %get-tuple-element.34), channel_id=1, source_target_pairs={{0,16},{32,48},{64,80},{96,112},{16,0},{48,32},{80,64},{112,96},{1... | collective-permute-start | bytes 921608 | tf_op jit(solution)/shard_map/ppermute | solution.py:424
  21.9 3.1 %collective-permute-start.3 = (bf16[1200,128]{1,0:T(8,128)(2,1)S(1)}, bf16[1200,128]{1,0:T(8,128)(2,1)S(1)}, u32[]{:S(2)}, u32[]{:S(2)}) collective-permute-start(bf16[1200,128]{1,0:T(8,128)(2,1)S(1)} %get-tuple-element.36), channel_id=1, source_target_pairs={{16,32},{48,64},{80,96},{32,16},{64,48},{96,80},{17,33},{49,65},{8... | collective-permute-start | bytes 921608 | tf_op jit(solution)/shard_map/ppermute | solution.py:424
  25.0 0.0 copy-start.4
  25.0 0.0 copy-start.5
  25.0 2.5 %shard_map.114 = (f32[4,320,128]{2,1,0:T(8,128)S(1)}, bf16[640,128]{1,0:T(8,128)(2,1)S(1)}, f32[512,128]{1,0:T(8,128)S(1)}, f32[4,288,128]{2,1,0:T(8,128)S(1)}) custom-call(bf16[1408,128]{1,0:T(8,128)(2,1)S(1)} %get-tuple-element.35.mid_ref, bf16[16,128]{1,0:T(8,128)(2,1)S(1)} %get-tuple-element.37.mask_ref, ...), custom_call_target="tpu_custom_call" | custom-call | flops 3000000000 | bytes 1000000 | tf_op jit(solution)/shard_map/pallas_call | solution.py:228
  27.6 0.0 collective-permute-done.2.near_ref
  27.6 2.5 %collective-permute-done.3.far_ref = bf16[1200,128]{1,0:T(8,128)(2,1)S(1)} collective-permute-done((bf16[1200,128]{1,0:T(8,128)(2,1)S(1)}, bf16[1200,128]{1,0:T(8,128)(2,1)S(1)}, u32[]{:S(2)}, u32[]{:S(2)}) %collective-permute-start.3) | collective-permute-done | bytes 307232 | tf_op jit(solution)/shard_map/ppermute | solution.py:424
  30.0 0.0 copy-done.4
  30.0 0.0 copy-done.5
  30.1 8.2 %shard_map.115 = (bf16[2,3584,128]{2,1,0:T(8,128)(2,1)S(1)}, bf16[256,128]{1,0:T(8,128)(2,1)S(1)}) custom-call(bf16[1200,128]{1,0:T(8,128)(2,1)S(1)} %collective-permute-done.2.near_ref, bf16[1408,128]{1,0:T(8,128)(2,1)S(1)} %get-tuple-element.35.mid_ref, bf16[1200,128]{1,0:T(8,128)(2,1)S(1)} %collective-permute-done.3.far_ref, ...), custom_call_target="tpu_custom_call" | custom-call | flops 8000000000 | bytes 1000000 | tf_op jit(solution)/shard_map/pallas_call | solution.py:228
  38.2 0.1 slice_bitcast_fusion
  38.3 0.3 collective-permute-start.4
  38.6 2.5 %collective-permute-done.4 = bf16[3584,128]{1,0:T(8,128)(2,1)S(1)} collective-permute-done((bf16[3584,128]{1,0:T(8,128)(2,1)S(1)}, bf16[3584,128]{1,0:T(8,128)(2,1)S(1)}, u32[]{:S(2)}, u32[]{:S(2)}) %collective-permute-start.4) | collective-permute-done | bytes 917536 | tf_op jit(solution)/shard_map/ppermute | solution.py:428
  41.0 0.2 fusion
  41.3 0.1 pad_maximum_fusion
  41.4 22.2 %all_to_all.21 = bf16[16,240,128]{2,1,0:T(8,128)(2,1)S(1)} all-to-all(bf16[16,240,128]{2,1,0:T(8,128)(2,1)S(1)} %pad_maximum_fusion), channel_id=1, replica_groups=mesh['y'=4,'c'=2,'z'=4,'x'=4] {'z','x'}, dimensions={0} | all-to-all | bytes 1966080 | tf_op jit(solution)/shard_map/all_to_all | solution.py:502
  63.6 0.1 slice_reduce_fusion
  63.7 2.3 %collective-permute-start.7 = (bf16[224,128]{1,0:T(8,128)(2,1)S(1)}, bf16[224,128]{1,0:T(8,128)(2,1)S(1)}, u32[]{:S(2)}, u32[]{:S(2)}) collective-permute-start(bf16[224,128]{1,0:T(8,128)(2,1)S(1)} %slice_reduce_fusion), channel_id=1, source_target_pairs={{0,96},{32,64},{64,32},{96,0},{1,97},{33,65},{65,33},{97,1},{2,98}... | collective-permute-start | bytes 172040 | tf_op jit(solution)/shard_map/ppermute | solution.py:440
  66.0 0.9 collective-permute-start.6
  66.9 0.2 collective-permute-start.5
  67.0 1.0 %collective-permute-done.7 = bf16[224,128]{1,0:T(8,128)(2,1)S(1)} collective-permute-done((bf16[224,128]{1,0:T(8,128)(2,1)S(1)}, bf16[224,128]{1,0:T(8,128)(2,1)S(1)}, u32[]{:S(2)}, u32[]{:S(2)}) %collective-permute-start.7) | collective-permute-done | bytes 57376 | tf_op jit(solution)/shard_map/ppermute | solution.py:440
  68.0 2.6 %collective-permute-done.6 = bf16[224,128]{1,0:T(8,128)(2,1)S(1)} collective-permute-done((bf16[224,128]{1,0:T(8,128)(2,1)S(1)}, bf16[224,128]{1,0:T(8,128)(2,1)S(1)}, u32[]{:S(2)}, u32[]{:S(2)}) %collective-permute-start.6) | collective-permute-done | bytes 57376 | tf_op jit(solution)/shard_map/ppermute | solution.py:440
  70.6 0.0 collective-permute-done.5
  70.7 0.1 broadcast_in_dim.2
  70.8 16.0 %all_to_all.22 = bf16[16,224,128]{2,1,0:T(8,128)(2,1)S(1)} all-to-all(bf16[16,224,128]{2,1,0:T(8,128)(2,1)S(1)} %broadcast_in_dim.2), channel_id=1, replica_groups=mesh['y'=4,'c'=2,'z'=4,'x'=4] {'z','x'}, dimensions={0} | all-to-all | bytes 1835008 | tf_op jit(solution)/shard_map/all_to_all | solution.py:510
  86.8 3.9 %collective-permute-start.8 = (bf16[3584,128]{1,0:T(8,128)(2,1)S(1)}, bf16[3584,128]{1,0:T(8,128)(2,1)S(1)}, u32[]{:S(2)}, u32[]{:S(2)}) collective-permute-start(bf16[3584,128]{1,0:T(8,128)(2,1)S(1)} %bitcast.20), channel_id=1, source_target_pairs={{0,16},{16,0},{1,17},{17,1},{2,18},{18,2},{3,19},{19,3},{4,20},{20... | collective-permute-start | bytes 2752520 | tf_op jit(solution)/shard_map/ppermute | solution.py:428
  90.7 0.7 reshape.44
  91.4 1.3 %shard_map.116 = (f32[2592,128]{1,0:T(8,128)}, f32[3456,128]{1,0:T(8,128)}, f32[1024,128]{1,0:T(8,128)}) custom-call(bf16[3584,128]{1,0:T(8,128)(2,1)S(1)} %bitcast.21), custom_call_target="tpu_custom_call" | custom-call | flops 10000000 | bytes 1000000 | tf_op jit(solution)/shard_map/pallas_call | solution.py:228
  92.7 0.1 collective-permute-done.8.half_ref
  92.8 1.3 %shard_map.117 = (f32[2592,128]{1,0:T(8,128)}, f32[3456,128]{1,0:T(8,128)}, f32[1024,128]{1,0:T(8,128)}) custom-call(bf16[3584,128]{1,0:T(8,128)(2,1)S(1)} %collective-permute-done.8.half_ref, f32[2592,128]{1,0:T(8,128)} %get-tuple-element.48.a, f32[3456,128]{1,0:T(8,128)} %get-tuple-element.49.b, ...), custom_call_target="tpu_custom_call", output_to_operand_aliasing={{0}: (1, {}), {1}: (2, {}), {2}: (3, {})} | custom-call | flops 10000000 | bytes 1000000 | tf_op jit(solution)/shard_map/pallas_call | solution.py:228
  (3 shorter events, 0.1 us)
Async XLA Ops:
  2.8 16.1 %all-to-all-start = ((bf16[16,8,1024]{2,1,0:T(8,128)(2,1)}), bf16[16,8,1024]{2,1,0:T(8,128)(2,1)S(1)}, u32[]{:S(2)}, u32[]{:S(2)}) async-start(bf16[16,8,1024]{2,1,0:T(8,128)(2,1)} %bitcast.28), calls=%async_computation | async-start | bytes 524288 | tf_op jit(solution)/shard_map/all_to_all | solution.py:466
  11.3 5.6 %collective-permute-start = (bf16[224,128]{1,0:T(8,128)(2,1)}, bf16[224,128]{1,0:T(8,128)(2,1)S(1)}, u32[]{:S(2)}, u32[]{:S(2)}) collective-permute-start(bf16[224,128]{1,0:T(8,128)(2,1)} %get-tuple-element.30), channel_id=1, source_target_pairs={{0,1},{2,3},{4,5},{6,7},{8,9},{10,11},{12,13},{14,15},{1,0},{3,2},... | collective-permute-start | bytes 172040 | tf_op jit(solution)/shard_map/ppermute | solution.py:424
  12.6 4.3 %collective-permute-start.1 = (bf16[224,128]{1,0:T(8,128)(2,1)}, bf16[224,128]{1,0:T(8,128)(2,1)S(1)}, u32[]{:S(2)}, u32[]{:S(2)}) collective-permute-start(bf16[224,128]{1,0:T(8,128)(2,1)} %get-tuple-element.31), channel_id=1, source_target_pairs={{1,2},{3,4},{5,6},{7,8},{9,10},{11,12},{13,14},{2,1},{4,3},{6,5},{... | collective-permute-start | bytes 172040 | tf_op jit(solution)/shard_map/ppermute | solution.py:424
  13.3 1.0 %copy-start = (bf16[1104,128]{1,0:T(8,128)(2,1)S(1)}, bf16[1104,128]{1,0:T(8,128)(2,1)}, u32[]{:S(2)}) copy-start(bf16[1104,128]{1,0:T(8,128)(2,1)} %get-tuple-element.29.after_ref.own_ref) | copy-start | bytes 847876
  14.3 1.2 %copy-start.2 = (bf16[27,128,128]{2,1,0:T(8,128)(2,1)S(1)}, bf16[27,128,128]{2,1,0:T(8,128)(2,1)}, u32[]{:S(2)}) copy-start(bf16[27,128,128]{2,1,0:T(8,128)(2,1)} %w2_ref.1) | copy-start | bytes 2654212
  15.4 1.1 %copy-start.3 = (bf16[27,96,128]{2,1,0:T(8,128)(2,1)S(1)}, bf16[27,96,128]{2,1,0:T(8,128)(2,1)}, u32[]{:S(2)}) copy-start(bf16[27,96,128]{2,1,0:T(8,128)(2,1)} %w1_ref.1) | copy-start | bytes 1990660
  16.5 2.4 %copy-start.1 = (bf16[1104,128]{1,0:T(8,128)(2,1)S(1)}, bf16[1104,128]{1,0:T(8,128)(2,1)}, u32[]{:S(2)}) copy-start(bf16[1104,128]{1,0:T(8,128)(2,1)} %get-tuple-element.29.after_ref.own_ref) | copy-start | bytes 847876
  19.2 8.4 %collective-permute-start.2 = (bf16[1200,128]{1,0:T(8,128)(2,1)S(1)}, bf16[1200,128]{1,0:T(8,128)(2,1)S(1)}, u32[]{:S(2)}, u32[]{:S(2)}) collective-permute-start(bf16[1200,128]{1,0:T(8,128)(2,1)S(1)} %get-tuple-element.34), channel_id=1, source_target_pairs={{0,16},{32,48},{64,80},{96,112},{16,0},{48,32},{80,64},{112,96},{1... | collective-permute-start | bytes 921608 | tf_op jit(solution)/shard_map/ppermute | solution.py:424
  21.9 8.2 %collective-permute-start.3 = (bf16[1200,128]{1,0:T(8,128)(2,1)S(1)}, bf16[1200,128]{1,0:T(8,128)(2,1)S(1)}, u32[]{:S(2)}, u32[]{:S(2)}) collective-permute-start(bf16[1200,128]{1,0:T(8,128)(2,1)S(1)} %get-tuple-element.36), channel_id=1, source_target_pairs={{16,32},{48,64},{80,96},{32,16},{64,48},{96,80},{17,33},{49,65},{8... | collective-permute-start | bytes 921608 | tf_op jit(solution)/shard_map/ppermute | solution.py:424
  25.0 5.1 %copy-start.4 = (bf16[8,128,128]{2,1,0:T(8,128)(2,1)S(1)}, bf16[8,128,128]{2,1,0:T(8,128)(2,1)}, u32[]{:S(2)}) copy-start(bf16[8,128,128]{2,1,0:T(8,128)(2,1)} %wd_ref.1) | copy-start | bytes 786436
  25.0 5.0 %copy-start.5 = (bf16[96,64]{1,0:T(8,128)(2,1)S(1)}, bf16[96,64]{1,0:T(8,128)(2,1)}, u32[]{:S(2)}) copy-start(bf16[96,64]{1,0:T(8,128)(2,1)} %constant.5.clone.up_ref) | copy-start | bytes 36868
  38.3 2.7 %collective-permute-start.4 = (bf16[3584,128]{1,0:T(8,128)(2,1)S(1)}, bf16[3584,128]{1,0:T(8,128)(2,1)S(1)}, u32[]{:S(2)}, u32[]{:S(2)}) collective-permute-start(bf16[3584,128]{1,0:T(8,128)(2,1)S(1)} %slice_bitcast_fusion), channel_id=1, source_target_pairs={{0,16},{16,0},{1,17},{17,1},{2,18},{18,2},{3,19},{19,3},{4,20},{20... | collective-permute-start | bytes 2752520 | tf_op jit(solution)/shard_map/ppermute | solution.py:428
  63.7 4.3 %collective-permute-start.7 = (bf16[224,128]{1,0:T(8,128)(2,1)S(1)}, bf16[224,128]{1,0:T(8,128)(2,1)S(1)}, u32[]{:S(2)}, u32[]{:S(2)}) collective-permute-start(bf16[224,128]{1,0:T(8,128)(2,1)S(1)} %slice_reduce_fusion), channel_id=1, source_target_pairs={{0,96},{32,64},{64,32},{96,0},{1,97},{33,65},{65,33},{97,1},{2,98}... | collective-permute-start | bytes 172040 | tf_op jit(solution)/shard_map/ppermute | solution.py:440
  66.0 4.6 %collective-permute-start.6 = (bf16[224,128]{1,0:T(8,128)(2,1)S(1)}, bf16[224,128]{1,0:T(8,128)(2,1)S(1)}, u32[]{:S(2)}, u32[]{:S(2)}) collective-permute-start(bf16[224,128]{1,0:T(8,128)(2,1)S(1)} %slice_reduce_fusion), channel_id=1, source_target_pairs={{0,64},{32,96},{64,0},{96,32},{1,65},{33,97},{65,1},{97,33},{2,66}... | collective-permute-start | bytes 172040 | tf_op jit(solution)/shard_map/ppermute | solution.py:440
  66.9 3.7 %collective-permute-start.5 = (bf16[224,128]{1,0:T(8,128)(2,1)S(1)}, bf16[224,128]{1,0:T(8,128)(2,1)S(1)}, u32[]{:S(2)}, u32[]{:S(2)}) collective-permute-start(bf16[224,128]{1,0:T(8,128)(2,1)S(1)} %slice_reduce_fusion), channel_id=1, source_target_pairs={{0,32},{32,0},{64,96},{96,64},{1,33},{33,1},{65,97},{97,65},{2,34}... | collective-permute-start | bytes 172040 | tf_op jit(solution)/shard_map/ppermute | solution.py:440
  86.8 6.0 %collective-permute-start.8 = (bf16[3584,128]{1,0:T(8,128)(2,1)S(1)}, bf16[3584,128]{1,0:T(8,128)(2,1)S(1)}, u32[]{:S(2)}, u32[]{:S(2)}) collective-permute-start(bf16[3584,128]{1,0:T(8,128)(2,1)S(1)} %bitcast.20), channel_id=1, source_target_pairs={{0,16},{16,0},{1,17},{17,1},{2,18},{18,2},{3,19},{19,3},{4,20},{20... | collective-permute-start | bytes 2752520 | tf_op jit(solution)/shard_map/ppermute | solution.py:428

commit v8 on v7

--- a/solution.py
+++ b/solution.py
@@ -383,6 +383,49 @@
         fill(far_ref, near_ref)
 
 
+def places():
+    core, z, x = lax.axis_index("c"), lax.axis_index("z"), lax.axis_index("x")
+    pick = lambda a, b: jnp.where(core == 0, a, b)
+    return pick(z, x), pick(x, z), pick(4, 1), pick(1, 4)
+
+
+def fold_cores(grads_ref, theirs_ref, bricks_ref, *out_refs):
+    first, _, a, b = places()
+    for n, out in enumerate(out_refs):
+        for t in range(4):
+            to = (first ^ n) * a + t * b
+            rows = pl.ds(pl.multiple_of(to * PART, 16), PART)
+            out[t * PART : (t + 1) * PART, :] = (
+                grads_ref[0, rows, :].astype(F32) + theirs_ref[rows, :].astype(F32)
+            ).astype(BF)
+            rows = pl.ds(pl.multiple_of(to * 16, 16), 16)
+            out[4 * PART + t * 16 : 4 * PART + (t + 1) * 16, :] = bricks_ref[rows, :]
+
+
+def fold_first(*refs):
+    got, outs = refs[:4], refs[4:]
+    _, second, _, _ = places()
+    for m, out in enumerate(outs):
+        to = second ^ m
+        rows = pl.ds(pl.multiple_of(to * PART, 16), PART)
+        v = [g[rows, :].astype(F32) for g in got]
+        out[:PART, :] = ((v[0] + v[1]) + (v[2] + v[3])).astype(BF)
+        rows = pl.ds(pl.multiple_of(4 * PART + to * 16, 16), 16)
+        for n, g in enumerate(got):
+            out[PART + n * 16 : PART + (n + 1) * 16, :] = g[rows, :]
+
+
+def fold_second(*refs):
+    got, (part_ref, bricks_ref) = refs[:4], refs[4:]
+    first, second, a, b = places()
+    v = [g[:PART, :].astype(F32) for g in got]
+    part_ref[...] = ((v[0] + v[1]) + (v[2] + v[3])).astype(BF)
+    for m, g in enumerate(got):
+        for n in range(4):
+            at = pl.multiple_of(((first ^ n) * a + (second ^ m) * b) * 16, 16)
+            bricks_ref[pl.ds(at, 16), :] = g[PART + n * 16 : PART + (n + 1) * 16, :]
+
+
 def unfold(half_ref, core, first_hbm, second_hbm, down_hbm, wide, sems):
     spans = {
         0: ((0, 27 * C, second_hbm, 0), (27 * C, 28 * C, down_hbm, 0)),
@@ -440,6 +483,17 @@
     return lax.ppermute(v, axis, [(i, i ^ bits) for i in range(lax.axis_size(axis))])
 
 
+def flip_by_core(v, axes, bits):
+    every = ("c", "z", "x")
+    size = [lax.axis_size(n) for n in every]
+    pairs = []
+    for d in range(size[0] * size[1] * size[2]):
+        at = [int(i) for i in np.unravel_index(d, size)]
+        at[every.index(axes[at[0]])] ^= bits
+        pairs.append((d, int(np.ravel_multi_index(at, size))))
+    return lax.ppermute(v, every, pairs)
+
+
 def per_device(features, block_mask, weight_first, weight_second, weight_down, owners, moved_grad):
     rows, own, beside, beyond = call(
         prepare,
@@ -497,14 +551,14 @@
         flops=8_000_000_000,
     )
 
-    theirs = swap_cores(grads[1])
-    half = (grads[0].astype(F32) + theirs.astype(F32)).astype(BF)
-    pieces = lax.all_to_all(
-        jnp.concatenate([half.reshape(16, PART, C), outgoing.reshape(16, 16, C)], axis=1),
-        GY, 0, 0, tiled=True,
-    )
-    moved = pieces[:, PART:].reshape(16, 8, 2, C).transpose(0, 2, 1, 3).reshape(1, 1, 32, 8 * C)
-    part = jnp.sum(pieces[:, :PART].astype(F32), axis=0).astype(BF)
+    blocks = call(
+        fold_cores, [((4 * PART + 64, C), BF)] * 4, (grads, swap_cores(grads[1]), outgoing)
+    )
+    blocks = [blocks[0]] + [flip_by_core(blocks[n], ("z", "x"), n) for n in (1, 2, 3)]
+    blocks = call(fold_first, [((PART + 64, C), BF)] * 4, blocks)
+    blocks = [blocks[0]] + [flip_by_core(blocks[n], ("x", "z"), n) for n in (1, 2, 3)]
+    part, arrived = call(fold_second, [((PART, C), BF), ((256, C), BF)], blocks)
+    moved = arrived.reshape(16, 8, 2, C).transpose(0, 2, 1, 3).reshape(1, 1, 32, 8 * C)
     others = [flip(part, "y", n).astype(F32) for n in (1, 2, 3)]
     part = ((part.astype(F32) + others[0]) + (others[1] + others[2])).astype(BF)
     part = lax.all_to_all(jnp.broadcast_to(part[None], (16, PART, C)), GY, 0, 0, tiled=True)

time: 94.7 us -> 93.1 us (0.983)
  blocking collectives: 38.3 us -> 14.8 us
  waiting for transfers between devices: 10.7 us -> 23.3 us
  starting transfers between devices: 23.7 us -> 32.9 us
    all_to_all x1 -> x0, blocking collectives: 22.2 us -> none  [per_device(): lax.all_to_all(jnp.concatenate([half.reshape(16, PART, C), outgoing.resha...]
    ppermute x0 -> x6, waiting for transfers between devices: none -> 12.5 us  [flip_by_core(): return lax.ppermute(v, every, pairs)]
    ppermute x0 -> x6, starting transfers between devices: none -> 8.18 us  [flip_by_core(): return lax.ppermute(v, every, pairs)]
    all_to_all x1, blocking collectives: 16 us -> 14.8 us  [per_device(): lax.all_to_all(jnp.broadcast_to(part[None], (16, PART, C)), GY, 0, 0, til...]
    ppermute x2, starting transfers between devices: 4.15 us -> 5.16 us  [swap_cores(): return lax.ppermute(v, 'c', [(0, 1), (1, 0)])]
    pallas_call x7 -> x10, Pallas kernels: 16.1 us -> 16.6 us  [call(): pl.pallas_call(kernel, out_shape=tuple((jax.ShapeDtypeStruct(shape, dtype...]
  transfers between devices with their start and end apart: 10 -> 16, of which waited for: 6 -> 11; matrix products, arithmetic and copies ran while one was open for 1% -> 1% of each run, Pallas kernels for 4% -> 5%
where the time goes in v8:
time: 93.1 us; the launch traced here: 92.7 us
  starting transfers between devices  32.9 us (35%)
  waiting for transfers between devices  23.3 us (25%)
  Pallas kernels  16.6 us (18%)
  blocking collectives  14.8 us (16%)
  local copies, waits for them, and re-layouts  4.08 us (4%)
  between operations  0.97 us (1%)
    pallas_call x10, Pallas kernels, call(): pl.pallas_call(kernel, out_shape=tuple((jax.ShapeDtypeStruct(shape, dtype...  16.6 us
    all_to_all x1, blocking collectives, per_device(): lax.all_to_all(jnp.broadcast_to(part[None], (16, PART, C)), GY, 0, 0, til...  14.8 us
    ppermute x6, waiting for transfers between devices, flip_by_core(): return lax.ppermute(v, every, pairs)  12.5 us
    all_to_all x1, starting transfers between devices, per_device(): rows = lax.all_to_all(rows, GY, 0, 0, tiled=True)  8.44 us
    ppermute x6, starting transfers between devices, flip_by_core(): return lax.ppermute(v, every, pairs)  8.18 us
    ppermute x4, starting transfers between devices, swap(): return lax.ppermute(v, axes, pairs + [(j, i) for i, j in pairs])  7.81 us
    ppermute x2, starting transfers between devices, swap_cores(): return lax.ppermute(v, 'c', [(0, 1), (1, 0)])  5.16 us
    ppermute x3, waiting for transfers between devices, flip(): lax.ppermute(v, axis, [(i, i ^ bits) for i in range(lax.axis_size(axis))])  3.73 us
  transfers between devices with their start and end apart: 16, of which 11 were waited for; matrix products, arithmetic and copies ran while one was open for 1% of the time, Pallas kernels for 5%

profile of v8, /device:TPU:1, one launch (start us, length us, event | category | flops | bytes accessed | tf_op | source)
XLA Modules:
  0.0 92.7 jit_solution(17133382038455659650)
XLA Ops:
  0.6 2.2 %shard_map.111 = (bf16[128,1024]{1,0:T(8,128)(2,1)}, bf16[1104,128]{1,0:T(8,128)(2,1)}, bf16[224,128]{1,0:T(8,128)(2,1)}, bf16[224,128]{1,0:T(8,128)(2,1)}) custom-call(bf16[1,1,32,1024]{3,2,1,0:T(8,128)(2,1)} %grad_hbm.1, bf16[4,16,1536]{2,1,0:T(8,128)(2,1)} %feat_hbm.1, s32[1,4,4]{2,1,0:T(4,128)} %blocks_hbm.1, s32[1,16]{1,0:T(1,128)} %bitcast.22), custom_call_target="tpu_custom_call" | custom-call | flops 10000000 | bytes 1000000 | tf_op jit(solution)/shard_map/pallas_call | solution.py:228
  2.8 8.4 %all-to-all-start = ((bf16[16,8,1024]{2,1,0:T(8,128)(2,1)}), bf16[16,8,1024]{2,1,0:T(8,128)(2,1)S(1)}, u32[]{:S(2)}, u32[]{:S(2)}) async-start(bf16[16,8,1024]{2,1,0:T(8,128)(2,1)} %bitcast.21), calls=%async_computation | async-start | bytes 524288 | tf_op jit(solution)/shard_map/all_to_all | solution.py:520
  11.3 1.4 %collective-permute-start = (bf16[224,128]{1,0:T(8,128)(2,1)}, bf16[224,128]{1,0:T(8,128)(2,1)S(1)}, u32[]{:S(2)}, u32[]{:S(2)}) collective-permute-start(bf16[224,128]{1,0:T(8,128)(2,1)} %get-tuple-element.40), channel_id=1, source_target_pairs={{0,1},{2,3},{4,5},{6,7},{8,9},{10,11},{12,13},{14,15},{1,0},{3,2},... | collective-permute-start | bytes 172040 | tf_op jit(solution)/shard_map/ppermute | solution.py:467
  12.6 0.7 collective-permute-start.1
  13.3 0.0 copy-start
  13.3 0.9 %copy-done = bf16[1104,128]{1,0:T(8,128)(2,1)S(1)} copy-done((bf16[1104,128]{1,0:T(8,128)(2,1)S(1)}, bf16[1104,128]{1,0:T(8,128)(2,1)}, u32[]{:S(2)}) %copy-start) | copy-done | bytes 282648
  14.3 0.0 copy-start.2
  14.3 1.2 %copy-done.2 = bf16[27,128,128]{2,1,0:T(8,128)(2,1)S(1)} copy-done((bf16[27,128,128]{2,1,0:T(8,128)(2,1)S(1)}, bf16[27,128,128]{2,1,0:T(8,128)(2,1)}, u32[]{:S(2)}) %copy-start.2) | copy-done | bytes 884760
  15.4 0.0 copy-start.3
  15.4 1.1 %copy-done.3 = bf16[27,96,128]{2,1,0:T(8,128)(2,1)S(1)} copy-done((bf16[27,96,128]{2,1,0:T(8,128)(2,1)S(1)}, bf16[27,96,128]{2,1,0:T(8,128)(2,1)}, u32[]{:S(2)}) %copy-start.3) | copy-done | bytes 663576
  16.5 0.0 copy-start.1
  16.5 0.4 shard_map.112
  16.9 0.0 collective-permute-done.beside_ref
  16.9 0.0 collective-permute-done.1.beyond_ref
  16.9 2.0 %all-to-all-done = bf16[16,8,1024]{2,1,0:T(8,128)(2,1)S(1)} async-done(((bf16[16,8,1024]{2,1,0:T(8,128)(2,1)}), bf16[16,8,1024]{2,1,0:T(8,128)(2,1)S(1)}, u32[]{:S(2)}, u32[]{:S(2)}) %all-to-all-start) | async-done | bytes 262176 | tf_op jit(solution)/shard_map/all_to_all | solution.py:520
  18.9 0.0 copy-done.1
  18.9 0.3 shard_map.113
  19.2 2.7 %collective-permute-start.2 = (bf16[1200,128]{1,0:T(8,128)(2,1)S(1)}, bf16[1200,128]{1,0:T(8,128)(2,1)S(1)}, u32[]{:S(2)}, u32[]{:S(2)}) collective-permute-start(bf16[1200,128]{1,0:T(8,128)(2,1)S(1)} %get-tuple-element.44), channel_id=1, source_target_pairs={{0,16},{32,48},{64,80},{96,112},{16,0},{48,32},{80,64},{112,96},{1... | collective-permute-start | bytes 921608 | tf_op jit(solution)/shard_map/ppermute | solution.py:467
  21.9 3.1 %collective-permute-start.3 = (bf16[1200,128]{1,0:T(8,128)(2,1)S(1)}, bf16[1200,128]{1,0:T(8,128)(2,1)S(1)}, u32[]{:S(2)}, u32[]{:S(2)}) collective-permute-start(bf16[1200,128]{1,0:T(8,128)(2,1)S(1)} %get-tuple-element.46), channel_id=1, source_target_pairs={{16,32},{48,64},{80,96},{32,16},{64,48},{96,80},{17,33},{49,65},{8... | collective-permute-start | bytes 921608 | tf_op jit(solution)/shard_map/ppermute | solution.py:467
  25.0 0.0 copy-start.4
  25.0 0.0 copy-start.5
  25.0 2.5 %shard_map.114 = (f32[4,320,128]{2,1,0:T(8,128)S(1)}, bf16[640,128]{1,0:T(8,128)(2,1)S(1)}, f32[512,128]{1,0:T(8,128)S(1)}, f32[4,288,128]{2,1,0:T(8,128)S(1)}) custom-call(bf16[1408,128]{1,0:T(8,128)(2,1)S(1)} %get-tuple-element.45.mid_ref, bf16[16,128]{1,0:T(8,128)(2,1)S(1)} %get-tuple-element.47.mask_ref, ...), custom_call_target="tpu_custom_call" | custom-call | flops 3000000000 | bytes 1000000 | tf_op jit(solution)/shard_map/pallas_call | solution.py:228
  27.6 0.0 collective-permute-done.2.near_ref
  27.6 2.5 %collective-permute-done.3.far_ref = bf16[1200,128]{1,0:T(8,128)(2,1)S(1)} collective-permute-done((bf16[1200,128]{1,0:T(8,128)(2,1)S(1)}, bf16[1200,128]{1,0:T(8,128)(2,1)S(1)}, u32[]{:S(2)}, u32[]{:S(2)}) %collective-permute-start.3) | collective-permute-done | bytes 307232 | tf_op jit(solution)/shard_map/ppermute | solution.py:467
  30.0 0.0 copy-done.4
  30.1 0.0 copy-done.5
  30.1 8.3 %shard_map.115 = (bf16[2,3584,128]{2,1,0:T(8,128)(2,1)S(1)}, bf16[256,128]{1,0:T(8,128)(2,1)S(1)}) custom-call(bf16[1200,128]{1,0:T(8,128)(2,1)S(1)} %collective-permute-done.2.near_ref, bf16[1408,128]{1,0:T(8,128)(2,1)S(1)} %get-tuple-element.45.mid_ref, bf16[1200,128]{1,0:T(8,128)(2,1)S(1)} %collective-permute-done.3.far_ref, ...), custom_call_target="tpu_custom_call" | custom-call | flops 8000000000 | bytes 1000000 | tf_op jit(solution)/shard_map/pallas_call | solution.py:228
  38.4 0.1 slice_bitcast_fusion
  38.4 0.1 collective-permute-start.4
  38.5 2.5 %collective-permute-done.4.theirs_ref = bf16[3584,128]{1,0:T(8,128)(2,1)S(1)} collective-permute-done((bf16[3584,128]{1,0:T(8,128)(2,1)S(1)}, bf16[3584,128]{1,0:T(8,128)(2,1)S(1)}, u32[]{:S(2)}, u32[]{:S(2)}) %collective-permute-start.4) | collective-permute-done | bytes 917536 | tf_op jit(solution)/shard_map/ppermute | solution.py:471
  41.0 0.2 shard_map.116
  41.2 1.3 %collective-permute-start.5 = (bf16[960,128]{1,0:T(8,128)(2,1)S(1)}, bf16[960,128]{1,0:T(8,128)(2,1)S(1)}, u32[]{:S(2)}, u32[]{:S(2)}) collective-permute-start(bf16[960,128]{1,0:T(8,128)(2,1)S(1)} %get-tuple-element.59), channel_id=1, source_target_pairs={{0,4},{1,5},{2,6},{3,7},{4,0},{5,1},{6,2},{7,3},{8,12},{9,13},{10,... | collective-permute-start | bytes 737288 | tf_op jit(solution)/shard_map/ppermute | solution.py:494
  42.5 2.9 %collective-permute-start.6 = (bf16[960,128]{1,0:T(8,128)(2,1)S(1)}, bf16[960,128]{1,0:T(8,128)(2,1)S(1)}, u32[]{:S(2)}, u32[]{:S(2)}) collective-permute-start(bf16[960,128]{1,0:T(8,128)(2,1)S(1)} %get-tuple-element.60), channel_id=1, source_target_pairs={{0,8},{1,9},{2,10},{3,11},{4,12},{5,13},{6,14},{7,15},{8,0},{9,1},... | collective-permute-start | bytes 737288 | tf_op jit(solution)/shard_map/ppermute | solution.py:494
  45.4 0.0 collective-permute-start.7
  45.4 1.4 %collective-permute-done.5.refs_1_ = bf16[960,128]{1,0:T(8,128)(2,1)S(1)} collective-permute-done((bf16[960,128]{1,0:T(8,128)(2,1)S(1)}, bf16[960,128]{1,0:T(8,128)(2,1)S(1)}, u32[]{:S(2)}, u32[]{:S(2)}) %collective-permute-start.5) | collective-permute-done | bytes 245792 | tf_op jit(solution)/shard_map/ppermute | solution.py:494
  46.8 5.2 %collective-permute-done.6.refs_2_ = bf16[960,128]{1,0:T(8,128)(2,1)S(1)} collective-permute-done((bf16[960,128]{1,0:T(8,128)(2,1)S(1)}, bf16[960,128]{1,0:T(8,128)(2,1)S(1)}, u32[]{:S(2)}, u32[]{:S(2)}) %collective-permute-start.6) | collective-permute-done | bytes 245792 | tf_op jit(solution)/shard_map/ppermute | solution.py:494
  52.0 2.6 %collective-permute-done.7.refs_3_ = bf16[960,128]{1,0:T(8,128)(2,1)S(1)} collective-permute-done((bf16[960,128]{1,0:T(8,128)(2,1)S(1)}, bf16[960,128]{1,0:T(8,128)(2,1)S(1)}, u32[]{:S(2)}, u32[]{:S(2)}) %collective-permute-start.7) | collective-permute-done | bytes 245792 | tf_op jit(solution)/shard_map/ppermute | solution.py:494
  54.6 0.1 shard_map.117
  54.7 1.0 %collective-permute-start.8 = (bf16[288,128]{1,0:T(8,128)(2,1)S(1)}, bf16[288,128]{1,0:T(8,128)(2,1)S(1)}, u32[]{:S(2)}, u32[]{:S(2)}) collective-permute-start(bf16[288,128]{1,0:T(8,128)(2,1)S(1)} %get-tuple-element.63), channel_id=1, source_target_pairs={{0,1},{1,0},{2,3},{3,2},{4,5},{5,4},{6,7},{7,6},{8,9},{9,8},{10,11... | collective-permute-start | bytes 221192 | tf_op jit(solution)/shard_map/ppermute | solution.py:494
  55.7 1.6 %collective-permute-start.9 = (bf16[288,128]{1,0:T(8,128)(2,1)S(1)}, bf16[288,128]{1,0:T(8,128)(2,1)S(1)}, u32[]{:S(2)}, u32[]{:S(2)}) collective-permute-start(bf16[288,128]{1,0:T(8,128)(2,1)S(1)} %get-tuple-element.64), channel_id=1, source_target_pairs={{0,2},{1,3},{2,0},{3,1},{4,6},{5,7},{6,4},{7,5},{8,10},{9,11},{10,... | collective-permute-start | bytes 221192 | tf_op jit(solution)/shard_map/ppermute | solution.py:494
  57.3 1.4 %collective-permute-start.10 = (bf16[288,128]{1,0:T(8,128)(2,1)S(1)}, bf16[288,128]{1,0:T(8,128)(2,1)S(1)}, u32[]{:S(2)}, u32[]{:S(2)}) collective-permute-start(bf16[288,128]{1,0:T(8,128)(2,1)S(1)} %get-tuple-element.65), channel_id=1, source_target_pairs={{0,3},{1,2},{2,1},{3,0},{4,7},{5,6},{6,5},{7,4},{8,11},{9,10},{10,... | collective-permute-start | bytes 221192 | tf_op jit(solution)/shard_map/ppermute | solution.py:494
  58.6 0.0 collective-permute-done.8.refs_1_
  58.6 1.7 %collective-permute-done.9.refs_2_ = bf16[288,128]{1,0:T(8,128)(2,1)S(1)} collective-permute-done((bf16[288,128]{1,0:T(8,128)(2,1)S(1)}, bf16[288,128]{1,0:T(8,128)(2,1)S(1)}, u32[]{:S(2)}, u32[]{:S(2)}) %collective-permute-start.9) | collective-permute-done | bytes 73760 | tf_op jit(solution)/shard_map/ppermute | solution.py:494
  60.4 1.6 %collective-permute-done.10.refs_3_ = bf16[288,128]{1,0:T(8,128)(2,1)S(1)} collective-permute-done((bf16[288,128]{1,0:T(8,128)(2,1)S(1)}, bf16[288,128]{1,0:T(8,128)(2,1)S(1)}, u32[]{:S(2)}, u32[]{:S(2)}) %collective-permute-start.10) | collective-permute-done | bytes 73760 | tf_op jit(solution)/shard_map/ppermute | solution.py:494
  62.0 2.5 %collective-permute-start.13 = (bf16[224,128]{1,0:T(8,128)(2,1)S(1)}, bf16[224,128]{1,0:T(8,128)(2,1)S(1)}, u32[]{:S(2)}, u32[]{:S(2)}) collective-permute-start(bf16[224,128]{1,0:T(8,128)(2,1)S(1)} %get-tuple-element.67), channel_id=1, source_target_pairs={{0,96},{32,64},{64,32},{96,0},{1,97},{33,65},{65,33},{97,1},{2,98}... | collective-permute-start | bytes 172040 | tf_op jit(solution)/shard_map/ppermute | solution.py:483
  64.5 0.7 collective-permute-start.12
  65.2 0.2 collective-permute-start.11
  65.4 1.0 %collective-permute-done.13 = bf16[224,128]{1,0:T(8,128)(2,1)S(1)} collective-permute-done((bf16[224,128]{1,0:T(8,128)(2,1)S(1)}, bf16[224,128]{1,0:T(8,128)(2,1)S(1)}, u32[]{:S(2)}, u32[]{:S(2)}) %collective-permute-start.13) | collective-permute-done | bytes 57376 | tf_op jit(solution)/shard_map/ppermute | solution.py:483
  66.4 2.7 %collective-permute-done.12 = bf16[224,128]{1,0:T(8,128)(2,1)S(1)} collective-permute-done((bf16[224,128]{1,0:T(8,128)(2,1)S(1)}, bf16[224,128]{1,0:T(8,128)(2,1)S(1)}, u32[]{:S(2)}, u32[]{:S(2)}) %collective-permute-start.12) | collective-permute-done | bytes 57376 | tf_op jit(solution)/shard_map/ppermute | solution.py:483
  69.1 0.0 collective-permute-done.11
  69.1 0.1 broadcast_in_dim.2
  69.3 14.8 %all_to_all.16 = bf16[16,224,128]{2,1,0:T(8,128)(2,1)S(1)} all-to-all(bf16[16,224,128]{2,1,0:T(8,128)(2,1)S(1)} %broadcast_in_dim.2), channel_id=1, replica_groups=mesh['y'=4,'c'=2,'z'=4,'x'=4] {'z','x'}, dimensions={0} | all-to-all | bytes 1835008 | tf_op jit(solution)/shard_map/all_to_all | solution.py:564
  84.0 5.1 %collective-permute-start.14 = (bf16[3584,128]{1,0:T(8,128)(2,1)S(1)}, bf16[3584,128]{1,0:T(8,128)(2,1)S(1)}, u32[]{:S(2)}, u32[]{:S(2)}) collective-permute-start(bf16[3584,128]{1,0:T(8,128)(2,1)S(1)} %bitcast.14), channel_id=1, source_target_pairs={{0,16},{16,0},{1,17},{17,1},{2,18},{18,2},{3,19},{19,3},{4,20},{20... | collective-permute-start | bytes 2752520 | tf_op jit(solution)/shard_map/ppermute | solution.py:471
  89.1 0.7 reshape.34
  89.8 1.3 %shard_map.119 = (f32[2592,128]{1,0:T(8,128)}, f32[3456,128]{1,0:T(8,128)}, f32[1024,128]{1,0:T(8,128)}) custom-call(bf16[3584,128]{1,0:T(8,128)(2,1)S(1)} %bitcast.15), custom_call_target="tpu_custom_call" | custom-call | flops 10000000 | bytes 1000000 | tf_op jit(solution)/shard_map/pallas_call | solution.py:228
  91.1 0.1 collective-permute-done.14.half_ref
  91.2 1.3 %shard_map.120 = (f32[2592,128]{1,0:T(8,128)}, f32[3456,128]{1,0:T(8,128)}, f32[1024,128]{1,0:T(8,128)}) custom-call(bf16[3584,128]{1,0:T(8,128)(2,1)S(1)} %collective-permute-done.14.half_ref, f32[2592,128]{1,0:T(8,128)} %get-tuple-element.68.a, f32[3456,128]{1,0:T(8,128)} %get-tuple-element.69.b, ...), custom_call_target="tpu_custom_call", output_to_operand_aliasing={{0}: (1, {}), {1}: (2, {}), {2}: (3, {})} | custom-call | flops 10000000 | bytes 1000000 | tf_op jit(solution)/shard_map/pallas_call | solution.py:228
  (3 shorter events, 0.1 us)
Async XLA Ops:
  2.8 16.1 %all-to-all-start = ((bf16[16,8,1024]{2,1,0:T(8,128)(2,1)}), bf16[16,8,1024]{2,1,0:T(8,128)(2,1)S(1)}, u32[]{:S(2)}, u32[]{:S(2)}) async-start(bf16[16,8,1024]{2,1,0:T(8,128)(2,1)} %bitcast.21), calls=%async_computation | async-start | bytes 524288 | tf_op jit(solution)/shard_map/all_to_all | solution.py:520
  11.3 5.6 %collective-permute-start = (bf16[224,128]{1,0:T(8,128)(2,1)}, bf16[224,128]{1,0:T(8,128)(2,1)S(1)}, u32[]{:S(2)}, u32[]{:S(2)}) collective-permute-start(bf16[224,128]{1,0:T(8,128)(2,1)} %get-tuple-element.40), channel_id=1, source_target_pairs={{0,1},{2,3},{4,5},{6,7},{8,9},{10,11},{12,13},{14,15},{1,0},{3,2},... | collective-permute-start | bytes 172040 | tf_op jit(solution)/shard_map/ppermute | solution.py:467
  12.6 4.3 %collective-permute-start.1 = (bf16[224,128]{1,0:T(8,128)(2,1)}, bf16[224,128]{1,0:T(8,128)(2,1)S(1)}, u32[]{:S(2)}, u32[]{:S(2)}) collective-permute-start(bf16[224,128]{1,0:T(8,128)(2,1)} %get-tuple-element.41), channel_id=1, source_target_pairs={{1,2},{3,4},{5,6},{7,8},{9,10},{11,12},{13,14},{2,1},{4,3},{6,5},{... | collective-permute-start | bytes 172040 | tf_op jit(solution)/shard_map/ppermute | solution.py:467
  13.3 1.0 %copy-start = (bf16[1104,128]{1,0:T(8,128)(2,1)S(1)}, bf16[1104,128]{1,0:T(8,128)(2,1)}, u32[]{:S(2)}) copy-start(bf16[1104,128]{1,0:T(8,128)(2,1)} %get-tuple-element.39.after_ref.own_ref) | copy-start | bytes 847876
  14.3 1.2 %copy-start.2 = (bf16[27,128,128]{2,1,0:T(8,128)(2,1)S(1)}, bf16[27,128,128]{2,1,0:T(8,128)(2,1)}, u32[]{:S(2)}) copy-start(bf16[27,128,128]{2,1,0:T(8,128)(2,1)} %w2_ref.1) | copy-start | bytes 2654212
  15.4 1.1 %copy-start.3 = (bf16[27,96,128]{2,1,0:T(8,128)(2,1)S(1)}, bf16[27,96,128]{2,1,0:T(8,128)(2,1)}, u32[]{:S(2)}) copy-start(bf16[27,96,128]{2,1,0:T(8,128)(2,1)} %w1_ref.1) | copy-start | bytes 1990660
  16.5 2.4 %copy-start.1 = (bf16[1104,128]{1,0:T(8,128)(2,1)S(1)}, bf16[1104,128]{1,0:T(8,128)(2,1)}, u32[]{:S(2)}) copy-start(bf16[1104,128]{1,0:T(8,128)(2,1)} %get-tuple-element.39.after_ref.own_ref) | copy-start | bytes 847876
  19.2 8.4 %collective-permute-start.2 = (bf16[1200,128]{1,0:T(8,128)(2,1)S(1)}, bf16[1200,128]{1,0:T(8,128)(2,1)S(1)}, u32[]{:S(2)}, u32[]{:S(2)}) collective-permute-start(bf16[1200,128]{1,0:T(8,128)(2,1)S(1)} %get-tuple-element.44), channel_id=1, source_target_pairs={{0,16},{32,48},{64,80},{96,112},{16,0},{48,32},{80,64},{112,96},{1... | collective-permute-start | bytes 921608 | tf_op jit(solution)/shard_map/ppermute | solution.py:467
  21.9 8.2 %collective-permute-start.3 = (bf16[1200,128]{1,0:T(8,128)(2,1)S(1)}, bf16[1200,128]{1,0:T(8,128)(2,1)S(1)}, u32[]{:S(2)}, u32[]{:S(2)}) collective-permute-start(bf16[1200,128]{1,0:T(8,128)(2,1)S(1)} %get-tuple-element.46), channel_id=1, source_target_pairs={{16,32},{48,64},{80,96},{32,16},{64,48},{96,80},{17,33},{49,65},{8... | collective-permute-start | bytes 921608 | tf_op jit(solution)/shard_map/ppermute | solution.py:467
  25.0 5.1 %copy-start.4 = (bf16[8,128,128]{2,1,0:T(8,128)(2,1)S(1)}, bf16[8,128,128]{2,1,0:T(8,128)(2,1)}, u32[]{:S(2)}) copy-start(bf16[8,128,128]{2,1,0:T(8,128)(2,1)} %wd_ref.1) | copy-start | bytes 786436
  25.0 5.0 %copy-start.5 = (bf16[96,64]{1,0:T(8,128)(2,1)S(1)}, bf16[96,64]{1,0:T(8,128)(2,1)}, u32[]{:S(2)}) copy-start(bf16[96,64]{1,0:T(8,128)(2,1)} %constant.2.clone.up_ref) | copy-start | bytes 36868
  38.4 2.6 %collective-permute-start.4 = (bf16[3584,128]{1,0:T(8,128)(2,1)S(1)}, bf16[3584,128]{1,0:T(8,128)(2,1)S(1)}, u32[]{:S(2)}, u32[]{:S(2)}) collective-permute-start(bf16[3584,128]{1,0:T(8,128)(2,1)S(1)} %slice_bitcast_fusion), channel_id=1, source_target_pairs={{0,16},{16,0},{1,17},{17,1},{2,18},{18,2},{3,19},{19,3},{4,20},{20... | collective-permute-start | bytes 2752520 | tf_op jit(solution)/shard_map/ppermute | solution.py:471
  41.2 5.6 %collective-permute-start.5 = (bf16[960,128]{1,0:T(8,128)(2,1)S(1)}, bf16[960,128]{1,0:T(8,128)(2,1)S(1)}, u32[]{:S(2)}, u32[]{:S(2)}) collective-permute-start(bf16[960,128]{1,0:T(8,128)(2,1)S(1)} %get-tuple-element.59), channel_id=1, source_target_pairs={{0,4},{1,5},{2,6},{3,7},{4,0},{5,1},{6,2},{7,3},{8,12},{9,13},{10,... | collective-permute-start | bytes 737288 | tf_op jit(solution)/shard_map/ppermute | solution.py:494
  42.5 9.5 %collective-permute-start.6 = (bf16[960,128]{1,0:T(8,128)(2,1)S(1)}, bf16[960,128]{1,0:T(8,128)(2,1)S(1)}, u32[]{:S(2)}, u32[]{:S(2)}) collective-permute-start(bf16[960,128]{1,0:T(8,128)(2,1)S(1)} %get-tuple-element.60), channel_id=1, source_target_pairs={{0,8},{1,9},{2,10},{3,11},{4,12},{5,13},{6,14},{7,15},{8,0},{9,1},... | collective-permute-start | bytes 737288 | tf_op jit(solution)/shard_map/ppermute | solution.py:494
  45.4 9.1 %collective-permute-start.7 = (bf16[960,128]{1,0:T(8,128)(2,1)S(1)}, bf16[960,128]{1,0:T(8,128)(2,1)S(1)}, u32[]{:S(2)}, u32[]{:S(2)}) collective-permute-start(bf16[960,128]{1,0:T(8,128)(2,1)S(1)} %get-tuple-element.61), channel_id=1, source_target_pairs={{0,12},{1,13},{2,14},{3,15},{4,8},{5,9},{6,10},{7,11},{8,4},{9,5},... | collective-permute-start | bytes 737288 | tf_op jit(solution)/shard_map/ppermute | solution.py:494
  54.7 3.9 %collective-permute-start.8 = (bf16[288,128]{1,0:T(8,128)(2,1)S(1)}, bf16[288,128]{1,0:T(8,128)(2,1)S(1)}, u32[]{:S(2)}, u32[]{:S(2)}) collective-permute-start(bf16[288,128]{1,0:T(8,128)(2,1)S(1)} %get-tuple-element.63), channel_id=1, source_target_pairs={{0,1},{1,0},{2,3},{3,2},{4,5},{5,4},{6,7},{7,6},{8,9},{9,8},{10,11... | collective-permute-start | bytes 221192 | tf_op jit(solution)/shard_map/ppermute | solution.py:494
  55.7 4.7 %collective-permute-start.9 = (bf16[288,128]{1,0:T(8,128)(2,1)S(1)}, bf16[288,128]{1,0:T(8,128)(2,1)S(1)}, u32[]{:S(2)}, u32[]{:S(2)}) collective-permute-start(bf16[288,128]{1,0:T(8,128)(2,1)S(1)} %get-tuple-element.64), channel_id=1, source_target_pairs={{0,2},{1,3},{2,0},{3,1},{4,6},{5,7},{6,4},{7,5},{8,10},{9,11},{10,... | collective-permute-start | bytes 221192 | tf_op jit(solution)/shard_map/ppermute | solution.py:494
  57.3 4.7 %collective-permute-start.10 = (bf16[288,128]{1,0:T(8,128)(2,1)S(1)}, bf16[288,128]{1,0:T(8,128)(2,1)S(1)}, u32[]{:S(2)}, u32[]{:S(2)}) collective-permute-start(bf16[288,128]{1,0:T(8,128)(2,1)S(1)} %get-tuple-element.65), channel_id=1, source_target_pairs={{0,3},{1,2},{2,1},{3,0},{4,7},{5,6},{6,5},{7,4},{8,11},{9,10},{10,... | collective-permute-start | bytes 221192 | tf_op jit(solution)/shard_map/ppermute | solution.py:494
  62.0 4.3 %collective-permute-start.13 = (bf16[224,128]{1,0:T(8,128)(2,1)S(1)}, bf16[224,128]{1,0:T(8,128)(2,1)S(1)}, u32[]{:S(2)}, u32[]{:S(2)}) collective-permute-start(bf16[224,128]{1,0:T(8,128)(2,1)S(1)} %get-tuple-element.67), channel_id=1, source_target_pairs={{0,96},{32,64},{64,32},{96,0},{1,97},{33,65},{65,33},{97,1},{2,98}... | collective-permute-start | bytes 172040 | tf_op jit(solution)/shard_map/ppermute | solution.py:483
  64.5 4.6 %collective-permute-start.12 = (bf16[224,128]{1,0:T(8,128)(2,1)S(1)}, bf16[224,128]{1,0:T(8,128)(2,1)S(1)}, u32[]{:S(2)}, u32[]{:S(2)}) collective-permute-start(bf16[224,128]{1,0:T(8,128)(2,1)S(1)} %get-tuple-element.67), channel_id=1, source_target_pairs={{0,64},{32,96},{64,0},{96,32},{1,65},{33,97},{65,1},{97,33},{2,66}... | collective-permute-start | bytes 172040 | tf_op jit(solution)/shard_map/ppermute | solution.py:483
  65.2 3.9 %collective-permute-start.11 = (bf16[224,128]{1,0:T(8,128)(2,1)S(1)}, bf16[224,128]{1,0:T(8,128)(2,1)S(1)}, u32[]{:S(2)}, u32[]{:S(2)}) collective-permute-start(bf16[224,128]{1,0:T(8,128)(2,1)S(1)} %get-tuple-element.67), channel_id=1, source_target_pairs={{0,32},{32,0},{64,96},{96,64},{1,33},{33,1},{65,97},{97,65},{2,34}... | collective-permute-start | bytes 172040 | tf_op jit(solution)/shard_map/ppermute | solution.py:483
  84.0 7.2 %collective-permute-start.14 = (bf16[3584,128]{1,0:T(8,128)(2,1)S(1)}, bf16[3584,128]{1,0:T(8,128)(2,1)S(1)}, u32[]{:S(2)}, u32[]{:S(2)}) collective-permute-start(bf16[3584,128]{1,0:T(8,128)(2,1)S(1)} %bitcast.14), channel_id=1, source_target_pairs={{0,16},{16,0},{1,17},{17,1},{2,18},{18,2},{3,19},{19,3},{4,20},{20... | collective-permute-start | bytes 2752520 | tf_op jit(solution)/shard_map/ppermute | solution.py:471

commit v9 on v8

--- a/solution.py
+++ b/solution.py
@@ -403,7 +403,7 @@
 
 
 def fold_first(*refs):
-    got, outs = refs[:4], refs[4:]
+    got, outs = [refs[i] for i in (0, 1, 3, 2)], refs[4:]
     _, second, _, _ = places()
     for m, out in enumerate(outs):
         to = second ^ m
@@ -416,7 +416,7 @@
 
 
 def fold_second(*refs):
-    got, (part_ref, bricks_ref) = refs[:4], refs[4:]
+    got, (part_ref, bricks_ref) = [refs[i] for i in (0, 1, 3, 2)], refs[4:]
     first, second, a, b = places()
     v = [g[:PART, :].astype(F32) for g in got]
     part_ref[...] = ((v[0] + v[1]) + (v[2] + v[3])).astype(BF)
@@ -554,9 +554,11 @@
     blocks = call(
         fold_cores, [((4 * PART + 64, C), BF)] * 4, (grads, swap_cores(grads[1]), outgoing)
     )
-    blocks = [blocks[0]] + [flip_by_core(blocks[n], ("z", "x"), n) for n in (1, 2, 3)]
+    far = flip_by_core(blocks[2], ("z", "x"), 2)
+    blocks = [blocks[0]] + [flip_by_core(blocks[n], ("z", "x"), n) for n in (1, 3)] + [far]
     blocks = call(fold_first, [((PART + 64, C), BF)] * 4, blocks)
-    blocks = [blocks[0]] + [flip_by_core(blocks[n], ("x", "z"), n) for n in (1, 2, 3)]
+    far = flip_by_core(blocks[2], ("x", "z"), 2)
+    blocks = [blocks[0]] + [flip_by_core(blocks[n], ("x", "z"), n) for n in (1, 3)] + [far]
     part, arrived = call(fold_second, [((PART, C), BF), ((256, C), BF)], blocks)
     moved = arrived.reshape(16, 8, 2, C).transpose(0, 2, 1, 3).reshape(1, 1, 32, 8 * C)
     others = [flip(part, "y", n).astype(F32) for n in (1, 2, 3)]

time: 93.1 us -> 92 us (0.988)
  waiting for transfers between devices: 23.3 us -> 21.2 us
  starting transfers between devices: 32.9 us -> 34 us
    ppermute x6, waiting for transfers between devices: 12.5 us -> 10.5 us  [flip_by_core(): return lax.ppermute(v, every, pairs)]
    ppermute x2, starting transfers between devices: 5.16 us -> 6.63 us  [swap_cores(): return lax.ppermute(v, 'c', [(0, 1), (1, 0)])]
where the time goes in v9:
time: 92 us; the launch traced here: 91.6 us
  starting transfers between devices  34 us (37%)
  waiting for transfers between devices  21.2 us (23%)
  Pallas kernels  16.6 us (18%)
  blocking collectives  14.8 us (16%)
  local copies, waits for them, and re-layouts  4.08 us (4%)
  between operations  0.97 us (1%)
    pallas_call x10, Pallas kernels, call(): pl.pallas_call(kernel, out_shape=tuple((jax.ShapeDtypeStruct(shape, dtype...  16.6 us
    all_to_all x1, blocking collectives, per_device(): lax.all_to_all(jnp.broadcast_to(part[None], (16, PART, C)), GY, 0, 0, til...  14.8 us
    ppermute x6, waiting for transfers between devices, flip_by_core(): return lax.ppermute(v, every, pairs)  10.5 us
    all_to_all x1, starting transfers between devices, per_device(): rows = lax.all_to_all(rows, GY, 0, 0, tiled=True)  8.44 us
    ppermute x4, starting transfers between devices, swap(): return lax.ppermute(v, axes, pairs + [(j, i) for i, j in pairs])  7.81 us
    ppermute x6, starting transfers between devices, flip_by_core(): return lax.ppermute(v, every, pairs)  7.76 us
    ppermute x2, starting transfers between devices, swap_cores(): return lax.ppermute(v, 'c', [(0, 1), (1, 0)])  6.63 us
    ppermute x3, waiting for transfers between devices, flip(): lax.ppermute(v, axis, [(i, i ^ bits) for i in range(lax.axis_size(axis))])  3.67 us
  transfers between devices with their start and end apart: 16, of which 11 were waited for; matrix products, arithmetic and copies ran while one was open for 1% of the time, Pallas kernels for 5%

profile of v9, /device:TPU:1, one launch (start us, length us, event | category | flops | bytes accessed | tf_op | source)
XLA Modules:
  0.0 91.6 jit_solution(14486184833040209991)
XLA Ops:
  0.6 2.2 %shard_map.111 = (bf16[128,1024]{1,0:T(8,128)(2,1)}, bf16[1104,128]{1,0:T(8,128)(2,1)}, bf16[224,128]{1,0:T(8,128)(2,1)}, bf16[224,128]{1,0:T(8,128)(2,1)}) custom-call(bf16[1,1,32,1024]{3,2,1,0:T(8,128)(2,1)} %grad_hbm.1, bf16[4,16,1536]{2,1,0:T(8,128)(2,1)} %feat_hbm.1, s32[1,4,4]{2,1,0:T(4,128)} %blocks_hbm.1, s32[1,16]{1,0:T(1,128)} %bitcast.22), custom_call_target="tpu_custom_call" | custom-call | flops 10000000 | bytes 1000000 | tf_op jit(solution)/shard_map/pallas_call | solution.py:228
  2.8 8.4 %all-to-all-start = ((bf16[16,8,1024]{2,1,0:T(8,128)(2,1)}), bf16[16,8,1024]{2,1,0:T(8,128)(2,1)S(1)}, u32[]{:S(2)}, u32[]{:S(2)}) async-start(bf16[16,8,1024]{2,1,0:T(8,128)(2,1)} %bitcast.21), calls=%async_computation | async-start | bytes 524288 | tf_op jit(solution)/shard_map/all_to_all | solution.py:520
  11.3 1.4 %collective-permute-start = (bf16[224,128]{1,0:T(8,128)(2,1)}, bf16[224,128]{1,0:T(8,128)(2,1)S(1)}, u32[]{:S(2)}, u32[]{:S(2)}) collective-permute-start(bf16[224,128]{1,0:T(8,128)(2,1)} %get-tuple-element.40), channel_id=1, source_target_pairs={{0,1},{2,3},{4,5},{6,7},{8,9},{10,11},{12,13},{14,15},{1,0},{3,2},... | collective-permute-start | bytes 172040 | tf_op jit(solution)/shard_map/ppermute | solution.py:467
  12.6 0.7 collective-permute-start.1
  13.3 0.0 copy-start
  13.3 0.9 %copy-done = bf16[1104,128]{1,0:T(8,128)(2,1)S(1)} copy-done((bf16[1104,128]{1,0:T(8,128)(2,1)S(1)}, bf16[1104,128]{1,0:T(8,128)(2,1)}, u32[]{:S(2)}) %copy-start) | copy-done | bytes 282648
  14.3 0.0 copy-start.2
  14.3 1.2 %copy-done.2 = bf16[27,128,128]{2,1,0:T(8,128)(2,1)S(1)} copy-done((bf16[27,128,128]{2,1,0:T(8,128)(2,1)S(1)}, bf16[27,128,128]{2,1,0:T(8,128)(2,1)}, u32[]{:S(2)}) %copy-start.2) | copy-done | bytes 884760
  15.4 0.0 copy-start.3
  15.4 1.1 %copy-done.3 = bf16[27,96,128]{2,1,0:T(8,128)(2,1)S(1)} copy-done((bf16[27,96,128]{2,1,0:T(8,128)(2,1)S(1)}, bf16[27,96,128]{2,1,0:T(8,128)(2,1)}, u32[]{:S(2)}) %copy-start.3) | copy-done | bytes 663576
  16.5 0.0 copy-start.1
  16.5 0.4 shard_map.112
  16.9 0.0 collective-permute-done.beside_ref
  16.9 0.0 collective-permute-done.1.beyond_ref
  16.9 2.0 %all-to-all-done = bf16[16,8,1024]{2,1,0:T(8,128)(2,1)S(1)} async-done(((bf16[16,8,1024]{2,1,0:T(8,128)(2,1)}), bf16[16,8,1024]{2,1,0:T(8,128)(2,1)S(1)}, u32[]{:S(2)}, u32[]{:S(2)}) %all-to-all-start) | async-done | bytes 262176 | tf_op jit(solution)/shard_map/all_to_all | solution.py:520
  18.9 0.0 copy-done.1
  18.9 0.3 shard_map.113
  19.2 2.7 %collective-permute-start.2 = (bf16[1200,128]{1,0:T(8,128)(2,1)S(1)}, bf16[1200,128]{1,0:T(8,128)(2,1)S(1)}, u32[]{:S(2)}, u32[]{:S(2)}) collective-permute-start(bf16[1200,128]{1,0:T(8,128)(2,1)S(1)} %get-tuple-element.44), channel_id=1, source_target_pairs={{0,16},{32,48},{64,80},{96,112},{16,0},{48,32},{80,64},{112,96},{1... | collective-permute-start | bytes 921608 | tf_op jit(solution)/shard_map/ppermute | solution.py:467
  21.9 3.1 %collective-permute-start.3 = (bf16[1200,128]{1,0:T(8,128)(2,1)S(1)}, bf16[1200,128]{1,0:T(8,128)(2,1)S(1)}, u32[]{:S(2)}, u32[]{:S(2)}) collective-permute-start(bf16[1200,128]{1,0:T(8,128)(2,1)S(1)} %get-tuple-element.46), channel_id=1, source_target_pairs={{16,32},{48,64},{80,96},{32,16},{64,48},{96,80},{17,33},{49,65},{8... | collective-permute-start | bytes 921608 | tf_op jit(solution)/shard_map/ppermute | solution.py:467
  25.0 0.0 copy-start.4
  25.0 0.0 copy-start.5
  25.0 2.5 %shard_map.114 = (f32[4,320,128]{2,1,0:T(8,128)S(1)}, bf16[640,128]{1,0:T(8,128)(2,1)S(1)}, f32[512,128]{1,0:T(8,128)S(1)}, f32[4,288,128]{2,1,0:T(8,128)S(1)}) custom-call(bf16[1408,128]{1,0:T(8,128)(2,1)S(1)} %get-tuple-element.45.mid_ref, bf16[16,128]{1,0:T(8,128)(2,1)S(1)} %get-tuple-element.47.mask_ref, ...), custom_call_target="tpu_custom_call" | custom-call | flops 3000000000 | bytes 1000000 | tf_op jit(solution)/shard_map/pallas_call | solution.py:228
  27.6 0.0 collective-permute-done.2.near_ref
  27.6 2.5 %collective-permute-done.3.far_ref = bf16[1200,128]{1,0:T(8,128)(2,1)S(1)} collective-permute-done((bf16[1200,128]{1,0:T(8,128)(2,1)S(1)}, bf16[1200,128]{1,0:T(8,128)(2,1)S(1)}, u32[]{:S(2)}, u32[]{:S(2)}) %collective-permute-start.3) | collective-permute-done | bytes 307232 | tf_op jit(solution)/shard_map/ppermute | solution.py:467
  30.0 0.0 copy-done.4
  30.1 0.0 copy-done.5
  30.1 8.3 %shard_map.115 = (bf16[2,3584,128]{2,1,0:T(8,128)(2,1)S(1)}, bf16[256,128]{1,0:T(8,128)(2,1)S(1)}) custom-call(bf16[1200,128]{1,0:T(8,128)(2,1)S(1)} %collective-permute-done.2.near_ref, bf16[1408,128]{1,0:T(8,128)(2,1)S(1)} %get-tuple-element.45.mid_ref, bf16[1200,128]{1,0:T(8,128)(2,1)S(1)} %collective-permute-done.3.far_ref, ...), custom_call_target="tpu_custom_call" | custom-call | flops 8000000000 | bytes 1000000 | tf_op jit(solution)/shard_map/pallas_call | solution.py:228
  38.4 0.1 slice_bitcast_fusion
  38.4 0.1 collective-permute-start.4
  38.5 2.5 %collective-permute-done.4.theirs_ref = bf16[3584,128]{1,0:T(8,128)(2,1)S(1)} collective-permute-done((bf16[3584,128]{1,0:T(8,128)(2,1)S(1)}, bf16[3584,128]{1,0:T(8,128)(2,1)S(1)}, u32[]{:S(2)}, u32[]{:S(2)}) %collective-permute-start.4) | collective-permute-done | bytes 917536 | tf_op jit(solution)/shard_map/ppermute | solution.py:471
  41.0 0.2 shard_map.116
  41.2 1.3 %collective-permute-start.5 = (bf16[960,128]{1,0:T(8,128)(2,1)S(1)}, bf16[960,128]{1,0:T(8,128)(2,1)S(1)}, u32[]{:S(2)}, u32[]{:S(2)}) collective-permute-start(bf16[960,128]{1,0:T(8,128)(2,1)S(1)} %get-tuple-element.59), channel_id=1, source_target_pairs={{0,4},{1,5},{2,6},{3,7},{4,0},{5,1},{6,2},{7,3},{8,12},{9,13},{10,... | collective-permute-start | bytes 737288 | tf_op jit(solution)/shard_map/ppermute | solution.py:494
  42.5 1.8 %collective-permute-start.6 = (bf16[960,128]{1,0:T(8,128)(2,1)S(1)}, bf16[960,128]{1,0:T(8,128)(2,1)S(1)}, u32[]{:S(2)}, u32[]{:S(2)}) collective-permute-start(bf16[960,128]{1,0:T(8,128)(2,1)S(1)} %get-tuple-element.60), channel_id=1, source_target_pairs={{0,12},{1,13},{2,14},{3,15},{4,8},{5,9},{6,10},{7,11},{8,4},{9,5},... | collective-permute-start | bytes 737288 | tf_op jit(solution)/shard_map/ppermute | solution.py:494
  44.4 1.1 %collective-permute-start.7 = (bf16[960,128]{1,0:T(8,128)(2,1)S(1)}, bf16[960,128]{1,0:T(8,128)(2,1)S(1)}, u32[]{:S(2)}, u32[]{:S(2)}) collective-permute-start(bf16[960,128]{1,0:T(8,128)(2,1)S(1)} %get-tuple-element.61), channel_id=1, source_target_pairs={{0,8},{1,9},{2,10},{3,11},{4,12},{5,13},{6,14},{7,15},{8,0},{9,1},... | collective-permute-start | bytes 737288 | tf_op jit(solution)/shard_map/ppermute | solution.py:494
  45.4 1.4 %collective-permute-done.5.refs_1_ = bf16[960,128]{1,0:T(8,128)(2,1)S(1)} collective-permute-done((bf16[960,128]{1,0:T(8,128)(2,1)S(1)}, bf16[960,128]{1,0:T(8,128)(2,1)S(1)}, u32[]{:S(2)}, u32[]{:S(2)}) %collective-permute-start.5) | collective-permute-done | bytes 245792 | tf_op jit(solution)/shard_map/ppermute | solution.py:494
  46.8 3.3 %collective-permute-done.6.refs_2_ = bf16[960,128]{1,0:T(8,128)(2,1)S(1)} collective-permute-done((bf16[960,128]{1,0:T(8,128)(2,1)S(1)}, bf16[960,128]{1,0:T(8,128)(2,1)S(1)}, u32[]{:S(2)}, u32[]{:S(2)}) %collective-permute-start.6) | collective-permute-done | bytes 245792 | tf_op jit(solution)/shard_map/ppermute | solution.py:494
  50.1 1.8 %collective-permute-done.7.refs_3_ = bf16[960,128]{1,0:T(8,128)(2,1)S(1)} collective-permute-done((bf16[960,128]{1,0:T(8,128)(2,1)S(1)}, bf16[960,128]{1,0:T(8,128)(2,1)S(1)}, u32[]{:S(2)}, u32[]{:S(2)}) %collective-permute-start.7) | collective-permute-done | bytes 245792 | tf_op jit(solution)/shard_map/ppermute | solution.py:494
  52.0 0.1 shard_map.117
  52.1 1.0 %collective-permute-start.8 = (bf16[288,128]{1,0:T(8,128)(2,1)S(1)}, bf16[288,128]{1,0:T(8,128)(2,1)S(1)}, u32[]{:S(2)}, u32[]{:S(2)}) collective-permute-start(bf16[288,128]{1,0:T(8,128)(2,1)S(1)} %get-tuple-element.63), channel_id=1, source_target_pairs={{0,1},{1,0},{2,3},{3,2},{4,5},{5,4},{6,7},{7,6},{8,9},{9,8},{10,11... | collective-permute-start | bytes 221192 | tf_op jit(solution)/shard_map/ppermute | solution.py:494
  53.0 1.8 %collective-permute-start.9 = (bf16[288,128]{1,0:T(8,128)(2,1)S(1)}, bf16[288,128]{1,0:T(8,128)(2,1)S(1)}, u32[]{:S(2)}, u32[]{:S(2)}) collective-permute-start(bf16[288,128]{1,0:T(8,128)(2,1)S(1)} %get-tuple-element.64), channel_id=1, source_target_pairs={{0,3},{1,2},{2,1},{3,0},{4,7},{5,6},{6,5},{7,4},{8,11},{9,10},{10,... | collective-permute-start | bytes 221192 | tf_op jit(solution)/shard_map/ppermute | solution.py:494
  54.8 0.8 collective-permute-start.10
  55.6 0.0 collective-permute-done.8.refs_1_
  55.6 1.9 %collective-permute-done.9.refs_2_ = bf16[288,128]{1,0:T(8,128)(2,1)S(1)} collective-permute-done((bf16[288,128]{1,0:T(8,128)(2,1)S(1)}, bf16[288,128]{1,0:T(8,128)(2,1)S(1)}, u32[]{:S(2)}, u32[]{:S(2)}) %collective-permute-start.9) | collective-permute-done | bytes 73760 | tf_op jit(solution)/shard_map/ppermute | solution.py:494
  57.5 2.1 %collective-permute-done.10.refs_3_ = bf16[288,128]{1,0:T(8,128)(2,1)S(1)} collective-permute-done((bf16[288,128]{1,0:T(8,128)(2,1)S(1)}, bf16[288,128]{1,0:T(8,128)(2,1)S(1)}, u32[]{:S(2)}, u32[]{:S(2)}) %collective-permute-start.10) | collective-permute-done | bytes 73760 | tf_op jit(solution)/shard_map/ppermute | solution.py:494
  59.6 2.5 %collective-permute-start.13 = (bf16[224,128]{1,0:T(8,128)(2,1)S(1)}, bf16[224,128]{1,0:T(8,128)(2,1)S(1)}, u32[]{:S(2)}, u32[]{:S(2)}) collective-permute-start(bf16[224,128]{1,0:T(8,128)(2,1)S(1)} %get-tuple-element.67), channel_id=1, source_target_pairs={{0,96},{32,64},{64,32},{96,0},{1,97},{33,65},{65,33},{97,1},{2,98}... | collective-permute-start | bytes 172040 | tf_op jit(solution)/shard_map/ppermute | solution.py:483
  62.1 0.7 collective-permute-start.12
  62.8 0.2 collective-permute-start.11
  62.9 1.0 %collective-permute-done.13 = bf16[224,128]{1,0:T(8,128)(2,1)S(1)} collective-permute-done((bf16[224,128]{1,0:T(8,128)(2,1)S(1)}, bf16[224,128]{1,0:T(8,128)(2,1)S(1)}, u32[]{:S(2)}, u32[]{:S(2)}) %collective-permute-start.13) | collective-permute-done | bytes 57376 | tf_op jit(solution)/shard_map/ppermute | solution.py:483
  63.9 2.7 %collective-permute-done.12 = bf16[224,128]{1,0:T(8,128)(2,1)S(1)} collective-permute-done((bf16[224,128]{1,0:T(8,128)(2,1)S(1)}, bf16[224,128]{1,0:T(8,128)(2,1)S(1)}, u32[]{:S(2)}, u32[]{:S(2)}) %collective-permute-start.12) | collective-permute-done | bytes 57376 | tf_op jit(solution)/shard_map/ppermute | solution.py:483
  66.6 0.0 collective-permute-done.11
  66.6 0.1 broadcast_in_dim.2
  66.8 14.8 %all_to_all.16 = bf16[16,224,128]{2,1,0:T(8,128)(2,1)S(1)} all-to-all(bf16[16,224,128]{2,1,0:T(8,128)(2,1)S(1)} %broadcast_in_dim.2), channel_id=1, replica_groups=mesh['y'=4,'c'=2,'z'=4,'x'=4] {'z','x'}, dimensions={0} | all-to-all | bytes 1835008 | tf_op jit(solution)/shard_map/all_to_all | solution.py:566
  81.5 6.5 %collective-permute-start.14 = (bf16[3584,128]{1,0:T(8,128)(2,1)S(1)}, bf16[3584,128]{1,0:T(8,128)(2,1)S(1)}, u32[]{:S(2)}, u32[]{:S(2)}) collective-permute-start(bf16[3584,128]{1,0:T(8,128)(2,1)S(1)} %bitcast.14), channel_id=1, source_target_pairs={{0,16},{16,0},{1,17},{17,1},{2,18},{18,2},{3,19},{19,3},{4,20},{20... | collective-permute-start | bytes 2752520 | tf_op jit(solution)/shard_map/ppermute | solution.py:471
  88.1 0.7 reshape.34
  88.8 1.3 %shard_map.119 = (f32[2592,128]{1,0:T(8,128)}, f32[3456,128]{1,0:T(8,128)}, f32[1024,128]{1,0:T(8,128)}) custom-call(bf16[3584,128]{1,0:T(8,128)(2,1)S(1)} %bitcast.15), custom_call_target="tpu_custom_call" | custom-call | flops 10000000 | bytes 1000000 | tf_op jit(solution)/shard_map/pallas_call | solution.py:228
  90.0 0.1 collective-permute-done.14.half_ref
  90.2 1.3 %shard_map.120 = (f32[2592,128]{1,0:T(8,128)}, f32[3456,128]{1,0:T(8,128)}, f32[1024,128]{1,0:T(8,128)}) custom-call(bf16[3584,128]{1,0:T(8,128)(2,1)S(1)} %collective-permute-done.14.half_ref, f32[2592,128]{1,0:T(8,128)} %get-tuple-element.68.a, f32[3456,128]{1,0:T(8,128)} %get-tuple-element.69.b, ...), custom_call_target="tpu_custom_call", output_to_operand_aliasing={{0}: (1, {}), {1}: (2, {}), {2}: (3, {})} | custom-call | flops 10000000 | bytes 1000000 | tf_op jit(solution)/shard_map/pallas_call | solution.py:228
  (3 shorter events, 0.1 us)
Async XLA Ops:
  2.8 16.1 %all-to-all-start = ((bf16[16,8,1024]{2,1,0:T(8,128)(2,1)}), bf16[16,8,1024]{2,1,0:T(8,128)(2,1)S(1)}, u32[]{:S(2)}, u32[]{:S(2)}) async-start(bf16[16,8,1024]{2,1,0:T(8,128)(2,1)} %bitcast.21), calls=%async_computation | async-start | bytes 524288 | tf_op jit(solution)/shard_map/all_to_all | solution.py:520
  11.3 5.6 %collective-permute-start = (bf16[224,128]{1,0:T(8,128)(2,1)}, bf16[224,128]{1,0:T(8,128)(2,1)S(1)}, u32[]{:S(2)}, u32[]{:S(2)}) collective-permute-start(bf16[224,128]{1,0:T(8,128)(2,1)} %get-tuple-element.40), channel_id=1, source_target_pairs={{0,1},{2,3},{4,5},{6,7},{8,9},{10,11},{12,13},{14,15},{1,0},{3,2},... | collective-permute-start | bytes 172040 | tf_op jit(solution)/shard_map/ppermute | solution.py:467
  12.6 4.3 %collective-permute-start.1 = (bf16[224,128]{1,0:T(8,128)(2,1)}, bf16[224,128]{1,0:T(8,128)(2,1)S(1)}, u32[]{:S(2)}, u32[]{:S(2)}) collective-permute-start(bf16[224,128]{1,0:T(8,128)(2,1)} %get-tuple-element.41), channel_id=1, source_target_pairs={{1,2},{3,4},{5,6},{7,8},{9,10},{11,12},{13,14},{2,1},{4,3},{6,5},{... | collective-permute-start | bytes 172040 | tf_op jit(solution)/shard_map/ppermute | solution.py:467
  13.3 1.0 %copy-start = (bf16[1104,128]{1,0:T(8,128)(2,1)S(1)}, bf16[1104,128]{1,0:T(8,128)(2,1)}, u32[]{:S(2)}) copy-start(bf16[1104,128]{1,0:T(8,128)(2,1)} %get-tuple-element.39.after_ref.own_ref) | copy-start | bytes 847876
  14.3 1.2 %copy-start.2 = (bf16[27,128,128]{2,1,0:T(8,128)(2,1)S(1)}, bf16[27,128,128]{2,1,0:T(8,128)(2,1)}, u32[]{:S(2)}) copy-start(bf16[27,128,128]{2,1,0:T(8,128)(2,1)} %w2_ref.1) | copy-start | bytes 2654212
  15.4 1.1 %copy-start.3 = (bf16[27,96,128]{2,1,0:T(8,128)(2,1)S(1)}, bf16[27,96,128]{2,1,0:T(8,128)(2,1)}, u32[]{:S(2)}) copy-start(bf16[27,96,128]{2,1,0:T(8,128)(2,1)} %w1_ref.1) | copy-start | bytes 1990660
  16.5 2.4 %copy-start.1 = (bf16[1104,128]{1,0:T(8,128)(2,1)S(1)}, bf16[1104,128]{1,0:T(8,128)(2,1)}, u32[]{:S(2)}) copy-start(bf16[1104,128]{1,0:T(8,128)(2,1)} %get-tuple-element.39.after_ref.own_ref) | copy-start | bytes 847876
  19.2 8.4 %collective-permute-start.2 = (bf16[1200,128]{1,0:T(8,128)(2,1)S(1)}, bf16[1200,128]{1,0:T(8,128)(2,1)S(1)}, u32[]{:S(2)}, u32[]{:S(2)}) collective-permute-start(bf16[1200,128]{1,0:T(8,128)(2,1)S(1)} %get-tuple-element.44), channel_id=1, source_target_pairs={{0,16},{32,48},{64,80},{96,112},{16,0},{48,32},{80,64},{112,96},{1... | collective-permute-start | bytes 921608 | tf_op jit(solution)/shard_map/ppermute | solution.py:467
  21.9 8.2 %collective-permute-start.3 = (bf16[1200,128]{1,0:T(8,128)(2,1)S(1)}, bf16[1200,128]{1,0:T(8,128)(2,1)S(1)}, u32[]{:S(2)}, u32[]{:S(2)}) collective-permute-start(bf16[1200,128]{1,0:T(8,128)(2,1)S(1)} %get-tuple-element.46), channel_id=1, source_target_pairs={{16,32},{48,64},{80,96},{32,16},{64,48},{96,80},{17,33},{49,65},{8... | collective-permute-start | bytes 921608 | tf_op jit(solution)/shard_map/ppermute | solution.py:467
  25.0 5.1 %copy-start.4 = (bf16[8,128,128]{2,1,0:T(8,128)(2,1)S(1)}, bf16[8,128,128]{2,1,0:T(8,128)(2,1)}, u32[]{:S(2)}) copy-start(bf16[8,128,128]{2,1,0:T(8,128)(2,1)} %wd_ref.1) | copy-start | bytes 786436
  25.0 5.0 %copy-start.5 = (bf16[96,64]{1,0:T(8,128)(2,1)S(1)}, bf16[96,64]{1,0:T(8,128)(2,1)}, u32[]{:S(2)}) copy-start(bf16[96,64]{1,0:T(8,128)(2,1)} %constant.2.clone.up_ref) | copy-start | bytes 36868
  38.4 2.6 %collective-permute-start.4 = (bf16[3584,128]{1,0:T(8,128)(2,1)S(1)}, bf16[3584,128]{1,0:T(8,128)(2,1)S(1)}, u32[]{:S(2)}, u32[]{:S(2)}) collective-permute-start(bf16[3584,128]{1,0:T(8,128)(2,1)S(1)} %slice_bitcast_fusion), channel_id=1, source_target_pairs={{0,16},{16,0},{1,17},{17,1},{2,18},{18,2},{3,19},{19,3},{4,20},{20... | collective-permute-start | bytes 2752520 | tf_op jit(solution)/shard_map/ppermute | solution.py:471
  41.2 5.6 %collective-permute-start.5 = (bf16[960,128]{1,0:T(8,128)(2,1)S(1)}, bf16[960,128]{1,0:T(8,128)(2,1)S(1)}, u32[]{:S(2)}, u32[]{:S(2)}) collective-permute-start(bf16[960,128]{1,0:T(8,128)(2,1)S(1)} %get-tuple-element.59), channel_id=1, source_target_pairs={{0,4},{1,5},{2,6},{3,7},{4,0},{5,1},{6,2},{7,3},{8,12},{9,13},{10,... | collective-permute-start | bytes 737288 | tf_op jit(solution)/shard_map/ppermute | solution.py:494
  42.5 7.6 %collective-permute-start.6 = (bf16[960,128]{1,0:T(8,128)(2,1)S(1)}, bf16[960,128]{1,0:T(8,128)(2,1)S(1)}, u32[]{:S(2)}, u32[]{:S(2)}) collective-permute-start(bf16[960,128]{1,0:T(8,128)(2,1)S(1)} %get-tuple-element.60), channel_id=1, source_target_pairs={{0,12},{1,13},{2,14},{3,15},{4,8},{5,9},{6,10},{7,11},{8,4},{9,5},... | collective-permute-start | bytes 737288 | tf_op jit(solution)/shard_map/ppermute | solution.py:494
  44.4 7.6 %collective-permute-start.7 = (bf16[960,128]{1,0:T(8,128)(2,1)S(1)}, bf16[960,128]{1,0:T(8,128)(2,1)S(1)}, u32[]{:S(2)}, u32[]{:S(2)}) collective-permute-start(bf16[960,128]{1,0:T(8,128)(2,1)S(1)} %get-tuple-element.61), channel_id=1, source_target_pairs={{0,8},{1,9},{2,10},{3,11},{4,12},{5,13},{6,14},{7,15},{8,0},{9,1},... | collective-permute-start | bytes 737288 | tf_op jit(solution)/shard_map/ppermute | solution.py:494
  52.1 3.5 %collective-permute-start.8 = (bf16[288,128]{1,0:T(8,128)(2,1)S(1)}, bf16[288,128]{1,0:T(8,128)(2,1)S(1)}, u32[]{:S(2)}, u32[]{:S(2)}) collective-permute-start(bf16[288,128]{1,0:T(8,128)(2,1)S(1)} %get-tuple-element.63), channel_id=1, source_target_pairs={{0,1},{1,0},{2,3},{3,2},{4,5},{5,4},{6,7},{7,6},{8,9},{9,8},{10,11... | collective-permute-start | bytes 221192 | tf_op jit(solution)/shard_map/ppermute | solution.py:494
  53.0 4.4 %collective-permute-start.9 = (bf16[288,128]{1,0:T(8,128)(2,1)S(1)}, bf16[288,128]{1,0:T(8,128)(2,1)S(1)}, u32[]{:S(2)}, u32[]{:S(2)}) collective-permute-start(bf16[288,128]{1,0:T(8,128)(2,1)S(1)} %get-tuple-element.64), channel_id=1, source_target_pairs={{0,3},{1,2},{2,1},{3,0},{4,7},{5,6},{6,5},{7,4},{8,11},{9,10},{10,... | collective-permute-start | bytes 221192 | tf_op jit(solution)/shard_map/ppermute | solution.py:494
  54.8 4.7 %collective-permute-start.10 = (bf16[288,128]{1,0:T(8,128)(2,1)S(1)}, bf16[288,128]{1,0:T(8,128)(2,1)S(1)}, u32[]{:S(2)}, u32[]{:S(2)}) collective-permute-start(bf16[288,128]{1,0:T(8,128)(2,1)S(1)} %get-tuple-element.65), channel_id=1, source_target_pairs={{0,2},{1,3},{2,0},{3,1},{4,6},{5,7},{6,4},{7,5},{8,10},{9,11},{10,... | collective-permute-start | bytes 221192 | tf_op jit(solution)/shard_map/ppermute | solution.py:494
  59.6 4.3 %collective-permute-start.13 = (bf16[224,128]{1,0:T(8,128)(2,1)S(1)}, bf16[224,128]{1,0:T(8,128)(2,1)S(1)}, u32[]{:S(2)}, u32[]{:S(2)}) collective-permute-start(bf16[224,128]{1,0:T(8,128)(2,1)S(1)} %get-tuple-element.67), channel_id=1, source_target_pairs={{0,96},{32,64},{64,32},{96,0},{1,97},{33,65},{65,33},{97,1},{2,98}... | collective-permute-start | bytes 172040 | tf_op jit(solution)/shard_map/ppermute | solution.py:483
  62.1 4.5 %collective-permute-start.12 = (bf16[224,128]{1,0:T(8,128)(2,1)S(1)}, bf16[224,128]{1,0:T(8,128)(2,1)S(1)}, u32[]{:S(2)}, u32[]{:S(2)}) collective-permute-start(bf16[224,128]{1,0:T(8,128)(2,1)S(1)} %get-tuple-element.67), channel_id=1, source_target_pairs={{0,64},{32,96},{64,0},{96,32},{1,65},{33,97},{65,1},{97,33},{2,66}... | collective-permute-start | bytes 172040 | tf_op jit(solution)/shard_map/ppermute | solution.py:483
  62.8 3.8 %collective-permute-start.11 = (bf16[224,128]{1,0:T(8,128)(2,1)S(1)}, bf16[224,128]{1,0:T(8,128)(2,1)S(1)}, u32[]{:S(2)}, u32[]{:S(2)}) collective-permute-start(bf16[224,128]{1,0:T(8,128)(2,1)S(1)} %get-tuple-element.67), channel_id=1, source_target_pairs={{0,32},{32,0},{64,96},{96,64},{1,33},{33,1},{65,97},{97,65},{2,34}... | collective-permute-start | bytes 172040 | tf_op jit(solution)/shard_map/ppermute | solution.py:483
  81.5 8.6 %collective-permute-start.14 = (bf16[3584,128]{1,0:T(8,128)(2,1)S(1)}, bf16[3584,128]{1,0:T(8,128)(2,1)S(1)}, u32[]{:S(2)}, u32[]{:S(2)}) collective-permute-start(bf16[3584,128]{1,0:T(8,128)(2,1)S(1)} %bitcast.14), channel_id=1, source_target_pairs={{0,16},{16,0},{1,17},{17,1},{2,18},{18,2},{3,19},{19,3},{4,20},{20... | collective-permute-start | bytes 2752520 | tf_op jit(solution)/shard_map/ppermute | solution.py:471

commit v10 on v9

--- a/solution.py
+++ b/solution.py
@@ -70,9 +70,10 @@
 
 
 def section(
-    near_ref, mid_ref, far_ref, mask_ref, gc_ref, place_ref, part1_ref, inner_ref, slope_ref, part2_ref, w1_ref, w2_ref, back_ref, wd_ref, up_ref,
+    near_ref, mid_ref, far_ref, mask_ref, gc_ref, place_ref, part1_ref, inner_ref, inner_sg1_ref, part2_ref,
+    near_first_ref, near_sg1_ref, near_second_ref, near_slope_ref, w1_ref, w2_ref, back_ref, wd_ref, up_ref,
     grads_ref, out_ref,
-    sides, first, sg1, second, ge, g2, gs, vt,
+    sides, first, sg1, second, slopes, ge, g2, gs, vt,
 ):
     core = lax.axis_index("c")
     sides[1 - core] = near_ref[...]
@@ -119,17 +120,29 @@
         gs[at : at + Y * Z, 2 * C : 3 * C] = from_below(g).astype(BF)
 
     first[3 * 20 * Z : 5 * 20 * Z, :] = inner_ref[...]
-    sg1[Y * Z : 3 * Y * Z, :] = slope_ref[...]
-    for x in (0, 1, 2, 5, 6, 7):
-        p = taps(cells, x, 20, w1_ref, lines=[i for i in range(3) if not 3 <= x + i < 7])
-        pre = lanes(p, 1) + from_below(lanes(p, 0)) + from_above(lanes(p, 2))
-        if x in EARLY:
-            pre = pre + part1_ref[EARLY[x]]
-        act = line(x - 2, -2, 20)
-        value, slope = silu(act * pre)
-        first[x * 20 * Z : (x + 1) * 20 * Z, :] = value.astype(BF)
-        if x in (2, 5):
-            sg1[(x - 2) * Y * Z : (x - 1) * Y * Z, :] = (act * slope)[2 * Z : 18 * Z]
+    sg1[Y * Z : 3 * Y * Z, :] = inner_sg1_ref[...]
+    for ref, got, unit, at in (
+        (first, near_first_ref, 20 * Z, 5),
+        (sg1, near_sg1_ref, Y * Z, 3),
+        (second, near_second_ref, Y * Z, 2),
+        (slopes, near_slope_ref, 18 * Z, 3),
+    ):
+        at = pl.multiple_of((1 - core) * (at * unit), 16)
+        ref[pl.ds(at, got.shape[0]), :] = got[...]
+
+    def put(ref, size):
+        def store(x, v):
+            ref[x * size : (x + 1) * size, :] = v
+
+        return store
+
+    for which in range(2):
+        pl.when(core == which)(
+            functools.partial(
+                half_forward, which == 1, cells, firsts, line, w1_ref, w2_ref, part1_ref, part2_ref,
+                put(first, 20 * Z), put(sg1, Y * Z), put(second, Y * Z), put(slopes, 18 * Z),
+            )
+        )
 
     even = z_of(6 * Z) % 2 == 0
     for u in range(4):
@@ -146,14 +159,6 @@
             ge[at : at + Z, C : 2 * C] = jnp.where(even[:Z], 0.0, t).astype(BF)
 
     for x in range(6):
-        p = taps(firsts, x, 18, w2_ref, lines=[i for i in range(3) if not 3 <= x + i < 5])
-        act = line(x - 1, -1, 18)
-        pre = lanes(p, 1) + from_below(lanes(p, 0)) + from_above(lanes(p, 2))
-        if 1 <= x < 5:
-            pre = pre + part2_ref[x - 1]
-        value, slope = silu(act * pre + firsts(x + 1, 1, 18).astype(F32))
-        if 1 <= x < 5:
-            second[(x - 1) * Y * Z : x * Y * Z, :] = value[Z : 17 * Z].astype(BF)
         u, a = (x + 1) // 2, (x + 1) % 2
         back = []
         for b in range(2):
@@ -163,7 +168,7 @@
         g = jnp.concatenate(
             [back[1 - y % 2][y // 2 * Z : (y // 2 + 1) * Z] for y in range(18)], axis=0
         )
-        g = (act * g * slope).astype(BF)
+        g = (g * slopes[x * 18 * Z : (x + 1) * 18 * Z, :]).astype(BF)
         g2[x * 18 * Z : (x + 1) * 18 * Z, :] = g
         if 1 <= x < 5:
             put_z_taps(x - 1, g[Z : 17 * Z].astype(F32))
@@ -246,6 +251,68 @@
             second_ref[m * C : (m + 1) * C, k * C : (k + 1) * C] = w2_ref[3 * m + k]
             back_ref[k * C : (k + 1) * C, m * C : (m + 1) * C] = w2_ref[3 * m + k]
         first_ref[m * C + CIN : (m + 1) * C, :] = jnp.zeros((C - CIN, 3 * C), BF)
+
+
+def half_forward(
+    high, cells, firsts, act, w1_ref, w2_ref, part1_ref, part2_ref, put_first, put_sg1, put_second, put_slope
+):
+    for x in (5, 6, 7) if high else (0, 1, 2):
+        p = taps(cells, x, 20, w1_ref, lines=[i for i in range(3) if not 3 <= x + i < 7])
+        pre = lanes(p, 1) + from_below(lanes(p, 0)) + from_above(lanes(p, 2))
+        if x in EARLY:
+            pre = pre + part1_ref[EARLY[x]]
+        on = act(x - 2, -2, 20)
+        value, slope = silu(on * pre)
+        put_first(x, value.astype(BF))
+        if x in (2, 5):
+            put_sg1(x - 2, (on * slope)[2 * Z : 18 * Z])
+    for x in (3, 4, 5) if high else (0, 1, 2):
+        p = taps(firsts, x, 18, w2_ref, lines=[i for i in range(3) if not 3 <= x + i < 5])
+        on = act(x - 1, -1, 18)
+        pre = lanes(p, 1) + from_below(lanes(p, 0)) + from_above(lanes(p, 2))
+        if 1 <= x < 5:
+            pre = pre + part2_ref[x - 1]
+        value, slope = silu(on * pre + firsts(x + 1, 1, 18).astype(F32))
+        if 1 <= x < 5:
+            put_second(x - 1, value[Z : 17 * Z].astype(BF))
+        put_slope(x, on * slope)
+
+
+def near_side(
+    near_ref, mask_ref, part1_ref, inner_ref, part2_ref, w1_ref, w2_ref,
+    first_ref, sg1_ref, second_ref, slope_ref,
+):
+    def run(high):
+        base = 5 if high else 0
+        tiles = near_ref[MASK:, :], mask_ref[...]
+        masks = [[spread(t, by) for by in range(6)] for t in tiles]
+
+        def cells(x, y, n):
+            x = x - 7 if high else x
+            return near_ref[(x * 22 + y) * Z : (x * 22 + y + n) * Z, :]
+
+        def firsts(x, y, n):
+            ref, x = (inner_ref, x - 3) if x in (3, 4) else (first_ref, x - base)
+            return ref[(x * 20 + y) * Z : (x * 20 + y + n) * Z, :]
+
+        def act(x, y0, n):
+            here = masks[1 if (x + 4) // 4 == 1 else 0]
+            return jnp.concatenate([here[(y + 4) // 4] for y in range(y0, y0 + n)], axis=0)
+
+        def put(ref, size, start):
+            def store(x, v):
+                ref[(x - start) * size : (x - start + 1) * size, :] = v
+
+            return store
+
+        half_forward(
+            high, cells, firsts, act, w1_ref, w2_ref, part1_ref, part2_ref,
+            put(first_ref, 20 * Z, base), put(sg1_ref, Y * Z, 3 if high else 0),
+            put(second_ref, Y * Z, 2 if high else 0), put(slope_ref, 18 * Z, 3 if high else 0),
+        )
+
+    for core in range(2):
+        pl.when(lax.axis_index("c") == core)(functools.partial(run, core == 0))
 
 
 def begin(mid_ref, mask_ref, w1_ref, w2_ref, part1_ref, first_ref, sg1_ref, part2_ref):
@@ -534,15 +601,23 @@
         flops=3_000_000_000,
     )
 
+    part1, inner, _, part2 = ahead
+    beside = call(
+        near_side,
+        [((60 * Z, C), BF), ((Y * Z, C), F32), ((2 * Y * Z, C), BF), ((3 * 18 * Z, C), F32)],
+        (near, mask, part1, inner, part2, w1, w2),
+        flops=3_000_000_000,
+    )
     grads, outgoing = call(
         section,
         [((2, HALF, C), BF), ((256, C), BF)],
-        (near, mid, far, mask, gc, place, *ahead, w1, w2, back, weight_down, up_matrix()),
+        (near, mid, far, mask, gc, place, *ahead, *beside, w1, w2, back, weight_down, up_matrix()),
         scratch=[
             ((2, STRIP, C), BF),
             ((8 * 20 * Z, C), BF),
             ((X * Y * Z, C), F32),
             ((X * Y * Z, C), BF),
+            ((6 * 18 * Z, C), F32),
             ((40 * Z, 2 * C), BF),
             ((6 * 18 * Z, C), BF),
             ((X * Y * Z, 3 * C), BF),

time: 92 us -> 90.7 us (0.986)
  waiting for transfers between devices: 21.2 us -> 19.4 us
    ppermute x4, waiting for transfers between devices: 2.47 us -> 0.64 us  [swap(): return lax.ppermute(v, axes, pairs + [(j, i) for i, j in pairs])]
    pallas_call x10 -> x11, Pallas kernels: 16.6 us -> 17.3 us  [call(): pl.pallas_call(kernel, out_shape=tuple((jax.ShapeDtypeStruct(shape, dtype...]
  transfers between devices with their start and end apart: 16 -> 16, of which waited for: 11 -> 11; matrix products, arithmetic and copies ran while one was open for 1% -> 1% of each run, Pallas kernels for 5% -> 7%
where the time goes in v10:
time: 90.7 us; the launch traced here: 90.3 us
  starting transfers between devices  33.8 us (37%)
  waiting for transfers between devices  19.4 us (21%)
  Pallas kernels  17.3 us (19%)
  blocking collectives  14.8 us (16%)
  local copies, waits for them, and re-layouts  4.08 us (4%)
  between operations  0.98 us (1%)
    pallas_call x11, Pallas kernels, call(): pl.pallas_call(kernel, out_shape=tuple((jax.ShapeDtypeStruct(shape, dtype...  17.3 us
    all_to_all x1, blocking collectives, per_device(): lax.all_to_all(jnp.broadcast_to(part[None], (16, PART, C)), GY, 0, 0, til...  14.8 us
    ppermute x6, waiting for transfers between devices, flip_by_core(): return lax.ppermute(v, every, pairs)  10.5 us
    all_to_all x1, starting transfers between devices, per_device(): rows = lax.all_to_all(rows, GY, 0, 0, tiled=True)  8.44 us
    ppermute x4, starting transfers between devices, swap(): return lax.ppermute(v, axes, pairs + [(j, i) for i, j in pairs])  7.81 us
    ppermute x6, starting transfers between devices, flip_by_core(): return lax.ppermute(v, every, pairs)  7.59 us
    ppermute x2, starting transfers between devices, swap_cores(): return lax.ppermute(v, 'c', [(0, 1), (1, 0)])  6.63 us
    ppermute x3, waiting for transfers between devices, flip(): lax.ppermute(v, axis, [(i, i ^ bits) for i in range(lax.axis_size(axis))])  3.69 us
  transfers between devices with their start and end apart: 16, of which 11 were waited for; matrix products, arithmetic and copies ran while one was open for 1% of the time, Pallas kernels for 7%

profile of v10, /device:TPU:1, one launch (start us, length us, event | category | flops | bytes accessed | tf_op | source)
XLA Modules:
  0.0 90.3 jit_solution(13437573925378700457)
XLA Ops:
  0.6 2.2 %shard_map.111 = (bf16[128,1024]{1,0:T(8,128)(2,1)}, bf16[1104,128]{1,0:T(8,128)(2,1)}, bf16[224,128]{1,0:T(8,128)(2,1)}, bf16[224,128]{1,0:T(8,128)(2,1)}) custom-call(bf16[1,1,32,1024]{3,2,1,0:T(8,128)(2,1)} %grad_hbm.1, bf16[4,16,1536]{2,1,0:T(8,128)(2,1)} %feat_hbm.1, s32[1,4,4]{2,1,0:T(4,128)} %blocks_hbm.1, s32[1,16]{1,0:T(1,128)} %bitcast.22), custom_call_target="tpu_custom_call" | custom-call | flops 10000000 | bytes 1000000 | tf_op jit(solution)/shard_map/pallas_call | solution.py:233
  2.8 8.4 %all-to-all-start = ((bf16[16,8,1024]{2,1,0:T(8,128)(2,1)}), bf16[16,8,1024]{2,1,0:T(8,128)(2,1)S(1)}, u32[]{:S(2)}, u32[]{:S(2)}) async-start(bf16[16,8,1024]{2,1,0:T(8,128)(2,1)} %bitcast.21), calls=%async_computation | async-start | bytes 524288 | tf_op jit(solution)/shard_map/all_to_all | solution.py:587
  11.3 1.4 %collective-permute-start = (bf16[224,128]{1,0:T(8,128)(2,1)}, bf16[224,128]{1,0:T(8,128)(2,1)S(1)}, u32[]{:S(2)}, u32[]{:S(2)}) collective-permute-start(bf16[224,128]{1,0:T(8,128)(2,1)} %get-tuple-element.44), channel_id=1, source_target_pairs={{0,1},{2,3},{4,5},{6,7},{8,9},{10,11},{12,13},{14,15},{1,0},{3,2},... | collective-permute-start | bytes 172040 | tf_op jit(solution)/shard_map/ppermute | solution.py:534
  12.6 0.7 collective-permute-start.1
  13.3 0.0 copy-start
  13.3 0.9 %copy-done = bf16[1104,128]{1,0:T(8,128)(2,1)S(1)} copy-done((bf16[1104,128]{1,0:T(8,128)(2,1)S(1)}, bf16[1104,128]{1,0:T(8,128)(2,1)}, u32[]{:S(2)}) %copy-start) | copy-done | bytes 282648
  14.3 0.0 copy-start.2
  14.3 1.2 %copy-done.2 = bf16[27,128,128]{2,1,0:T(8,128)(2,1)S(1)} copy-done((bf16[27,128,128]{2,1,0:T(8,128)(2,1)S(1)}, bf16[27,128,128]{2,1,0:T(8,128)(2,1)}, u32[]{:S(2)}) %copy-start.2) | copy-done | bytes 884760
  15.4 0.0 copy-start.3
  15.4 1.1 %copy-done.3 = bf16[27,96,128]{2,1,0:T(8,128)(2,1)S(1)} copy-done((bf16[27,96,128]{2,1,0:T(8,128)(2,1)S(1)}, bf16[27,96,128]{2,1,0:T(8,128)(2,1)}, u32[]{:S(2)}) %copy-start.3) | copy-done | bytes 663576
  16.5 0.0 copy-start.1
  16.5 0.4 shard_map.112
  16.9 0.0 collective-permute-done.beside_ref
  16.9 0.0 collective-permute-done.1.beyond_ref
  16.9 2.0 %all-to-all-done = bf16[16,8,1024]{2,1,0:T(8,128)(2,1)S(1)} async-done(((bf16[16,8,1024]{2,1,0:T(8,128)(2,1)}), bf16[16,8,1024]{2,1,0:T(8,128)(2,1)S(1)}, u32[]{:S(2)}, u32[]{:S(2)}) %all-to-all-start) | async-done | bytes 262176 | tf_op jit(solution)/shard_map/all_to_all | solution.py:587
  18.9 0.0 copy-done.1
  18.9 0.3 shard_map.113
  19.2 2.7 %collective-permute-start.2 = (bf16[1200,128]{1,0:T(8,128)(2,1)S(1)}, bf16[1200,128]{1,0:T(8,128)(2,1)S(1)}, u32[]{:S(2)}, u32[]{:S(2)}) collective-permute-start(bf16[1200,128]{1,0:T(8,128)(2,1)S(1)} %get-tuple-element.48), channel_id=1, source_target_pairs={{0,16},{32,48},{64,80},{96,112},{16,0},{48,32},{80,64},{112,96},{1... | collective-permute-start | bytes 921608 | tf_op jit(solution)/shard_map/ppermute | solution.py:534
  21.9 3.1 %collective-permute-start.3 = (bf16[1200,128]{1,0:T(8,128)(2,1)S(1)}, bf16[1200,128]{1,0:T(8,128)(2,1)S(1)}, u32[]{:S(2)}, u32[]{:S(2)}) collective-permute-start(bf16[1200,128]{1,0:T(8,128)(2,1)S(1)} %get-tuple-element.50), channel_id=1, source_target_pairs={{16,32},{48,64},{80,96},{32,16},{64,48},{96,80},{17,33},{49,65},{8... | collective-permute-start | bytes 921608 | tf_op jit(solution)/shard_map/ppermute | solution.py:534
  25.0 2.5 %shard_map.114 = (f32[4,320,128]{2,1,0:T(8,128)S(1)}, bf16[640,128]{1,0:T(8,128)(2,1)S(1)}, f32[512,128]{1,0:T(8,128)S(1)}, f32[4,288,128]{2,1,0:T(8,128)S(1)}) custom-call(bf16[1408,128]{1,0:T(8,128)(2,1)S(1)} %get-tuple-element.49.mid_ref, bf16[16,128]{1,0:T(8,128)(2,1)S(1)} %get-tuple-element.51.mask_ref, ...), custom_call_target="tpu_custom_call" | custom-call | flops 3000000000 | bytes 1000000 | tf_op jit(solution)/shard_map/pallas_call | solution.py:233
  27.5 0.0 collective-permute-done.2.near_ref
  27.5 0.0 copy-start.4
  27.6 0.0 copy-start.5
  27.6 1.8 %shard_map.115 = (bf16[960,128]{1,0:T(8,128)(2,1)S(1)}, f32[256,128]{1,0:T(8,128)S(1)}, bf16[512,128]{1,0:T(8,128)(2,1)S(1)}, f32[864,128]{1,0:T(8,128)S(1)}) custom-call(bf16[1200,128]{1,0:T(8,128)(2,1)S(1)} %collective-permute-done.2.near_ref, bf16[16,128]{1,0:T(8,128)(2,1)S(1)} %get-tuple-element.51.mask_ref, ...), custom_call_target="tpu_custom_call" | custom-call | flops 3000000000 | bytes 1000000 | tf_op jit(solution)/shard_map/pallas_call | solution.py:233
  29.4 0.6 collective-permute-done.3.far_ref
  30.0 0.0 copy-done.4
  30.0 0.0 copy-done.5
  30.1 7.1 %shard_map.116 = (bf16[2,3584,128]{2,1,0:T(8,128)(2,1)S(1)}, bf16[256,128]{1,0:T(8,128)(2,1)S(1)}) custom-call(bf16[1200,128]{1,0:T(8,128)(2,1)S(1)} %collective-permute-done.2.near_ref, bf16[1408,128]{1,0:T(8,128)(2,1)S(1)} %get-tuple-element.49.mid_ref, bf16[1200,128]{1,0:T(8,128)(2,1)S(1)} %collective-permute-done.3.far_ref, ...), custom_call_target="tpu_custom_call" | custom-call | flops 8000000000 | bytes 1000000 | tf_op jit(solution)/shard_map/pallas_call | solution.py:233
  37.2 0.1 slice_bitcast_fusion
  37.2 0.1 collective-permute-start.4
  37.3 2.5 %collective-permute-done.4.theirs_ref = bf16[3584,128]{1,0:T(8,128)(2,1)S(1)} collective-permute-done((bf16[3584,128]{1,0:T(8,128)(2,1)S(1)}, bf16[3584,128]{1,0:T(8,128)(2,1)S(1)}, u32[]{:S(2)}, u32[]{:S(2)}) %collective-permute-start.4) | collective-permute-done | bytes 917536 | tf_op jit(solution)/shard_map/ppermute | solution.py:538
  39.8 0.3 shard_map.117
  40.0 1.1 %collective-permute-start.5 = (bf16[960,128]{1,0:T(8,128)(2,1)S(1)}, bf16[960,128]{1,0:T(8,128)(2,1)S(1)}, u32[]{:S(2)}, u32[]{:S(2)}) collective-permute-start(bf16[960,128]{1,0:T(8,128)(2,1)S(1)} %get-tuple-element.67), channel_id=1, source_target_pairs={{0,4},{1,5},{2,6},{3,7},{4,0},{5,1},{6,2},{7,3},{8,12},{9,13},{10,... | collective-permute-start | bytes 737288 | tf_op jit(solution)/shard_map/ppermute | solution.py:561
  41.2 1.8 %collective-permute-start.6 = (bf16[960,128]{1,0:T(8,128)(2,1)S(1)}, bf16[960,128]{1,0:T(8,128)(2,1)S(1)}, u32[]{:S(2)}, u32[]{:S(2)}) collective-permute-start(bf16[960,128]{1,0:T(8,128)(2,1)S(1)} %get-tuple-element.68), channel_id=1, source_target_pairs={{0,12},{1,13},{2,14},{3,15},{4,8},{5,9},{6,10},{7,11},{8,4},{9,5},... | collective-permute-start | bytes 737288 | tf_op jit(solution)/shard_map/ppermute | solution.py:561
  43.0 1.1 %collective-permute-start.7 = (bf16[960,128]{1,0:T(8,128)(2,1)S(1)}, bf16[960,128]{1,0:T(8,128)(2,1)S(1)}, u32[]{:S(2)}, u32[]{:S(2)}) collective-permute-start(bf16[960,128]{1,0:T(8,128)(2,1)S(1)} %get-tuple-element.69), channel_id=1, source_target_pairs={{0,8},{1,9},{2,10},{3,11},{4,12},{5,13},{6,14},{7,15},{8,0},{9,1},... | collective-permute-start | bytes 737288 | tf_op jit(solution)/shard_map/ppermute | solution.py:561
  44.1 1.4 %collective-permute-done.5.refs_1_ = bf16[960,128]{1,0:T(8,128)(2,1)S(1)} collective-permute-done((bf16[960,128]{1,0:T(8,128)(2,1)S(1)}, bf16[960,128]{1,0:T(8,128)(2,1)S(1)}, u32[]{:S(2)}, u32[]{:S(2)}) %collective-permute-start.5) | collective-permute-done | bytes 245792 | tf_op jit(solution)/shard_map/ppermute | solution.py:561
  45.5 3.3 %collective-permute-done.6.refs_2_ = bf16[960,128]{1,0:T(8,128)(2,1)S(1)} collective-permute-done((bf16[960,128]{1,0:T(8,128)(2,1)S(1)}, bf16[960,128]{1,0:T(8,128)(2,1)S(1)}, u32[]{:S(2)}, u32[]{:S(2)}) %collective-permute-start.6) | collective-permute-done | bytes 245792 | tf_op jit(solution)/shard_map/ppermute | solution.py:561
  48.8 1.8 %collective-permute-done.7.refs_3_ = bf16[960,128]{1,0:T(8,128)(2,1)S(1)} collective-permute-done((bf16[960,128]{1,0:T(8,128)(2,1)S(1)}, bf16[960,128]{1,0:T(8,128)(2,1)S(1)}, u32[]{:S(2)}, u32[]{:S(2)}) %collective-permute-start.7) | collective-permute-done | bytes 245792 | tf_op jit(solution)/shard_map/ppermute | solution.py:561
  50.6 0.1 shard_map.118
  50.7 1.0 %collective-permute-start.8 = (bf16[288,128]{1,0:T(8,128)(2,1)S(1)}, bf16[288,128]{1,0:T(8,128)(2,1)S(1)}, u32[]{:S(2)}, u32[]{:S(2)}) collective-permute-start(bf16[288,128]{1,0:T(8,128)(2,1)S(1)} %get-tuple-element.71), channel_id=1, source_target_pairs={{0,1},{1,0},{2,3},{3,2},{4,5},{5,4},{6,7},{7,6},{8,9},{9,8},{10,11... | collective-permute-start | bytes 221192 | tf_op jit(solution)/shard_map/ppermute | solution.py:561
  51.7 1.8 %collective-permute-start.9 = (bf16[288,128]{1,0:T(8,128)(2,1)S(1)}, bf16[288,128]{1,0:T(8,128)(2,1)S(1)}, u32[]{:S(2)}, u32[]{:S(2)}) collective-permute-start(bf16[288,128]{1,0:T(8,128)(2,1)S(1)} %get-tuple-element.72), channel_id=1, source_target_pairs={{0,3},{1,2},{2,1},{3,0},{4,7},{5,6},{6,5},{7,4},{8,11},{9,10},{10,... | collective-permute-start | bytes 221192 | tf_op jit(solution)/shard_map/ppermute | solution.py:561
  53.5 0.8 collective-permute-start.10
  54.3 0.0 collective-permute-done.8.refs_1_
  54.3 1.9 %collective-permute-done.9.refs_2_ = bf16[288,128]{1,0:T(8,128)(2,1)S(1)} collective-permute-done((bf16[288,128]{1,0:T(8,128)(2,1)S(1)}, bf16[288,128]{1,0:T(8,128)(2,1)S(1)}, u32[]{:S(2)}, u32[]{:S(2)}) %collective-permute-start.9) | collective-permute-done | bytes 73760 | tf_op jit(solution)/shard_map/ppermute | solution.py:561
  56.1 2.1 %collective-permute-done.10.refs_3_ = bf16[288,128]{1,0:T(8,128)(2,1)S(1)} collective-permute-done((bf16[288,128]{1,0:T(8,128)(2,1)S(1)}, bf16[288,128]{1,0:T(8,128)(2,1)S(1)}, u32[]{:S(2)}, u32[]{:S(2)}) %collective-permute-start.10) | collective-permute-done | bytes 73760 | tf_op jit(solution)/shard_map/ppermute | solution.py:561
  58.3 2.5 %collective-permute-start.13 = (bf16[224,128]{1,0:T(8,128)(2,1)S(1)}, bf16[224,128]{1,0:T(8,128)(2,1)S(1)}, u32[]{:S(2)}, u32[]{:S(2)}) collective-permute-start(bf16[224,128]{1,0:T(8,128)(2,1)S(1)} %get-tuple-element.75), channel_id=1, source_target_pairs={{0,96},{32,64},{64,32},{96,0},{1,97},{33,65},{65,33},{97,1},{2,98}... | collective-permute-start | bytes 172040 | tf_op jit(solution)/shard_map/ppermute | solution.py:550
  60.7 0.7 collective-permute-start.12
  61.4 0.2 collective-permute-start.11
  61.6 1.0 %collective-permute-done.13 = bf16[224,128]{1,0:T(8,128)(2,1)S(1)} collective-permute-done((bf16[224,128]{1,0:T(8,128)(2,1)S(1)}, bf16[224,128]{1,0:T(8,128)(2,1)S(1)}, u32[]{:S(2)}, u32[]{:S(2)}) %collective-permute-start.13) | collective-permute-done | bytes 57376 | tf_op jit(solution)/shard_map/ppermute | solution.py:550
  62.6 2.7 %collective-permute-done.12 = bf16[224,128]{1,0:T(8,128)(2,1)S(1)} collective-permute-done((bf16[224,128]{1,0:T(8,128)(2,1)S(1)}, bf16[224,128]{1,0:T(8,128)(2,1)S(1)}, u32[]{:S(2)}, u32[]{:S(2)}) %collective-permute-start.12) | collective-permute-done | bytes 57376 | tf_op jit(solution)/shard_map/ppermute | solution.py:550
  65.3 0.0 collective-permute-done.11
  65.3 0.1 broadcast_in_dim.2
  65.4 14.8 %all_to_all.16 = bf16[16,224,128]{2,1,0:T(8,128)(2,1)S(1)} all-to-all(bf16[16,224,128]{2,1,0:T(8,128)(2,1)S(1)} %broadcast_in_dim.2), channel_id=1, replica_groups=mesh['y'=4,'c'=2,'z'=4,'x'=4] {'z','x'}, dimensions={0} | all-to-all | bytes 1835008 | tf_op jit(solution)/shard_map/all_to_all | solution.py:641
  80.2 6.5 %collective-permute-start.14 = (bf16[3584,128]{1,0:T(8,128)(2,1)S(1)}, bf16[3584,128]{1,0:T(8,128)(2,1)S(1)}, u32[]{:S(2)}, u32[]{:S(2)}) collective-permute-start(bf16[3584,128]{1,0:T(8,128)(2,1)S(1)} %bitcast.14), channel_id=1, source_target_pairs={{0,16},{16,0},{1,17},{17,1},{2,18},{18,2},{3,19},{19,3},{4,20},{20... | collective-permute-start | bytes 2752520 | tf_op jit(solution)/shard_map/ppermute | solution.py:538
  86.8 0.7 reshape.34
  87.5 1.3 %shard_map.120 = (f32[2592,128]{1,0:T(8,128)}, f32[3456,128]{1,0:T(8,128)}, f32[1024,128]{1,0:T(8,128)}) custom-call(bf16[3584,128]{1,0:T(8,128)(2,1)S(1)} %bitcast.15), custom_call_target="tpu_custom_call" | custom-call | flops 10000000 | bytes 1000000 | tf_op jit(solution)/shard_map/pallas_call | solution.py:233
  88.7 0.1 collective-permute-done.14.half_ref
  88.9 1.3 %shard_map.121 = (f32[2592,128]{1,0:T(8,128)}, f32[3456,128]{1,0:T(8,128)}, f32[1024,128]{1,0:T(8,128)}) custom-call(bf16[3584,128]{1,0:T(8,128)(2,1)S(1)} %collective-permute-done.14.half_ref, f32[2592,128]{1,0:T(8,128)} %get-tuple-element.76.a, f32[3456,128]{1,0:T(8,128)} %get-tuple-element.77.b, ...), custom_call_target="tpu_custom_call", output_to_operand_aliasing={{0}: (1, {}), {1}: (2, {}), {2}: (3, {})} | custom-call | flops 10000000 | bytes 1000000 | tf_op jit(solution)/shard_map/pallas_call | solution.py:233
  (3 shorter events, 0.1 us)
Async XLA Ops:
  2.8 16.1 %all-to-all-start = ((bf16[16,8,1024]{2,1,0:T(8,128)(2,1)}), bf16[16,8,1024]{2,1,0:T(8,128)(2,1)S(1)}, u32[]{:S(2)}, u32[]{:S(2)}) async-start(bf16[16,8,1024]{2,1,0:T(8,128)(2,1)} %bitcast.21), calls=%async_computation | async-start | bytes 524288 | tf_op jit(solution)/shard_map/all_to_all | solution.py:587
  11.3 5.6 %collective-permute-start = (bf16[224,128]{1,0:T(8,128)(2,1)}, bf16[224,128]{1,0:T(8,128)(2,1)S(1)}, u32[]{:S(2)}, u32[]{:S(2)}) collective-permute-start(bf16[224,128]{1,0:T(8,128)(2,1)} %get-tuple-element.44), channel_id=1, source_target_pairs={{0,1},{2,3},{4,5},{6,7},{8,9},{10,11},{12,13},{14,15},{1,0},{3,2},... | collective-permute-start | bytes 172040 | tf_op jit(solution)/shard_map/ppermute | solution.py:534
  12.6 4.3 %collective-permute-start.1 = (bf16[224,128]{1,0:T(8,128)(2,1)}, bf16[224,128]{1,0:T(8,128)(2,1)S(1)}, u32[]{:S(2)}, u32[]{:S(2)}) collective-permute-start(bf16[224,128]{1,0:T(8,128)(2,1)} %get-tuple-element.45), channel_id=1, source_target_pairs={{1,2},{3,4},{5,6},{7,8},{9,10},{11,12},{13,14},{2,1},{4,3},{6,5},{... | collective-permute-start | bytes 172040 | tf_op jit(solution)/shard_map/ppermute | solution.py:534
  13.3 1.0 %copy-start = (bf16[1104,128]{1,0:T(8,128)(2,1)S(1)}, bf16[1104,128]{1,0:T(8,128)(2,1)}, u32[]{:S(2)}) copy-start(bf16[1104,128]{1,0:T(8,128)(2,1)} %get-tuple-element.43.after_ref.own_ref) | copy-start | bytes 847876
  14.3 1.2 %copy-start.2 = (bf16[27,128,128]{2,1,0:T(8,128)(2,1)S(1)}, bf16[27,128,128]{2,1,0:T(8,128)(2,1)}, u32[]{:S(2)}) copy-start(bf16[27,128,128]{2,1,0:T(8,128)(2,1)} %w2_ref.1) | copy-start | bytes 2654212
  15.4 1.1 %copy-start.3 = (bf16[27,96,128]{2,1,0:T(8,128)(2,1)S(1)}, bf16[27,96,128]{2,1,0:T(8,128)(2,1)}, u32[]{:S(2)}) copy-start(bf16[27,96,128]{2,1,0:T(8,128)(2,1)} %w1_ref.1) | copy-start | bytes 1990660
  16.5 2.4 %copy-start.1 = (bf16[1104,128]{1,0:T(8,128)(2,1)S(1)}, bf16[1104,128]{1,0:T(8,128)(2,1)}, u32[]{:S(2)}) copy-start(bf16[1104,128]{1,0:T(8,128)(2,1)} %get-tuple-element.43.after_ref.own_ref) | copy-start | bytes 847876
  19.2 8.3 %collective-permute-start.2 = (bf16[1200,128]{1,0:T(8,128)(2,1)S(1)}, bf16[1200,128]{1,0:T(8,128)(2,1)S(1)}, u32[]{:S(2)}, u32[]{:S(2)}) collective-permute-start(bf16[1200,128]{1,0:T(8,128)(2,1)S(1)} %get-tuple-element.48), channel_id=1, source_target_pairs={{0,16},{32,48},{64,80},{96,112},{16,0},{48,32},{80,64},{112,96},{1... | collective-permute-start | bytes 921608 | tf_op jit(solution)/shard_map/ppermute | solution.py:534
  21.9 8.2 %collective-permute-start.3 = (bf16[1200,128]{1,0:T(8,128)(2,1)S(1)}, bf16[1200,128]{1,0:T(8,128)(2,1)S(1)}, u32[]{:S(2)}, u32[]{:S(2)}) collective-permute-start(bf16[1200,128]{1,0:T(8,128)(2,1)S(1)} %get-tuple-element.50), channel_id=1, source_target_pairs={{16,32},{48,64},{80,96},{32,16},{64,48},{96,80},{17,33},{49,65},{8... | collective-permute-start | bytes 921608 | tf_op jit(solution)/shard_map/ppermute | solution.py:534
  27.5 2.5 %copy-start.4 = (bf16[8,128,128]{2,1,0:T(8,128)(2,1)S(1)}, bf16[8,128,128]{2,1,0:T(8,128)(2,1)}, u32[]{:S(2)}) copy-start(bf16[8,128,128]{2,1,0:T(8,128)(2,1)} %wd_ref.1) | copy-start | bytes 786436
  27.6 2.5 %copy-start.5 = (bf16[96,64]{1,0:T(8,128)(2,1)S(1)}, bf16[96,64]{1,0:T(8,128)(2,1)}, u32[]{:S(2)}) copy-start(bf16[96,64]{1,0:T(8,128)(2,1)} %constant.2.clone.up_ref) | copy-start | bytes 36868
  37.2 2.6 %collective-permute-start.4 = (bf16[3584,128]{1,0:T(8,128)(2,1)S(1)}, bf16[3584,128]{1,0:T(8,128)(2,1)S(1)}, u32[]{:S(2)}, u32[]{:S(2)}) collective-permute-start(bf16[3584,128]{1,0:T(8,128)(2,1)S(1)} %slice_bitcast_fusion), channel_id=1, source_target_pairs={{0,16},{16,0},{1,17},{17,1},{2,18},{18,2},{3,19},{19,3},{4,20},{20... | collective-permute-start | bytes 2752520 | tf_op jit(solution)/shard_map/ppermute | solution.py:538
  40.0 5.4 %collective-permute-start.5 = (bf16[960,128]{1,0:T(8,128)(2,1)S(1)}, bf16[960,128]{1,0:T(8,128)(2,1)S(1)}, u32[]{:S(2)}, u32[]{:S(2)}) collective-permute-start(bf16[960,128]{1,0:T(8,128)(2,1)S(1)} %get-tuple-element.67), channel_id=1, source_target_pairs={{0,4},{1,5},{2,6},{3,7},{4,0},{5,1},{6,2},{7,3},{8,12},{9,13},{10,... | collective-permute-start | bytes 737288 | tf_op jit(solution)/shard_map/ppermute | solution.py:561
  41.2 7.6 %collective-permute-start.6 = (bf16[960,128]{1,0:T(8,128)(2,1)S(1)}, bf16[960,128]{1,0:T(8,128)(2,1)S(1)}, u32[]{:S(2)}, u32[]{:S(2)}) collective-permute-start(bf16[960,128]{1,0:T(8,128)(2,1)S(1)} %get-tuple-element.68), channel_id=1, source_target_pairs={{0,12},{1,13},{2,14},{3,15},{4,8},{5,9},{6,10},{7,11},{8,4},{9,5},... | collective-permute-start | bytes 737288 | tf_op jit(solution)/shard_map/ppermute | solution.py:561
  43.0 7.6 %collective-permute-start.7 = (bf16[960,128]{1,0:T(8,128)(2,1)S(1)}, bf16[960,128]{1,0:T(8,128)(2,1)S(1)}, u32[]{:S(2)}, u32[]{:S(2)}) collective-permute-start(bf16[960,128]{1,0:T(8,128)(2,1)S(1)} %get-tuple-element.69), channel_id=1, source_target_pairs={{0,8},{1,9},{2,10},{3,11},{4,12},{5,13},{6,14},{7,15},{8,0},{9,1},... | collective-permute-start | bytes 737288 | tf_op jit(solution)/shard_map/ppermute | solution.py:561
  50.7 3.5 %collective-permute-start.8 = (bf16[288,128]{1,0:T(8,128)(2,1)S(1)}, bf16[288,128]{1,0:T(8,128)(2,1)S(1)}, u32[]{:S(2)}, u32[]{:S(2)}) collective-permute-start(bf16[288,128]{1,0:T(8,128)(2,1)S(1)} %get-tuple-element.71), channel_id=1, source_target_pairs={{0,1},{1,0},{2,3},{3,2},{4,5},{5,4},{6,7},{7,6},{8,9},{9,8},{10,11... | collective-permute-start | bytes 221192 | tf_op jit(solution)/shard_map/ppermute | solution.py:561
  51.7 4.4 %collective-permute-start.9 = (bf16[288,128]{1,0:T(8,128)(2,1)S(1)}, bf16[288,128]{1,0:T(8,128)(2,1)S(1)}, u32[]{:S(2)}, u32[]{:S(2)}) collective-permute-start(bf16[288,128]{1,0:T(8,128)(2,1)S(1)} %get-tuple-element.72), channel_id=1, source_target_pairs={{0,3},{1,2},{2,1},{3,0},{4,7},{5,6},{6,5},{7,4},{8,11},{9,10},{10,... | collective-permute-start | bytes 221192 | tf_op jit(solution)/shard_map/ppermute | solution.py:561
  53.5 4.7 %collective-permute-start.10 = (bf16[288,128]{1,0:T(8,128)(2,1)S(1)}, bf16[288,128]{1,0:T(8,128)(2,1)S(1)}, u32[]{:S(2)}, u32[]{:S(2)}) collective-permute-start(bf16[288,128]{1,0:T(8,128)(2,1)S(1)} %get-tuple-element.73), channel_id=1, source_target_pairs={{0,2},{1,3},{2,0},{3,1},{4,6},{5,7},{6,4},{7,5},{8,10},{9,11},{10,... | collective-permute-start | bytes 221192 | tf_op jit(solution)/shard_map/ppermute | solution.py:561
  58.3 4.3 %collective-permute-start.13 = (bf16[224,128]{1,0:T(8,128)(2,1)S(1)}, bf16[224,128]{1,0:T(8,128)(2,1)S(1)}, u32[]{:S(2)}, u32[]{:S(2)}) collective-permute-start(bf16[224,128]{1,0:T(8,128)(2,1)S(1)} %get-tuple-element.75), channel_id=1, source_target_pairs={{0,96},{32,64},{64,32},{96,0},{1,97},{33,65},{65,33},{97,1},{2,98}... | collective-permute-start | bytes 172040 | tf_op jit(solution)/shard_map/ppermute | solution.py:550
  60.7 4.5 %collective-permute-start.12 = (bf16[224,128]{1,0:T(8,128)(2,1)S(1)}, bf16[224,128]{1,0:T(8,128)(2,1)S(1)}, u32[]{:S(2)}, u32[]{:S(2)}) collective-permute-start(bf16[224,128]{1,0:T(8,128)(2,1)S(1)} %get-tuple-element.75), channel_id=1, source_target_pairs={{0,64},{32,96},{64,0},{96,32},{1,65},{33,97},{65,1},{97,33},{2,66}... | collective-permute-start | bytes 172040 | tf_op jit(solution)/shard_map/ppermute | solution.py:550
  61.4 3.9 %collective-permute-start.11 = (bf16[224,128]{1,0:T(8,128)(2,1)S(1)}, bf16[224,128]{1,0:T(8,128)(2,1)S(1)}, u32[]{:S(2)}, u32[]{:S(2)}) collective-permute-start(bf16[224,128]{1,0:T(8,128)(2,1)S(1)} %get-tuple-element.75), channel_id=1, source_target_pairs={{0,32},{32,0},{64,96},{96,64},{1,33},{33,1},{65,97},{97,65},{2,34}... | collective-permute-start | bytes 172040 | tf_op jit(solution)/shard_map/ppermute | solution.py:550
  80.2 8.6 %collective-permute-start.14 = (bf16[3584,128]{1,0:T(8,128)(2,1)S(1)}, bf16[3584,128]{1,0:T(8,128)(2,1)S(1)}, u32[]{:S(2)}, u32[]{:S(2)}) collective-permute-start(bf16[3584,128]{1,0:T(8,128)(2,1)S(1)} %bitcast.14), channel_id=1, source_target_pairs={{0,16},{16,0},{1,17},{17,1},{2,18},{18,2},{3,19},{19,3},{4,20},{20... | collective-permute-start | bytes 2752520 | tf_op jit(solution)/shard_map/ppermute | solution.py:538

commit v11 on v10

--- a/solution.py
+++ b/solution.py
@@ -70,7 +70,7 @@
 
 
 def section(
-    near_ref, mid_ref, far_ref, mask_ref, gc_ref, place_ref, part1_ref, inner_ref, inner_sg1_ref, part2_ref,
+    near_ref, mid_ref, far_ref, mask_ref, own_ge_ref, place_ref, part1_ref, inner_ref, inner_sg1_ref, part2_ref,
     near_first_ref, near_sg1_ref, near_second_ref, near_slope_ref, w1_ref, w2_ref, back_ref, wd_ref, up_ref,
     grads_ref, out_ref,
     sides, first, sg1, second, slopes, ge, g2, gs, vt,
@@ -94,8 +94,6 @@
     masks = [[spread(t, by) for by in range(6)] for t in packed]
 
     def cotangent(u, q):
-        if u in (1, 2):
-            return gc_ref[u - 1, q]
         return (low_ref if u == 0 else high_ref)[COTS + q * 32 : COTS + (q + 1) * 32, :]
 
     def line(x, y0, cells):
@@ -144,19 +142,9 @@
             )
         )
 
-    even = z_of(6 * Z) % 2 == 0
-    for u in range(4):
-        both = jnp.concatenate(
-            [jnp.concatenate([cotangent(u, 2 * b + c) for b in range(2)], axis=1) for c in range(2)],
-            axis=0,
-        )
-        r = mm(up_ref[...], both)
-        for v in range(10):
-            by, b = (v + 1) // 2, (v + 1) % 2
-            t = r[by * Z : (by + 1) * Z, b * C : (b + 1) * C]
-            at = (u * 10 + v) * Z
-            ge[at : at + Z, 0:C] = jnp.where(even[:Z], t, 0.0).astype(BF)
-            ge[at : at + Z, C : 2 * C] = jnp.where(even[:Z], 0.0, t).astype(BF)
+    for u in (0, 3):
+        repeat_along_z([cotangent(u, q) for q in range(4)], up_ref, ge, u * 160)
+    ge[160:480, :] = own_ge_ref[...]
 
     for x in range(6):
         u, a = (x + 1) // 2, (x + 1) % 2
@@ -315,13 +303,32 @@
         pl.when(lax.axis_index("c") == core)(functools.partial(run, core == 0))
 
 
-def begin(mid_ref, mask_ref, w1_ref, w2_ref, part1_ref, first_ref, sg1_ref, part2_ref):
+def repeat_along_z(cots, up_ref, out_ref, at):
+    both = jnp.concatenate(
+        [jnp.concatenate([cots[2 * b + c] for b in range(2)], axis=1) for c in range(2)], axis=0
+    )
+    r = mm(up_ref[...], both)
+    even = z_of(Z) % 2 == 0
+    for v in range(10):
+        by, b = (v + 1) // 2, (v + 1) % 2
+        t = r[by * Z : (by + 1) * Z, b * C : (b + 1) * C]
+        rows = slice(at + v * Z, at + (v + 1) * Z)
+        out_ref[rows, 0:C] = jnp.where(even, t, 0.0).astype(BF)
+        out_ref[rows, C : 2 * C] = jnp.where(even, 0.0, t).astype(BF)
+
+
+def begin(
+    mid_ref, mask_ref, w1_ref, w2_ref, gc_ref, up_ref,
+    part1_ref, first_ref, sg1_ref, part2_ref, ge_ref,
+):
     def cells(x, y, n):
         return mid_ref[((x - 3) * 22 + y) * Z : ((x - 3) * 22 + y + n) * Z, :]
 
     def firsts(x, y, n):
         return first_ref[((x - 3) * 20 + y) * Z : ((x - 3) * 20 + y + n) * Z, :]
 
+    for u in range(2):
+        repeat_along_z([gc_ref[u, q] for q in range(4)], up_ref, ge_ref, u * 160)
     masks = [spread(mask_ref[...], by) for by in range(6)]
     act = jnp.concatenate([masks[(y + 4) // 4] for y in range(-2, 18)], axis=0)
     for x in (3, 4, 1, 2, 5, 6):
@@ -596,11 +603,12 @@
     far, near = swap(far, GX, 1), swap(near, GX, 0)
     ahead = call(
         begin,
-        [((4, 20 * Z, C), F32), ((40 * Z, C), BF), ((2 * Y * Z, C), F32), ((4, 18 * Z, C), F32)],
-        (mid, mask, w1, w2),
+        [((4, 20 * Z, C), F32), ((40 * Z, C), BF), ((2 * Y * Z, C), F32), ((4, 18 * Z, C), F32), ((320, 2 * C), BF)],
+        (mid, mask, w1, w2, gc, up_matrix()),
         flops=3_000_000_000,
     )
 
+    *ahead, own_ge = ahead
     part1, inner, _, part2 = ahead
     beside = call(
         near_side,
@@ -611,7 +619,7 @@
     grads, outgoing = call(
         section,
         [((2, HALF, C), BF), ((256, C), BF)],
-        (near, mid, far, mask, gc, place, *ahead, *beside, w1, w2, back, weight_down, up_matrix()),
+        (near, mid, far, mask, own_ge, place, *ahead, *beside, w1, w2, back, weight_down, up_matrix()),
         scratch=[
             ((2, STRIP, C), BF),
             ((8 * 20 * Z, C), BF),

time: 90.7 us -> 90.7 us (level)
  no operation moved by 1% of the time
where the time goes in v11:
time: 90.7 us; the launch traced here: 90.3 us
  starting transfers between devices  33.8 us (37%)
  waiting for transfers between devices  19.4 us (21%)
  Pallas kernels  17.2 us (19%)
  blocking collectives  14.8 us (16%)
  local copies, waits for them, and re-layouts  4.08 us (4%)
  between operations  0.98 us (1%)
    pallas_call x11, Pallas kernels, call(): pl.pallas_call(kernel, out_shape=tuple((jax.ShapeDtypeStruct(shape, dtype...  17.2 us
    all_to_all x1, blocking collectives, per_device(): lax.all_to_all(jnp.broadcast_to(part[None], (16, PART, C)), GY, 0, 0, til...  14.8 us
    ppermute x6, waiting for transfers between devices, flip_by_core(): return lax.ppermute(v, every, pairs)  10.5 us
    all_to_all x1, starting transfers between devices, per_device(): rows = lax.all_to_all(rows, GY, 0, 0, tiled=True)  8.44 us
    ppermute x4, starting transfers between devices, swap(): return lax.ppermute(v, axes, pairs + [(j, i) for i, j in pairs])  7.81 us
    ppermute x6, starting transfers between devices, flip_by_core(): return lax.ppermute(v, every, pairs)  7.58 us
    ppermute x2, starting transfers between devices, swap_cores(): return lax.ppermute(v, 'c', [(0, 1), (1, 0)])  6.64 us
    ppermute x3, waiting for transfers between devices, flip(): lax.ppermute(v, axis, [(i, i ^ bits) for i in range(lax.axis_size(axis))])  3.69 us
  transfers between devices with their start and end apart: 16, of which 11 were waited for; matrix products, arithmetic and copies ran while one was open for 1% of the time, Pallas kernels for 7%

profile of v11, /device:TPU:1, one launch (start us, length us, event | category | flops | bytes accessed | tf_op | source)
XLA Modules:
  0.0 90.3 jit_solution(6374344079129998615)
XLA Ops:
  0.6 2.2 %shard_map.120 = (bf16[128,1024]{1,0:T(8,128)(2,1)}, bf16[1104,128]{1,0:T(8,128)(2,1)}, bf16[224,128]{1,0:T(8,128)(2,1)}, bf16[224,128]{1,0:T(8,128)(2,1)}) custom-call(bf16[1,1,32,1024]{3,2,1,0:T(8,128)(2,1)} %grad_hbm.1, bf16[4,16,1536]{2,1,0:T(8,128)(2,1)} %feat_hbm.1, s32[1,4,4]{2,1,0:T(4,128)} %blocks_hbm.1, s32[1,16]{1,0:T(1,128)} %bitcast.22), custom_call_target="tpu_custom_call" | custom-call | flops 10000000 | bytes 1000000 | tf_op jit(solution)/shard_map/pallas_call | solution.py:221
  2.8 8.4 %all-to-all-start = ((bf16[16,8,1024]{2,1,0:T(8,128)(2,1)}), bf16[16,8,1024]{2,1,0:T(8,128)(2,1)S(1)}, u32[]{:S(2)}, u32[]{:S(2)}) async-start(bf16[16,8,1024]{2,1,0:T(8,128)(2,1)} %bitcast.21), calls=%async_computation | async-start | bytes 524288 | tf_op jit(solution)/shard_map/all_to_all | solution.py:594
  11.3 1.4 %collective-permute-start = (bf16[224,128]{1,0:T(8,128)(2,1)}, bf16[224,128]{1,0:T(8,128)(2,1)S(1)}, u32[]{:S(2)}, u32[]{:S(2)}) collective-permute-start(bf16[224,128]{1,0:T(8,128)(2,1)} %get-tuple-element.45), channel_id=1, source_target_pairs={{0,1},{2,3},{4,5},{6,7},{8,9},{10,11},{12,13},{14,15},{1,0},{3,2},... | collective-permute-start | bytes 172040 | tf_op jit(solution)/shard_map/ppermute | solution.py:541
  12.6 0.7 collective-permute-start.1
  13.3 0.0 copy-start
  13.3 0.9 %copy-done = bf16[1104,128]{1,0:T(8,128)(2,1)S(1)} copy-done((bf16[1104,128]{1,0:T(8,128)(2,1)S(1)}, bf16[1104,128]{1,0:T(8,128)(2,1)}, u32[]{:S(2)}) %copy-start) | copy-done | bytes 282648
  14.3 0.0 copy-start.2
  14.3 1.2 %copy-done.2 = bf16[27,128,128]{2,1,0:T(8,128)(2,1)S(1)} copy-done((bf16[27,128,128]{2,1,0:T(8,128)(2,1)S(1)}, bf16[27,128,128]{2,1,0:T(8,128)(2,1)}, u32[]{:S(2)}) %copy-start.2) | copy-done | bytes 884760
  15.4 0.0 copy-start.3
  15.4 1.1 %copy-done.3 = bf16[27,96,128]{2,1,0:T(8,128)(2,1)S(1)} copy-done((bf16[27,96,128]{2,1,0:T(8,128)(2,1)S(1)}, bf16[27,96,128]{2,1,0:T(8,128)(2,1)}, u32[]{:S(2)}) %copy-start.3) | copy-done | bytes 663576
  16.5 0.0 copy-start.1
  16.5 0.0 copy-start.5
  16.5 0.4 shard_map.121
  16.9 0.0 collective-permute-done.beside_ref
  16.9 0.0 collective-permute-done.1.beyond_ref
  16.9 2.0 %all-to-all-done = bf16[16,8,1024]{2,1,0:T(8,128)(2,1)S(1)} async-done(((bf16[16,8,1024]{2,1,0:T(8,128)(2,1)}), bf16[16,8,1024]{2,1,0:T(8,128)(2,1)S(1)}, u32[]{:S(2)}, u32[]{:S(2)}) %all-to-all-start) | async-done | bytes 262176 | tf_op jit(solution)/shard_map/all_to_all | solution.py:594
  18.9 0.0 copy-done.1
  18.9 0.3 shard_map.122
  19.2 2.7 %collective-permute-start.2 = (bf16[1200,128]{1,0:T(8,128)(2,1)S(1)}, bf16[1200,128]{1,0:T(8,128)(2,1)S(1)}, u32[]{:S(2)}, u32[]{:S(2)}) collective-permute-start(bf16[1200,128]{1,0:T(8,128)(2,1)S(1)} %get-tuple-element.49), channel_id=1, source_target_pairs={{0,16},{32,48},{64,80},{96,112},{16,0},{48,32},{80,64},{112,96},{1... | collective-permute-start | bytes 921608 | tf_op jit(solution)/shard_map/ppermute | solution.py:541
  21.9 3.1 %collective-permute-start.3 = (bf16[1200,128]{1,0:T(8,128)(2,1)S(1)}, bf16[1200,128]{1,0:T(8,128)(2,1)S(1)}, u32[]{:S(2)}, u32[]{:S(2)}) collective-permute-start(bf16[1200,128]{1,0:T(8,128)(2,1)S(1)} %get-tuple-element.51), channel_id=1, source_target_pairs={{16,32},{48,64},{80,96},{32,16},{64,48},{96,80},{17,33},{49,65},{8... | collective-permute-start | bytes 921608 | tf_op jit(solution)/shard_map/ppermute | solution.py:541
  25.0 0.0 copy-done.5
  25.0 2.6 %shard_map.123 = (f32[4,320,128]{2,1,0:T(8,128)S(1)}, bf16[640,128]{1,0:T(8,128)(2,1)S(1)}, f32[512,128]{1,0:T(8,128)S(1)}, f32[4,288,128]{2,1,0:T(8,128)S(1)}, bf16[320,256]{1,0:T(8,128)(2,1)S(1)}) custom-call(bf16[1408,128]{1,0:T(8,128)(2,1)S(1)} %get-tuple-element.50.mid_ref, bf16[16,128]{1,0:T(8,128)(2,1)S(1)} %get-tuple-element.52.mask_ref, ...), custom_call_target="tpu_custom_call" | custom-call | flops 3000000000 | bytes 1000000 | tf_op jit(solution)/shard_map/pallas_call | solution.py:221
  27.6 0.0 collective-permute-done.2.near_ref
  27.6 0.0 copy-start.4
  27.6 1.8 %shard_map.124 = (bf16[960,128]{1,0:T(8,128)(2,1)S(1)}, f32[256,128]{1,0:T(8,128)S(1)}, bf16[512,128]{1,0:T(8,128)(2,1)S(1)}, f32[864,128]{1,0:T(8,128)S(1)}) custom-call(bf16[1200,128]{1,0:T(8,128)(2,1)S(1)} %collective-permute-done.2.near_ref, bf16[16,128]{1,0:T(8,128)(2,1)S(1)} %get-tuple-element.52.mask_ref, ...), custom_call_target="tpu_custom_call" | custom-call | flops 3000000000 | bytes 1000000 | tf_op jit(solution)/shard_map/pallas_call | solution.py:221
  29.4 0.6 collective-permute-done.3.far_ref
  30.0 0.0 copy-done.4
  30.1 7.1 %shard_map.125 = (bf16[2,3584,128]{2,1,0:T(8,128)(2,1)S(1)}, bf16[256,128]{1,0:T(8,128)(2,1)S(1)}) custom-call(bf16[1200,128]{1,0:T(8,128)(2,1)S(1)} %collective-permute-done.2.near_ref, bf16[1408,128]{1,0:T(8,128)(2,1)S(1)} %get-tuple-element.50.mid_ref, bf16[1200,128]{1,0:T(8,128)(2,1)S(1)} %collective-permute-done.3.far_ref, ...), custom_call_target="tpu_custom_call" | custom-call | flops 8000000000 | bytes 1000000 | tf_op jit(solution)/shard_map/pallas_call | solution.py:221
  37.1 0.1 slice_bitcast_fusion
  37.2 0.1 collective-permute-start.4
  37.3 2.5 %collective-permute-done.4.theirs_ref = bf16[3584,128]{1,0:T(8,128)(2,1)S(1)} collective-permute-done((bf16[3584,128]{1,0:T(8,128)(2,1)S(1)}, bf16[3584,128]{1,0:T(8,128)(2,1)S(1)}, u32[]{:S(2)}, u32[]{:S(2)}) %collective-permute-start.4) | collective-permute-done | bytes 917536 | tf_op jit(solution)/shard_map/ppermute | solution.py:545
  39.7 0.3 shard_map.126
  40.0 1.1 %collective-permute-start.5 = (bf16[960,128]{1,0:T(8,128)(2,1)S(1)}, bf16[960,128]{1,0:T(8,128)(2,1)S(1)}, u32[]{:S(2)}, u32[]{:S(2)}) collective-permute-start(bf16[960,128]{1,0:T(8,128)(2,1)S(1)} %get-tuple-element.69), channel_id=1, source_target_pairs={{0,4},{1,5},{2,6},{3,7},{4,0},{5,1},{6,2},{7,3},{8,12},{9,13},{10,... | collective-permute-start | bytes 737288 | tf_op jit(solution)/shard_map/ppermute | solution.py:568
  41.1 1.8 %collective-permute-start.6 = (bf16[960,128]{1,0:T(8,128)(2,1)S(1)}, bf16[960,128]{1,0:T(8,128)(2,1)S(1)}, u32[]{:S(2)}, u32[]{:S(2)}) collective-permute-start(bf16[960,128]{1,0:T(8,128)(2,1)S(1)} %get-tuple-element.70), channel_id=1, source_target_pairs={{0,12},{1,13},{2,14},{3,15},{4,8},{5,9},{6,10},{7,11},{8,4},{9,5},... | collective-permute-start | bytes 737288 | tf_op jit(solution)/shard_map/ppermute | solution.py:568
  43.0 1.1 %collective-permute-start.7 = (bf16[960,128]{1,0:T(8,128)(2,1)S(1)}, bf16[960,128]{1,0:T(8,128)(2,1)S(1)}, u32[]{:S(2)}, u32[]{:S(2)}) collective-permute-start(bf16[960,128]{1,0:T(8,128)(2,1)S(1)} %get-tuple-element.71), channel_id=1, source_target_pairs={{0,8},{1,9},{2,10},{3,11},{4,12},{5,13},{6,14},{7,15},{8,0},{9,1},... | collective-permute-start | bytes 737288 | tf_op jit(solution)/shard_map/ppermute | solution.py:568
  44.1 1.4 %collective-permute-done.5.refs_1_ = bf16[960,128]{1,0:T(8,128)(2,1)S(1)} collective-permute-done((bf16[960,128]{1,0:T(8,128)(2,1)S(1)}, bf16[960,128]{1,0:T(8,128)(2,1)S(1)}, u32[]{:S(2)}, u32[]{:S(2)}) %collective-permute-start.5) | collective-permute-done | bytes 245792 | tf_op jit(solution)/shard_map/ppermute | solution.py:568
  45.4 3.3 %collective-permute-done.6.refs_2_ = bf16[960,128]{1,0:T(8,128)(2,1)S(1)} collective-permute-done((bf16[960,128]{1,0:T(8,128)(2,1)S(1)}, bf16[960,128]{1,0:T(8,128)(2,1)S(1)}, u32[]{:S(2)}, u32[]{:S(2)}) %collective-permute-start.6) | collective-permute-done | bytes 245792 | tf_op jit(solution)/shard_map/ppermute | solution.py:568
  48.8 1.8 %collective-permute-done.7.refs_3_ = bf16[960,128]{1,0:T(8,128)(2,1)S(1)} collective-permute-done((bf16[960,128]{1,0:T(8,128)(2,1)S(1)}, bf16[960,128]{1,0:T(8,128)(2,1)S(1)}, u32[]{:S(2)}, u32[]{:S(2)}) %collective-permute-start.7) | collective-permute-done | bytes 245792 | tf_op jit(solution)/shard_map/ppermute | solution.py:568
  50.6 0.1 shard_map.127
  50.7 1.0 %collective-permute-start.8 = (bf16[288,128]{1,0:T(8,128)(2,1)S(1)}, bf16[288,128]{1,0:T(8,128)(2,1)S(1)}, u32[]{:S(2)}, u32[]{:S(2)}) collective-permute-start(bf16[288,128]{1,0:T(8,128)(2,1)S(1)} %get-tuple-element.73), channel_id=1, source_target_pairs={{0,1},{1,0},{2,3},{3,2},{4,5},{5,4},{6,7},{7,6},{8,9},{9,8},{10,11... | collective-permute-start | bytes 221192 | tf_op jit(solution)/shard_map/ppermute | solution.py:568
  51.7 1.8 %collective-permute-start.9 = (bf16[288,128]{1,0:T(8,128)(2,1)S(1)}, bf16[288,128]{1,0:T(8,128)(2,1)S(1)}, u32[]{:S(2)}, u32[]{:S(2)}) collective-permute-start(bf16[288,128]{1,0:T(8,128)(2,1)S(1)} %get-tuple-element.74), channel_id=1, source_target_pairs={{0,3},{1,2},{2,1},{3,0},{4,7},{5,6},{6,5},{7,4},{8,11},{9,10},{10,... | collective-permute-start | bytes 221192 | tf_op jit(solution)/shard_map/ppermute | solution.py:568
  53.5 0.8 collective-permute-start.10
  54.2 0.0 collective-permute-done.8.refs_1_
  54.2 1.9 %collective-permute-done.9.refs_2_ = bf16[288,128]{1,0:T(8,128)(2,1)S(1)} collective-permute-done((bf16[288,128]{1,0:T(8,128)(2,1)S(1)}, bf16[288,128]{1,0:T(8,128)(2,1)S(1)}, u32[]{:S(2)}, u32[]{:S(2)}) %collective-permute-start.9) | collective-permute-done | bytes 73760 | tf_op jit(solution)/shard_map/ppermute | solution.py:568
  56.1 2.1 %collective-permute-done.10.refs_3_ = bf16[288,128]{1,0:T(8,128)(2,1)S(1)} collective-permute-done((bf16[288,128]{1,0:T(8,128)(2,1)S(1)}, bf16[288,128]{1,0:T(8,128)(2,1)S(1)}, u32[]{:S(2)}, u32[]{:S(2)}) %collective-permute-start.10) | collective-permute-done | bytes 73760 | tf_op jit(solution)/shard_map/ppermute | solution.py:568
  58.2 2.5 %collective-permute-start.13 = (bf16[224,128]{1,0:T(8,128)(2,1)S(1)}, bf16[224,128]{1,0:T(8,128)(2,1)S(1)}, u32[]{:S(2)}, u32[]{:S(2)}) collective-permute-start(bf16[224,128]{1,0:T(8,128)(2,1)S(1)} %get-tuple-element.77), channel_id=1, source_target_pairs={{0,96},{32,64},{64,32},{96,0},{1,97},{33,65},{65,33},{97,1},{2,98}... | collective-permute-start | bytes 172040 | tf_op jit(solution)/shard_map/ppermute | solution.py:557
  60.7 0.7 collective-permute-start.12
  61.4 0.2 collective-permute-start.11
  61.5 1.0 %collective-permute-done.13 = bf16[224,128]{1,0:T(8,128)(2,1)S(1)} collective-permute-done((bf16[224,128]{1,0:T(8,128)(2,1)S(1)}, bf16[224,128]{1,0:T(8,128)(2,1)S(1)}, u32[]{:S(2)}, u32[]{:S(2)}) %collective-permute-start.13) | collective-permute-done | bytes 57376 | tf_op jit(solution)/shard_map/ppermute | solution.py:557
  62.5 2.7 %collective-permute-done.12 = bf16[224,128]{1,0:T(8,128)(2,1)S(1)} collective-permute-done((bf16[224,128]{1,0:T(8,128)(2,1)S(1)}, bf16[224,128]{1,0:T(8,128)(2,1)S(1)}, u32[]{:S(2)}, u32[]{:S(2)}) %collective-permute-start.12) | collective-permute-done | bytes 57376 | tf_op jit(solution)/shard_map/ppermute | solution.py:557
  65.2 0.0 collective-permute-done.11
  65.3 0.1 broadcast_in_dim.2
  65.4 14.8 %all_to_all.16 = bf16[16,224,128]{2,1,0:T(8,128)(2,1)S(1)} all-to-all(bf16[16,224,128]{2,1,0:T(8,128)(2,1)S(1)} %broadcast_in_dim.2), channel_id=1, replica_groups=mesh['y'=4,'c'=2,'z'=4,'x'=4] {'z','x'}, dimensions={0} | all-to-all | bytes 1835008 | tf_op jit(solution)/shard_map/all_to_all | solution.py:649
  80.2 6.6 %collective-permute-start.14 = (bf16[3584,128]{1,0:T(8,128)(2,1)S(1)}, bf16[3584,128]{1,0:T(8,128)(2,1)S(1)}, u32[]{:S(2)}, u32[]{:S(2)}) collective-permute-start(bf16[3584,128]{1,0:T(8,128)(2,1)S(1)} %bitcast.14), channel_id=1, source_target_pairs={{0,16},{16,0},{1,17},{17,1},{2,18},{18,2},{3,19},{19,3},{4,20},{20... | collective-permute-start | bytes 2752520 | tf_op jit(solution)/shard_map/ppermute | solution.py:545
  86.8 0.7 reshape.34
  87.4 1.3 %shard_map.129 = (f32[2592,128]{1,0:T(8,128)}, f32[3456,128]{1,0:T(8,128)}, f32[1024,128]{1,0:T(8,128)}) custom-call(bf16[3584,128]{1,0:T(8,128)(2,1)S(1)} %bitcast.15), custom_call_target="tpu_custom_call" | custom-call | flops 10000000 | bytes 1000000 | tf_op jit(solution)/shard_map/pallas_call | solution.py:221
  88.7 0.1 collective-permute-done.14.half_ref
  88.8 1.3 %shard_map.130 = (f32[2592,128]{1,0:T(8,128)}, f32[3456,128]{1,0:T(8,128)}, f32[1024,128]{1,0:T(8,128)}) custom-call(bf16[3584,128]{1,0:T(8,128)(2,1)S(1)} %collective-permute-done.14.half_ref, f32[2592,128]{1,0:T(8,128)} %get-tuple-element.78.a, f32[3456,128]{1,0:T(8,128)} %get-tuple-element.79.b, ...), custom_call_target="tpu_custom_call", output_to_operand_aliasing={{0}: (1, {}), {1}: (2, {}), {2}: (3, {})} | custom-call | flops 10000000 | bytes 1000000 | tf_op jit(solution)/shard_map/pallas_call | solution.py:221
  (3 shorter events, 0.1 us)
Async XLA Ops:
  2.8 16.1 %all-to-all-start = ((bf16[16,8,1024]{2,1,0:T(8,128)(2,1)}), bf16[16,8,1024]{2,1,0:T(8,128)(2,1)S(1)}, u32[]{:S(2)}, u32[]{:S(2)}) async-start(bf16[16,8,1024]{2,1,0:T(8,128)(2,1)} %bitcast.21), calls=%async_computation | async-start | bytes 524288 | tf_op jit(solution)/shard_map/all_to_all | solution.py:594
  11.3 5.6 %collective-permute-start = (bf16[224,128]{1,0:T(8,128)(2,1)}, bf16[224,128]{1,0:T(8,128)(2,1)S(1)}, u32[]{:S(2)}, u32[]{:S(2)}) collective-permute-start(bf16[224,128]{1,0:T(8,128)(2,1)} %get-tuple-element.45), channel_id=1, source_target_pairs={{0,1},{2,3},{4,5},{6,7},{8,9},{10,11},{12,13},{14,15},{1,0},{3,2},... | collective-permute-start | bytes 172040 | tf_op jit(solution)/shard_map/ppermute | solution.py:541
  12.6 4.3 %collective-permute-start.1 = (bf16[224,128]{1,0:T(8,128)(2,1)}, bf16[224,128]{1,0:T(8,128)(2,1)S(1)}, u32[]{:S(2)}, u32[]{:S(2)}) collective-permute-start(bf16[224,128]{1,0:T(8,128)(2,1)} %get-tuple-element.46), channel_id=1, source_target_pairs={{1,2},{3,4},{5,6},{7,8},{9,10},{11,12},{13,14},{2,1},{4,3},{6,5},{... | collective-permute-start | bytes 172040 | tf_op jit(solution)/shard_map/ppermute | solution.py:541
  13.3 1.0 %copy-start = (bf16[1104,128]{1,0:T(8,128)(2,1)S(1)}, bf16[1104,128]{1,0:T(8,128)(2,1)}, u32[]{:S(2)}) copy-start(bf16[1104,128]{1,0:T(8,128)(2,1)} %get-tuple-element.44.after_ref.own_ref) | copy-start | bytes 847876
  14.3 1.2 %copy-start.2 = (bf16[27,128,128]{2,1,0:T(8,128)(2,1)S(1)}, bf16[27,128,128]{2,1,0:T(8,128)(2,1)}, u32[]{:S(2)}) copy-start(bf16[27,128,128]{2,1,0:T(8,128)(2,1)} %w2_ref.1) | copy-start | bytes 2654212
  15.4 1.1 %copy-start.3 = (bf16[27,96,128]{2,1,0:T(8,128)(2,1)S(1)}, bf16[27,96,128]{2,1,0:T(8,128)(2,1)}, u32[]{:S(2)}) copy-start(bf16[27,96,128]{2,1,0:T(8,128)(2,1)} %w1_ref.1) | copy-start | bytes 1990660
  16.5 2.4 %copy-start.1 = (bf16[1104,128]{1,0:T(8,128)(2,1)S(1)}, bf16[1104,128]{1,0:T(8,128)(2,1)}, u32[]{:S(2)}) copy-start(bf16[1104,128]{1,0:T(8,128)(2,1)} %get-tuple-element.44.after_ref.own_ref) | copy-start | bytes 847876
  16.5 8.5 %copy-start.5 = (bf16[96,64]{1,0:T(8,128)(2,1)S(1)}, bf16[96,64]{1,0:T(8,128)(2,1)}, u32[]{:S(2)}) copy-start(bf16[96,64]{1,0:T(8,128)(2,1)} %constant.2.clone.up_ref) | copy-start | bytes 36868
  19.2 8.4 %collective-permute-start.2 = (bf16[1200,128]{1,0:T(8,128)(2,1)S(1)}, bf16[1200,128]{1,0:T(8,128)(2,1)S(1)}, u32[]{:S(2)}, u32[]{:S(2)}) collective-permute-start(bf16[1200,128]{1,0:T(8,128)(2,1)S(1)} %get-tuple-element.49), channel_id=1, source_target_pairs={{0,16},{32,48},{64,80},{96,112},{16,0},{48,32},{80,64},{112,96},{1... | collective-permute-start | bytes 921608 | tf_op jit(solution)/shard_map/ppermute | solution.py:541
  21.9 8.2 %collective-permute-start.3 = (bf16[1200,128]{1,0:T(8,128)(2,1)S(1)}, bf16[1200,128]{1,0:T(8,128)(2,1)S(1)}, u32[]{:S(2)}, u32[]{:S(2)}) collective-permute-start(bf16[1200,128]{1,0:T(8,128)(2,1)S(1)} %get-tuple-element.51), channel_id=1, source_target_pairs={{16,32},{48,64},{80,96},{32,16},{64,48},{96,80},{17,33},{49,65},{8... | collective-permute-start | bytes 921608 | tf_op jit(solution)/shard_map/ppermute | solution.py:541
  27.6 2.5 %copy-start.4 = (bf16[8,128,128]{2,1,0:T(8,128)(2,1)S(1)}, bf16[8,128,128]{2,1,0:T(8,128)(2,1)}, u32[]{:S(2)}) copy-start(bf16[8,128,128]{2,1,0:T(8,128)(2,1)} %wd_ref.1) | copy-start | bytes 786436
  37.2 2.6 %collective-permute-start.4 = (bf16[3584,128]{1,0:T(8,128)(2,1)S(1)}, bf16[3584,128]{1,0:T(8,128)(2,1)S(1)}, u32[]{:S(2)}, u32[]{:S(2)}) collective-permute-start(bf16[3584,128]{1,0:T(8,128)(2,1)S(1)} %slice_bitcast_fusion), channel_id=1, source_target_pairs={{0,16},{16,0},{1,17},{17,1},{2,18},{18,2},{3,19},{19,3},{4,20},{20... | collective-permute-start | bytes 2752520 | tf_op jit(solution)/shard_map/ppermute | solution.py:545
  40.0 5.4 %collective-permute-start.5 = (bf16[960,128]{1,0:T(8,128)(2,1)S(1)}, bf16[960,128]{1,0:T(8,128)(2,1)S(1)}, u32[]{:S(2)}, u32[]{:S(2)}) collective-permute-start(bf16[960,128]{1,0:T(8,128)(2,1)S(1)} %get-tuple-element.69), channel_id=1, source_target_pairs={{0,4},{1,5},{2,6},{3,7},{4,0},{5,1},{6,2},{7,3},{8,12},{9,13},{10,... | collective-permute-start | bytes 737288 | tf_op jit(solution)/shard_map/ppermute | solution.py:568
  41.1 7.6 %collective-permute-start.6 = (bf16[960,128]{1,0:T(8,128)(2,1)S(1)}, bf16[960,128]{1,0:T(8,128)(2,1)S(1)}, u32[]{:S(2)}, u32[]{:S(2)}) collective-permute-start(bf16[960,128]{1,0:T(8,128)(2,1)S(1)} %get-tuple-element.70), channel_id=1, source_target_pairs={{0,12},{1,13},{2,14},{3,15},{4,8},{5,9},{6,10},{7,11},{8,4},{9,5},... | collective-permute-start | bytes 737288 | tf_op jit(solution)/shard_map/ppermute | solution.py:568
  43.0 7.6 %collective-permute-start.7 = (bf16[960,128]{1,0:T(8,128)(2,1)S(1)}, bf16[960,128]{1,0:T(8,128)(2,1)S(1)}, u32[]{:S(2)}, u32[]{:S(2)}) collective-permute-start(bf16[960,128]{1,0:T(8,128)(2,1)S(1)} %get-tuple-element.71), channel_id=1, source_target_pairs={{0,8},{1,9},{2,10},{3,11},{4,12},{5,13},{6,14},{7,15},{8,0},{9,1},... | collective-permute-start | bytes 737288 | tf_op jit(solution)/shard_map/ppermute | solution.py:568
  50.7 3.5 %collective-permute-start.8 = (bf16[288,128]{1,0:T(8,128)(2,1)S(1)}, bf16[288,128]{1,0:T(8,128)(2,1)S(1)}, u32[]{:S(2)}, u32[]{:S(2)}) collective-permute-start(bf16[288,128]{1,0:T(8,128)(2,1)S(1)} %get-tuple-element.73), channel_id=1, source_target_pairs={{0,1},{1,0},{2,3},{3,2},{4,5},{5,4},{6,7},{7,6},{8,9},{9,8},{10,11... | collective-permute-start | bytes 221192 | tf_op jit(solution)/shard_map/ppermute | solution.py:568
  51.7 4.4 %collective-permute-start.9 = (bf16[288,128]{1,0:T(8,128)(2,1)S(1)}, bf16[288,128]{1,0:T(8,128)(2,1)S(1)}, u32[]{:S(2)}, u32[]{:S(2)}) collective-permute-start(bf16[288,128]{1,0:T(8,128)(2,1)S(1)} %get-tuple-element.74), channel_id=1, source_target_pairs={{0,3},{1,2},{2,1},{3,0},{4,7},{5,6},{6,5},{7,4},{8,11},{9,10},{10,... | collective-permute-start | bytes 221192 | tf_op jit(solution)/shard_map/ppermute | solution.py:568
  53.5 4.7 %collective-permute-start.10 = (bf16[288,128]{1,0:T(8,128)(2,1)S(1)}, bf16[288,128]{1,0:T(8,128)(2,1)S(1)}, u32[]{:S(2)}, u32[]{:S(2)}) collective-permute-start(bf16[288,128]{1,0:T(8,128)(2,1)S(1)} %get-tuple-element.75), channel_id=1, source_target_pairs={{0,2},{1,3},{2,0},{3,1},{4,6},{5,7},{6,4},{7,5},{8,10},{9,11},{10,... | collective-permute-start | bytes 221192 | tf_op jit(solution)/shard_map/ppermute | solution.py:568
  58.2 4.3 %collective-permute-start.13 = (bf16[224,128]{1,0:T(8,128)(2,1)S(1)}, bf16[224,128]{1,0:T(8,128)(2,1)S(1)}, u32[]{:S(2)}, u32[]{:S(2)}) collective-permute-start(bf16[224,128]{1,0:T(8,128)(2,1)S(1)} %get-tuple-element.77), channel_id=1, source_target_pairs={{0,96},{32,64},{64,32},{96,0},{1,97},{33,65},{65,33},{97,1},{2,98}... | collective-permute-start | bytes 172040 | tf_op jit(solution)/shard_map/ppermute | solution.py:557
  60.7 4.5 %collective-permute-start.12 = (bf16[224,128]{1,0:T(8,128)(2,1)S(1)}, bf16[224,128]{1,0:T(8,128)(2,1)S(1)}, u32[]{:S(2)}, u32[]{:S(2)}) collective-permute-start(bf16[224,128]{1,0:T(8,128)(2,1)S(1)} %get-tuple-element.77), channel_id=1, source_target_pairs={{0,64},{32,96},{64,0},{96,32},{1,65},{33,97},{65,1},{97,33},{2,66}... | collective-permute-start | bytes 172040 | tf_op jit(solution)/shard_map/ppermute | solution.py:557
  61.4 3.9 %collective-permute-start.11 = (bf16[224,128]{1,0:T(8,128)(2,1)S(1)}, bf16[224,128]{1,0:T(8,128)(2,1)S(1)}, u32[]{:S(2)}, u32[]{:S(2)}) collective-permute-start(bf16[224,128]{1,0:T(8,128)(2,1)S(1)} %get-tuple-element.77), channel_id=1, source_target_pairs={{0,32},{32,0},{64,96},{96,64},{1,33},{33,1},{65,97},{97,65},{2,34}... | collective-permute-start | bytes 172040 | tf_op jit(solution)/shard_map/ppermute | solution.py:557
  80.2 8.7 %collective-permute-start.14 = (bf16[3584,128]{1,0:T(8,128)(2,1)S(1)}, bf16[3584,128]{1,0:T(8,128)(2,1)S(1)}, u32[]{:S(2)}, u32[]{:S(2)}) collective-permute-start(bf16[3584,128]{1,0:T(8,128)(2,1)S(1)} %bitcast.14), channel_id=1, source_target_pairs={{0,16},{16,0},{1,17},{17,1},{2,18},{18,2},{3,19},{19,3},{4,20},{20... | collective-permute-start | bytes 2752520 | tf_op jit(solution)/shard_map/ppermute | solution.py:545

commit v12 on v11

--- a/solution.py
+++ b/solution.py
@@ -71,7 +71,7 @@
 
 def section(
     near_ref, mid_ref, far_ref, mask_ref, own_ge_ref, place_ref, part1_ref, inner_ref, inner_sg1_ref, part2_ref,
-    near_first_ref, near_sg1_ref, near_second_ref, near_slope_ref, w1_ref, w2_ref, back_ref, wd_ref, up_ref,
+    near_first_ref, near_sg1_ref, near_second_ref, near_slope_ref, near_ge_ref, w1_ref, w2_ref, back_ref, wd_ref, up_ref,
     grads_ref, out_ref,
     sides, first, sg1, second, slopes, ge, g2, gs, vt,
 ):
@@ -142,8 +142,11 @@
             )
         )
 
-    for u in (0, 3):
-        repeat_along_z([cotangent(u, q) for q in range(4)], up_ref, ge, u * 160)
+    for which in range(2):
+        u = 3 * which
+        cots_far = [cotangent(u, q) for q in range(4)]
+        pl.when(core == which)(functools.partial(repeat_along_z, cots_far, up_ref, ge, u * 160))
+    ge[pl.ds(pl.multiple_of((1 - core) * 480, 16), 160), :] = near_ge_ref[...]
     ge[160:480, :] = own_ge_ref[...]
 
     for x in range(6):
@@ -267,8 +270,8 @@
 
 
 def near_side(
-    near_ref, mask_ref, part1_ref, inner_ref, part2_ref, w1_ref, w2_ref,
-    first_ref, sg1_ref, second_ref, slope_ref,
+    near_ref, mask_ref, part1_ref, inner_ref, part2_ref, w1_ref, w2_ref, up_ref,
+    first_ref, sg1_ref, second_ref, slope_ref, ge_ref,
 ):
     def run(high):
         base = 5 if high else 0
@@ -299,6 +302,8 @@
             put(second_ref, Y * Z, 2 if high else 0), put(slope_ref, 18 * Z, 3 if high else 0),
         )
 
+    cots = [near_ref[COTS + q * 32 : COTS + (q + 1) * 32, :] for q in range(4)]
+    repeat_along_z(cots, up_ref, ge_ref, 0)
     for core in range(2):
         pl.when(lax.axis_index("c") == core)(functools.partial(run, core == 0))
 
@@ -612,8 +617,8 @@
     part1, inner, _, part2 = ahead
     beside = call(
         near_side,
-        [((60 * Z, C), BF), ((Y * Z, C), F32), ((2 * Y * Z, C), BF), ((3 * 18 * Z, C), F32)],
-        (near, mask, part1, inner, part2, w1, w2),
+        [((60 * Z, C), BF), ((Y * Z, C), F32), ((2 * Y * Z, C), BF), ((3 * 18 * Z, C), F32), ((160, 2 * C), BF)],
+        (near, mask, part1, inner, part2, w1, w2, up_matrix()),
         flops=3_000_000_000,
     )
     grads, outgoing = call(

time: 90.7 us -> 90.7 us (level)
  no operation moved by 1% of the time
where the time goes in v12:
time: 90.7 us; the launch traced here: 90.3 us
  starting transfers between devices  33.8 us (37%)
  waiting for transfers between devices  19.2 us (21%)
  Pallas kernels  17.4 us (19%)
  blocking collectives  14.8 us (16%)
  local copies, waits for them, and re-layouts  4.08 us (4%)
  between operations  0.98 us (1%)
    pallas_call x11, Pallas kernels, call(): pl.pallas_call(kernel, out_shape=tuple((jax.ShapeDtypeStruct(shape, dtype...  17.4 us
    all_to_all x1, blocking collectives, per_device(): lax.all_to_all(jnp.broadcast_to(part[None], (16, PART, C)), GY, 0, 0, til...  14.8 us
    ppermute x6, waiting for transfers between devices, flip_by_core(): return lax.ppermute(v, every, pairs)  10.4 us
    all_to_all x1, starting transfers between devices, per_device(): rows = lax.all_to_all(rows, GY, 0, 0, tiled=True)  8.44 us
    ppermute x4, starting transfers between devices, swap(): return lax.ppermute(v, axes, pairs + [(j, i) for i, j in pairs])  7.81 us
    ppermute x6, starting transfers between devices, flip_by_core(): return lax.ppermute(v, every, pairs)  7.59 us
    ppermute x2, starting transfers between devices, swap_cores(): return lax.ppermute(v, 'c', [(0, 1), (1, 0)])  6.63 us
    ppermute x3, waiting for transfers between devices, flip(): lax.ppermute(v, axis, [(i, i ^ bits) for i in range(lax.axis_size(axis))])  3.68 us
  transfers between devices with their start and end apart: 16, of which 11 were waited for; matrix products, arithmetic and copies ran while one was open for 1% of the time, Pallas kernels for 7%

profile of v12, /device:TPU:1, one launch (start us, length us, event | category | flops | bytes accessed | tf_op | source)
XLA Modules:
  0.0 90.3 jit_solution(18235401360351927653)
XLA Ops:
  0.6 2.2 %shard_map.129 = (bf16[128,1024]{1,0:T(8,128)(2,1)}, bf16[1104,128]{1,0:T(8,128)(2,1)}, bf16[224,128]{1,0:T(8,128)(2,1)}, bf16[224,128]{1,0:T(8,128)(2,1)}) custom-call(bf16[1,1,32,1024]{3,2,1,0:T(8,128)(2,1)} %grad_hbm.1, bf16[4,16,1536]{2,1,0:T(8,128)(2,1)} %feat_hbm.1, s32[1,4,4]{2,1,0:T(4,128)} %blocks_hbm.1, s32[1,16]{1,0:T(1,128)} %bitcast.22), custom_call_target="tpu_custom_call" | custom-call | flops 10000000 | bytes 1000000 | tf_op jit(solution)/shard_map/pallas_call | solution.py:224
  2.8 8.4 %all-to-all-start = ((bf16[16,8,1024]{2,1,0:T(8,128)(2,1)}), bf16[16,8,1024]{2,1,0:T(8,128)(2,1)S(1)}, u32[]{:S(2)}, u32[]{:S(2)}) async-start(bf16[16,8,1024]{2,1,0:T(8,128)(2,1)} %bitcast.21), calls=%async_computation | async-start | bytes 524288 | tf_op jit(solution)/shard_map/all_to_all | solution.py:599
  11.3 1.4 %collective-permute-start = (bf16[224,128]{1,0:T(8,128)(2,1)}, bf16[224,128]{1,0:T(8,128)(2,1)S(1)}, u32[]{:S(2)}, u32[]{:S(2)}) collective-permute-start(bf16[224,128]{1,0:T(8,128)(2,1)} %get-tuple-element.46), channel_id=1, source_target_pairs={{0,1},{2,3},{4,5},{6,7},{8,9},{10,11},{12,13},{14,15},{1,0},{3,2},... | collective-permute-start | bytes 172040 | tf_op jit(solution)/shard_map/ppermute | solution.py:546
  12.6 0.7 collective-permute-start.1
  13.3 0.0 copy-start
  13.3 0.9 %copy-done = bf16[1104,128]{1,0:T(8,128)(2,1)S(1)} copy-done((bf16[1104,128]{1,0:T(8,128)(2,1)S(1)}, bf16[1104,128]{1,0:T(8,128)(2,1)}, u32[]{:S(2)}) %copy-start) | copy-done | bytes 282648
  14.3 0.0 copy-start.2
  14.3 1.2 %copy-done.2 = bf16[27,128,128]{2,1,0:T(8,128)(2,1)S(1)} copy-done((bf16[27,128,128]{2,1,0:T(8,128)(2,1)S(1)}, bf16[27,128,128]{2,1,0:T(8,128)(2,1)}, u32[]{:S(2)}) %copy-start.2) | copy-done | bytes 884760
  15.4 0.0 copy-start.3
  15.4 1.1 %copy-done.3 = bf16[27,96,128]{2,1,0:T(8,128)(2,1)S(1)} copy-done((bf16[27,96,128]{2,1,0:T(8,128)(2,1)S(1)}, bf16[27,96,128]{2,1,0:T(8,128)(2,1)}, u32[]{:S(2)}) %copy-start.3) | copy-done | bytes 663576
  16.5 0.0 copy-start.1
  16.5 0.0 copy-start.5
  16.5 0.4 shard_map.130
  16.9 0.0 collective-permute-done.beside_ref
  16.9 0.0 collective-permute-done.1.beyond_ref
  16.9 2.0 %all-to-all-done = bf16[16,8,1024]{2,1,0:T(8,128)(2,1)S(1)} async-done(((bf16[16,8,1024]{2,1,0:T(8,128)(2,1)}), bf16[16,8,1024]{2,1,0:T(8,128)(2,1)S(1)}, u32[]{:S(2)}, u32[]{:S(2)}) %all-to-all-start) | async-done | bytes 262176 | tf_op jit(solution)/shard_map/all_to_all | solution.py:599
  18.9 0.0 copy-done.1
  18.9 0.3 shard_map.131
  19.2 2.7 %collective-permute-start.2 = (bf16[1200,128]{1,0:T(8,128)(2,1)S(1)}, bf16[1200,128]{1,0:T(8,128)(2,1)S(1)}, u32[]{:S(2)}, u32[]{:S(2)}) collective-permute-start(bf16[1200,128]{1,0:T(8,128)(2,1)S(1)} %get-tuple-element.50), channel_id=1, source_target_pairs={{0,16},{32,48},{64,80},{96,112},{16,0},{48,32},{80,64},{112,96},{1... | collective-permute-start | bytes 921608 | tf_op jit(solution)/shard_map/ppermute | solution.py:546
  21.9 3.1 %collective-permute-start.3 = (bf16[1200,128]{1,0:T(8,128)(2,1)S(1)}, bf16[1200,128]{1,0:T(8,128)(2,1)S(1)}, u32[]{:S(2)}, u32[]{:S(2)}) collective-permute-start(bf16[1200,128]{1,0:T(8,128)(2,1)S(1)} %get-tuple-element.52), channel_id=1, source_target_pairs={{16,32},{48,64},{80,96},{32,16},{64,48},{96,80},{17,33},{49,65},{8... | collective-permute-start | bytes 921608 | tf_op jit(solution)/shard_map/ppermute | solution.py:546
  25.0 0.0 copy-done.5
  25.0 2.5 %shard_map.132 = (f32[4,320,128]{2,1,0:T(8,128)S(1)}, bf16[640,128]{1,0:T(8,128)(2,1)S(1)}, f32[512,128]{1,0:T(8,128)S(1)}, f32[4,288,128]{2,1,0:T(8,128)S(1)}, bf16[320,256]{1,0:T(8,128)(2,1)S(1)}) custom-call(bf16[1408,128]{1,0:T(8,128)(2,1)S(1)} %get-tuple-element.51.mid_ref, bf16[16,128]{1,0:T(8,128)(2,1)S(1)} %get-tuple-element.53.mask_ref, ...), custom_call_target="tpu_custom_call" | custom-call | flops 3000000000 | bytes 1000000 | tf_op jit(solution)/shard_map/pallas_call | solution.py:224
  27.6 0.0 collective-permute-done.2.near_ref
  27.6 0.0 copy-start.4
  27.6 2.0 %shard_map.133 = (bf16[960,128]{1,0:T(8,128)(2,1)S(1)}, f32[256,128]{1,0:T(8,128)S(1)}, bf16[512,128]{1,0:T(8,128)(2,1)S(1)}, f32[864,128]{1,0:T(8,128)S(1)}, bf16[160,256]{1,0:T(8,128)(2,1)S(1)}) custom-call(bf16[1200,128]{1,0:T(8,128)(2,1)S(1)} %collective-permute-done.2.near_ref, bf16[16,128]{1,0:T(8,128)(2,1)S(1)} %get-tuple-element.53.mask_ref, ...), custom_call_target="tpu_custom_call" | custom-call | flops 3000000000 | bytes 1000000 | tf_op jit(solution)/shard_map/pallas_call | solution.py:224
  29.5 0.5 collective-permute-done.3.far_ref
  30.0 0.0 copy-done.4
  30.1 7.1 %shard_map.134 = (bf16[2,3584,128]{2,1,0:T(8,128)(2,1)S(1)}, bf16[256,128]{1,0:T(8,128)(2,1)S(1)}) custom-call(bf16[1200,128]{1,0:T(8,128)(2,1)S(1)} %collective-permute-done.2.near_ref, bf16[1408,128]{1,0:T(8,128)(2,1)S(1)} %get-tuple-element.51.mid_ref, bf16[1200,128]{1,0:T(8,128)(2,1)S(1)} %collective-permute-done.3.far_ref, ...), custom_call_target="tpu_custom_call" | custom-call | flops 8000000000 | bytes 1000000 | tf_op jit(solution)/shard_map/pallas_call | solution.py:224
  37.2 0.1 slice_bitcast_fusion
  37.3 0.1 collective-permute-start.4
  37.4 2.5 %collective-permute-done.4.theirs_ref = bf16[3584,128]{1,0:T(8,128)(2,1)S(1)} collective-permute-done((bf16[3584,128]{1,0:T(8,128)(2,1)S(1)}, bf16[3584,128]{1,0:T(8,128)(2,1)S(1)}, u32[]{:S(2)}, u32[]{:S(2)}) %collective-permute-start.4) | collective-permute-done | bytes 917536 | tf_op jit(solution)/shard_map/ppermute | solution.py:550
  39.8 0.2 shard_map.135
  40.0 1.1 %collective-permute-start.5 = (bf16[960,128]{1,0:T(8,128)(2,1)S(1)}, bf16[960,128]{1,0:T(8,128)(2,1)S(1)}, u32[]{:S(2)}, u32[]{:S(2)}) collective-permute-start(bf16[960,128]{1,0:T(8,128)(2,1)S(1)} %get-tuple-element.71), channel_id=1, source_target_pairs={{0,4},{1,5},{2,6},{3,7},{4,0},{5,1},{6,2},{7,3},{8,12},{9,13},{10,... | collective-permute-start | bytes 737288 | tf_op jit(solution)/shard_map/ppermute | solution.py:573
  41.2 1.8 %collective-permute-start.6 = (bf16[960,128]{1,0:T(8,128)(2,1)S(1)}, bf16[960,128]{1,0:T(8,128)(2,1)S(1)}, u32[]{:S(2)}, u32[]{:S(2)}) collective-permute-start(bf16[960,128]{1,0:T(8,128)(2,1)S(1)} %get-tuple-element.72), channel_id=1, source_target_pairs={{0,12},{1,13},{2,14},{3,15},{4,8},{5,9},{6,10},{7,11},{8,4},{9,5},... | collective-permute-start | bytes 737288 | tf_op jit(solution)/shard_map/ppermute | solution.py:573
  43.0 1.1 %collective-permute-start.7 = (bf16[960,128]{1,0:T(8,128)(2,1)S(1)}, bf16[960,128]{1,0:T(8,128)(2,1)S(1)}, u32[]{:S(2)}, u32[]{:S(2)}) collective-permute-start(bf16[960,128]{1,0:T(8,128)(2,1)S(1)} %get-tuple-element.73), channel_id=1, source_target_pairs={{0,8},{1,9},{2,10},{3,11},{4,12},{5,13},{6,14},{7,15},{8,0},{9,1},... | collective-permute-start | bytes 737288 | tf_op jit(solution)/shard_map/ppermute | solution.py:573
  44.1 1.4 %collective-permute-done.5.refs_1_ = bf16[960,128]{1,0:T(8,128)(2,1)S(1)} collective-permute-done((bf16[960,128]{1,0:T(8,128)(2,1)S(1)}, bf16[960,128]{1,0:T(8,128)(2,1)S(1)}, u32[]{:S(2)}, u32[]{:S(2)}) %collective-permute-start.5) | collective-permute-done | bytes 245792 | tf_op jit(solution)/shard_map/ppermute | solution.py:573
  45.5 3.3 %collective-permute-done.6.refs_2_ = bf16[960,128]{1,0:T(8,128)(2,1)S(1)} collective-permute-done((bf16[960,128]{1,0:T(8,128)(2,1)S(1)}, bf16[960,128]{1,0:T(8,128)(2,1)S(1)}, u32[]{:S(2)}, u32[]{:S(2)}) %collective-permute-start.6) | collective-permute-done | bytes 245792 | tf_op jit(solution)/shard_map/ppermute | solution.py:573
  48.8 1.8 %collective-permute-done.7.refs_3_ = bf16[960,128]{1,0:T(8,128)(2,1)S(1)} collective-permute-done((bf16[960,128]{1,0:T(8,128)(2,1)S(1)}, bf16[960,128]{1,0:T(8,128)(2,1)S(1)}, u32[]{:S(2)}, u32[]{:S(2)}) %collective-permute-start.7) | collective-permute-done | bytes 245792 | tf_op jit(solution)/shard_map/ppermute | solution.py:573
  50.6 0.1 shard_map.136
  50.7 1.0 %collective-permute-start.8 = (bf16[288,128]{1,0:T(8,128)(2,1)S(1)}, bf16[288,128]{1,0:T(8,128)(2,1)S(1)}, u32[]{:S(2)}, u32[]{:S(2)}) collective-permute-start(bf16[288,128]{1,0:T(8,128)(2,1)S(1)} %get-tuple-element.75), channel_id=1, source_target_pairs={{0,1},{1,0},{2,3},{3,2},{4,5},{5,4},{6,7},{7,6},{8,9},{9,8},{10,11... | collective-permute-start | bytes 221192 | tf_op jit(solution)/shard_map/ppermute | solution.py:573
  51.7 1.8 %collective-permute-start.9 = (bf16[288,128]{1,0:T(8,128)(2,1)S(1)}, bf16[288,128]{1,0:T(8,128)(2,1)S(1)}, u32[]{:S(2)}, u32[]{:S(2)}) collective-permute-start(bf16[288,128]{1,0:T(8,128)(2,1)S(1)} %get-tuple-element.76), channel_id=1, source_target_pairs={{0,3},{1,2},{2,1},{3,0},{4,7},{5,6},{6,5},{7,4},{8,11},{9,10},{10,... | collective-permute-start | bytes 221192 | tf_op jit(solution)/shard_map/ppermute | solution.py:573
  53.5 0.8 collective-permute-start.10
  54.2 0.0 collective-permute-done.8.refs_1_
  54.3 1.9 %collective-permute-done.9.refs_2_ = bf16[288,128]{1,0:T(8,128)(2,1)S(1)} collective-permute-done((bf16[288,128]{1,0:T(8,128)(2,1)S(1)}, bf16[288,128]{1,0:T(8,128)(2,1)S(1)}, u32[]{:S(2)}, u32[]{:S(2)}) %collective-permute-start.9) | collective-permute-done | bytes 73760 | tf_op jit(solution)/shard_map/ppermute | solution.py:573
  56.1 2.1 %collective-permute-done.10.refs_3_ = bf16[288,128]{1,0:T(8,128)(2,1)S(1)} collective-permute-done((bf16[288,128]{1,0:T(8,128)(2,1)S(1)}, bf16[288,128]{1,0:T(8,128)(2,1)S(1)}, u32[]{:S(2)}, u32[]{:S(2)}) %collective-permute-start.10) | collective-permute-done | bytes 73760 | tf_op jit(solution)/shard_map/ppermute | solution.py:573
  58.2 2.5 %collective-permute-start.13 = (bf16[224,128]{1,0:T(8,128)(2,1)S(1)}, bf16[224,128]{1,0:T(8,128)(2,1)S(1)}, u32[]{:S(2)}, u32[]{:S(2)}) collective-permute-start(bf16[224,128]{1,0:T(8,128)(2,1)S(1)} %get-tuple-element.79), channel_id=1, source_target_pairs={{0,96},{32,64},{64,32},{96,0},{1,97},{33,65},{65,33},{97,1},{2,98}... | collective-permute-start | bytes 172040 | tf_op jit(solution)/shard_map/ppermute | solution.py:562
  60.7 0.7 collective-permute-start.12
  61.4 0.2 collective-permute-start.11
  61.6 1.0 %collective-permute-done.13 = bf16[224,128]{1,0:T(8,128)(2,1)S(1)} collective-permute-done((bf16[224,128]{1,0:T(8,128)(2,1)S(1)}, bf16[224,128]{1,0:T(8,128)(2,1)S(1)}, u32[]{:S(2)}, u32[]{:S(2)}) %collective-permute-start.13) | collective-permute-done | bytes 57376 | tf_op jit(solution)/shard_map/ppermute | solution.py:562
  62.6 2.7 %collective-permute-done.12 = bf16[224,128]{1,0:T(8,128)(2,1)S(1)} collective-permute-done((bf16[224,128]{1,0:T(8,128)(2,1)S(1)}, bf16[224,128]{1,0:T(8,128)(2,1)S(1)}, u32[]{:S(2)}, u32[]{:S(2)}) %collective-permute-start.12) | collective-permute-done | bytes 57376 | tf_op jit(solution)/shard_map/ppermute | solution.py:562
  65.3 0.0 collective-permute-done.11
  65.3 0.1 broadcast_in_dim.2
  65.4 14.8 %all_to_all.16 = bf16[16,224,128]{2,1,0:T(8,128)(2,1)S(1)} all-to-all(bf16[16,224,128]{2,1,0:T(8,128)(2,1)S(1)} %broadcast_in_dim.2), channel_id=1, replica_groups=mesh['y'=4,'c'=2,'z'=4,'x'=4] {'z','x'}, dimensions={0} | all-to-all | bytes 1835008 | tf_op jit(solution)/shard_map/all_to_all | solution.py:654
  80.2 6.5 %collective-permute-start.14 = (bf16[3584,128]{1,0:T(8,128)(2,1)S(1)}, bf16[3584,128]{1,0:T(8,128)(2,1)S(1)}, u32[]{:S(2)}, u32[]{:S(2)}) collective-permute-start(bf16[3584,128]{1,0:T(8,128)(2,1)S(1)} %bitcast.14), channel_id=1, source_target_pairs={{0,16},{16,0},{1,17},{17,1},{2,18},{18,2},{3,19},{19,3},{4,20},{20... | collective-permute-start | bytes 2752520 | tf_op jit(solution)/shard_map/ppermute | solution.py:550
  86.8 0.7 reshape.34
  87.4 1.3 %shard_map.138 = (f32[2592,128]{1,0:T(8,128)}, f32[3456,128]{1,0:T(8,128)}, f32[1024,128]{1,0:T(8,128)}) custom-call(bf16[3584,128]{1,0:T(8,128)(2,1)S(1)} %bitcast.15), custom_call_target="tpu_custom_call" | custom-call | flops 10000000 | bytes 1000000 | tf_op jit(solution)/shard_map/pallas_call | solution.py:224
  88.7 0.1 collective-permute-done.14.half_ref
  88.9 1.3 %shard_map.139 = (f32[2592,128]{1,0:T(8,128)}, f32[3456,128]{1,0:T(8,128)}, f32[1024,128]{1,0:T(8,128)}) custom-call(bf16[3584,128]{1,0:T(8,128)(2,1)S(1)} %collective-permute-done.14.half_ref, f32[2592,128]{1,0:T(8,128)} %get-tuple-element.80.a, f32[3456,128]{1,0:T(8,128)} %get-tuple-element.81.b, ...), custom_call_target="tpu_custom_call", output_to_operand_aliasing={{0}: (1, {}), {1}: (2, {}), {2}: (3, {})} | custom-call | flops 10000000 | bytes 1000000 | tf_op jit(solution)/shard_map/pallas_call | solution.py:224
  (3 shorter events, 0.1 us)
Async XLA Ops:
  2.8 16.1 %all-to-all-start = ((bf16[16,8,1024]{2,1,0:T(8,128)(2,1)}), bf16[16,8,1024]{2,1,0:T(8,128)(2,1)S(1)}, u32[]{:S(2)}, u32[]{:S(2)}) async-start(bf16[16,8,1024]{2,1,0:T(8,128)(2,1)} %bitcast.21), calls=%async_computation | async-start | bytes 524288 | tf_op jit(solution)/shard_map/all_to_all | solution.py:599
  11.3 5.6 %collective-permute-start = (bf16[224,128]{1,0:T(8,128)(2,1)}, bf16[224,128]{1,0:T(8,128)(2,1)S(1)}, u32[]{:S(2)}, u32[]{:S(2)}) collective-permute-start(bf16[224,128]{1,0:T(8,128)(2,1)} %get-tuple-element.46), channel_id=1, source_target_pairs={{0,1},{2,3},{4,5},{6,7},{8,9},{10,11},{12,13},{14,15},{1,0},{3,2},... | collective-permute-start | bytes 172040 | tf_op jit(solution)/shard_map/ppermute | solution.py:546
  12.6 4.3 %collective-permute-start.1 = (bf16[224,128]{1,0:T(8,128)(2,1)}, bf16[224,128]{1,0:T(8,128)(2,1)S(1)}, u32[]{:S(2)}, u32[]{:S(2)}) collective-permute-start(bf16[224,128]{1,0:T(8,128)(2,1)} %get-tuple-element.47), channel_id=1, source_target_pairs={{1,2},{3,4},{5,6},{7,8},{9,10},{11,12},{13,14},{2,1},{4,3},{6,5},{... | collective-permute-start | bytes 172040 | tf_op jit(solution)/shard_map/ppermute | solution.py:546
  13.3 1.0 %copy-start = (bf16[1104,128]{1,0:T(8,128)(2,1)S(1)}, bf16[1104,128]{1,0:T(8,128)(2,1)}, u32[]{:S(2)}) copy-start(bf16[1104,128]{1,0:T(8,128)(2,1)} %get-tuple-element.45.after_ref.own_ref) | copy-start | bytes 847876
  14.3 1.2 %copy-start.2 = (bf16[27,128,128]{2,1,0:T(8,128)(2,1)S(1)}, bf16[27,128,128]{2,1,0:T(8,128)(2,1)}, u32[]{:S(2)}) copy-start(bf16[27,128,128]{2,1,0:T(8,128)(2,1)} %w2_ref.1) | copy-start | bytes 2654212
  15.4 1.1 %copy-start.3 = (bf16[27,96,128]{2,1,0:T(8,128)(2,1)S(1)}, bf16[27,96,128]{2,1,0:T(8,128)(2,1)}, u32[]{:S(2)}) copy-start(bf16[27,96,128]{2,1,0:T(8,128)(2,1)} %w1_ref.1) | copy-start | bytes 1990660
  16.5 2.4 %copy-start.1 = (bf16[1104,128]{1,0:T(8,128)(2,1)S(1)}, bf16[1104,128]{1,0:T(8,128)(2,1)}, u32[]{:S(2)}) copy-start(bf16[1104,128]{1,0:T(8,128)(2,1)} %get-tuple-element.45.after_ref.own_ref) | copy-start | bytes 847876
  16.5 8.5 %copy-start.5 = (bf16[96,64]{1,0:T(8,128)(2,1)S(1)}, bf16[96,64]{1,0:T(8,128)(2,1)}, u32[]{:S(2)}) copy-start(bf16[96,64]{1,0:T(8,128)(2,1)} %constant.2.clone.up_ref) | copy-start | bytes 36868
  19.2 8.4 %collective-permute-start.2 = (bf16[1200,128]{1,0:T(8,128)(2,1)S(1)}, bf16[1200,128]{1,0:T(8,128)(2,1)S(1)}, u32[]{:S(2)}, u32[]{:S(2)}) collective-permute-start(bf16[1200,128]{1,0:T(8,128)(2,1)S(1)} %get-tuple-element.50), channel_id=1, source_target_pairs={{0,16},{32,48},{64,80},{96,112},{16,0},{48,32},{80,64},{112,96},{1... | collective-permute-start | bytes 921608 | tf_op jit(solution)/shard_map/ppermute | solution.py:546
  21.9 8.2 %collective-permute-start.3 = (bf16[1200,128]{1,0:T(8,128)(2,1)S(1)}, bf16[1200,128]{1,0:T(8,128)(2,1)S(1)}, u32[]{:S(2)}, u32[]{:S(2)}) collective-permute-start(bf16[1200,128]{1,0:T(8,128)(2,1)S(1)} %get-tuple-element.52), channel_id=1, source_target_pairs={{16,32},{48,64},{80,96},{32,16},{64,48},{96,80},{17,33},{49,65},{8... | collective-permute-start | bytes 921608 | tf_op jit(solution)/shard_map/ppermute | solution.py:546
  27.6 2.5 %copy-start.4 = (bf16[8,128,128]{2,1,0:T(8,128)(2,1)S(1)}, bf16[8,128,128]{2,1,0:T(8,128)(2,1)}, u32[]{:S(2)}) copy-start(bf16[8,128,128]{2,1,0:T(8,128)(2,1)} %wd_ref.1) | copy-start | bytes 786436
  37.3 2.6 %collective-permute-start.4 = (bf16[3584,128]{1,0:T(8,128)(2,1)S(1)}, bf16[3584,128]{1,0:T(8,128)(2,1)S(1)}, u32[]{:S(2)}, u32[]{:S(2)}) collective-permute-start(bf16[3584,128]{1,0:T(8,128)(2,1)S(1)} %slice_bitcast_fusion), channel_id=1, source_target_pairs={{0,16},{16,0},{1,17},{17,1},{2,18},{18,2},{3,19},{19,3},{4,20},{20... | collective-permute-start | bytes 2752520 | tf_op jit(solution)/shard_map/ppermute | solution.py:550
  40.0 5.4 %collective-permute-start.5 = (bf16[960,128]{1,0:T(8,128)(2,1)S(1)}, bf16[960,128]{1,0:T(8,128)(2,1)S(1)}, u32[]{:S(2)}, u32[]{:S(2)}) collective-permute-start(bf16[960,128]{1,0:T(8,128)(2,1)S(1)} %get-tuple-element.71), channel_id=1, source_target_pairs={{0,4},{1,5},{2,6},{3,7},{4,0},{5,1},{6,2},{7,3},{8,12},{9,13},{10,... | collective-permute-start | bytes 737288 | tf_op jit(solution)/shard_map/ppermute | solution.py:573
  41.2 7.6 %collective-permute-start.6 = (bf16[960,128]{1,0:T(8,128)(2,1)S(1)}, bf16[960,128]{1,0:T(8,128)(2,1)S(1)}, u32[]{:S(2)}, u32[]{:S(2)}) collective-permute-start(bf16[960,128]{1,0:T(8,128)(2,1)S(1)} %get-tuple-element.72), channel_id=1, source_target_pairs={{0,12},{1,13},{2,14},{3,15},{4,8},{5,9},{6,10},{7,11},{8,4},{9,5},... | collective-permute-start | bytes 737288 | tf_op jit(solution)/shard_map/ppermute | solution.py:573
  43.0 7.6 %collective-permute-start.7 = (bf16[960,128]{1,0:T(8,128)(2,1)S(1)}, bf16[960,128]{1,0:T(8,128)(2,1)S(1)}, u32[]{:S(2)}, u32[]{:S(2)}) collective-permute-start(bf16[960,128]{1,0:T(8,128)(2,1)S(1)} %get-tuple-element.73), channel_id=1, source_target_pairs={{0,8},{1,9},{2,10},{3,11},{4,12},{5,13},{6,14},{7,15},{8,0},{9,1},... | collective-permute-start | bytes 737288 | tf_op jit(solution)/shard_map/ppermute | solution.py:573
  50.7 3.5 %collective-permute-start.8 = (bf16[288,128]{1,0:T(8,128)(2,1)S(1)}, bf16[288,128]{1,0:T(8,128)(2,1)S(1)}, u32[]{:S(2)}, u32[]{:S(2)}) collective-permute-start(bf16[288,128]{1,0:T(8,128)(2,1)S(1)} %get-tuple-element.75), channel_id=1, source_target_pairs={{0,1},{1,0},{2,3},{3,2},{4,5},{5,4},{6,7},{7,6},{8,9},{9,8},{10,11... | collective-permute-start | bytes 221192 | tf_op jit(solution)/shard_map/ppermute | solution.py:573
  51.7 4.4 %collective-permute-start.9 = (bf16[288,128]{1,0:T(8,128)(2,1)S(1)}, bf16[288,128]{1,0:T(8,128)(2,1)S(1)}, u32[]{:S(2)}, u32[]{:S(2)}) collective-permute-start(bf16[288,128]{1,0:T(8,128)(2,1)S(1)} %get-tuple-element.76), channel_id=1, source_target_pairs={{0,3},{1,2},{2,1},{3,0},{4,7},{5,6},{6,5},{7,4},{8,11},{9,10},{10,... | collective-permute-start | bytes 221192 | tf_op jit(solution)/shard_map/ppermute | solution.py:573
  53.5 4.7 %collective-permute-start.10 = (bf16[288,128]{1,0:T(8,128)(2,1)S(1)}, bf16[288,128]{1,0:T(8,128)(2,1)S(1)}, u32[]{:S(2)}, u32[]{:S(2)}) collective-permute-start(bf16[288,128]{1,0:T(8,128)(2,1)S(1)} %get-tuple-element.77), channel_id=1, source_target_pairs={{0,2},{1,3},{2,0},{3,1},{4,6},{5,7},{6,4},{7,5},{8,10},{9,11},{10,... | collective-permute-start | bytes 221192 | tf_op jit(solution)/shard_map/ppermute | solution.py:573
  58.2 4.3 %collective-permute-start.13 = (bf16[224,128]{1,0:T(8,128)(2,1)S(1)}, bf16[224,128]{1,0:T(8,128)(2,1)S(1)}, u32[]{:S(2)}, u32[]{:S(2)}) collective-permute-start(bf16[224,128]{1,0:T(8,128)(2,1)S(1)} %get-tuple-element.79), channel_id=1, source_target_pairs={{0,96},{32,64},{64,32},{96,0},{1,97},{33,65},{65,33},{97,1},{2,98}... | collective-permute-start | bytes 172040 | tf_op jit(solution)/shard_map/ppermute | solution.py:562
  60.7 4.5 %collective-permute-start.12 = (bf16[224,128]{1,0:T(8,128)(2,1)S(1)}, bf16[224,128]{1,0:T(8,128)(2,1)S(1)}, u32[]{:S(2)}, u32[]{:S(2)}) collective-permute-start(bf16[224,128]{1,0:T(8,128)(2,1)S(1)} %get-tuple-element.79), channel_id=1, source_target_pairs={{0,64},{32,96},{64,0},{96,32},{1,65},{33,97},{65,1},{97,33},{2,66}... | collective-permute-start | bytes 172040 | tf_op jit(solution)/shard_map/ppermute | solution.py:562
  61.4 3.9 %collective-permute-start.11 = (bf16[224,128]{1,0:T(8,128)(2,1)S(1)}, bf16[224,128]{1,0:T(8,128)(2,1)S(1)}, u32[]{:S(2)}, u32[]{:S(2)}) collective-permute-start(bf16[224,128]{1,0:T(8,128)(2,1)S(1)} %get-tuple-element.79), channel_id=1, source_target_pairs={{0,32},{32,0},{64,96},{96,64},{1,33},{33,1},{65,97},{97,65},{2,34}... | collective-permute-start | bytes 172040 | tf_op jit(solution)/shard_map/ppermute | solution.py:562
  80.2 8.6 %collective-permute-start.14 = (bf16[3584,128]{1,0:T(8,128)(2,1)S(1)}, bf16[3584,128]{1,0:T(8,128)(2,1)S(1)}, u32[]{:S(2)}, u32[]{:S(2)}) collective-permute-start(bf16[3584,128]{1,0:T(8,128)(2,1)S(1)} %bitcast.14), channel_id=1, source_target_pairs={{0,16},{16,0},{1,17},{17,1},{2,18},{18,2},{3,19},{19,3},{4,20},{20... | collective-permute-start | bytes 2752520 | tf_op jit(solution)/shard_map/ppermute | solution.py:550
